TPU v7x, 256 devices: a whole 4x4x8 slice. The times are simulated.
256 devices in a mesh: tile: 128 (over z, x, y), pos: 2 (over core).
Axes of the slice: x: 4, y: 4, z: 8, core: 2. Of those that a mesh axis runs over, the one named last changes fastest.
Arguments:
- object_field: float32 [2, 16384, 1024], P(None, 'tile'), may hold values from -10 to 10
- probe_field: float32 [2, 128, 128], replicated, may hold values from -4 to 4
- amplitudes: float32 [128, 2, 32, 128, 128], P('tile', 'pos'), may hold values from 0 to 2
- scan_rows: int32 [128, 2, 32], P('tile', 'pos'), may hold values from 0 to 127
- scan_cols: int32 [128, 2, 32], P('tile', 'pos'), may hold values from 0 to 1023
- live_count: int32 [128, 2], P('tile', 'pos'), may hold values from 8 to 32, as said below
Outputs:
- object_out: float32 [2, 16384, 1024], P(None, 'tile')
- probe_out: float32 [2, 128, 128], replicated
Inputs may be any that keep to these rules, and one draw needn't show every extreme that they name: Slot j of device (t, p) holds a scan position exactly when j < live_count[t, p]; some device holds 32.
All inputs are finite; a program needn't handle non-finite values.
Results may differ from a plain program's by a relative error of at most 0.0003.
Values sent between devices are 32-bit elements; how exact they have to be, the bound alone decides.
No kernel may reach another device: no remote copies, remote signals or barrier semaphores. Data moves between devices by JAX's collectives and lax.ppermute only.
A program may use at most 64 MiB of HBM per device.

v0:
```python
import math

import jax
import jax.numpy as jnp
from jax import lax
from jax.sharding import Mesh
from jax.sharding import PartitionSpec as P

PATCH = 128
STRIP = 128
COLS = 1024
ITERS = 2
TILE = ("tile_0", "tile_1", "tile_2")
TILE_POS = ("tile_0", "tile_1", "tile_2", "pos")


MODULUS_FLOOR = 0.2
OBJECT_RELAX = 1.0
HIGHEST = lax.Precision.HIGHEST


def partner(value, axis, apart):
    return lax.ppermute(value, axis, [(i, i ^ 1 << apart) for i in range(lax.axis_size(axis))])


def from_behind(block, axis, distance):
    devices = range(lax.axis_size(axis))
    route = [((i - distance) % len(devices), i) for i in devices]
    return lax.ppermute(block, axis, route)


def sent_to_all(value, axis):
    count = lax.axis_size(axis)
    return lax.all_to_all(
        jnp.broadcast_to(value[None], (count, *value.shape)), axis, 0, 0, tiled=True
    )


def in_order(pieces, dim):
    pieces = jnp.moveaxis(pieces, 0, dim)
    dims = pieces.shape
    return pieces.reshape(*dims[:dim], dims[dim] * dims[dim + 1], *dims[dim + 2 :])


def gathered_copies(value, axis, dim):
    pieces = sent_to_all(value, axis)
    return in_order(pieces, dim)


def split_up(value, dim, count):
    before, after = (value.shape[:dim], value.shape[dim + 1 :])
    return jnp.moveaxis(value.reshape(*before, count, -1, *after), dim, 0)


def summed_on_arrival(value, axis, dim):
    pieces = split_up(value, dim, lax.axis_size(axis))
    arrived = lax.all_to_all(pieces, axis, split_axis=0, concat_axis=0, tiled=True)
    return arrived.sum(axis=0)


def padded_to(lines, count):
    spare = -lines.shape[0] % count
    if not spare:
        return lines
    return jnp.concatenate([lines, jnp.zeros((spare, *lines.shape[1:]), lines.dtype)])


def sum_in_order(pieces, axes, turns):
    dims = [lax.axis_size(a) for a in axes]
    pieces = pieces.reshape(*dims, *pieces.shape[1:])
    pieces = pieces.transpose(*turns, *range(len(axes), pieces.ndim))
    pieces = pieces.reshape(-1, *pieces.shape[len(axes) :])
    for k in turns:
        pieces = lax.psum_scatter(pieces, axes[k], scatter_dimension=0, tiled=True)
    return pieces[0]


def all_blocks(value, axes, turns):
    pieces = value[None]
    for k in turns:
        pieces = lax.all_gather(pieces, axes[k], axis=0, tiled=True)
    current = [lax.axis_size(axes[k]) for k in reversed(turns)]
    pieces = pieces.reshape(*current, *value.shape)
    turned = sorted(range(len(turns)), key=lambda place: turns[len(turns) - 1 - place])
    return pieces.transpose(*turned, *range(len(turns), pieces.ndim)).reshape(-1, *value.shape)


def sum_by_parts(value, axes, turns):
    count, lines = (lax.axis_size(axes), value.reshape(-1, *value.shape[1:][-1:]))
    pieces = padded_to(lines, count).reshape(count, -1, *lines.shape[1:])
    own = sum_in_order(pieces, axes, turns)
    whole = all_blocks(own, axes, turns[::-1]).reshape(-1, *lines.shape[1:])
    return whole[: len(lines)].reshape(value.shape)


def dft_tables(length):
    counter = jnp.arange(length, dtype=jnp.int32)
    product = counter[:, None] * counter[None, :] % length
    phase_angle = product.astype(jnp.float32) * (2.0 * math.pi / length)
    factor = 1.0 / math.sqrt(length)
    return (jnp.cos(phase_angle) * factor, jnp.sin(phase_angle) * factor)


def transform(real_part, imag_part, cosine_table, sine_table, direction):
    stacked = jnp.stack([real_part, imag_part], axis=1)
    left_cos = jnp.einsum("uv,bcvk->bcuk", cosine_table, stacked, precision=HIGHEST)
    left_sin = jnp.einsum("uv,bcvk->bcuk", sine_table, stacked, precision=HIGHEST)
    middle = jnp.stack(
        [left_cos[:, 0] + direction * left_sin[:, 1], left_cos[:, 1] - direction * left_sin[:, 0]],
        axis=1,
    )
    right_cos = jnp.einsum("bcav,vk->bcak", middle, cosine_table, precision=HIGHEST)
    right_sin = jnp.einsum("bcav,vk->bcak", middle, sine_table, precision=HIGHEST)
    return (
        right_cos[:, 0] + direction * right_sin[:, 1],
        right_cos[:, 1] - direction * right_sin[:, 0],
    )


def visit_block(
    strip_band, probe_field, amp_block, row_block, col_block, live_block, cosine_table, sine_table
):

    def cut_patch(row_start, col_start):
        return lax.dynamic_slice(strip_band, (0, row_start, col_start), (2, PATCH, PATCH))

    patches = jax.vmap(cut_patch)(row_block, col_block)
    probe_real = probe_field[0]
    probe_imag = probe_field[1]
    exit_real = probe_real * patches[:, 0] - probe_imag * patches[:, 1]
    exit_imag = probe_real * patches[:, 1] + probe_imag * patches[:, 0]
    far_real, far_imag = transform(exit_real, exit_imag, cosine_table, sine_table, 1.0)
    magnitude = jnp.sqrt(far_real * far_real + far_imag * far_imag)
    scale_ratio = amp_block / jnp.maximum(magnitude, MODULUS_FLOOR)
    back_real, back_imag = transform(
        far_real * scale_ratio, far_imag * scale_ratio, cosine_table, sine_table, -1.0
    )
    probe_power = jnp.broadcast_to(
        probe_real * probe_real + probe_imag * probe_imag, back_real.shape
    )
    object_terms = jnp.stack(
        [
            probe_real * back_real + probe_imag * back_imag,
            probe_real * back_imag - probe_imag * back_real,
            probe_power,
        ],
        axis=1,
    )
    live_wide = live_block[:, None, None, None]
    object_terms = jnp.where(live_wide, object_terms, 0.0)
    patch_real = patches[:, 0]
    patch_imag = patches[:, 1]
    probe_terms = jnp.stack(
        [
            patch_real * back_real + patch_imag * back_imag,
            patch_real * back_imag - patch_imag * back_real,
            patch_real * patch_real + patch_imag * patch_imag,
        ],
        axis=1,
    )
    probe_terms = jnp.sum(jnp.where(live_wide, probe_terms, 0.0), axis=0)
    return (object_terms, probe_terms)


def run_positions(
    strip_band,
    probe_field,
    amp_table,
    row_table,
    col_table,
    first_index,
    live_total,
    split_index,
    slot_gap,
    cosine_table,
    sine_table,
):
    block_size = math.gcd(amp_table.shape[0], 8)
    last_slot = amp_table.shape[0] - 1
    initial = (
        jnp.zeros((3,) + strip_band.shape[1:], jnp.float32),
        jnp.zeros((3, PATCH, PATCH), jnp.float32),
    )

    def visit_step(block_number, state_pair):
        band_sums, probe_sums = state_pair
        position = block_number * block_size + jnp.arange(block_size, dtype=jnp.int32)
        live_block = position < live_total
        union_index = first_index + position
        slot_index = jnp.where(union_index < split_index, union_index, union_index + slot_gap)
        slot_index = jnp.clip(slot_index, 0, last_slot)
        amp_block = jnp.take(amp_table, slot_index, axis=0)
        row_block = jnp.take(row_table, slot_index, axis=0)
        col_block = jnp.take(col_table, slot_index, axis=0)
        object_terms, probe_terms = visit_block(
            strip_band,
            probe_field,
            amp_block,
            row_block,
            col_block,
            live_block,
            cosine_table,
            sine_table,
        )
        for member in range(block_size):
            corner = (0, row_block[member], col_block[member])
            current = lax.dynamic_slice(band_sums, corner, (3, PATCH, PATCH))
            band_sums = lax.dynamic_update_slice(band_sums, current + object_terms[member], corner)
        return (band_sums, probe_sums + probe_terms)

    block_count = (live_total + block_size - 1) // block_size
    return lax.fori_loop(0, block_count, visit_step, initial)


def on_device(object_field, probe_field, amplitudes, scan_rows, scan_cols, live_count):
    cosine_table, sine_table = dft_tables(PATCH)
    own_amps = amplitudes[0, 0]
    own_rows = scan_rows[0, 0]
    own_cols = scan_cols[0, 0]
    own_total = live_count[0, 0]
    slot_count = own_amps.shape[0]
    partner_amps = partner(own_amps, "pos", 0)
    offsets, partner_count = partner((jnp.stack([own_rows, own_cols]), live_count[0]), "pos", 0)
    partner_total = partner_count[0]
    core_number = lax.axis_index("pos")
    leading = core_number == 0
    amp_table = jnp.where(
        leading,
        jnp.concatenate([own_amps, partner_amps]),
        jnp.concatenate([partner_amps, own_amps]),
    )
    row_table = jnp.where(
        leading, jnp.concatenate([own_rows, offsets[0]]), jnp.concatenate([offsets[0], own_rows])
    )
    col_table = jnp.where(
        leading, jnp.concatenate([own_cols, offsets[1]]), jnp.concatenate([offsets[1], own_cols])
    )
    first_total = jnp.where(leading, own_total, partner_total)
    union_total = own_total + partner_total
    half_total = (union_total + 1) // 2
    first_index = core_number * half_total
    live_here = jnp.minimum(union_total, first_index + half_total) - first_index
    slot_gap = slot_count - first_total
    probe_relax = slot_count * lax.axis_size(TILE) * lax.axis_size("pos") / 4.0
    column_share = COLS // lax.axis_size("pos")
    for round_number in range(ITERS):
        own_columns = lax.dynamic_slice_in_dim(
            object_field, lax.axis_index("pos") * column_share, column_share, 2
        )
        next_share = from_behind(own_columns, TILE, -1)
        next_rows = gathered_copies(next_share, "pos", 2)
        strip_band = jnp.concatenate([object_field, next_rows], axis=1)
        strip_band = jnp.concatenate([strip_band, strip_band[:, :, :PATCH]], axis=2)
        band_sums, probe_sums = run_positions(
            strip_band,
            probe_field,
            amp_table,
            row_table,
            col_table,
            first_index,
            live_here,
            first_total,
            slot_gap,
            cosine_table,
            sine_table,
        )
        folded = band_sums[:, :, :COLS].at[:, :, :PATCH].add(band_sums[:, :, COLS:])
        column_sums = summed_on_arrival(folded, "pos", 2)
        from_above = from_behind(column_sums[:, STRIP:], TILE, 1)
        share_sums = column_sums[:, :STRIP] + from_above
        own_columns = lax.dynamic_slice_in_dim(
            object_field, lax.axis_index("pos") * column_share, column_share, 2
        )
        updated = (share_sums[:2] + OBJECT_RELAX * own_columns) / (share_sums[2] + OBJECT_RELAX)[
            None
        ]
        new_object = lax.all_gather(updated, "pos", axis=2, tiled=True)
        probe_total = sum_by_parts(probe_sums, TILE_POS, (3, 1, 0, 2))
        probe_field = (probe_total[:2] + probe_relax * probe_field) / (
            probe_total[2] + probe_relax
        )[None]
        object_field = new_object
    return (object_field, probe_field)


def solution(mesh):
    torus = Mesh(
        mesh.devices.reshape(8, 4, 4, mesh.shape["pos"]), ("tile_0", "tile_1", "tile_2", "pos")
    )
    return jax.shard_map(
        on_device,
        mesh=torus,
        in_specs=(
            P(None, TILE, None),
            P(),
            P(TILE, "pos", None, None, None),
            P(TILE, "pos", None),
            P(TILE, "pos", None),
            P(TILE, "pos"),
        ),
        out_specs=(P(None, TILE, None), P()),
        check_vma=False,
    )
```

profile of v0, /device:TPU:1, one launch (start us, length us, event | category | flops | bytes accessed | tf_op | source)
XLA Modules:
  0.0 1300.2 jit_solution(16142459743591218330)
XLA Ops:
  13.4 8.6 collective-permute-start.2
  24.8 8.4 collective-permute-done.2
  33.6 5.1 all_to_all.20
  43.4 6.6 maximum_select_fusion.4
  52.1 464.9 %while.43 = (s32[]{:T(128)}, f32[3,256,1152]{1,2,0:T(8,128)}, f32[3,128,128]{1,2,0:T(8,128)S(1)}, s32[]{:T(128)}, s32[]{:T(128)}, /*index=5*/s32[]{:T(128)}, s32...) while((s32[]{:T(128)}, f32[3,256,1152]{1,2,0:T(8,128)}, ...), condition=%wide.region_2.5_spmd.clone.clone, body=%wide.region_0.4_spmd.clone.clone.sunk | while | flops 3233809664 | bytes 54073152 | solution.py:212
  87.4 25.2 %while.46 = (s32[]{:T(128)}, f32[2,256,1152]{2,1,0:T(8,128)}, s32[8,3]{0,1:T(4,128)S(1)}, f32[8,2,128,128]{2,3,1,0:T(8,128)S(1)}, s32[]{:T(128)}) while((s32[]{:T(128)}, f32[2,256,1152]{2,1,0:T(8,128)}, s32[8,3]{0,1:T(4,128)S(1)}, f32[8,2,128,128]{2,3,1,0:T(8,128)S(1)}, s32[]{:T(128)}) %tuple.240), condition=%wide.while_cond.2, body=%wide.while_body.2.sunk | while | flops 2 | bytes 786557 | solution.py:125
  128.3 4.0 dynamic_update_slice.128
  138.7 4.0 dynamic_update_slice.130
  148.7 4.0 dynamic_update_slice.132
  153.9 4.0 dynamic_update_slice.133
  164.2 4.1 dynamic_update_slice.135
  203.4 25.2 %while.46 = (s32[]{:T(128)}, f32[2,256,1152]{2,1,0:T(8,128)}, s32[8,3]{0,1:T(4,128)S(1)}, f32[8,2,128,128]{2,3,1,0:T(8,128)S(1)}, s32[]{:T(128)}) while((s32[]{:T(128)}, f32[2,256,1152]{2,1,0:T(8,128)}, s32[8,3]{0,1:T(4,128)S(1)}, f32[8,2,128,128]{2,3,1,0:T(8,128)S(1)}, s32[]{:T(128)}) %tuple.240), condition=%wide.while_cond.2, body=%wide.while_body.2.sunk | while | flops 2 | bytes 786557 | solution.py:125
  244.4 4.0 dynamic_update_slice.128
  249.5 4.0 dynamic_update_slice.129
  265.0 4.0 dynamic_update_slice.132
  319.4 25.2 %while.46 = (s32[]{:T(128)}, f32[2,256,1152]{2,1,0:T(8,128)}, s32[8,3]{0,1:T(4,128)S(1)}, f32[8,2,128,128]{2,3,1,0:T(8,128)S(1)}, s32[]{:T(128)}) while((s32[]{:T(128)}, f32[2,256,1152]{2,1,0:T(8,128)}, s32[8,3]{0,1:T(4,128)S(1)}, f32[8,2,128,128]{2,3,1,0:T(8,128)S(1)}, s32[]{:T(128)}) %tuple.240), condition=%wide.while_cond.2, body=%wide.while_body.2.sunk | while | flops 2 | bytes 786557 | solution.py:125
  360.4 4.0 dynamic_update_slice.128
  370.7 4.0 dynamic_update_slice.130
  381.0 4.1 dynamic_update_slice.132
  391.4 4.0 dynamic_update_slice.134
  396.6 4.1 dynamic_update_slice.135
  435.7 25.2 %while.46 = (s32[]{:T(128)}, f32[2,256,1152]{2,1,0:T(8,128)}, s32[8,3]{0,1:T(4,128)S(1)}, f32[8,2,128,128]{2,3,1,0:T(8,128)S(1)}, s32[]{:T(128)}) while((s32[]{:T(128)}, f32[2,256,1152]{2,1,0:T(8,128)}, s32[8,3]{0,1:T(4,128)S(1)}, f32[8,2,128,128]{2,3,1,0:T(8,128)S(1)}, s32[]{:T(128)}) %tuple.240), condition=%wide.while_cond.2, body=%wide.while_body.2.sunk | while | flops 2 | bytes 786557 | solution.py:125
  481.5 4.1 dynamic_update_slice.129
  507.3 4.1 dynamic_update_slice.134
  520.6 6.3 all_to_all.21
  531.7 12.4 reduce-scatter.7.cloned.1.call-done
  544.2 11.0 collective-permute-done.4
  559.5 8.5 reduce-scatter.9.cloned.1.call-done
  568.0 23.6 %all-reduce.2 = f32[32,2,128]{2,0,1:T(8,128)S(1)} all-reduce(f32[32,2,128]{2,0,1:T(8,128)} %reduce-scatter.9.cloned.1.call-done), channel_id=4, replica_groups=mesh['tile_0'=8,'tile_1'=4,'tile_2'=4,'pos'=2] {'tile_0'}, use_global_device_ids=true, to_apply=%region_6.9.clone | all-reduce | flops 8192 | bytes 65536
  591.7 8.4 all-reduce.3
  600.8 5.2 all_gather.30
  606.1 18.1 %all_gather.31 = f32[32,2,128]{2,1,0:T(2,128)S(1)} all-gather(f32[4,2,128]{2,1,0:T(2,128)S(1)} %all_gather.30), channel_id=1, replica_groups=mesh['tile_0'=8,'tile_1'=4,'tile_2'=4,'pos'=2] {'tile_0'}, dimensions={0}, use_global_device_ids=true | all-gather | bytes 36864 | tf_op jit(solution)/shard_map/all_gather | solution.py:81
  624.2 9.1 all_gather.32
  633.2 24.8 %all_gather.33 = f32[256,2,128]{2,0,1:T(8,128)S(1)} all-gather(f32[128,2,128]{2,0,1:T(8,128)S(1)} %all_gather.32), channel_id=1, replica_groups=mesh['tile_0'=8,'tile_1'=4,'tile_2'=4,'pos'=2] {'pos'}, dimensions={0}, use_global_device_ids=true | all-gather | bytes 393216 | tf_op jit(solution)/shard_map/all_gather | solution.py:81
  661.1 11.8 collective-permute-done.5
  673.3 5.1 all_to_all.22
  685.5 462.3 %while.45 = (s32[]{:T(128)}, f32[3,256,1152]{1,2,0:T(8,128)}, f32[3,128,128]{1,2,0:T(8,128)S(1)}, s32[]{:T(128)}, s32[]{:T(128)}, /*index=5*/s32[]{:T(128)}, s32...) while((s32[]{:T(128)}, f32[3,256,1152]{1,2,0:T(8,128)}, ...), condition=%wide.region_10.13_spmd.clone.clone, body=%wide.region_8.12_spmd.clone.clone.sunk | while | flops 3233809664 | bytes 54073152 | solution.py:212
  720.3 25.0 %while.47 = (s32[]{:T(128)}, f32[2,256,1152]{2,1,0:T(8,128)}, s32[8,3]{0,1:T(4,128)S(1)}, f32[8,2,128,128]{2,3,1,0:T(8,128)S(1)}, s32[]{:T(128)}) while((s32[]{:T(128)}, f32[2,256,1152]{2,1,0:T(8,128)}, s32[8,3]{0,1:T(4,128)S(1)}, f32[8,2,128,128]{2,3,1,0:T(8,128)S(1)}, s32[]{:T(128)}) %tuple.237), condition=%wide.while_cond.3, body=%wide.while_body.3.sunk | while | flops 2 | bytes 786557 | solution.py:125
  771.5 4.0 dynamic_update_slice.138
  781.5 4.0 dynamic_update_slice.140
  786.7 4.0 dynamic_update_slice.141
  797.0 4.1 dynamic_update_slice.143
  835.8 25.0 %while.47 = (s32[]{:T(128)}, f32[2,256,1152]{2,1,0:T(8,128)}, s32[8,3]{0,1:T(4,128)S(1)}, f32[8,2,128,128]{2,3,1,0:T(8,128)S(1)}, s32[]{:T(128)}) while((s32[]{:T(128)}, f32[2,256,1152]{2,1,0:T(8,128)}, s32[8,3]{0,1:T(4,128)S(1)}, f32[8,2,128,128]{2,3,1,0:T(8,128)S(1)}, s32[]{:T(128)}) %tuple.237), condition=%wide.while_cond.3, body=%wide.while_body.3.sunk | while | flops 2 | bytes 786557 | solution.py:125
  876.6 4.0 dynamic_update_slice.136
  881.7 4.0 dynamic_update_slice.137
  897.2 4.0 dynamic_update_slice.140
  951.2 25.0 %while.47 = (s32[]{:T(128)}, f32[2,256,1152]{2,1,0:T(8,128)}, s32[8,3]{0,1:T(4,128)S(1)}, f32[8,2,128,128]{2,3,1,0:T(8,128)S(1)}, s32[]{:T(128)}) while((s32[]{:T(128)}, f32[2,256,1152]{2,1,0:T(8,128)}, s32[8,3]{0,1:T(4,128)S(1)}, f32[8,2,128,128]{2,3,1,0:T(8,128)S(1)}, s32[]{:T(128)}) %tuple.237), condition=%wide.while_cond.3, body=%wide.while_body.3.sunk | while | flops 2 | bytes 786557 | solution.py:125
  992.0 4.0 dynamic_update_slice.136
  1002.3 4.0 dynamic_update_slice.138
  1012.7 4.1 dynamic_update_slice.140
  1028.2 4.1 dynamic_update_slice.143
  1066.9 25.0 %while.47 = (s32[]{:T(128)}, f32[2,256,1152]{2,1,0:T(8,128)}, s32[8,3]{0,1:T(4,128)S(1)}, f32[8,2,128,128]{2,3,1,0:T(8,128)S(1)}, s32[]{:T(128)}) while((s32[]{:T(128)}, f32[2,256,1152]{2,1,0:T(8,128)}, s32[8,3]{0,1:T(4,128)S(1)}, f32[8,2,128,128]{2,3,1,0:T(8,128)S(1)}, s32[]{:T(128)}) %tuple.237), condition=%wide.while_cond.3, body=%wide.while_body.3.sunk | while | flops 2 | bytes 786557 | solution.py:125
  1112.5 4.1 dynamic_update_slice.137
  1138.4 4.1 dynamic_update_slice.142
  1151.4 6.3 all_to_all.23
  1162.6 13.4 %reduce-scatter.11.cloned.1.call-done = f32[128,2,128]{2,0,1:T(8,128)} async-done(((f32[256,2,128]{2,0,1:T(8,128)}), f32[128,2,128]{2,0,1:T(8,128)}) %reduce-scatter.11.cloned.1.call-update) | async-done | bytes 131088 | tf_op jit(solution)/shard_map/reduce_scatter | solution.py:74
  1176.0 10.0 collective-permute-done.6
  1188.2 11.5 reduce-scatter.13.cloned.1.call-done
  1199.8 23.6 %all-reduce.4 = f32[32,2,128]{2,0,1:T(8,128)S(1)} all-reduce(f32[32,2,128]{2,0,1:T(8,128)} %reduce-scatter.13.cloned.1.call-done), channel_id=8, replica_groups=mesh['tile_0'=8,'tile_1'=4,'tile_2'=4,'pos'=2] {'tile_0'}, use_global_device_ids=true, to_apply=%region_14.17.clone | all-reduce | flops 8192 | bytes 65536
  1223.4 8.5 all-reduce.5
  1232.6 5.2 all_gather.36
  1237.8 18.1 %all_gather.37 = f32[32,2,128]{2,1,0:T(2,128)S(1)} all-gather(f32[4,2,128]{2,1,0:T(2,128)S(1)} %all_gather.36), channel_id=1, replica_groups=mesh['tile_0'=8,'tile_1'=4,'tile_2'=4,'pos'=2] {'tile_0'}, dimensions={0}, use_global_device_ids=true | all-gather | bytes 36864 | tf_op jit(solution)/shard_map/all_gather | solution.py:81
  1255.9 9.1 all_gather.38
  1265.0 24.7 %all_gather.39 = f32[256,2,128]{2,0,1:T(8,128)S(1)} all-gather(f32[128,2,128]{2,0,1:T(8,128)S(1)} %all_gather.38), channel_id=1, replica_groups=mesh['tile_0'=8,'tile_1'=4,'tile_2'=4,'pos'=2] {'pos'}, dimensions={0}, use_global_device_ids=true | all-gather | bytes 393216 | tf_op jit(solution)/shard_map/all_gather | solution.py:81
  (767 shorter events, 626.5 us)
Async XLA Ops:
  7.2 17.5 %copy-start.9 = (s32[1,1,32]{2,1,0:T(1,128)S(1)}, s32[1,1,32]{2,1,0:T(1,128)}, u32[]{:S(2)}) copy-start(s32[1,1,32]{2,1,0:T(1,128)} %param.21) | copy-start | bytes 388
  7.2 17.5 %copy-start.8 = (s32[1,1,32]{2,1,0:T(1,128)S(1)}, s32[1,1,32]{2,1,0:T(1,128)}, u32[]{:S(2)}) copy-start(s32[1,1,32]{2,1,0:T(1,128)} %param.22) | copy-start | bytes 388
  7.2 15.4 %copy-start.6 = (f32[2,128,128]{2,1,0:T(8,128)S(1)}, f32[2,128,128]{2,1,0:T(8,128)}, u32[]{:S(2)}) copy-start(f32[2,128,128]{2,1,0:T(8,128)} %param.19) | copy-start | bytes 393220
  7.2 536.9 %reduce-scatter.7.cloned.1.call-start = ((), (), s32[]{:S(2)}) async-start(), calls=%async_computation.8 | async-start | bytes 393216 | tf_op jit(solution)/shard_map/reduce_scatter | solution.py:74
  7.2 36.2 %collective-permute-start.3 = (f32[32,128,128]{2,1,0:T(8,128)}, f32[32,128,128]{2,1,0:T(8,128)}, u32[]{:S(2)}, u32[]{:S(2)}) collective-permute-start(f32[32,128,128]{2,1,0:T(8,128)} %bitcast.498), channel_id=1, source_target_pairs={{0,1},{1,0},{2,3},{3,2},{4,5},{5,4},{6,7},{7,6},{8,9},{9,8},{10,11... | collective-permute-start | bytes 6291464 | tf_op jit(solution)/shard_map/ppermute | solution.py:23
  10.6 12.8 collective-permute-start
  11.4 13.3 %collective-permute-start.1 = (s32[2,32]{1,0:T(2,128)S(1)}, s32[2,32]{1,0:T(2,128)S(1)}, u32[]{:S(2)}, u32[]{:S(2)}) collective-permute-start(s32[2,32]{1,0:T(2,128)S(1)} %pad_add_fusion.2), channel_id=1, source_target_pairs={{0,1},{1,0},{2,3},{3,2},{4,5},{5,4},{6,7},{7,6},{8,9},{9,8},{10,11... | collective-permute-start | bytes 776 | tf_op jit(solution)/shard_map/ppermute | solution.py:23
  13.3 26.6 %copy-start = (f32[2,128,1024]{1,2,0:T(8,128)}, f32[2,128,1024]{1,2,0:T(8,128)S(1)}, u32[]{:S(2)}) copy-start(f32[2,128,1024]{1,2,0:T(8,128)S(1)} %copy.197) | copy-start | bytes 3145732
  13.4 19.9 %collective-permute-start.2 = (f32[2,128,512]{1,2,0:T(8,128)S(1)}, f32[2,128,512]{1,2,0:T(8,128)S(1)}, u32[]{:S(2)}, u32[]{:S(2)}) collective-permute-start(f32[2,128,512]{1,2,0:T(8,128)S(1)} %constant_dynamic-slice_fusion.7), channel_id=1, source_target_pairs={{2,0},{4,2},{6,4},{8,6},{10,8},{12,10},{14,12},{16,14},{18,16},{20... | collective-permute-start | bytes 1572872 | tf_op jit(solution)/shard_map/ppermute | solution.py:29
  50.0 2.1 copy-start.5
  528.5 26.7 %copy-start.3 = (f32[3,256,512]{1,2,0:T(8,128)S(1)}, f32[3,256,512]{1,2,0:T(8,128)}, u32[]{:S(2)}) copy-start(f32[3,256,512]{1,2,0:T(8,128)} %reduce_sum.40) | copy-start | bytes 4718596
  530.7 25.8 %copy-start.1 = (f32[2,128,1024]{1,2,0:T(8,128)S(1)}, f32[2,128,1024]{1,2,0:T(8,128)}, u32[]{:S(2)}) copy-start(f32[2,128,1024]{1,2,0:T(8,128)} %copy-done) | copy-start | bytes 3145732
  530.7 24.5 %collective-permute-start.4 = (f32[3,128,512]{1,2,0:T(8,128)}, f32[3,128,512]{1,2,0:T(8,128)}, u32[]{:S(2)}, u32[]{:S(2)}) collective-permute-start(f32[3,128,512]{1,2,0:T(8,128)} %slice.887), channel_id=1, source_target_pairs={{254,0},{0,2},{2,4},{4,6},{6,8},{8,10},{10,12},{12,14},{14,16},{16... | collective-permute-start | bytes 2359304 | tf_op jit(solution)/shard_map/ppermute | solution.py:29
  531.7 36.3 %reduce-scatter.9.cloned.1.call-start = ((), (), s32[]{:S(2)}) async-start(), calls=%async_computation.9 | async-start | bytes 163840 | tf_op jit(solution)/shard_map/reduce_scatter | solution.py:74
  544.1 13.4 %copy-start.11 = (u32[256]{0:T(256)S(1)}, u32[256]{0:T(256)}, u32[]{:S(2)}) copy-start(u32[256]{0:T(256)} %constant.265) | copy-start | bytes 3076
  544.1 14.0 %copy-start.10 = (u32[256]{0:T(256)S(1)}, u32[256]{0:T(256)}, u32[]{:S(2)}) copy-start(u32[256]{0:T(256)} %constant.261) | copy-start | bytes 3076
  544.1 113.9 %all-gather.3.cloned.1.call-start = ((), (), s32[]{:S(2)}) async-start(), calls=%async_computation.10 | async-start | bytes 1572864 | tf_op jit(solution)/shard_map/all_gather | solution.py:277
  556.5 104.4 %copy-start.7 = (f32[2,128,128]{2,1,0:T(8,128)S(1)}, f32[2,128,128]{2,1,0:T(8,128)}, u32[]{:S(2)}) copy-start(f32[2,128,128]{2,1,0:T(8,128)} %param.19) | copy-start | bytes 393220
  557.4 618.6 %reduce-scatter.11.cloned.1.call-start = ((), (), s32[]{:S(2)}) async-start(), calls=%async_computation.12 | async-start | bytes 393216 | tf_op jit(solution)/shard_map/reduce_scatter | solution.py:74
  659.1 13.8 %collective-permute-start.5 = (f32[2,128,512]{1,2,0:T(8,128)S(1)}, f32[2,128,512]{1,2,0:T(8,128)S(1)}, u32[]{:S(2)}, u32[]{:S(2)}) collective-permute-start(f32[2,128,512]{1,2,0:T(8,128)S(1)} %constant_dynamic-slice_fusion.6), channel_id=1, source_target_pairs={{2,0},{4,2},{6,4},{8,6},{10,8},{12,10},{14,12},{16,14},{18,16},{20... | collective-permute-start | bytes 1572872 | tf_op jit(solution)/shard_map/ppermute | solution.py:29
  1159.3 26.7 %copy-start.2 = (f32[3,256,512]{1,2,0:T(8,128)S(1)}, f32[3,256,512]{1,2,0:T(8,128)}, u32[]{:S(2)}) copy-start(f32[3,256,512]{1,2,0:T(8,128)} %reduce_sum.41) | copy-start | bytes 4718596
  1161.5 25.8 %copy-start.4 = (f32[2,128,1024]{1,2,0:T(8,128)S(1)}, f32[2,128,1024]{1,2,0:T(8,128)}, u32[]{:S(2)}) copy-start(f32[2,128,1024]{1,2,0:T(8,128)} %all-gather.3.cloned.1.call-done) | copy-start | bytes 3145732
  1161.5 24.5 %collective-permute-start.6 = (f32[3,128,512]{1,2,0:T(8,128)}, f32[3,128,512]{1,2,0:T(8,128)}, u32[]{:S(2)}, u32[]{:S(2)}) collective-permute-start(f32[3,128,512]{1,2,0:T(8,128)} %slice.893), channel_id=1, source_target_pairs={{254,0},{0,2},{2,4},{4,6},{6,8},{8,10},{10,12},{12,14},{14,16},{16... | collective-permute-start | bytes 2359304 | tf_op jit(solution)/shard_map/ppermute | solution.py:29
  1162.5 37.2 %reduce-scatter.13.cloned.1.call-start = ((), (), s32[]{:S(2)}) async-start(), calls=%async_computation.13 | async-start | bytes 163840 | tf_op jit(solution)/shard_map/reduce_scatter | solution.py:74
  1176.0 114.6 %all-gather.5.cloned.1.call-start = ((), (), s32[]{:S(2)}) async-start(), calls=%async_computation.11 | async-start | bytes 1572864 | tf_op jit(solution)/shard_map/all_gather | solution.py:277
Sparse Core Ops, SparseCore 0:
  531.8 12.2 reduce-scatter.6
  546.7 21.2 reduce-scatter.8
  570.4 17.0 all-gather.2
  1162.6 13.2 reduce-scatter.10
  1178.5 21.2 reduce-scatter.12
  1202.0 17.0 all-gather.4
where the time goes:
time: 1320 us; the launch traced here: 1300 us
  local copies, waits for them, and re-layouts  530 us (40%)
  loops' own time  240 us (18%)
  blocking collectives  201 us (15%)
  other arithmetic  108 us (8%)
  matrix products  103 us (8%)
  waiting for transfers between devices  87.2 us (7%)
  between operations  17.4 us (1%)
  starting transfers between devices  14.2 us (1%)
    dynamic_update_slice x64, local copies, waits for them, and re-layouts, visit_step(): lax.dynamic_update_slice(band_sums, current + object_terms[member], corner)  256 us
    another operation x2, loops' own time, run_positions(): return lax.fori_loop(0, block_count, visit_step, initial)  237 us
    gather x320, local copies, waits for them, and re-layouts  198 us
    all_gather x8, blocking collectives, all_blocks(): pieces = lax.all_gather(pieces, axes[k], axis=0, tiled=True)  114 us
    add x64, other arithmetic, visit_step(): current + object_terms[member]  72.1 us
    unnamed x4, blocking collectives  64.2 us
    reduce_scatter x4, waiting for transfers between devices, sum_in_order(): pieces = lax.psum_scatter(pieces, axes[k], scatter_dimension=0, tiled=True)  45.8 us
    ppermute x4, waiting for transfers between devices, from_behind(): return lax.ppermute(block, axis, route)  41.3 us
  transfers between devices with their start and end apart: 13, of which 8 were waited for; matrix products, arithmetic and copies ran while one was open for 1% of the time, Pallas kernels for 0%

commit v1 on v0

v1 whole, which is shorter than its diff:
```python
import math

import jax
import jax.numpy as jnp
import numpy as np
from jax import lax
from jax.experimental import pallas as pl
from jax.experimental.pallas import tpu as pltpu
from jax.sharding import Mesh
from jax.sharding import PartitionSpec as P

PATCH = 128
STRIP = 128
COLS = 1024
BLOCKS = COLS // PATCH
HALF = BLOCKS // 2
BAND = 2 * STRIP
GROUP = 4
ITERS = 2
TILE = ("tile_0", "tile_1", "tile_2")
MODULUS_FLOOR = 0.2
OBJECT_RELAX = 1.0
ANY = pl.BlockSpec(memory_space=pl.ANY)
SMEM = pl.BlockSpec(memory_space=pltpu.SMEM)
VMEM = pl.BlockSpec(memory_space=pltpu.VMEM)


def swapped(value):
    return lax.ppermute(value, "pos", [(0, 1), (1, 0)])


def from_tile(value, distance):
    count = lax.axis_size(TILE)
    return lax.ppermute(value, TILE, [((i + distance) % count, i) for i in range(count)])


def two_terms(value):
    high = value.astype(jnp.bfloat16)
    low = (value - high.astype(jnp.float32)).astype(jnp.bfloat16)
    return high, low


def dft_tables():
    counter = np.arange(PATCH)
    angle = (counter[:, None] * counter[None, :] % PATCH) * (2.0 * math.pi / PATCH)
    cosine = np.cos(angle) / math.sqrt(PATCH)
    sine = np.sin(angle) / math.sqrt(PATCH)

    def split(table):
        table = table.astype(np.float32)
        high = table.astype(jnp.bfloat16)
        low = (table - high.astype(np.float32)).astype(jnp.bfloat16)
        return high, low

    right, left = [], []
    for sign in (1.0, -1.0):
        high, low = split(np.block([[cosine, -sign * sine], [sign * sine, cosine]]))
        right.append(np.concatenate([high, high, low], axis=0))
        high, low = split(np.block([[cosine, sign * sine], [-sign * sine, cosine]]))
        left.append(np.concatenate([high, high, low], axis=1))
    return jnp.asarray(np.stack(right)), jnp.asarray(np.stack(left))


def times_right(real, imag, table):
    stacked = jnp.concatenate(
        [jnp.concatenate([r, i], axis=1) for r, i in zip(real, imag)], axis=0
    )
    high, low = two_terms(stacked)
    wide = jnp.concatenate([high, low, high], axis=1)
    out = jnp.dot(wide, table, preferred_element_type=jnp.float32)
    return (
        [out[k * PATCH : (k + 1) * PATCH, :PATCH] for k in range(len(real))],
        [out[k * PATCH : (k + 1) * PATCH, PATCH:] for k in range(len(real))],
    )


def times_left(real, imag, table):
    stacked = jnp.concatenate(
        [jnp.concatenate(real, axis=1), jnp.concatenate(imag, axis=1)], axis=0
    )
    high, low = two_terms(stacked)
    tall = jnp.concatenate([high, low, high], axis=0)
    out = jnp.dot(table, tall, preferred_element_type=jnp.float32)
    return (
        [out[:PATCH, k * PATCH : (k + 1) * PATCH] for k in range(len(real))],
        [out[PATCH:, k * PATCH : (k + 1) * PATCH] for k in range(len(real))],
    )


def column_place(col, own_first):
    block = col // PATCH
    near = block ^ own_first
    far = ((block + 1) % BLOCKS) ^ own_first
    return near, far, col % PATCH


def positions_kernel(
    from_strips,
    core_ref,
    rows_ref,
    cols_ref,
    live_ref,
    probe_ref,
    amps_ref,
    right_ref,
    left_ref,
    first_ref,
    mine_ref,
    other_ref,
    keep_up_ref,
    keep_low_ref,
    give_up_ref,
    give_low_ref,
    probe_sums_ref,
    band,
    sums,
    sems,
):
    own_first = core_ref[0] * HALF
    copies = []
    if from_strips:
        for k in range(BLOCKS):
            start = pl.multiple_of((k ^ own_first) * PATCH, PATCH)
            copies.append((first_ref.at[:, :, pl.ds(start, PATCH)], band.at[:, k, :STRIP, :]))
        copies.append((mine_ref, band.at[:, :HALF, STRIP:, :]))
        copies.append((other_ref, band.at[:, HALF:, STRIP:, :]))
    else:
        copies.append((mine_ref, band.at[:, :HALF]))
        copies.append((other_ref, band.at[:, HALF:]))
    started = [pltpu.make_async_copy(a, b, sems.at[n]) for n, (a, b) in enumerate(copies)]
    for copy in started:
        copy.start()
    sums[...] = jnp.zeros_like(sums)
    probe_sums_ref[...] = jnp.zeros_like(probe_sums_ref)
    for copy in started:
        copy.wait()
    live = live_ref[0]
    lane = lax.broadcasted_iota(jnp.int32, (PATCH, PATCH), 1)

    def visit(step, carry):
        slots = [step * GROUP + k for k in range(GROUP)]
        places = [column_place(cols_ref[s], own_first) for s in slots]
        rows = [rows_ref[s] for s in slots]
        alive = [s < live for s in slots]
        probe_real = probe_ref[0]
        probe_imag = probe_ref[1]
        patches = []
        exits = []
        for (near, far, shift), row in zip(places, rows):
            back = (PATCH - shift) % PATCH
            patch = []
            for plane in range(2):
                a = band[plane, near, pl.ds(row, PATCH), :]
                b = band[plane, far, pl.ds(row, PATCH), :]
                patch.append(pltpu.roll(jnp.where(lane >= shift, a, b), back, 1))
            patches.append(patch)
            exits.append(
                (
                    probe_real * patch[0] - probe_imag * patch[1],
                    probe_real * patch[1] + probe_imag * patch[0],
                )
            )
        revised = []
        for pair in range(0, GROUP, 2):
            real = [exits[pair + k][0] for k in range(2)]
            imag = [exits[pair + k][1] for k in range(2)]
            real, imag = times_right(real, imag, right_ref[0])
            real, imag = times_left(real, imag, left_ref[0])
            for k in range(2):
                power = real[k] * real[k] + imag[k] * imag[k]
                ratio = amps_ref[slots[pair + k]] * lax.rsqrt(
                    jnp.maximum(power, MODULUS_FLOOR * MODULUS_FLOOR)
                )
                real[k] = real[k] * ratio
                imag[k] = imag[k] * ratio
            real, imag = times_left(real, imag, left_ref[1])
            real, imag = times_right(real, imag, right_ref[1])
            revised.extend(zip(real, imag))
        totals = [probe_sums_ref[plane] for plane in range(3)]
        for k in range(GROUP):
            back_real = jnp.where(alive[k], revised[k][0], 0.0)
            back_imag = jnp.where(alive[k], revised[k][1], 0.0)
            patch_real = jnp.where(alive[k], patches[k][0], 0.0)
            patch_imag = jnp.where(alive[k], patches[k][1], 0.0)
            totals[0] += patch_real * back_real + patch_imag * back_imag
            totals[1] += patch_real * back_imag - patch_imag * back_real
            totals[2] += patch_real * patch_real + patch_imag * patch_imag
            near, far, shift = places[k]
            terms = (
                probe_real * back_real + probe_imag * back_imag,
                probe_real * back_imag - probe_imag * back_real,
            )
            for plane in range(2):
                turned = pltpu.roll(terms[plane], shift, 1)
                inside = lane >= shift
                sums[plane, near, pl.ds(rows[k], PATCH), :] += jnp.where(inside, turned, 0.0)
                sums[plane, far, pl.ds(rows[k], PATCH), :] += jnp.where(inside, 0.0, turned)
        for plane in range(3):
            probe_sums_ref[plane] = totals[plane]
        return carry

    lax.fori_loop(0, (live + GROUP - 1) // GROUP, visit, 0)
    outs = (
        (sums.at[:, :HALF, :STRIP, :], keep_up_ref),
        (sums.at[:, :HALF, STRIP:, :], keep_low_ref),
        (sums.at[:, HALF:, :STRIP, :], give_up_ref),
        (sums.at[:, HALF:, STRIP:, :], give_low_ref),
    )
    started = [pltpu.make_async_copy(a, b, sems.at[n]) for n, (a, b) in enumerate(outs)]
    for copy in started:
        copy.start()
    for copy in started:
        copy.wait()


def run_positions(scalars, probe, amps, tables, first, mine, other):
    from_strips = first is not None
    quarter = jax.ShapeDtypeStruct((2, HALF, STRIP, PATCH), jnp.float32)

    def kernel(*refs):
        if from_strips:
            positions_kernel(True, *refs)
        else:
            positions_kernel(False, *refs[:8], None, *refs[8:])

    pieces = (first, mine, other) if from_strips else (mine, other)
    return pl.pallas_call(
        kernel,
        out_shape=(quarter,) * 4 + (jax.ShapeDtypeStruct((3, PATCH, PATCH), jnp.float32),),
        in_specs=[SMEM] * 4 + [VMEM] * 4 + [ANY] * len(pieces),
        out_specs=(ANY,) * 4 + (VMEM,),
        scratch_shapes=[
            pltpu.VMEM((2, BLOCKS, BAND, PATCH), jnp.float32),
            pltpu.VMEM((2, BLOCKS, BAND, PATCH), jnp.float32),
            pltpu.SemaphoreType.DMA((BLOCKS + 2,)),
        ],
        compiler_params=pltpu.CompilerParams(vmem_limit_bytes=40 * 2**20),
        cost_estimate=pl.CostEstimate(
            flops=13 * 10**9, bytes_accessed=8 * 2**20, transcendentals=2**19
        ),
        name="positions",
    )(*scalars, probe, amps, *tables, *pieces)


def weights_kernel(sources, core_ref, meta_ref, probe_ref, out_ref, total, power):
    own_first = core_ref[0] * HALF
    total[...] = jnp.zeros_like(total)
    power[...] = probe_ref[0] * probe_ref[0] + probe_ref[1] * probe_ref[1]
    lane = lax.broadcasted_iota(jnp.int32, (PATCH, PATCH), 1)
    slots = (meta_ref.shape[1] - 2) // 2
    for source in range(sources):
        for core in range(2):
            line = source * 2 + core

            def visit(slot, carry, line=line, source=source):
                row = meta_ref[line, slot] + source * STRIP
                near, far, shift = column_place(meta_ref[line, slots + slot], own_first)

                @pl.when(near < HALF)
                def _():
                    turned = pltpu.roll(power[...], shift, 1)
                    total[near, pl.ds(row, PATCH), :] += jnp.where(lane >= shift, turned, 0.0)

                @pl.when(far < HALF)
                def _():
                    turned = pltpu.roll(power[...], shift, 1)
                    total[far, pl.ds(row, PATCH), :] += jnp.where(lane >= shift, 0.0, turned)

                return carry

            lax.fori_loop(0, meta_ref[line, 2 * slots], visit, 0)
    height = out_ref.shape[1]
    out_ref[...] = total[:, STRIP : STRIP + height, :] + OBJECT_RELAX


def run_weights(core, meta, probe, sources):
    height = (sources - 1) * STRIP

    def kernel(*refs):
        weights_kernel(sources, *refs)

    return pl.pallas_call(
        kernel,
        out_shape=jax.ShapeDtypeStruct((HALF, height, PATCH), jnp.float32),
        in_specs=[SMEM, SMEM, VMEM],
        out_specs=VMEM,
        scratch_shapes=[
            pltpu.VMEM((HALF, (sources + 1) * STRIP, PATCH), jnp.float32),
            pltpu.VMEM((PATCH, PATCH), jnp.float32),
        ],
        compiler_params=pltpu.CompilerParams(vmem_limit_bytes=16 * 2**20),
        cost_estimate=pl.CostEstimate(
            flops=4 * 10**9, bytes_accessed=2 * 2**20, transcendentals=0
        ),
        name="weights",
    )(core, meta, probe)


def probe_sum_everywhere(value):
    core = lax.axis_index("pos")
    lines = value.reshape(2, -1, PATCH)
    mine = lax.dynamic_index_in_dim(lines, core, 0, False)
    other = lax.dynamic_index_in_dim(lines, 1 - core, 0, False)
    part = mine + swapped(other)
    for axis in TILE[::-1]:
        count = lax.axis_size(axis)
        stride = 1
        while stride < count:
            fan = 4 if count % (stride * 4) == 0 else 2
            part = shifts_among(part, axis, stride, fan)
            stride *= fan
    other = swapped(part)
    low = jnp.where(core == 0, part, other)
    high = jnp.where(core == 0, other, part)
    return jnp.concatenate([low, high]).reshape(value.shape)


def shifts_among(value, axis, stride, fan):
    count = lax.axis_size(axis)
    total = value
    for step in range(1, fan):
        route = []
        for i in range(count):
            place = i // stride % fan
            route.append((i, i + ((place + step) % fan - place) * stride))
        total = total + lax.ppermute(value, axis, route)
    return total


def halves_of(value, core):
    lines = value.reshape(*value.shape[:2], 2, HALF, PATCH)
    mine = lax.dynamic_index_in_dim(lines, core, 2, False)
    return mine.transpose(0, 2, 1, 3)


def on_device(object_field, probe_field, amplitudes, scan_rows, scan_cols, live_count):
    tables = dft_tables()
    core = lax.axis_index("pos")
    core_line = core.reshape(1).astype(jnp.int32)
    amps, rows, cols, live = (
        amplitudes[0, 0],
        scan_rows[0, 0],
        scan_cols[0, 0],
        live_count[0],
    )
    scalars = (core_line, rows, cols, live)
    probe_relax = amps.shape[0] * lax.axis_size(TILE) * lax.axis_size("pos") / 4.0
    own_half = halves_of(object_field, core)
    halo = from_tile(own_half, 1)
    meta = jnp.concatenate([rows, cols, live, live])[None]
    meta = jnp.concatenate([meta, swapped(meta)])
    meta = jnp.concatenate([from_tile(meta, -1), meta, from_tile(meta, 1)])
    halo_other = swapped(halo)
    weight = run_weights(core_line, meta, probe_field, 3)
    up, low, give_up, give_low, probe_sums = run_positions(
        scalars, probe_field, amps, tables, object_field, halo, halo_other
    )

    def next_probe(sums, probe):
        total = probe_sum_everywhere(sums)
        return (total[:2] + probe_relax * probe) / (total[2] + probe_relax)[None]

    low = low + swapped(give_low)
    up = up + swapped(give_up)
    above = from_tile(low, -1)
    below = from_tile(up, 1)
    probe_field = next_probe(probe_sums, probe_field)
    up = (up + above + OBJECT_RELAX * own_half) / weight[:, :STRIP]
    low = (low + below + OBJECT_RELAX * halo) / weight[:, STRIP:]
    mine = jnp.concatenate([up, low], axis=2)
    other = swapped(mine)
    own_half = up
    weight = run_weights(core_line, meta[:4], probe_field, 2)
    up, low, give_up, give_low, probe_sums = run_positions(
        scalars, probe_field, amps, tables, None, mine, other
    )
    low = low + swapped(give_low)
    up = up + swapped(give_up)
    above = from_tile(low, -1)
    probe_out = next_probe(probe_sums, probe_field)
    mine = (up + above + OBJECT_RELAX * own_half) / weight
    other = swapped(mine)
    left = jnp.where(core == 0, mine, other)
    right = jnp.where(core == 0, other, mine)
    object_out = jnp.concatenate([left, right], axis=1).transpose(0, 2, 1, 3)
    return object_out.reshape(object_field.shape), probe_out


def torus_of(mesh):
    shape = (mesh.shape["tile"],)
    shape = (8, 4, 4) if shape == (128,) else (1, 1, *shape)
    return Mesh(mesh.devices.reshape(*shape, mesh.shape["pos"]), (*TILE, "pos"))


def solution(mesh):
    return jax.shard_map(
        on_device,
        mesh=torus_of(mesh),
        in_specs=(
            P(None, TILE, None),
            P(),
            P(TILE, "pos", None, None, None),
            P(TILE, "pos", None),
            P(TILE, "pos", None),
            P(TILE, "pos"),
        ),
        out_specs=(P(None, TILE, None), P()),
        check_vma=False,
    )
```

time: 1320 us -> 223 us (0.17); the launches traced: 1300 us -> 219 us
  local copies, waits for them, and re-layouts: 530 us -> 11.4 us
  loops' own time: 240 us -> 0 us
  blocking collectives: 201 us -> 0 us
  other arithmetic: 108 us -> 1.97 us
  matrix products: 103 us -> 0 us
  starting transfers between devices: 14.2 us -> 93.1 us
  Pallas kernels: 0 us -> 46.9 us
  waiting for transfers between devices: 87.2 us -> 63.9 us
  between operations: 17.4 us -> 1.73 us
    dynamic_update_slice x64 -> x0, local copies, waits for them, and re-layouts: 256 us -> none  [visit_step(): lax.dynamic_update_slice(band_sums, current + object_terms[member], corner)]
    another operation x10 -> x0, loops' own time: 240 us -> none  [the longest x2 237 us: run_positions(): return lax.fori_loop(0, block_count, visit_step, initial)]
    gather x344 -> x0, local copies, waits for them, and re-layouts: 231 us -> none
    all_gather x8 -> x0, blocking collectives: 114 us -> none  [all_blocks(): pieces = lax.all_gather(pieces, axes[k], axis=0, tiled=True)]
    dot_general x64 -> x0, matrix products: 103 us -> none  [the longest x16 26.3 us: transform(): jnp.einsum('bcav,vk->bcak', middle, sine_table, precision=HIGHEST)]
    ppermute x7 -> x38, starting transfers between devices: 14 us -> 93.1 us  [the longest x20 35.9 us: shifts_among(): total = total + lax.ppermute(value, axis, route)]
    add x102 -> x14, other arithmetic: 79.4 us -> 0.36 us  [the longest x8 0.18 us: shifts_among(): total = total + lax.ppermute(value, axis, route)]
    unnamed x4 -> x0, blocking collectives: 64.2 us -> none
  transfers between devices with their start and end apart: 13 -> 38, of which waited for: 8 -> 16; matrix products, arithmetic and copies ran while one was open for 1% -> 1% of each run, Pallas kernels for 0% -> 15%
where the time goes in v1:
time: 223 us; the launch traced here: 219 us
  starting transfers between devices  93.1 us (42%)
  waiting for transfers between devices  63.9 us (29%)
  Pallas kernels  46.9 us (21%)
  local copies, waits for them, and re-layouts  11.4 us (5%)
    ppermute x6, waiting for transfers between devices, from_tile(): lax.ppermute(value, TILE, [((i + distance) % count, i) for i in range(cou...  39.4 us
    ppermute x20, starting transfers between devices, shifts_among(): total = total + lax.ppermute(value, axis, route)  35.9 us
    ppermute x12, starting transfers between devices, swapped(): return lax.ppermute(value, 'pos', [(0, 1), (1, 0)])  32.3 us
    pallas_call x2, Pallas kernels, run_positions(): pl.pallas_call(kernel, out_shape=(quarter,) * 4 + (jax.ShapeDtypeStruct((...  27.5 us
    ppermute x6, starting transfers between devices, from_tile(): lax.ppermute(value, TILE, [((i + distance) % count, i) for i in range(cou...  24.9 us
    ppermute x20, waiting for transfers between devices, shifts_among(): total = total + lax.ppermute(value, axis, route)  20 us
    pallas_call x2, Pallas kernels, run_weights(): pl.pallas_call(kernel, out_shape=jax.ShapeDtypeStruct((HALF, height, PATC...  19.3 us
    unnamed x26, local copies, waits for them, and re-layouts  9.07 us
  transfers between devices with their start and end apart: 38, of which 16 were waited for; matrix products, arithmetic and copies ran while one was open for 1% of the time, Pallas kernels for 15%

profile of v1, /device:TPU:1, one launch (start us, length us, event | category | flops | bytes accessed | tf_op | source)
XLA Modules:
  0.0 218.9 jit_solution(11712065672736753138)
XLA Ops:
  0.7 1.8 reshape.37
  2.5 0.1 constant_dynamic-slice_fusion
  2.6 11.1 %collective-permute-start = (f32[2,4,128,128]{3,2,1,0:T(8,128)S(1)}, f32[2,4,128,128]{3,2,1,0:T(8,128)S(1)}, u32[]{:S(2)}, u32[]{:S(2)}) collective-permute-start(f32[2,4,128,128]{3,2,1,0:T(8,128)S(1)} %bitcast.47), channel_id=1, source_target_pairs={{2,0},{4,2},{6,4},{8,6},{10,8},{12,10},{14,12},{16,14},{18,16},{20... | collective-permute-start | bytes 1572872 | tf_op jit(solution)/shard_map/ppermute | solution.py:34
  13.8 10.6 %collective-permute-done.refs_9_ = f32[2,4,128,128]{3,2,1,0:T(8,128)S(1)} collective-permute-done((f32[2,4,128,128]{3,2,1,0:T(8,128)S(1)}, f32[2,4,128,128]{3,2,1,0:T(8,128)S(1)}, u32[]{:S(2)}, u32[]{:S(2)}) %collective-permute-start) | collective-permute-done | bytes 524320 | tf_op jit(solution)/shard_map/ppermute | solution.py:34
  24.4 1.5 collective-permute-start.1
  26.7 0.7 collective-permute-done.1.refs_10_
  27.5 1.6 copy-done.4
  29.0 1.1 copy-done.6
  30.2 1.1 copy-done.8
  31.3 14.1 %positions.2 = (f32[2,4,128,128]{3,2,1,0:T(8,128)S(1)}, f32[2,4,128,128]{3,2,1,0:T(8,128)S(1)}, f32[2,4,128,128]{3,2,1,0:T(8,128)}, f32[2,4,128,128]{3,2,1,0:T(8,128)S(1)}, f32[3,128,128]{2,1,0:T(8,128)S(1)}) custom-call(s32[1]{0:T(128)} %bitcast.refs_0_, s32[32]{0:T(128)S(1)} %bitcast.37, s32[32]{0:T(128)S(1)} %bitcast.40, s32[1]{0:T(128)} %bitcast.29.refs_3_, ...), custom_call_target="tpu_custom_call" | custom-call | flops 12999999488 | bytes 8388608 | tf_op jit(solution)/shard_map/positions/pallas_call | solution.py:227
  45.5 7.8 %collective-permute-start.14 = (f32[2,4,128,128]{3,2,1,0:T(8,128)}, f32[2,4,128,128]{3,2,1,0:T(8,128)S(1)}, u32[]{:S(2)}, u32[]{:S(2)}) collective-permute-start(f32[2,4,128,128]{3,2,1,0:T(8,128)} %get-tuple-element.14), channel_id=1, source_target_pairs={{0,1},{1,0},{2,3},{3,2},{4,5},{5,4},{6,7},{7,6},{8,9},{9,8},{10,11... | collective-permute-start | bytes 1572872 | tf_op jit(solution)/shard_map/ppermute | solution.py:29
  53.4 6.9 %collective-permute-start.19 = (s32[2,66]{1,0:T(2,128)S(1)}, s32[2,66]{1,0:T(2,128)S(1)}, u32[]{:S(2)}, u32[]{:S(2)}) collective-permute-start(s32[2,66]{1,0:T(2,128)S(1)} %pad_add_fusion.2), channel_id=1, source_target_pairs={{2,0},{4,2},{6,4},{8,6},{10,8},{12,10},{14,12},{16,14},{18,16},{20... | collective-permute-start | bytes 1592 | tf_op jit(solution)/shard_map/ppermute | solution.py:34
  60.2 1.0 collective-permute-done.18
  61.2 11.9 %weights.2 = f32[4,256,128]{2,1,0:T(8,128)S(1)} custom-call(s32[1]{0:T(128)} %bitcast.refs_0_, s32[6,66]{1,0:T(8,128)S(1)} %pad_add_fusion.refs_1_, f32[2,128,128]{2,1,0:T(8,128)S(1)} %copy-done.1), custom_call_target="tpu_custom_call" | custom-call | flops 4000000000 | bytes 2097152 | tf_op jit(solution)/shard_map/weights/pallas_call | solution.py:282
  73.2 1.4 collective-permute-start.15
  74.6 6.4 %collective-permute-start.20 = (f32[2,4,128,128]{3,2,1,0:T(8,128)S(1)}, f32[2,4,128,128]{3,2,1,0:T(8,128)S(1)}, u32[]{:S(2)}, u32[]{:S(2)}) collective-permute-start(f32[2,4,128,128]{3,2,1,0:T(8,128)S(1)} %add.139), channel_id=1, source_target_pairs={{2,0},{4,2},{6,4},{8,6},{10,8},{12,10},{14,12},{16,14},{18,16},{20... | collective-permute-start | bytes 1572872 | tf_op jit(solution)/shard_map/ppermute | solution.py:34
  81.1 0.4 collective-permute-start.2
  81.5 1.0 collective-permute-done.2
  82.7 2.6 %collective-permute-start.5 = (f32[192,128]{1,0:T(8,128)S(1)}, f32[192,128]{1,0:T(8,128)S(1)}, u32[]{:S(2)}, u32[]{:S(2)}) collective-permute-start(f32[192,128]{1,0:T(8,128)S(1)} %bitcast_add_fusion.1), channel_id=1, source_target_pairs={{0,6},{2,0},{4,2},{6,4},{1,7},{3,1},{5,3},{7,5},{8,14},{10,8},{12,... | collective-permute-start | bytes 294920 | tf_op jit(solution)/shard_map/ppermute | solution.py:326
  85.2 8.8 %collective-permute-done.20 = f32[2,4,128,128]{3,2,1,0:T(8,128)S(1)} collective-permute-done((f32[2,4,128,128]{3,2,1,0:T(8,128)S(1)}, f32[2,4,128,128]{3,2,1,0:T(8,128)S(1)}, u32[]{:S(2)}, u32[]{:S(2)}) %collective-permute-start.20) | collective-permute-done | bytes 524320 | tf_op jit(solution)/shard_map/ppermute | solution.py:34
  94.1 0.2 add_divide_fusion.1
  94.3 0.3 collective-permute-start.16
  94.8 2.6 %collective-permute-start.8 = (f32[192,128]{1,0:T(8,128)S(1)}, f32[192,128]{1,0:T(8,128)S(1)}, u32[]{:S(2)}, u32[]{:S(2)}) collective-permute-start(f32[192,128]{1,0:T(8,128)S(1)} %add_add_fusion.5), channel_id=1, source_target_pairs={{0,24},{8,0},{16,8},{24,16},{1,25},{9,1},{17,9},{25,17},{2,26},{10... | collective-permute-start | bytes 294920 | tf_op jit(solution)/shard_map/ppermute | solution.py:326
  97.4 4.9 %collective-permute-done.6 = f32[192,128]{1,0:T(8,128)S(1)} collective-permute-done((f32[192,128]{1,0:T(8,128)S(1)}, f32[192,128]{1,0:T(8,128)S(1)}, u32[]{:S(2)}, u32[]{:S(2)}) %collective-permute-start.6) | collective-permute-done | bytes 98336 | tf_op jit(solution)/shard_map/ppermute | solution.py:326
  102.3 0.1 collective-permute-start.10
  102.4 6.6 %collective-permute-start.11 = (f32[192,128]{1,0:T(8,128)S(1)}, f32[192,128]{1,0:T(8,128)S(1)}, u32[]{:S(2)}, u32[]{:S(2)}) collective-permute-start(f32[192,128]{1,0:T(8,128)S(1)} %add_add_fusion.4), channel_id=1, source_target_pairs={{0,96},{32,0},{64,32},{96,64},{128,224},{160,128},{192,160},{224,1... | collective-permute-start | bytes 294920 | tf_op jit(solution)/shard_map/ppermute | solution.py:326
  109.0 0.2 collective-permute-start.9
  109.2 4.3 %collective-permute-done.16 = f32[2,4,128,128]{3,2,1,0:T(8,128)S(1)} collective-permute-done((f32[2,4,128,128]{3,2,1,0:T(8,128)S(1)}, f32[2,4,128,128]{3,2,1,0:T(8,128)S(1)}, u32[]{:S(2)}, u32[]{:S(2)}) %collective-permute-start.16) | collective-permute-done | bytes 524320 | tf_op jit(solution)/shard_map/ppermute | solution.py:34
  113.5 0.1 add_divide_fusion.2
  113.7 1.6 collective-permute-start.21
  115.4 5.6 %collective-permute-start.12 = (f32[192,128]{1,0:T(8,128)S(1)}, f32[192,128]{1,0:T(8,128)S(1)}, u32[]{:S(2)}, u32[]{:S(2)}) collective-permute-start(f32[192,128]{1,0:T(8,128)S(1)} %add_add_fusion.3), channel_id=1, source_target_pairs={{0,128},{32,160},{64,192},{96,224},{128,0},{160,32},{192,64},{224,... | collective-permute-start | bytes 294920 | tf_op jit(solution)/shard_map/ppermute | solution.py:326
  121.0 3.2 %collective-permute-done.12 = f32[192,128]{1,0:T(8,128)S(1)} collective-permute-done((f32[192,128]{1,0:T(8,128)S(1)}, f32[192,128]{1,0:T(8,128)S(1)}, u32[]{:S(2)}, u32[]{:S(2)}) %collective-permute-start.12) | collective-permute-done | bytes 98336 | tf_op jit(solution)/shard_map/ppermute | solution.py:326
  124.2 2.4 %collective-permute-start.13 = (f32[192,128]{1,0:T(8,128)S(1)}, f32[192,128]{1,0:T(8,128)S(1)}, u32[]{:S(2)}, u32[]{:S(2)}) collective-permute-start(f32[192,128]{1,0:T(8,128)S(1)} %add.136), channel_id=1, source_target_pairs={{0,1},{1,0},{2,3},{3,2},{4,5},{5,4},{6,7},{7,6},{8,9},{9,8},{10,11... | collective-permute-start | bytes 294920 | tf_op jit(solution)/shard_map/ppermute | solution.py:29
  126.5 0.9 collective-permute-done.13
  127.6 1.6 copy-done.5
  129.2 1.1 copy-done.7
  130.3 1.1 copy-done.9
  131.4 13.4 %positions.3 = (f32[2,4,128,128]{3,2,1,0:T(8,128)S(1)}, f32[2,4,128,128]{3,2,1,0:T(8,128)S(1)}, f32[2,4,128,128]{3,2,1,0:T(8,128)S(1)}, f32[2,4,128,128]{3,2,1,0:T(8,128)S(1)}, f32[3,128,128]{2,1,0:T(8,128)S(1)}) custom-call(s32[1]{0:T(128)} %bitcast.refs_0_, s32[32]{0:T(128)S(1)} %bitcast.38, s32[32]{0:T(128)S(1)} %bitcast.41, s32[1]{0:T(128)} %bitcast.31.refs_3_, ...), custom_call_target="tpu_custom_call" | custom-call | flops 12999999488 | bytes 8388608 | tf_op jit(solution)/shard_map/positions/pallas_call | solution.py:227
  144.9 7.8 %collective-permute-start.26 = (f32[192,128]{1,0:T(8,128)S(1)}, f32[192,128]{1,0:T(8,128)S(1)}, u32[]{:S(2)}, u32[]{:S(2)}) collective-permute-start(f32[192,128]{1,0:T(8,128)S(1)} %dynamic-slice_bitcast_fusion), channel_id=1, source_target_pairs={{0,1},{1,0},{2,3},{3,2},{4,5},{5,4},{6,7},{7,6},{8,9},{9,8},{10,11... | collective-permute-start | bytes 294920 | tf_op jit(solution)/shard_map/ppermute | solution.py:29
  152.7 0.9 collective-permute-done.26
  153.8 3.8 %collective-permute-start.28 = (f32[192,128]{1,0:T(8,128)S(1)}, f32[192,128]{1,0:T(8,128)S(1)}, u32[]{:S(2)}, u32[]{:S(2)}) collective-permute-start(f32[192,128]{1,0:T(8,128)S(1)} %bitcast_add_fusion), channel_id=1, source_target_pairs={{0,4},{2,6},{4,0},{6,2},{1,5},{3,7},{5,1},{7,3},{8,12},{10,14},{12... | collective-permute-start | bytes 294920 | tf_op jit(solution)/shard_map/ppermute | solution.py:326
  157.6 2.0 collective-permute-start.29
  159.6 2.9 %collective-permute-done.28 = f32[192,128]{1,0:T(8,128)S(1)} collective-permute-done((f32[192,128]{1,0:T(8,128)S(1)}, f32[192,128]{1,0:T(8,128)S(1)}, u32[]{:S(2)}, u32[]{:S(2)}) %collective-permute-start.28) | collective-permute-done | bytes 98336 | tf_op jit(solution)/shard_map/ppermute | solution.py:326
  162.6 1.0 collective-permute-start.31
  163.7 1.6 collective-permute-start.32
  165.3 1.4 collective-permute-start.23
  166.7 3.2 %collective-permute-done.30 = f32[192,128]{1,0:T(8,128)S(1)} collective-permute-done((f32[192,128]{1,0:T(8,128)S(1)}, f32[192,128]{1,0:T(8,128)S(1)}, u32[]{:S(2)}, u32[]{:S(2)}) %collective-permute-start.30) | collective-permute-done | bytes 98336 | tf_op jit(solution)/shard_map/ppermute | solution.py:326
  169.9 2.7 %collective-permute-start.33 = (f32[192,128]{1,0:T(8,128)S(1)}, f32[192,128]{1,0:T(8,128)S(1)}, u32[]{:S(2)}, u32[]{:S(2)}) collective-permute-start(f32[192,128]{1,0:T(8,128)S(1)} %add_add_fusion.1), channel_id=1, source_target_pairs={{0,32},{32,64},{64,96},{96,0},{128,160},{160,192},{192,224},{224,1... | collective-permute-start | bytes 294920 | tf_op jit(solution)/shard_map/ppermute | solution.py:326
  172.7 0.8 collective-permute-start.34
  173.5 1.4 collective-permute-start.35
  174.8 0.4 collective-permute-done.33
  175.3 5.4 %collective-permute-done.34 = f32[192,128]{1,0:T(8,128)S(1)} collective-permute-done((f32[192,128]{1,0:T(8,128)S(1)}, f32[192,128]{1,0:T(8,128)S(1)}, u32[]{:S(2)}, u32[]{:S(2)}) %collective-permute-start.34) | collective-permute-done | bytes 98336 | tf_op jit(solution)/shard_map/ppermute | solution.py:326
  180.7 4.4 %collective-permute-start.36 = (f32[192,128]{1,0:T(8,128)S(1)}, f32[192,128]{1,0:T(8,128)S(1)}, u32[]{:S(2)}, u32[]{:S(2)}) collective-permute-start(f32[192,128]{1,0:T(8,128)S(1)} %add_add_fusion), channel_id=1, source_target_pairs={{0,128},{32,160},{64,192},{96,224},{128,0},{160,32},{192,64},{224,... | collective-permute-start | bytes 294920 | tf_op jit(solution)/shard_map/ppermute | solution.py:326
  185.1 4.2 %collective-permute-start.22 = (f32[2,4,128,128]{3,2,1,0:T(8,128)S(1)}, f32[2,4,128,128]{3,2,1,0:T(8,128)S(1)}, u32[]{:S(2)}, u32[]{:S(2)}) collective-permute-start(f32[2,4,128,128]{3,2,1,0:T(8,128)S(1)} %get-tuple-element.18), channel_id=1, source_target_pairs={{0,1},{1,0},{2,3},{3,2},{4,5},{5,4},{6,7},{7,6},{8,9},{9,8},{10,11... | collective-permute-start | bytes 1572872 | tf_op jit(solution)/shard_map/ppermute | solution.py:29
  189.2 3.1 %collective-permute-start.37 = (f32[192,128]{1,0:T(8,128)S(1)}, f32[192,128]{1,0:T(8,128)S(1)}, u32[]{:S(2)}, u32[]{:S(2)}) collective-permute-start(f32[192,128]{1,0:T(8,128)S(1)} %add.159), channel_id=1, source_target_pairs={{0,1},{1,0},{2,3},{3,2},{4,5},{5,4},{6,7},{7,6},{8,9},{9,8},{10,11... | collective-permute-start | bytes 294920 | tf_op jit(solution)/shard_map/ppermute | solution.py:29
  192.5 7.4 %weights.3 = f32[4,128,128]{2,1,0:T(8,128)S(1)} custom-call(s32[1]{0:T(128)} %bitcast.refs_0_, s32[4,66]{1,0:T(4,128)S(1)} %pad_add_fusion.1.refs_1_, f32[2,128,128]{2,1,0:T(8,128)S(1)} %add_divide_fusion.4.refs_4_.refs_2_), custom_call_target="tpu_custom_call" | custom-call | flops 4000000000 | bytes 2097152 | tf_op jit(solution)/shard_map/weights/pallas_call | solution.py:282
  199.9 14.8 %collective-permute-done.24 = f32[2,4,128,128]{3,2,1,0:T(8,128)S(1)} collective-permute-done((f32[2,4,128,128]{3,2,1,0:T(8,128)S(1)}, f32[2,4,128,128]{3,2,1,0:T(8,128)S(1)}, u32[]{:S(2)}, u32[]{:S(2)}) %collective-permute-start.24) | collective-permute-done | bytes 524320 | tf_op jit(solution)/shard_map/ppermute | solution.py:34
  214.7 0.2 add_divide_fusion
  214.9 0.7 collective-permute-start.25
  215.6 0.7 add_divide_fusion.3
  216.3 0.8 collective-permute-done.25
  217.1 0.1 broadcast_select_fusion.1
  217.3 0.3 copy.12
  217.6 1.3 copy.13
  (78 shorter events, 1.6 us)
Async XLA Ops:
  0.6 25.9 %copy-start.2 = (s32[1,1,32]{2,1,0:T(1,128)S(1)}, s32[1,1,32]{2,1,0:T(1,128)}, u32[]{:S(2)}) copy-start(s32[1,1,32]{2,1,0:T(1,128)} %param.11) | copy-start | bytes 388
  0.6 25.9 %copy-start.3 = (s32[1,1,32]{2,1,0:T(1,128)S(1)}, s32[1,1,32]{2,1,0:T(1,128)}, u32[]{:S(2)}) copy-start(s32[1,1,32]{2,1,0:T(1,128)} %param.12) | copy-start | bytes 388
  0.7 26.8 %copy-start = (f32[2,128,1024]{2,1,0:T(8,128)S(1)}, f32[2,128,1024]{2,1,0:T(8,128)}, u32[]{:S(2)}) copy-start(f32[2,128,1024]{2,1,0:T(8,128)} %refs_8_.1) | copy-start | bytes 3145732
  0.7 26.8 %copy-start.1 = (f32[2,128,128]{2,1,0:T(8,128)S(1)}, f32[2,128,128]{2,1,0:T(8,128)}, u32[]{:S(2)}) copy-start(f32[2,128,128]{2,1,0:T(8,128)} %refs_2_.1) | copy-start | bytes 393220
  2.6 24.9 %copy-start.10 = (f32[2,128,1,4,128]{4,3,2,1,0:T(4,128)}, f32[2,128,1,4,128]{4,3,2,1,0:T(4,128)S(1)}, u32[]{:S(2)}) copy-start(f32[2,128,1,4,128]{4,3,2,1,0:T(4,128)S(1)} %constant_dynamic-slice_fusion) | copy-start | bytes 1572868
  2.6 21.7 %collective-permute-start = (f32[2,4,128,128]{3,2,1,0:T(8,128)S(1)}, f32[2,4,128,128]{3,2,1,0:T(8,128)S(1)}, u32[]{:S(2)}, u32[]{:S(2)}) collective-permute-start(f32[2,4,128,128]{3,2,1,0:T(8,128)S(1)} %bitcast.47), channel_id=1, source_target_pairs={{2,0},{4,2},{6,4},{8,6},{10,8},{12,10},{14,12},{16,14},{18,16},{20... | collective-permute-start | bytes 1572872 | tf_op jit(solution)/shard_map/ppermute | solution.py:34
  24.4 3.1 %collective-permute-start.1 = (f32[2,4,128,128]{3,2,1,0:T(8,128)S(1)}, f32[2,4,128,128]{3,2,1,0:T(8,128)S(1)}, u32[]{:S(2)}, u32[]{:S(2)}) collective-permute-start(f32[2,4,128,128]{3,2,1,0:T(8,128)S(1)} %collective-permute-done.refs_9_), channel_id=1, source_target_pairs={{0,1},{1,0},{2,3},{3,2},{4,5},{5,4},{6,7},{7,6},{8,9},{9,8},{10,11... | collective-permute-start | bytes 1572872 | tf_op jit(solution)/shard_map/ppermute | solution.py:29
  26.6 26.6 %collective-permute-start.17 = (s32[1,66]{1,0:T(1,128)S(1)}, s32[1,66]{1,0:T(1,128)S(1)}, u32[]{:S(2)}, u32[]{:S(2)}) collective-permute-start(s32[1,66]{1,0:T(1,128)S(1)} %add_bitcast_fusion), channel_id=1, source_target_pairs={{0,1},{1,0},{2,3},{3,2},{4,5},{5,4},{6,7},{7,6},{8,9},{9,8},{10,11... | collective-permute-start | bytes 800 | tf_op jit(solution)/shard_map/ppermute | solution.py:29
  27.4 1.6 copy-start.4
  29.0 1.1 copy-start.6
  30.2 1.1 copy-start.8
  45.5 29.1 %collective-permute-start.14 = (f32[2,4,128,128]{3,2,1,0:T(8,128)}, f32[2,4,128,128]{3,2,1,0:T(8,128)S(1)}, u32[]{:S(2)}, u32[]{:S(2)}) collective-permute-start(f32[2,4,128,128]{3,2,1,0:T(8,128)} %get-tuple-element.14), channel_id=1, source_target_pairs={{0,1},{1,0},{2,3},{3,2},{4,5},{5,4},{6,7},{7,6},{8,9},{9,8},{10,11... | collective-permute-start | bytes 1572872 | tf_op jit(solution)/shard_map/ppermute | solution.py:29
  53.3 7.9 %collective-permute-start.18 = (s32[2,66]{1,0:T(2,128)S(1)}, s32[2,66]{1,0:T(2,128)S(1)}, u32[]{:S(2)}, u32[]{:S(2)}) collective-permute-start(s32[2,66]{1,0:T(2,128)S(1)} %pad_add_fusion.2), channel_id=1, source_target_pairs={{254,0},{0,2},{2,4},{4,6},{6,8},{8,10},{10,12},{12,14},{14,16},{16... | collective-permute-start | bytes 1592 | tf_op jit(solution)/shard_map/ppermute | solution.py:34
  53.4 7.8 %collective-permute-start.19 = (s32[2,66]{1,0:T(2,128)S(1)}, s32[2,66]{1,0:T(2,128)S(1)}, u32[]{:S(2)}, u32[]{:S(2)}) collective-permute-start(s32[2,66]{1,0:T(2,128)S(1)} %pad_add_fusion.2), channel_id=1, source_target_pairs={{2,0},{4,2},{6,4},{8,6},{10,8},{12,10},{14,12},{16,14},{18,16},{20... | collective-permute-start | bytes 1592 | tf_op jit(solution)/shard_map/ppermute | solution.py:34
  73.2 12.1 %collective-permute-start.15 = (f32[2,4,128,128]{3,2,1,0:T(8,128)S(1)}, f32[2,4,128,128]{3,2,1,0:T(8,128)S(1)}, u32[]{:S(2)}, u32[]{:S(2)}) collective-permute-start(f32[2,4,128,128]{3,2,1,0:T(8,128)S(1)} %get-tuple-element.16), channel_id=1, source_target_pairs={{0,1},{1,0},{2,3},{3,2},{4,5},{5,4},{6,7},{7,6},{8,9},{9,8},{10,11... | collective-permute-start | bytes 1572872 | tf_op jit(solution)/shard_map/ppermute | solution.py:29
  74.6 19.5 %collective-permute-start.20 = (f32[2,4,128,128]{3,2,1,0:T(8,128)S(1)}, f32[2,4,128,128]{3,2,1,0:T(8,128)S(1)}, u32[]{:S(2)}, u32[]{:S(2)}) collective-permute-start(f32[2,4,128,128]{3,2,1,0:T(8,128)S(1)} %add.139), channel_id=1, source_target_pairs={{2,0},{4,2},{6,4},{8,6},{10,8},{12,10},{14,12},{16,14},{18,16},{20... | collective-permute-start | bytes 1572872 | tf_op jit(solution)/shard_map/ppermute | solution.py:34
  81.1 1.4 collective-permute-start.2
  82.5 12.1 %collective-permute-start.3 = (f32[192,128]{1,0:T(8,128)S(1)}, f32[192,128]{1,0:T(8,128)S(1)}, u32[]{:S(2)}, u32[]{:S(2)}) collective-permute-start(f32[192,128]{1,0:T(8,128)S(1)} %bitcast_add_fusion.1), channel_id=1, source_target_pairs={{0,2},{2,4},{4,6},{6,0},{1,3},{3,5},{5,7},{7,1},{8,10},{10,12},{12... | collective-permute-start | bytes 294920 | tf_op jit(solution)/shard_map/ppermute | solution.py:326
  82.6 12.0 %collective-permute-start.4 = (f32[192,128]{1,0:T(8,128)S(1)}, f32[192,128]{1,0:T(8,128)S(1)}, u32[]{:S(2)}, u32[]{:S(2)}) collective-permute-start(f32[192,128]{1,0:T(8,128)S(1)} %bitcast_add_fusion.1), channel_id=1, source_target_pairs={{0,4},{2,6},{4,0},{6,2},{1,5},{3,7},{5,1},{7,3},{8,12},{10,14},{12... | collective-permute-start | bytes 294920 | tf_op jit(solution)/shard_map/ppermute | solution.py:326
  82.7 11.9 %collective-permute-start.5 = (f32[192,128]{1,0:T(8,128)S(1)}, f32[192,128]{1,0:T(8,128)S(1)}, u32[]{:S(2)}, u32[]{:S(2)}) collective-permute-start(f32[192,128]{1,0:T(8,128)S(1)} %bitcast_add_fusion.1), channel_id=1, source_target_pairs={{0,6},{2,0},{4,2},{6,4},{1,7},{3,1},{5,3},{7,5},{8,14},{10,8},{12,... | collective-permute-start | bytes 294920 | tf_op jit(solution)/shard_map/ppermute | solution.py:326
  94.1 19.4 %copy-start.11 = (f32[2,128,1,4,128]{4,3,2,1,0:T(4,128)S(1)}, f32[2,128,1,4,128]{4,3,2,1,0:T(4,128)}, u32[]{:S(2)}) copy-start(f32[2,128,1,4,128]{4,3,2,1,0:T(4,128)} %copy-done.10) | copy-start | bytes 1572868
  94.3 19.3 %collective-permute-start.16 = (f32[2,4,128,128]{3,2,1,0:T(8,128)S(1)}, f32[2,4,128,128]{3,2,1,0:T(8,128)S(1)}, u32[]{:S(2)}, u32[]{:S(2)}) collective-permute-start(f32[2,4,128,128]{3,2,1,0:T(8,128)S(1)} %get-tuple-element.25), channel_id=1, source_target_pairs={{254,0},{0,2},{2,4},{4,6},{6,8},{8,10},{10,12},{12,14},{14,16},{16... | collective-permute-start | bytes 1572872 | tf_op jit(solution)/shard_map/ppermute | solution.py:34
  94.6 7.7 %collective-permute-start.6 = (f32[192,128]{1,0:T(8,128)S(1)}, f32[192,128]{1,0:T(8,128)S(1)}, u32[]{:S(2)}, u32[]{:S(2)}) collective-permute-start(f32[192,128]{1,0:T(8,128)S(1)} %add_add_fusion.5), channel_id=1, source_target_pairs={{0,8},{8,16},{16,24},{24,0},{1,9},{9,17},{17,25},{25,1},{2,10},{10... | collective-permute-start | bytes 294920 | tf_op jit(solution)/shard_map/ppermute | solution.py:326
  94.7 7.6 %collective-permute-start.7 = (f32[192,128]{1,0:T(8,128)S(1)}, f32[192,128]{1,0:T(8,128)S(1)}, u32[]{:S(2)}, u32[]{:S(2)}) collective-permute-start(f32[192,128]{1,0:T(8,128)S(1)} %add_add_fusion.5), channel_id=1, source_target_pairs={{0,16},{8,24},{16,0},{24,8},{1,17},{9,25},{17,1},{25,9},{2,18},{10... | collective-permute-start | bytes 294920 | tf_op jit(solution)/shard_map/ppermute | solution.py:326
  94.8 7.5 %collective-permute-start.8 = (f32[192,128]{1,0:T(8,128)S(1)}, f32[192,128]{1,0:T(8,128)S(1)}, u32[]{:S(2)}, u32[]{:S(2)}) collective-permute-start(f32[192,128]{1,0:T(8,128)S(1)} %add_add_fusion.5), channel_id=1, source_target_pairs={{0,24},{8,0},{16,8},{24,16},{1,25},{9,1},{17,9},{25,17},{2,26},{10... | collective-permute-start | bytes 294920 | tf_op jit(solution)/shard_map/ppermute | solution.py:326
  102.3 13.0 %collective-permute-start.10 = (f32[192,128]{1,0:T(8,128)S(1)}, f32[192,128]{1,0:T(8,128)S(1)}, u32[]{:S(2)}, u32[]{:S(2)}) collective-permute-start(f32[192,128]{1,0:T(8,128)S(1)} %add_add_fusion.4), channel_id=1, source_target_pairs={{0,64},{32,96},{64,0},{96,32},{128,192},{160,224},{192,128},{224,1... | collective-permute-start | bytes 294920 | tf_op jit(solution)/shard_map/ppermute | solution.py:326
  102.4 12.9 %collective-permute-start.11 = (f32[192,128]{1,0:T(8,128)S(1)}, f32[192,128]{1,0:T(8,128)S(1)}, u32[]{:S(2)}, u32[]{:S(2)}) collective-permute-start(f32[192,128]{1,0:T(8,128)S(1)} %add_add_fusion.4), channel_id=1, source_target_pairs={{0,96},{32,0},{64,32},{96,64},{128,224},{160,128},{192,160},{224,1... | collective-permute-start | bytes 294920 | tf_op jit(solution)/shard_map/ppermute | solution.py:326
  109.0 6.3 %collective-permute-start.9 = (f32[192,128]{1,0:T(8,128)S(1)}, f32[192,128]{1,0:T(8,128)S(1)}, u32[]{:S(2)}, u32[]{:S(2)}) collective-permute-start(f32[192,128]{1,0:T(8,128)S(1)} %add_add_fusion.4), channel_id=1, source_target_pairs={{0,32},{32,64},{64,96},{96,0},{128,160},{160,192},{192,224},{224,1... | collective-permute-start | bytes 294920 | tf_op jit(solution)/shard_map/ppermute | solution.py:326
  113.7 13.8 %collective-permute-start.21 = (f32[2,4,256,128]{3,2,1,0:T(8,128)S(1)}, f32[2,4,256,128]{3,2,1,0:T(8,128)S(1)}, u32[]{:S(2)}, u32[]{:S(2)}) collective-permute-start(f32[2,4,256,128]{3,2,1,0:T(8,128)S(1)} %pad_maximum_fusion.refs_8_), channel_id=1, source_target_pairs={{0,1},{1,0},{2,3},{3,2},{4,5},{5,4},{6,7},{7,6},{8,9},{9,8},{10,11... | collective-permute-start | bytes 3145736 | tf_op jit(solution)/shard_map/ppermute | solution.py:29
  115.4 8.8 %collective-permute-start.12 = (f32[192,128]{1,0:T(8,128)S(1)}, f32[192,128]{1,0:T(8,128)S(1)}, u32[]{:S(2)}, u32[]{:S(2)}) collective-permute-start(f32[192,128]{1,0:T(8,128)S(1)} %add_add_fusion.3), channel_id=1, source_target_pairs={{0,128},{32,160},{64,192},{96,224},{128,0},{160,32},{192,64},{224,... | collective-permute-start | bytes 294920 | tf_op jit(solution)/shard_map/ppermute | solution.py:326
  124.2 3.3 %collective-permute-start.13 = (f32[192,128]{1,0:T(8,128)S(1)}, f32[192,128]{1,0:T(8,128)S(1)}, u32[]{:S(2)}, u32[]{:S(2)}) collective-permute-start(f32[192,128]{1,0:T(8,128)S(1)} %add.136), channel_id=1, source_target_pairs={{0,1},{1,0},{2,3},{3,2},{4,5},{5,4},{6,7},{7,6},{8,9},{9,8},{10,11... | collective-permute-start | bytes 294920 | tf_op jit(solution)/shard_map/ppermute | solution.py:29
  127.6 1.6 copy-start.5
  129.2 1.1 copy-start.7
  130.3 1.1 copy-start.9
  144.9 8.8 %collective-permute-start.26 = (f32[192,128]{1,0:T(8,128)S(1)}, f32[192,128]{1,0:T(8,128)S(1)}, u32[]{:S(2)}, u32[]{:S(2)}) collective-permute-start(f32[192,128]{1,0:T(8,128)S(1)} %dynamic-slice_bitcast_fusion), channel_id=1, source_target_pairs={{0,1},{1,0},{2,3},{3,2},{4,5},{5,4},{6,7},{7,6},{8,9},{9,8},{10,11... | collective-permute-start | bytes 294920 | tf_op jit(solution)/shard_map/ppermute | solution.py:29
  153.7 5.9 %collective-permute-start.27 = (f32[192,128]{1,0:T(8,128)S(1)}, f32[192,128]{1,0:T(8,128)S(1)}, u32[]{:S(2)}, u32[]{:S(2)}) collective-permute-start(f32[192,128]{1,0:T(8,128)S(1)} %bitcast_add_fusion), channel_id=1, source_target_pairs={{0,2},{2,4},{4,6},{6,0},{1,3},{3,5},{5,7},{7,1},{8,10},{10,12},{12... | collective-permute-start | bytes 294920 | tf_op jit(solution)/shard_map/ppermute | solution.py:326
  153.8 8.7 %collective-permute-start.28 = (f32[192,128]{1,0:T(8,128)S(1)}, f32[192,128]{1,0:T(8,128)S(1)}, u32[]{:S(2)}, u32[]{:S(2)}) collective-permute-start(f32[192,128]{1,0:T(8,128)S(1)} %bitcast_add_fusion), channel_id=1, source_target_pairs={{0,4},{2,6},{4,0},{6,2},{1,5},{3,7},{5,1},{7,3},{8,12},{10,14},{12... | collective-permute-start | bytes 294920 | tf_op jit(solution)/shard_map/ppermute | solution.py:326
  157.6 4.9 %collective-permute-start.29 = (f32[192,128]{1,0:T(8,128)S(1)}, f32[192,128]{1,0:T(8,128)S(1)}, u32[]{:S(2)}, u32[]{:S(2)}) collective-permute-start(f32[192,128]{1,0:T(8,128)S(1)} %bitcast_add_fusion), channel_id=1, source_target_pairs={{0,6},{2,0},{4,2},{6,4},{1,7},{3,1},{5,3},{7,5},{8,14},{10,8},{12,... | collective-permute-start | bytes 294920 | tf_op jit(solution)/shard_map/ppermute | solution.py:326
  162.5 7.3 %collective-permute-start.30 = (f32[192,128]{1,0:T(8,128)S(1)}, f32[192,128]{1,0:T(8,128)S(1)}, u32[]{:S(2)}, u32[]{:S(2)}) collective-permute-start(f32[192,128]{1,0:T(8,128)S(1)} %add_add_fusion.2), channel_id=1, source_target_pairs={{0,8},{8,16},{16,24},{24,0},{1,9},{9,17},{17,25},{25,1},{2,10},{10... | collective-permute-start | bytes 294920 | tf_op jit(solution)/shard_map/ppermute | solution.py:326
  162.6 7.3 %collective-permute-start.31 = (f32[192,128]{1,0:T(8,128)S(1)}, f32[192,128]{1,0:T(8,128)S(1)}, u32[]{:S(2)}, u32[]{:S(2)}) collective-permute-start(f32[192,128]{1,0:T(8,128)S(1)} %add_add_fusion.2), channel_id=1, source_target_pairs={{0,16},{8,24},{16,0},{24,8},{1,17},{9,25},{17,1},{25,9},{2,18},{10... | collective-permute-start | bytes 294920 | tf_op jit(solution)/shard_map/ppermute | solution.py:326
  163.7 6.2 %collective-permute-start.32 = (f32[192,128]{1,0:T(8,128)S(1)}, f32[192,128]{1,0:T(8,128)S(1)}, u32[]{:S(2)}, u32[]{:S(2)}) collective-permute-start(f32[192,128]{1,0:T(8,128)S(1)} %add_add_fusion.2), channel_id=1, source_target_pairs={{0,24},{8,0},{16,8},{24,16},{1,25},{9,1},{17,9},{25,17},{2,26},{10... | collective-permute-start | bytes 294920 | tf_op jit(solution)/shard_map/ppermute | solution.py:326
  165.3 27.0 %collective-permute-start.23 = (f32[2,4,128,128]{3,2,1,0:T(8,128)S(1)}, f32[2,4,128,128]{3,2,1,0:T(8,128)S(1)}, u32[]{:S(2)}, u32[]{:S(2)}) collective-permute-start(f32[2,4,128,128]{3,2,1,0:T(8,128)S(1)} %get-tuple-element.20), channel_id=1, source_target_pairs={{0,1},{1,0},{2,3},{3,2},{4,5},{5,4},{6,7},{7,6},{8,9},{9,8},{10,11... | collective-permute-start | bytes 1572872 | tf_op jit(solution)/shard_map/ppermute | solution.py:29
  169.9 5.3 %collective-permute-start.33 = (f32[192,128]{1,0:T(8,128)S(1)}, f32[192,128]{1,0:T(8,128)S(1)}, u32[]{:S(2)}, u32[]{:S(2)}) collective-permute-start(f32[192,128]{1,0:T(8,128)S(1)} %add_add_fusion.1), channel_id=1, source_target_pairs={{0,32},{32,64},{64,96},{96,0},{128,160},{160,192},{192,224},{224,1... | collective-permute-start | bytes 294920 | tf_op jit(solution)/shard_map/ppermute | solution.py:326
  172.7 8.0 %collective-permute-start.34 = (f32[192,128]{1,0:T(8,128)S(1)}, f32[192,128]{1,0:T(8,128)S(1)}, u32[]{:S(2)}, u32[]{:S(2)}) collective-permute-start(f32[192,128]{1,0:T(8,128)S(1)} %add_add_fusion.1), channel_id=1, source_target_pairs={{0,64},{32,96},{64,0},{96,32},{128,192},{160,224},{192,128},{224,1... | collective-permute-start | bytes 294920 | tf_op jit(solution)/shard_map/ppermute | solution.py:326
  173.5 7.2 %collective-permute-start.35 = (f32[192,128]{1,0:T(8,128)S(1)}, f32[192,128]{1,0:T(8,128)S(1)}, u32[]{:S(2)}, u32[]{:S(2)}) collective-permute-start(f32[192,128]{1,0:T(8,128)S(1)} %add_add_fusion.1), channel_id=1, source_target_pairs={{0,96},{32,0},{64,32},{96,64},{128,224},{160,128},{192,160},{224,1... | collective-permute-start | bytes 294920 | tf_op jit(solution)/shard_map/ppermute | solution.py:326
  180.7 8.5 %collective-permute-start.36 = (f32[192,128]{1,0:T(8,128)S(1)}, f32[192,128]{1,0:T(8,128)S(1)}, u32[]{:S(2)}, u32[]{:S(2)}) collective-permute-start(f32[192,128]{1,0:T(8,128)S(1)} %add_add_fusion), channel_id=1, source_target_pairs={{0,128},{32,160},{64,192},{96,224},{128,0},{160,32},{192,64},{224,... | collective-permute-start | bytes 294920 | tf_op jit(solution)/shard_map/ppermute | solution.py:326
  185.1 14.9 %collective-permute-start.22 = (f32[2,4,128,128]{3,2,1,0:T(8,128)S(1)}, f32[2,4,128,128]{3,2,1,0:T(8,128)S(1)}, u32[]{:S(2)}, u32[]{:S(2)}) collective-permute-start(f32[2,4,128,128]{3,2,1,0:T(8,128)S(1)} %get-tuple-element.18), channel_id=1, source_target_pairs={{0,1},{1,0},{2,3},{3,2},{4,5},{5,4},{6,7},{7,6},{8,9},{9,8},{10,11... | collective-permute-start | bytes 1572872 | tf_op jit(solution)/shard_map/ppermute | solution.py:29
  189.2 10.6 %collective-permute-start.37 = (f32[192,128]{1,0:T(8,128)S(1)}, f32[192,128]{1,0:T(8,128)S(1)}, u32[]{:S(2)}, u32[]{:S(2)}) collective-permute-start(f32[192,128]{1,0:T(8,128)S(1)} %add.159), channel_id=1, source_target_pairs={{0,1},{1,0},{2,3},{3,2},{4,5},{5,4},{6,7},{7,6},{8,9},{9,8},{10,11... | collective-permute-start | bytes 294920 | tf_op jit(solution)/shard_map/ppermute | solution.py:29
  192.4 22.3 %collective-permute-start.24 = (f32[2,4,128,128]{3,2,1,0:T(8,128)S(1)}, f32[2,4,128,128]{3,2,1,0:T(8,128)S(1)}, u32[]{:S(2)}, u32[]{:S(2)}) collective-permute-start(f32[2,4,128,128]{3,2,1,0:T(8,128)S(1)} %add.146), channel_id=1, source_target_pairs={{254,0},{0,2},{2,4},{4,6},{6,8},{8,10},{10,12},{12,14},{14,16},{16... | collective-permute-start | bytes 1572872 | tf_op jit(solution)/shard_map/ppermute | solution.py:34
  214.9 2.2 %collective-permute-start.25 = (f32[2,4,128,128]{3,2,1,0:T(8,128)S(1)}, f32[2,4,128,128]{3,2,1,0:T(8,128)S(1)}, u32[]{:S(2)}, u32[]{:S(2)}) collective-permute-start(f32[2,4,128,128]{3,2,1,0:T(8,128)S(1)} %add_divide_fusion), channel_id=1, source_target_pairs={{0,1},{1,0},{2,3},{3,2},{4,5},{5,4},{6,7},{7,6},{8,9},{9,8},{10,11... | collective-permute-start | bytes 1572872 | tf_op jit(solution)/shard_map/ppermute | solution.py:29

commit v2 on v1

v2 whole, which is shorter than its diff:
```python
import math

import jax
import jax.numpy as jnp
import numpy as np
from jax import lax
from jax.experimental import pallas as pl
from jax.experimental.pallas import tpu as pltpu
from jax.sharding import Mesh
from jax.sharding import PartitionSpec as P

PATCH = 128
STRIP = 128
COLS = 1024
BLOCKS = COLS // PATCH
HALF = BLOCKS // 2
BAND = 2 * STRIP
GROUP = 4
ITERS = 2
TILE = ("tile_0", "tile_1", "tile_2")
MODULUS_FLOOR = 0.2
OBJECT_RELAX = 1.0
ANY = pl.BlockSpec(memory_space=pl.ANY)
SMEM = pl.BlockSpec(memory_space=pltpu.SMEM)
VMEM = pl.BlockSpec(memory_space=pltpu.VMEM)


def swapped(value):
    return lax.ppermute(value, "pos", [(0, 1), (1, 0)])


def from_tile(value, distance):
    count = lax.axis_size(TILE)
    return lax.ppermute(value, TILE, [((i + distance) % count, i) for i in range(count)])


def two_terms(value):
    high = value.astype(jnp.bfloat16)
    low = (value - high.astype(jnp.float32)).astype(jnp.bfloat16)
    return high, low


def dft_tables():
    counter = np.arange(PATCH)
    angle = (counter[:, None] * counter[None, :] % PATCH) * (2.0 * math.pi / PATCH)
    cosine = np.cos(angle) / math.sqrt(PATCH)
    sine = np.sin(angle) / math.sqrt(PATCH)
    tables = []
    for sign in (1.0, -1.0):
        for turn in (1.0, -1.0):
            cross = sign * turn * sine
            table = np.block([[cosine, -cross], [cross, cosine]]).astype(np.float32)
            high = table.astype(jnp.bfloat16)
            tables += [high, (table - high.astype(np.float32)).astype(jnp.bfloat16)]
    return jnp.asarray(np.stack(tables))


def times_right(real, imag, high_table, low_table):
    stacked = jnp.concatenate(
        [jnp.concatenate([r, i], axis=1) for r, i in zip(real, imag)], axis=0
    )
    high, low = two_terms(stacked)
    wide = jnp.concatenate([high, low, high], axis=1)
    table = jnp.concatenate([high_table, high_table, low_table], axis=0)
    out = jnp.dot(wide, table, preferred_element_type=jnp.float32)
    return (
        [out[k * PATCH : (k + 1) * PATCH, :PATCH] for k in range(len(real))],
        [out[k * PATCH : (k + 1) * PATCH, PATCH:] for k in range(len(real))],
    )


def times_left(real, imag, high_table, low_table):
    stacked = jnp.concatenate(
        [jnp.concatenate(real, axis=1), jnp.concatenate(imag, axis=1)], axis=0
    )
    high, low = two_terms(stacked)
    tall = jnp.concatenate([high, low, high], axis=0)
    table = jnp.concatenate([high_table, high_table, low_table], axis=1)
    out = jnp.dot(table, tall, preferred_element_type=jnp.float32)
    return (
        [out[:PATCH, k * PATCH : (k + 1) * PATCH] for k in range(len(real))],
        [out[PATCH:, k * PATCH : (k + 1) * PATCH] for k in range(len(real))],
    )


def column_place(col, own_first):
    block = col // PATCH
    near = block ^ own_first
    far = ((block + 1) % BLOCKS) ^ own_first
    return near, far, col % PATCH


def positions_kernel(
    from_strips,
    core_ref,
    rows_ref,
    cols_ref,
    live_ref,
    probe_ref,
    amps_hbm,
    tables_hbm,
    first_ref,
    mine_ref,
    other_ref,
    keep_up_ref,
    keep_low_ref,
    give_up_ref,
    give_low_ref,
    probe_sums_ref,
    band,
    sums,
    amps_ref,
    tables,
    sems,
    amp_sems,
):
    own_first = core_ref[0] * HALF
    groups = amps_ref.shape[0] // GROUP

    def amp_copy(group):
        place = pl.ds(group * GROUP, GROUP)
        return pltpu.make_async_copy(amps_hbm.at[place], amps_ref.at[place], amp_sems.at[group])

    copies = [(tables_hbm, tables)]
    if from_strips:
        for k in range(BLOCKS):
            start = pl.multiple_of((k ^ own_first) * PATCH, PATCH)
            copies.append((first_ref.at[:, :, pl.ds(start, PATCH)], band.at[:, k, :STRIP, :]))
            half = mine_ref if k < HALF else other_ref
            columns = pl.ds(k % HALF * PATCH, PATCH)
            copies.append((half.at[:, :, columns], band.at[:, k, STRIP:, :]))
    else:
        copies.append((mine_ref, band.at[:, :HALF]))
        copies.append((other_ref, band.at[:, HALF:]))
    started = [pltpu.make_async_copy(a, b, sems.at[n]) for n, (a, b) in enumerate(copies)]
    for copy in started:
        copy.start()
    for group in range(groups):
        amp_copy(group).start()
    sums[...] = jnp.zeros_like(sums)
    probe_sums_ref[...] = jnp.zeros_like(probe_sums_ref)
    for copy in started:
        copy.wait()
    live = live_ref[0]
    lane = lax.broadcasted_iota(jnp.int32, (PATCH, PATCH), 1)

    def visit(step, carry):
        amp_copy(step).wait()
        slots = [step * GROUP + k for k in range(GROUP)]
        places = [column_place(cols_ref[s], own_first) for s in slots]
        rows = [rows_ref[s] for s in slots]
        alive = [s < live for s in slots]
        probe_real = probe_ref[0]
        probe_imag = probe_ref[1]
        patches = []
        exits = []
        for (near, far, shift), row in zip(places, rows):
            back = (PATCH - shift) % PATCH
            patch = []
            for plane in range(2):
                a = band[plane, near, pl.ds(row, PATCH), :]
                b = band[plane, far, pl.ds(row, PATCH), :]
                patch.append(pltpu.roll(jnp.where(lane >= shift, a, b), back, 1))
            patches.append(patch)
            exits.append(
                (
                    probe_real * patch[0] - probe_imag * patch[1],
                    probe_real * patch[1] + probe_imag * patch[0],
                )
            )
        revised = []
        for pair in range(0, GROUP, 2):
            real = [exits[pair + k][0] for k in range(2)]
            imag = [exits[pair + k][1] for k in range(2)]
            real, imag = times_right(real, imag, tables[0], tables[1])
            real, imag = times_left(real, imag, tables[2], tables[3])
            for k in range(2):
                power = real[k] * real[k] + imag[k] * imag[k]
                ratio = amps_ref[slots[pair + k]] * lax.rsqrt(
                    jnp.maximum(power, MODULUS_FLOOR * MODULUS_FLOOR)
                )
                real[k] = real[k] * ratio
                imag[k] = imag[k] * ratio
            real, imag = times_left(real, imag, tables[6], tables[7])
            real, imag = times_right(real, imag, tables[4], tables[5])
            revised.extend(zip(real, imag))
        totals = [probe_sums_ref[plane] for plane in range(3)]
        probe_power = probe_real * probe_real + probe_imag * probe_imag
        for k in range(GROUP):
            back_real = jnp.where(alive[k], revised[k][0], 0.0)
            back_imag = jnp.where(alive[k], revised[k][1], 0.0)
            patch_real = jnp.where(alive[k], patches[k][0], 0.0)
            patch_imag = jnp.where(alive[k], patches[k][1], 0.0)
            totals[0] += patch_real * back_real + patch_imag * back_imag
            totals[1] += patch_real * back_imag - patch_imag * back_real
            totals[2] += patch_real * patch_real + patch_imag * patch_imag
            near, far, shift = places[k]
            terms = (
                probe_real * back_real + probe_imag * back_imag,
                probe_real * back_imag - probe_imag * back_real,
                jnp.where(alive[k], probe_power, 0.0),
            )
            for plane in range(3):
                turned = pltpu.roll(terms[plane], shift, 1)
                inside = lane >= shift
                sums[plane, near, pl.ds(rows[k], PATCH), :] += jnp.where(inside, turned, 0.0)
                sums[plane, far, pl.ds(rows[k], PATCH), :] += jnp.where(inside, 0.0, turned)
        for plane in range(3):
            probe_sums_ref[plane] = totals[plane]
        return carry

    def skip(step, carry):
        amp_copy(step).wait()
        return carry

    steps = (live + GROUP - 1) // GROUP
    lax.fori_loop(0, steps, visit, 0)
    outs = (
        (sums.at[:, HALF:, STRIP:, :], give_low_ref),
        (sums.at[:, HALF:, :STRIP, :], give_up_ref),
        (sums.at[:, :HALF, STRIP:, :], keep_low_ref),
        (sums.at[:, :HALF, :STRIP, :], keep_up_ref),
    )
    started = [pltpu.make_async_copy(a, b, sems.at[n]) for n, (a, b) in enumerate(outs)]
    for copy in started:
        copy.start()
    lax.fori_loop(steps, groups, skip, 0)
    for copy in started:
        copy.wait()


def run_positions(scalars, probe, amps, tables, first, mine, other):
    from_strips = first is not None
    quarter = jax.ShapeDtypeStruct((3, HALF, STRIP, PATCH), jnp.float32)

    def kernel(*refs):
        if from_strips:
            positions_kernel(True, *refs)
        else:
            positions_kernel(False, *refs[:7], None, *refs[7:])

    pieces = (first, mine, other) if from_strips else (mine, other)
    return pl.pallas_call(
        kernel,
        out_shape=(quarter,) * 4 + (jax.ShapeDtypeStruct((3, PATCH, PATCH), jnp.float32),),
        in_specs=[SMEM] * 4 + [VMEM] + [ANY] * (2 + len(pieces)),
        out_specs=(ANY,) * 4 + (VMEM,),
        scratch_shapes=[
            pltpu.VMEM((2, BLOCKS, BAND, PATCH), jnp.float32),
            pltpu.VMEM((3, BLOCKS, BAND, PATCH), jnp.float32),
            pltpu.VMEM(amps.shape, jnp.float32),
            pltpu.VMEM(tables.shape, tables.dtype),
            pltpu.SemaphoreType.DMA((2 * BLOCKS + 1,)),
            pltpu.SemaphoreType.DMA((amps.shape[0] // GROUP,)),
        ],
        compiler_params=pltpu.CompilerParams(vmem_limit_bytes=40 * 2**20),
        cost_estimate=pl.CostEstimate(
            flops=13 * 10**9, bytes_accessed=8 * 2**20, transcendentals=2**19
        ),
        name="positions",
    )(*scalars, probe, amps, tables, *pieces)


def probe_sum_everywhere(value):
    core = lax.axis_index("pos")
    lines = value.reshape(2, -1, PATCH)
    mine = lax.dynamic_index_in_dim(lines, core, 0, False)
    other = lax.dynamic_index_in_dim(lines, 1 - core, 0, False)
    part = mine + swapped(other)
    for axis in TILE[::-1]:
        count = lax.axis_size(axis)
        stride = 1
        while stride < count:
            fan = 4 if count % (stride * 4) == 0 else 2
            part = shifts_among(part, axis, stride, fan)
            stride *= fan
    other = swapped(part)
    low = jnp.where(core == 0, part, other)
    high = jnp.where(core == 0, other, part)
    return jnp.concatenate([low, high]).reshape(value.shape)


def shifts_among(value, axis, stride, fan):
    count = lax.axis_size(axis)
    total = value
    for step in range(1, fan):
        route = []
        for i in range(count):
            place = i // stride % fan
            route.append((i, i + ((place + step) % fan - place) * stride))
        total = total + lax.ppermute(value, axis, route)
    return total


def in_blocks(value):
    lines = value.reshape(*value.shape[:2], HALF, PATCH)
    return lines.transpose(0, 2, 1, 3)


def on_device(object_field, probe_field, amplitudes, scan_rows, scan_cols, live_count):
    tables = dft_tables()
    core = lax.axis_index("pos")
    amps = amplitudes[0, 0]
    scalars = (
        core.reshape(1).astype(jnp.int32),
        scan_rows[0, 0],
        scan_cols[0, 0],
        live_count[0],
    )
    probe_relax = amps.shape[0] * lax.axis_size(TILE) * lax.axis_size("pos") / 4.0
    own_half = lax.dynamic_slice_in_dim(object_field, core * (COLS // 2), COLS // 2, 2)
    halo = from_tile(own_half, 1)
    halo_other = swapped(halo)
    up, low, give_up, give_low, probe_sums = run_positions(
        scalars, probe_field, amps, tables, object_field, halo, halo_other
    )

    def next_probe(sums, probe):
        total = probe_sum_everywhere(sums)
        return (total[:2] + probe_relax * probe) / (total[2] + probe_relax)[None]

    def updated(sums, field):
        return (sums[:2] + OBJECT_RELAX * field) / (sums[2] + OBJECT_RELAX)[None]

    low = low + swapped(give_low)
    up = up + swapped(give_up)
    above = from_tile(low, -1)
    below = from_tile(up, 1)
    probe_field = next_probe(probe_sums, probe_field)
    own_half = updated(up + above, in_blocks(own_half))
    mine = jnp.concatenate([own_half, updated(low + below, in_blocks(halo))], axis=2)
    other = swapped(mine)
    up, low, give_up, give_low, probe_sums = run_positions(
        scalars, probe_field, amps, tables, None, mine, other
    )
    low = low + swapped(give_low)
    up = up + swapped(give_up)
    above = from_tile(low, -1)
    probe_out = next_probe(probe_sums, probe_field)
    mine = updated(up + above, own_half).transpose(0, 2, 1, 3).reshape(2, STRIP, COLS // 2)
    other = swapped(mine)
    left = jnp.where(core == 0, mine, other)
    right = jnp.where(core == 0, other, mine)
    return jnp.concatenate([left, right], axis=2), probe_out


def torus_of(mesh):
    shape = (mesh.shape["tile"],)
    shape = (8, 4, 4) if shape == (128,) else (1, 1, *shape)
    return Mesh(mesh.devices.reshape(*shape, mesh.shape["pos"]), (*TILE, "pos"))


def solution(mesh):
    return jax.shard_map(
        on_device,
        mesh=torus_of(mesh),
        in_specs=(
            P(None, TILE, None),
            P(),
            P(TILE, "pos", None, None, None),
            P(TILE, "pos", None),
            P(TILE, "pos", None),
            P(TILE, "pos"),
        ),
        out_specs=(P(None, TILE, None), P()),
        check_vma=False,
    )
```

time: 223 us -> 203 us (0.910)
  the two profiles are of different devices: /device:TPU:1 before, /device:TPU:63 now
where the time goes in v2:
time: 203 us; the launch traced here: 204 us
  starting transfers between devices  89 us (44%)
  waiting for transfers between devices  74.4 us (37%)
  Pallas kernels  18.9 us (9%)
  local copies, waits for them, and re-layouts  13.5 us (7%)
  other arithmetic  6.35 us (3%)
    ppermute x20, starting transfers between devices, shifts_among(): total = total + lax.ppermute(value, axis, route)  53.4 us
    ppermute x20, waiting for transfers between devices, shifts_among(): total = total + lax.ppermute(value, axis, route)  48.9 us
    ppermute x4, starting transfers between devices, from_tile(): lax.ppermute(value, TILE, [((i + distance) % count, i) for i in range(cou...  20.4 us
    pallas_call x2, Pallas kernels, run_positions(): pl.pallas_call(kernel, out_shape=(quarter,) * 4 + (jax.ShapeDtypeStruct((...  18.9 us
    ppermute x4, waiting for transfers between devices, from_tile(): lax.ppermute(value, TILE, [((i + distance) % count, i) for i in range(cou...  17.3 us
    ppermute x11, starting transfers between devices, swapped(): return lax.ppermute(value, 'pos', [(0, 1), (1, 0)])  15.3 us
    unnamed x31, local copies, waits for them, and re-layouts  9.6 us
    ppermute x11, waiting for transfers between devices, swapped(): return lax.ppermute(value, 'pos', [(0, 1), (1, 0)])  8.29 us
  transfers between devices with their start and end apart: 35, of which 17 were waited for; matrix products, arithmetic and copies ran while one was open for 4% of the time, Pallas kernels for 0%

profile of v2, /device:TPU:63, one launch (start us, length us, event | category | flops | bytes accessed | tf_op | source)
XLA Modules:
  0.0 203.9 jit_solution(12561022432395906808)
XLA Ops:
  0.6 1.1 constant_dynamic-slice_fusion
  1.7 0.5 collective-permute-start
  2.3 16.5 %collective-permute-done.refs_8_ = f32[2,128,512]{2,1,0:T(8,128)S(1)} collective-permute-done((f32[2,128,512]{2,1,0:T(8,128)S(1)}, f32[2,128,512]{2,1,0:T(8,128)S(1)}, u32[]{:S(2)}, u32[]{:S(2)}) %collective-permute-start) | collective-permute-done | bytes 524320 | tf_op jit(solution)/shard_map/ppermute | solution.py:34
  18.8 1.5 collective-permute-start.1
  21.0 0.9 collective-permute-done.1.refs_9_
  21.9 1.2 copy-done
  23.1 0.9 copy-done.1
  24.0 1.6 copy-done.3
  25.6 0.7 copy-done.5
  26.3 0.7 copy-done.7
  26.9 1.2 copy-done.9
  28.2 9.1 %positions.2 = (f32[3,4,128,128]{3,2,1,0:T(8,128)S(1)}, f32[3,4,128,128]{3,2,1,0:T(8,128)S(1)}, f32[3,4,128,128]{3,2,1,0:T(8,128)S(1)}, f32[3,4,128,128]{3,2,1,0:T(8,128)S(1)}, f32[3,128,128]{2,1,0:T(8,128)S(1)}) custom-call(s32[1]{0:T(128)} %bitcast.refs_0_, s32[32]{0:T(128)S(1)} %bitcast.42, s32[32]{0:T(128)S(1)} %bitcast.44, s32[1]{0:T(128)} %bitcast.34.refs_3_, ...), custom_call_target="tpu_custom_call" | custom-call | flops 12999999488 | bytes 8388608 | tf_op jit(solution)/shard_map/positions/pallas_call | solution.py:243
  37.4 0.5 collective-permute-start.15
  37.9 1.9 collective-permute-done.14
  39.9 6.0 %collective-permute-start.17 = (f32[3,4,128,128]{3,2,1,0:T(8,128)S(1)}, f32[3,4,128,128]{3,2,1,0:T(8,128)}, u32[]{:S(2)}, u32[]{:S(2)}) collective-permute-start(f32[3,4,128,128]{3,2,1,0:T(8,128)S(1)} %add.153), channel_id=1, source_target_pairs={{2,0},{4,2},{6,4},{8,6},{10,8},{12,10},{14,12},{16,14},{18,16},{20... | collective-permute-start | bytes 2359304 | tf_op jit(solution)/shard_map/ppermute | solution.py:34
  45.9 0.7 collective-permute-start.2
  46.6 0.9 collective-permute-done.2
  47.8 2.6 %collective-permute-start.3 = (f32[192,128]{1,0:T(8,128)S(1)}, f32[192,128]{1,0:T(8,128)S(1)}, u32[]{:S(2)}, u32[]{:S(2)}) collective-permute-start(f32[192,128]{1,0:T(8,128)S(1)} %bitcast_add_fusion.1), channel_id=1, source_target_pairs={{0,2},{2,4},{4,6},{6,0},{1,3},{3,5},{5,7},{7,1},{8,10},{10,12},{12... | collective-permute-start | bytes 294920 | tf_op jit(solution)/shard_map/ppermute | solution.py:291
  50.4 18.4 %collective-permute-done.5 = f32[192,128]{1,0:T(8,128)S(1)} collective-permute-done((f32[192,128]{1,0:T(8,128)S(1)}, f32[192,128]{1,0:T(8,128)S(1)}, u32[]{:S(2)}, u32[]{:S(2)}) %collective-permute-start.5) | collective-permute-done | bytes 98336 | tf_op jit(solution)/shard_map/ppermute | solution.py:291
  69.0 2.6 %collective-permute-start.6 = (f32[192,128]{1,0:T(8,128)S(1)}, f32[192,128]{1,0:T(8,128)}, u32[]{:S(2)}, u32[]{:S(2)}) collective-permute-start(f32[192,128]{1,0:T(8,128)S(1)} %add_add_fusion.6), channel_id=1, source_target_pairs={{0,8},{8,16},{16,24},{24,0},{1,9},{9,17},{17,25},{25,1},{2,10},{10... | collective-permute-start | bytes 294920 | tf_op jit(solution)/shard_map/ppermute | solution.py:291
  71.6 2.4 %fusion.7 = (f32[3,4,128,128]{3,2,1,0:T(8,128)S(1)}, f32[3,4,128,128]{3,2,1,0:T(8,128)}) fusion(f32[3,4,128,128]{3,2,1,0:T(8,128)} %collective-permute-done.17, f32[3,4,128,128]{3,2,1,0:T(8,128)S(1)} %get-tuple-element.15, f32[3,4,128,128]{3,2,1,0:T(8,128)} %collective-permute-done.15), kind=kLoop, calls=%fused_computation.39 | loop fusion | flops 393216 | bytes 3932160 | tf_op jit(solution)/shard_map/add | solution.py:331
  74.0 1.5 collective-permute-start.16
  75.5 1.0 copy.9
  76.5 1.2 copy.10
  77.7 0.2 copy.11
  77.9 0.2 copy.12
  78.2 1.0 add_add_fusion.5
  79.2 6.9 %collective-permute-start.11 = (f32[192,128]{1,0:T(8,128)S(1)}, f32[192,128]{1,0:T(8,128)S(1)}, u32[]{:S(2)}, u32[]{:S(2)}) collective-permute-start(f32[192,128]{1,0:T(8,128)S(1)} %add_add_fusion.5), channel_id=1, source_target_pairs={{0,96},{32,0},{64,32},{96,64},{128,224},{160,128},{192,160},{224,1... | collective-permute-start | bytes 294920 | tf_op jit(solution)/shard_map/ppermute | solution.py:291
  86.1 3.1 %collective-permute-start.10 = (f32[192,128]{1,0:T(8,128)S(1)}, f32[192,128]{1,0:T(8,128)S(1)}, u32[]{:S(2)}, u32[]{:S(2)}) collective-permute-start(f32[192,128]{1,0:T(8,128)S(1)} %add_add_fusion.5), channel_id=1, source_target_pairs={{0,64},{32,96},{64,0},{96,32},{128,192},{160,224},{192,128},{224,1... | collective-permute-start | bytes 294920 | tf_op jit(solution)/shard_map/ppermute | solution.py:291
  89.2 2.3 %collective-permute-start.9 = (f32[192,128]{1,0:T(8,128)S(1)}, f32[192,128]{1,0:T(8,128)S(1)}, u32[]{:S(2)}, u32[]{:S(2)}) collective-permute-start(f32[192,128]{1,0:T(8,128)S(1)} %add_add_fusion.5), channel_id=1, source_target_pairs={{0,32},{32,64},{64,96},{96,0},{128,160},{160,192},{192,224},{224,1... | collective-permute-start | bytes 294920 | tf_op jit(solution)/shard_map/ppermute | solution.py:291
  91.6 0.7 collective-permute-done.16
  92.3 1.2 add.155
  93.6 0.8 copy-done.11
  94.5 4.5 %collective-permute-start.18 = (f32[2,4,256,128]{3,2,1,0:T(8,128)S(1)}, f32[2,4,256,128]{3,2,1,0:T(8,128)}, u32[]{:S(2)}, u32[]{:S(2)}) collective-permute-start(f32[2,4,256,128]{3,2,1,0:T(8,128)S(1)} %pad_maximum_fusion.refs_7_), channel_id=1, source_target_pairs={{0,1},{1,0},{2,3},{3,2},{4,5},{5,4},{6,7},{7,6},{8,9},{9,8},{10,11... | collective-permute-start | bytes 3145736 | tf_op jit(solution)/shard_map/ppermute | solution.py:29
  99.1 5.0 %collective-permute-done.9 = f32[192,128]{1,0:T(8,128)S(1)} collective-permute-done((f32[192,128]{1,0:T(8,128)S(1)}, f32[192,128]{1,0:T(8,128)S(1)}, u32[]{:S(2)}, u32[]{:S(2)}) %collective-permute-start.9) | collective-permute-done | bytes 98336 | tf_op jit(solution)/shard_map/ppermute | solution.py:291
  104.1 8.4 %collective-permute-start.12 = (f32[192,128]{1,0:T(8,128)S(1)}, f32[192,128]{1,0:T(8,128)S(1)}, u32[]{:S(2)}, u32[]{:S(2)}) collective-permute-start(f32[192,128]{1,0:T(8,128)S(1)} %add_add_fusion.4), channel_id=1, source_target_pairs={{0,128},{32,160},{64,192},{96,224},{128,0},{160,32},{192,64},{224,... | collective-permute-start | bytes 294920 | tf_op jit(solution)/shard_map/ppermute | solution.py:291
  112.5 3.7 %collective-permute-done.12 = f32[192,128]{1,0:T(8,128)S(1)} collective-permute-done((f32[192,128]{1,0:T(8,128)S(1)}, f32[192,128]{1,0:T(8,128)S(1)}, u32[]{:S(2)}, u32[]{:S(2)}) %collective-permute-start.12) | collective-permute-done | bytes 98336 | tf_op jit(solution)/shard_map/ppermute | solution.py:291
  116.2 1.3 collective-permute-start.13
  117.5 0.9 collective-permute-done.13
  118.6 1.2 copy-done.10
  119.8 9.7 %positions.3 = (f32[3,4,128,128]{3,2,1,0:T(8,128)S(1)}, f32[3,4,128,128]{3,2,1,0:T(8,128)S(1)}, f32[3,4,128,128]{3,2,1,0:T(8,128)S(1)}, f32[3,4,128,128]{3,2,1,0:T(8,128)S(1)}, f32[3,128,128]{2,1,0:T(8,128)S(1)}) custom-call(s32[1]{0:T(128)} %bitcast.refs_0_, s32[32]{0:T(128)S(1)} %bitcast.43, s32[32]{0:T(128)S(1)} %bitcast.45, s32[1]{0:T(128)} %bitcast.35.refs_3_, ...), custom_call_target="tpu_custom_call" | custom-call | flops 12999999488 | bytes 8388608 | tf_op jit(solution)/shard_map/positions/pallas_call | solution.py:243
  129.7 0.6 collective-permute-start.23
  130.2 1.8 collective-permute-done.23
  132.1 3.9 %collective-permute-start.26 = (f32[192,128]{1,0:T(8,128)S(1)}, f32[192,128]{1,0:T(8,128)S(1)}, u32[]{:S(2)}, u32[]{:S(2)}) collective-permute-start(f32[192,128]{1,0:T(8,128)S(1)} %bitcast_add_fusion), channel_id=1, source_target_pairs={{0,6},{2,0},{4,2},{6,4},{1,7},{3,1},{5,3},{7,5},{8,14},{10,8},{12,... | collective-permute-start | bytes 294920 | tf_op jit(solution)/shard_map/ppermute | solution.py:291
  136.0 2.5 %collective-permute-start.24 = (f32[192,128]{1,0:T(8,128)S(1)}, f32[192,128]{1,0:T(8,128)S(1)}, u32[]{:S(2)}, u32[]{:S(2)}) collective-permute-start(f32[192,128]{1,0:T(8,128)S(1)} %bitcast_add_fusion), channel_id=1, source_target_pairs={{0,2},{2,4},{4,6},{6,0},{1,3},{3,5},{5,7},{7,1},{8,10},{10,12},{12... | collective-permute-start | bytes 294920 | tf_op jit(solution)/shard_map/ppermute | solution.py:291
  138.5 2.5 %collective-permute-done.25 = f32[192,128]{1,0:T(8,128)S(1)} collective-permute-done((f32[192,128]{1,0:T(8,128)S(1)}, f32[192,128]{1,0:T(8,128)S(1)}, u32[]{:S(2)}, u32[]{:S(2)}) %collective-permute-start.25) | collective-permute-done | bytes 98336 | tf_op jit(solution)/shard_map/ppermute | solution.py:291
  141.2 5.0 %collective-permute-start.28 = (f32[192,128]{1,0:T(8,128)S(1)}, f32[192,128]{1,0:T(8,128)S(1)}, u32[]{:S(2)}, u32[]{:S(2)}) collective-permute-start(f32[192,128]{1,0:T(8,128)S(1)} %add_add_fusion.3), channel_id=1, source_target_pairs={{0,16},{8,24},{16,0},{24,8},{1,17},{9,25},{17,1},{25,9},{2,18},{10... | collective-permute-start | bytes 294920 | tf_op jit(solution)/shard_map/ppermute | solution.py:291
  146.2 1.8 collective-permute-start.19
  148.1 12.4 %collective-permute-start.21 = (f32[3,4,128,128]{3,2,1,0:T(8,128)S(1)}, f32[3,4,128,128]{3,2,1,0:T(8,128)S(1)}, u32[]{:S(2)}, u32[]{:S(2)}) collective-permute-start(f32[3,4,128,128]{3,2,1,0:T(8,128)S(1)} %add.162), channel_id=1, source_target_pairs={{254,0},{0,2},{2,4},{4,6},{6,8},{8,10},{10,12},{12,14},{14,16},{16... | collective-permute-start | bytes 2359304 | tf_op jit(solution)/shard_map/ppermute | solution.py:34
  160.5 3.1 %collective-permute-start.32 = (f32[192,128]{1,0:T(8,128)S(1)}, f32[192,128]{1,0:T(8,128)S(1)}, u32[]{:S(2)}, u32[]{:S(2)}) collective-permute-start(f32[192,128]{1,0:T(8,128)S(1)} %add_add_fusion.2), channel_id=1, source_target_pairs={{0,96},{32,0},{64,32},{96,64},{128,224},{160,128},{192,160},{224,1... | collective-permute-start | bytes 294920 | tf_op jit(solution)/shard_map/ppermute | solution.py:291
  163.6 3.3 %collective-permute-start.31 = (f32[192,128]{1,0:T(8,128)S(1)}, f32[192,128]{1,0:T(8,128)S(1)}, u32[]{:S(2)}, u32[]{:S(2)}) collective-permute-start(f32[192,128]{1,0:T(8,128)S(1)} %add_add_fusion.2), channel_id=1, source_target_pairs={{0,64},{32,96},{64,0},{96,32},{128,192},{160,224},{192,128},{224,1... | collective-permute-start | bytes 294920 | tf_op jit(solution)/shard_map/ppermute | solution.py:291
  166.9 2.3 %collective-permute-start.30 = (f32[192,128]{1,0:T(8,128)S(1)}, f32[192,128]{1,0:T(8,128)S(1)}, u32[]{:S(2)}, u32[]{:S(2)}) collective-permute-start(f32[192,128]{1,0:T(8,128)S(1)} %add_add_fusion.2), channel_id=1, source_target_pairs={{0,32},{32,64},{64,96},{96,0},{128,160},{160,192},{192,224},{224,1... | collective-permute-start | bytes 294920 | tf_op jit(solution)/shard_map/ppermute | solution.py:291
  169.1 14.6 %collective-permute-done.31 = f32[192,128]{1,0:T(8,128)S(1)} collective-permute-done((f32[192,128]{1,0:T(8,128)S(1)}, f32[192,128]{1,0:T(8,128)S(1)}, u32[]{:S(2)}, u32[]{:S(2)}) %collective-permute-start.31) | collective-permute-done | bytes 98336 | tf_op jit(solution)/shard_map/ppermute | solution.py:291
  183.7 2.1 %collective-permute-done.30 = f32[192,128]{1,0:T(8,128)S(1)} collective-permute-done((f32[192,128]{1,0:T(8,128)S(1)}, f32[192,128]{1,0:T(8,128)S(1)}, u32[]{:S(2)}, u32[]{:S(2)}) %collective-permute-start.30) | collective-permute-done | bytes 98336 | tf_op jit(solution)/shard_map/ppermute | solution.py:291
  185.9 7.1 %collective-permute-start.33 = (f32[192,128]{1,0:T(8,128)S(1)}, f32[192,128]{1,0:T(8,128)S(1)}, u32[]{:S(2)}, u32[]{:S(2)}) collective-permute-start(f32[192,128]{1,0:T(8,128)S(1)} %add_add_fusion.1), channel_id=1, source_target_pairs={{0,128},{32,160},{64,192},{96,224},{128,0},{160,32},{192,64},{224,... | collective-permute-start | bytes 294920 | tf_op jit(solution)/shard_map/ppermute | solution.py:291
  193.0 2.4 %collective-permute-done.33 = f32[192,128]{1,0:T(8,128)S(1)} collective-permute-done((f32[192,128]{1,0:T(8,128)S(1)}, f32[192,128]{1,0:T(8,128)S(1)}, u32[]{:S(2)}, u32[]{:S(2)}) %collective-permute-start.33) | collective-permute-done | bytes 98336 | tf_op jit(solution)/shard_map/ppermute | solution.py:291
  195.4 3.6 %collective-permute-start.34 = (f32[192,128]{1,0:T(8,128)S(1)}, f32[192,128]{1,0:T(8,128)S(1)}, u32[]{:S(2)}, u32[]{:S(2)}) collective-permute-start(f32[192,128]{1,0:T(8,128)S(1)} %add.176), channel_id=1, source_target_pairs={{0,1},{1,0},{2,3},{3,2},{4,5},{5,4},{6,7},{7,6},{8,9},{9,8},{10,11... | collective-permute-start | bytes 294920 | tf_op jit(solution)/shard_map/ppermute | solution.py:29
  199.0 0.9 collective-permute-done.34
  200.0 0.1 add_add_fusion
  200.3 0.2 copy.13
  200.5 0.4 collective-permute-start.22
  201.0 0.7 add_divide_fusion
  201.6 0.8 collective-permute-done.22
  202.6 1.3 copy.14
  (79 shorter events, 1.8 us)
Async XLA Ops:
  1.7 20.2 %copy-start.13 = (f32[2,128,512]{2,1,0:T(8,128)}, f32[2,128,512]{2,1,0:T(8,128)S(1)}, u32[]{:S(2)}) copy-start(f32[2,128,512]{2,1,0:T(8,128)S(1)} %constant_dynamic-slice_fusion) | copy-start | bytes 1572868
  1.7 17.1 %collective-permute-start = (f32[2,128,512]{2,1,0:T(8,128)S(1)}, f32[2,128,512]{2,1,0:T(8,128)S(1)}, u32[]{:S(2)}, u32[]{:S(2)}) collective-permute-start(f32[2,128,512]{2,1,0:T(8,128)S(1)} %constant_dynamic-slice_fusion), channel_id=1, source_target_pairs={{2,0},{4,2},{6,4},{8,6},{10,8},{12,10},{14,12},{16,14},{18,16},{20... | collective-permute-start | bytes 1572872 | tf_op jit(solution)/shard_map/ppermute | solution.py:34
  18.8 3.1 %collective-permute-start.1 = (f32[2,128,512]{2,1,0:T(8,128)S(1)}, f32[2,128,512]{2,1,0:T(8,128)S(1)}, u32[]{:S(2)}, u32[]{:S(2)}) collective-permute-start(f32[2,128,512]{2,1,0:T(8,128)S(1)} %collective-permute-done.refs_8_), channel_id=1, source_target_pairs={{0,1},{1,0},{2,3},{3,2},{4,5},{5,4},{6,7},{7,6},{8,9},{9,8},{10,11... | collective-permute-start | bytes 1572872 | tf_op jit(solution)/shard_map/ppermute | solution.py:29
  21.9 1.2 copy-start
  23.1 0.9 copy-start.1
  24.0 1.6 copy-start.3
  25.6 0.7 copy-start.5
  26.3 0.7 copy-start.7
  26.9 1.2 copy-start.9
  37.3 2.5 %collective-permute-start.14 = (f32[3,4,128,128]{3,2,1,0:T(8,128)S(1)}, f32[3,4,128,128]{3,2,1,0:T(8,128)S(1)}, u32[]{:S(2)}, u32[]{:S(2)}) collective-permute-start(f32[3,4,128,128]{3,2,1,0:T(8,128)S(1)} %get-tuple-element.14), channel_id=1, source_target_pairs={{0,1},{1,0},{2,3},{3,2},{4,5},{5,4},{6,7},{7,6},{8,9},{9,8},{10,11... | collective-permute-start | bytes 2359304 | tf_op jit(solution)/shard_map/ppermute | solution.py:29
  37.4 34.2 %collective-permute-start.15 = (f32[3,4,128,128]{3,2,1,0:T(8,128)S(1)}, f32[3,4,128,128]{3,2,1,0:T(8,128)}, u32[]{:S(2)}, u32[]{:S(2)}) collective-permute-start(f32[3,4,128,128]{3,2,1,0:T(8,128)S(1)} %get-tuple-element.16), channel_id=1, source_target_pairs={{0,1},{1,0},{2,3},{3,2},{4,5},{5,4},{6,7},{7,6},{8,9},{9,8},{10,11... | collective-permute-start | bytes 2359304 | tf_op jit(solution)/shard_map/ppermute | solution.py:29
  39.9 31.7 %collective-permute-start.17 = (f32[3,4,128,128]{3,2,1,0:T(8,128)S(1)}, f32[3,4,128,128]{3,2,1,0:T(8,128)}, u32[]{:S(2)}, u32[]{:S(2)}) collective-permute-start(f32[3,4,128,128]{3,2,1,0:T(8,128)S(1)} %add.153), channel_id=1, source_target_pairs={{2,0},{4,2},{6,4},{8,6},{10,8},{12,10},{14,12},{16,14},{18,16},{20... | collective-permute-start | bytes 2359304 | tf_op jit(solution)/shard_map/ppermute | solution.py:34
  45.9 1.7 collective-permute-start.2
  47.6 27.9 %copy-start.14 = (f32[2,128,512]{2,1,0:T(8,128)S(1)}, f32[2,128,512]{2,1,0:T(8,128)}, u32[]{:S(2)}) copy-start(f32[2,128,512]{2,1,0:T(8,128)} %copy-done.13) | copy-start | bytes 1572868
  47.6 21.2 %collective-permute-start.5 = (f32[192,128]{1,0:T(8,128)S(1)}, f32[192,128]{1,0:T(8,128)S(1)}, u32[]{:S(2)}, u32[]{:S(2)}) collective-permute-start(f32[192,128]{1,0:T(8,128)S(1)} %bitcast_add_fusion.1), channel_id=1, source_target_pairs={{0,6},{2,0},{4,2},{6,4},{1,7},{3,1},{5,3},{7,5},{8,14},{10,8},{12,... | collective-permute-start | bytes 294920 | tf_op jit(solution)/shard_map/ppermute | solution.py:291
  47.7 21.1 %collective-permute-start.4 = (f32[192,128]{1,0:T(8,128)S(1)}, f32[192,128]{1,0:T(8,128)S(1)}, u32[]{:S(2)}, u32[]{:S(2)}) collective-permute-start(f32[192,128]{1,0:T(8,128)S(1)} %bitcast_add_fusion.1), channel_id=1, source_target_pairs={{0,4},{2,6},{4,0},{6,2},{1,5},{3,7},{5,1},{7,3},{8,12},{10,14},{12... | collective-permute-start | bytes 294920 | tf_op jit(solution)/shard_map/ppermute | solution.py:291
  47.8 21.0 %collective-permute-start.3 = (f32[192,128]{1,0:T(8,128)S(1)}, f32[192,128]{1,0:T(8,128)S(1)}, u32[]{:S(2)}, u32[]{:S(2)}) collective-permute-start(f32[192,128]{1,0:T(8,128)S(1)} %bitcast_add_fusion.1), channel_id=1, source_target_pairs={{0,2},{2,4},{4,6},{6,0},{1,3},{3,5},{5,7},{7,1},{8,10},{10,12},{12... | collective-permute-start | bytes 294920 | tf_op jit(solution)/shard_map/ppermute | solution.py:291
  68.8 9.3 %collective-permute-start.8 = (f32[192,128]{1,0:T(8,128)S(1)}, f32[192,128]{1,0:T(8,128)}, u32[]{:S(2)}, u32[]{:S(2)}) collective-permute-start(f32[192,128]{1,0:T(8,128)S(1)} %add_add_fusion.6), channel_id=1, source_target_pairs={{0,24},{8,0},{16,8},{24,16},{1,25},{9,1},{17,9},{25,17},{2,26},{10... | collective-permute-start | bytes 294920 | tf_op jit(solution)/shard_map/ppermute | solution.py:291
  68.9 9.2 %collective-permute-start.7 = (f32[192,128]{1,0:T(8,128)S(1)}, f32[192,128]{1,0:T(8,128)}, u32[]{:S(2)}, u32[]{:S(2)}) collective-permute-start(f32[192,128]{1,0:T(8,128)S(1)} %add_add_fusion.6), channel_id=1, source_target_pairs={{0,16},{8,24},{16,0},{24,8},{1,17},{9,25},{17,1},{25,9},{2,18},{10... | collective-permute-start | bytes 294920 | tf_op jit(solution)/shard_map/ppermute | solution.py:291
  69.0 9.1 %collective-permute-start.6 = (f32[192,128]{1,0:T(8,128)S(1)}, f32[192,128]{1,0:T(8,128)}, u32[]{:S(2)}, u32[]{:S(2)}) collective-permute-start(f32[192,128]{1,0:T(8,128)S(1)} %add_add_fusion.6), channel_id=1, source_target_pairs={{0,8},{8,16},{16,24},{24,0},{1,9},{9,17},{17,25},{25,1},{2,10},{10... | collective-permute-start | bytes 294920 | tf_op jit(solution)/shard_map/ppermute | solution.py:291
  74.0 18.3 %collective-permute-start.16 = (f32[3,4,128,128]{3,2,1,0:T(8,128)}, f32[3,4,128,128]{3,2,1,0:T(8,128)}, u32[]{:S(2)}, u32[]{:S(2)}) collective-permute-start(f32[3,4,128,128]{3,2,1,0:T(8,128)} %get-tuple-element.25), channel_id=1, source_target_pairs={{254,0},{0,2},{2,4},{4,6},{6,8},{8,10},{10,12},{12,14},{14,16},{16... | collective-permute-start | bytes 2359304 | tf_op jit(solution)/shard_map/ppermute | solution.py:34
  79.2 19.9 %collective-permute-start.11 = (f32[192,128]{1,0:T(8,128)S(1)}, f32[192,128]{1,0:T(8,128)S(1)}, u32[]{:S(2)}, u32[]{:S(2)}) collective-permute-start(f32[192,128]{1,0:T(8,128)S(1)} %add_add_fusion.5), channel_id=1, source_target_pairs={{0,96},{32,0},{64,32},{96,64},{128,224},{160,128},{192,160},{224,1... | collective-permute-start | bytes 294920 | tf_op jit(solution)/shard_map/ppermute | solution.py:291
  86.1 13.0 %collective-permute-start.10 = (f32[192,128]{1,0:T(8,128)S(1)}, f32[192,128]{1,0:T(8,128)S(1)}, u32[]{:S(2)}, u32[]{:S(2)}) collective-permute-start(f32[192,128]{1,0:T(8,128)S(1)} %add_add_fusion.5), channel_id=1, source_target_pairs={{0,64},{32,96},{64,0},{96,32},{128,192},{160,224},{192,128},{224,1... | collective-permute-start | bytes 294920 | tf_op jit(solution)/shard_map/ppermute | solution.py:291
  89.2 14.8 %collective-permute-start.9 = (f32[192,128]{1,0:T(8,128)S(1)}, f32[192,128]{1,0:T(8,128)S(1)}, u32[]{:S(2)}, u32[]{:S(2)}) collective-permute-start(f32[192,128]{1,0:T(8,128)S(1)} %add_add_fusion.5), channel_id=1, source_target_pairs={{0,32},{32,64},{64,96},{96,0},{128,160},{160,192},{192,224},{224,1... | collective-permute-start | bytes 294920 | tf_op jit(solution)/shard_map/ppermute | solution.py:291
  93.6 0.8 copy-start.11
  94.4 24.1 %copy-start.2 = (f32[2,128,128]{2,1,0:T(8,128)S(1)}, f32[2,128,128]{2,1,0:T(8,128)}, u32[]{:S(2)}) copy-start(f32[2,128,128]{2,1,0:T(8,128)} %refs_4_.1) | copy-start | bytes 393220
  94.4 24.1 %copy-start.4 = (f32[1,1,32,128,128]{4,3,2,1,0:T(8,128)S(1)}, f32[1,1,32,128,128]{4,3,2,1,0:T(8,128)}, u32[]{:S(2)}) copy-start(f32[1,1,32,128,128]{4,3,2,1,0:T(8,128)} %param.9) | copy-start | bytes 6291460
  94.4 24.1 %copy-start.6 = (s32[1,1,32]{2,1,0:T(1,128)S(1)}, s32[1,1,32]{2,1,0:T(1,128)}, u32[]{:S(2)}) copy-start(s32[1,1,32]{2,1,0:T(1,128)} %param.10) | copy-start | bytes 388
  94.4 24.1 %copy-start.8 = (s32[1,1,32]{2,1,0:T(1,128)S(1)}, s32[1,1,32]{2,1,0:T(1,128)}, u32[]{:S(2)}) copy-start(s32[1,1,32]{2,1,0:T(1,128)} %param.11) | copy-start | bytes 388
  94.5 24.0 %collective-permute-start.18 = (f32[2,4,256,128]{3,2,1,0:T(8,128)S(1)}, f32[2,4,256,128]{3,2,1,0:T(8,128)}, u32[]{:S(2)}, u32[]{:S(2)}) collective-permute-start(f32[2,4,256,128]{3,2,1,0:T(8,128)S(1)} %pad_maximum_fusion.refs_7_), channel_id=1, source_target_pairs={{0,1},{1,0},{2,3},{3,2},{4,5},{5,4},{6,7},{7,6},{8,9},{9,8},{10,11... | collective-permute-start | bytes 3145736 | tf_op jit(solution)/shard_map/ppermute | solution.py:29
  104.1 12.1 %collective-permute-start.12 = (f32[192,128]{1,0:T(8,128)S(1)}, f32[192,128]{1,0:T(8,128)S(1)}, u32[]{:S(2)}, u32[]{:S(2)}) collective-permute-start(f32[192,128]{1,0:T(8,128)S(1)} %add_add_fusion.4), channel_id=1, source_target_pairs={{0,128},{32,160},{64,192},{96,224},{128,0},{160,32},{192,64},{224,... | collective-permute-start | bytes 294920 | tf_op jit(solution)/shard_map/ppermute | solution.py:291
  116.2 2.2 %collective-permute-start.13 = (f32[192,128]{1,0:T(8,128)S(1)}, f32[192,128]{1,0:T(8,128)S(1)}, u32[]{:S(2)}, u32[]{:S(2)}) collective-permute-start(f32[192,128]{1,0:T(8,128)S(1)} %add.150), channel_id=1, source_target_pairs={{0,1},{1,0},{2,3},{3,2},{4,5},{5,4},{6,7},{7,6},{8,9},{9,8},{10,11... | collective-permute-start | bytes 294920 | tf_op jit(solution)/shard_map/ppermute | solution.py:29
  118.6 1.2 copy-start.10
  129.5 18.5 %collective-permute-start.20 = (f32[3,4,128,128]{3,2,1,0:T(8,128)S(1)}, f32[3,4,128,128]{3,2,1,0:T(8,128)S(1)}, u32[]{:S(2)}, u32[]{:S(2)}) collective-permute-start(f32[3,4,128,128]{3,2,1,0:T(8,128)S(1)} %get-tuple-element.20), channel_id=1, source_target_pairs={{0,1},{1,0},{2,3},{3,2},{4,5},{5,4},{6,7},{7,6},{8,9},{9,8},{10,11... | collective-permute-start | bytes 2359304 | tf_op jit(solution)/shard_map/ppermute | solution.py:29
  129.7 2.4 %collective-permute-start.23 = (f32[192,128]{1,0:T(8,128)S(1)}, f32[192,128]{1,0:T(8,128)S(1)}, u32[]{:S(2)}, u32[]{:S(2)}) collective-permute-start(f32[192,128]{1,0:T(8,128)S(1)} %dynamic-slice_bitcast_fusion), channel_id=1, source_target_pairs={{0,1},{1,0},{2,3},{3,2},{4,5},{5,4},{6,7},{7,6},{8,9},{9,8},{10,11... | collective-permute-start | bytes 294920 | tf_op jit(solution)/shard_map/ppermute | solution.py:29
  132.1 6.4 %collective-permute-start.26 = (f32[192,128]{1,0:T(8,128)S(1)}, f32[192,128]{1,0:T(8,128)S(1)}, u32[]{:S(2)}, u32[]{:S(2)}) collective-permute-start(f32[192,128]{1,0:T(8,128)S(1)} %bitcast_add_fusion), channel_id=1, source_target_pairs={{0,6},{2,0},{4,2},{6,4},{1,7},{3,1},{5,3},{7,5},{8,14},{10,8},{12,... | collective-permute-start | bytes 294920 | tf_op jit(solution)/shard_map/ppermute | solution.py:291
  136.0 5.0 %collective-permute-start.25 = (f32[192,128]{1,0:T(8,128)S(1)}, f32[192,128]{1,0:T(8,128)S(1)}, u32[]{:S(2)}, u32[]{:S(2)}) collective-permute-start(f32[192,128]{1,0:T(8,128)S(1)} %bitcast_add_fusion), channel_id=1, source_target_pairs={{0,4},{2,6},{4,0},{6,2},{1,5},{3,7},{5,1},{7,3},{8,12},{10,14},{12... | collective-permute-start | bytes 294920 | tf_op jit(solution)/shard_map/ppermute | solution.py:291
  136.0 5.1 %collective-permute-start.24 = (f32[192,128]{1,0:T(8,128)S(1)}, f32[192,128]{1,0:T(8,128)S(1)}, u32[]{:S(2)}, u32[]{:S(2)}) collective-permute-start(f32[192,128]{1,0:T(8,128)S(1)} %bitcast_add_fusion), channel_id=1, source_target_pairs={{0,2},{2,4},{4,6},{6,0},{1,3},{3,5},{5,7},{7,1},{8,10},{10,12},{12... | collective-permute-start | bytes 294920 | tf_op jit(solution)/shard_map/ppermute | solution.py:291
  141.1 19.3 %collective-permute-start.29 = (f32[192,128]{1,0:T(8,128)S(1)}, f32[192,128]{1,0:T(8,128)S(1)}, u32[]{:S(2)}, u32[]{:S(2)}) collective-permute-start(f32[192,128]{1,0:T(8,128)S(1)} %add_add_fusion.3), channel_id=1, source_target_pairs={{0,24},{8,0},{16,8},{24,16},{1,25},{9,1},{17,9},{25,17},{2,26},{10... | collective-permute-start | bytes 294920 | tf_op jit(solution)/shard_map/ppermute | solution.py:291
  141.2 19.3 %collective-permute-start.28 = (f32[192,128]{1,0:T(8,128)S(1)}, f32[192,128]{1,0:T(8,128)S(1)}, u32[]{:S(2)}, u32[]{:S(2)}) collective-permute-start(f32[192,128]{1,0:T(8,128)S(1)} %add_add_fusion.3), channel_id=1, source_target_pairs={{0,16},{8,24},{16,0},{24,8},{1,17},{9,25},{17,1},{25,9},{2,18},{10... | collective-permute-start | bytes 294920 | tf_op jit(solution)/shard_map/ppermute | solution.py:291
  146.2 14.3 %collective-permute-start.27 = (f32[192,128]{1,0:T(8,128)S(1)}, f32[192,128]{1,0:T(8,128)S(1)}, u32[]{:S(2)}, u32[]{:S(2)}) collective-permute-start(f32[192,128]{1,0:T(8,128)S(1)} %add_add_fusion.3), channel_id=1, source_target_pairs={{0,8},{8,16},{16,24},{24,0},{1,9},{9,17},{17,25},{25,1},{2,10},{10... | collective-permute-start | bytes 294920 | tf_op jit(solution)/shard_map/ppermute | solution.py:291
  146.2 53.8 %collective-permute-start.19 = (f32[3,4,128,128]{3,2,1,0:T(8,128)S(1)}, f32[3,4,128,128]{3,2,1,0:T(8,128)S(1)}, u32[]{:S(2)}, u32[]{:S(2)}) collective-permute-start(f32[3,4,128,128]{3,2,1,0:T(8,128)S(1)} %get-tuple-element.18), channel_id=1, source_target_pairs={{0,1},{1,0},{2,3},{3,2},{4,5},{5,4},{6,7},{7,6},{8,9},{9,8},{10,11... | collective-permute-start | bytes 2359304 | tf_op jit(solution)/shard_map/ppermute | solution.py:29
  148.1 51.9 %collective-permute-start.21 = (f32[3,4,128,128]{3,2,1,0:T(8,128)S(1)}, f32[3,4,128,128]{3,2,1,0:T(8,128)S(1)}, u32[]{:S(2)}, u32[]{:S(2)}) collective-permute-start(f32[3,4,128,128]{3,2,1,0:T(8,128)S(1)} %add.162), channel_id=1, source_target_pairs={{254,0},{0,2},{2,4},{4,6},{6,8},{8,10},{10,12},{12,14},{14,16},{16... | collective-permute-start | bytes 2359304 | tf_op jit(solution)/shard_map/ppermute | solution.py:34
  160.5 8.6 %collective-permute-start.32 = (f32[192,128]{1,0:T(8,128)S(1)}, f32[192,128]{1,0:T(8,128)S(1)}, u32[]{:S(2)}, u32[]{:S(2)}) collective-permute-start(f32[192,128]{1,0:T(8,128)S(1)} %add_add_fusion.2), channel_id=1, source_target_pairs={{0,96},{32,0},{64,32},{96,64},{128,224},{160,128},{192,160},{224,1... | collective-permute-start | bytes 294920 | tf_op jit(solution)/shard_map/ppermute | solution.py:291
  163.6 20.1 %collective-permute-start.31 = (f32[192,128]{1,0:T(8,128)S(1)}, f32[192,128]{1,0:T(8,128)S(1)}, u32[]{:S(2)}, u32[]{:S(2)}) collective-permute-start(f32[192,128]{1,0:T(8,128)S(1)} %add_add_fusion.2), channel_id=1, source_target_pairs={{0,64},{32,96},{64,0},{96,32},{128,192},{160,224},{192,128},{224,1... | collective-permute-start | bytes 294920 | tf_op jit(solution)/shard_map/ppermute | solution.py:291
  166.9 19.0 %collective-permute-start.30 = (f32[192,128]{1,0:T(8,128)S(1)}, f32[192,128]{1,0:T(8,128)S(1)}, u32[]{:S(2)}, u32[]{:S(2)}) collective-permute-start(f32[192,128]{1,0:T(8,128)S(1)} %add_add_fusion.2), channel_id=1, source_target_pairs={{0,32},{32,64},{64,96},{96,0},{128,160},{160,192},{192,224},{224,1... | collective-permute-start | bytes 294920 | tf_op jit(solution)/shard_map/ppermute | solution.py:291
  185.9 9.5 %collective-permute-start.33 = (f32[192,128]{1,0:T(8,128)S(1)}, f32[192,128]{1,0:T(8,128)S(1)}, u32[]{:S(2)}, u32[]{:S(2)}) collective-permute-start(f32[192,128]{1,0:T(8,128)S(1)} %add_add_fusion.1), channel_id=1, source_target_pairs={{0,128},{32,160},{64,192},{96,224},{128,0},{160,32},{192,64},{224,... | collective-permute-start | bytes 294920 | tf_op jit(solution)/shard_map/ppermute | solution.py:291
  195.4 4.8 %copy-start.12 = (f32[2,4,128,128]{3,2,1,0:T(8,128)S(1)}, f32[2,4,128,128]{3,2,1,0:T(8,128)}, u32[]{:S(2)}) copy-start(f32[2,4,128,128]{3,2,1,0:T(8,128)} %copy-done.11) | copy-start | bytes 1572868
  195.4 4.6 %collective-permute-start.34 = (f32[192,128]{1,0:T(8,128)S(1)}, f32[192,128]{1,0:T(8,128)S(1)}, u32[]{:S(2)}, u32[]{:S(2)}) collective-permute-start(f32[192,128]{1,0:T(8,128)S(1)} %add.176), channel_id=1, source_target_pairs={{0,1},{1,0},{2,3},{3,2},{4,5},{5,4},{6,7},{7,6},{8,9},{9,8},{10,11... | collective-permute-start | bytes 294920 | tf_op jit(solution)/shard_map/ppermute | solution.py:29
  200.5 2.0 collective-permute-start.22

commit v3 on v2

--- a/solution.py
+++ b/solution.py
@@ -15,13 +15,12 @@
 BLOCKS = COLS // PATCH
 HALF = BLOCKS // 2
 BAND = 2 * STRIP
-GROUP = 4
+GROUP = 8
 ITERS = 2
 TILE = ("tile_0", "tile_1", "tile_2")
 MODULUS_FLOOR = 0.2
 OBJECT_RELAX = 1.0
 ANY = pl.BlockSpec(memory_space=pl.ANY)
-SMEM = pl.BlockSpec(memory_space=pltpu.SMEM)
 VMEM = pl.BlockSpec(memory_space=pltpu.VMEM)
 
 
@@ -92,10 +91,7 @@
 
 def positions_kernel(
     from_strips,
-    core_ref,
-    rows_ref,
-    cols_ref,
-    live_ref,
+    scalars_hbm,
     probe_ref,
     amps_hbm,
     tables_hbm,
@@ -111,16 +107,24 @@
     sums,
     amps_ref,
     tables,
+    scalars,
     sems,
     amp_sems,
 ):
-    own_first = core_ref[0] * HALF
     groups = amps_ref.shape[0] // GROUP
+    fetch = pltpu.make_async_copy(scalars_hbm, scalars, sems.at[2 * BLOCKS + 1])
+    fetch.start()
 
     def amp_copy(group):
         place = pl.ds(group * GROUP, GROUP)
         return pltpu.make_async_copy(amps_hbm.at[place], amps_ref.at[place], amp_sems.at[group])
 
+    for group in range(groups):
+        amp_copy(group).start()
+    sums[...] = jnp.zeros_like(sums)
+    probe_sums_ref[...] = jnp.zeros_like(probe_sums_ref)
+    fetch.wait()
+    own_first = scalars[2, 1] * HALF
     copies = [(tables_hbm, tables)]
     if from_strips:
         for k in range(BLOCKS):
@@ -135,78 +139,90 @@
     started = [pltpu.make_async_copy(a, b, sems.at[n]) for n, (a, b) in enumerate(copies)]
     for copy in started:
         copy.start()
-    for group in range(groups):
-        amp_copy(group).start()
-    sums[...] = jnp.zeros_like(sums)
-    probe_sums_ref[...] = jnp.zeros_like(probe_sums_ref)
     for copy in started:
         copy.wait()
-    live = live_ref[0]
+    live = scalars[2, 0]
     lane = lax.broadcasted_iota(jnp.int32, (PATCH, PATCH), 1)
 
     def visit(step, carry):
         amp_copy(step).wait()
         slots = [step * GROUP + k for k in range(GROUP)]
-        places = [column_place(cols_ref[s], own_first) for s in slots]
-        rows = [rows_ref[s] for s in slots]
-        alive = [s < live for s in slots]
-        probe_real = probe_ref[0]
-        probe_imag = probe_ref[1]
-        patches = []
-        exits = []
-        for (near, far, shift), row in zip(places, rows):
-            back = (PATCH - shift) % PATCH
-            patch = []
-            for plane in range(2):
-                a = band[plane, near, pl.ds(row, PATCH), :]
-                b = band[plane, far, pl.ds(row, PATCH), :]
-                patch.append(pltpu.roll(jnp.where(lane >= shift, a, b), back, 1))
-            patches.append(patch)
-            exits.append(
-                (
-                    probe_real * patch[0] - probe_imag * patch[1],
-                    probe_real * patch[1] + probe_imag * patch[0],
-                )
-            )
-        revised = []
-        for pair in range(0, GROUP, 2):
-            real = [exits[pair + k][0] for k in range(2)]
-            imag = [exits[pair + k][1] for k in range(2)]
-            real, imag = times_right(real, imag, tables[0], tables[1])
-            real, imag = times_left(real, imag, tables[2], tables[3])
+        places = [column_place(scalars[1, s], own_first) for s in slots]
+        rows = [scalars[0, s] for s in slots]
+        patches = {}
+        waves = {}
+
+        def cut(pair):
+            probe_real, probe_imag = probe_ref[0], probe_ref[1]
+            real, imag = [], []
+            for k in (2 * pair, 2 * pair + 1):
+                near, far, shift = places[k]
+                back = (PATCH - shift) % PATCH
+                patch = []
+                for plane in range(2):
+                    a = band[plane, near, pl.ds(rows[k], PATCH), :]
+                    b = band[plane, far, pl.ds(rows[k], PATCH), :]
+                    patch.append(pltpu.roll(jnp.where(lane >= shift, a, b), back, 1))
+                patches[k] = patch
+                real.append(probe_real * patch[0] - probe_imag * patch[1])
+                imag.append(probe_real * patch[1] + probe_imag * patch[0])
+            waves[pair] = (real, imag)
+
+        def rescale(pair):
+            real, imag = waves[pair]
             for k in range(2):
+                slot = slots[2 * pair + k]
                 power = real[k] * real[k] + imag[k] * imag[k]
-                ratio = amps_ref[slots[pair + k]] * lax.rsqrt(
+                ratio = jnp.where(slot < live, amps_ref[slot], 0.0) * lax.rsqrt(
                     jnp.maximum(power, MODULUS_FLOOR * MODULUS_FLOOR)
                 )
                 real[k] = real[k] * ratio
                 imag[k] = imag[k] * ratio
-            real, imag = times_left(real, imag, tables[6], tables[7])
-            real, imag = times_right(real, imag, tables[4], tables[5])
-            revised.extend(zip(real, imag))
-        totals = [probe_sums_ref[plane] for plane in range(3)]
-        probe_power = probe_real * probe_real + probe_imag * probe_imag
-        for k in range(GROUP):
-            back_real = jnp.where(alive[k], revised[k][0], 0.0)
-            back_imag = jnp.where(alive[k], revised[k][1], 0.0)
-            patch_real = jnp.where(alive[k], patches[k][0], 0.0)
-            patch_imag = jnp.where(alive[k], patches[k][1], 0.0)
-            totals[0] += patch_real * back_real + patch_imag * back_imag
-            totals[1] += patch_real * back_imag - patch_imag * back_real
-            totals[2] += patch_real * patch_real + patch_imag * patch_imag
-            near, far, shift = places[k]
-            terms = (
-                probe_real * back_real + probe_imag * back_imag,
-                probe_real * back_imag - probe_imag * back_real,
-                jnp.where(alive[k], probe_power, 0.0),
-            )
+
+        def right(pair, table):
+            waves[pair] = times_right(*waves[pair], tables[table], tables[table + 1])
+
+        def left(pair, table):
+            waves[pair] = times_left(*waves[pair], tables[table], tables[table + 1])
+
+        def collect(pair):
+            probe_real, probe_imag = probe_ref[0], probe_ref[1]
+            probe_power = probe_real * probe_real + probe_imag * probe_imag
+            totals = [0.0, 0.0, 0.0]
+            for back_real, back_imag, k in zip(*waves[pair], (2 * pair, 2 * pair + 1)):
+                alive = slots[k] < live
+                patch_real, patch_imag = patches[k]
+                patch_power = patch_real * patch_real + patch_imag * patch_imag
+                totals[0] += patch_real * back_real + patch_imag * back_imag
+                totals[1] += patch_real * back_imag - patch_imag * back_real
+                totals[2] += jnp.where(alive, patch_power, 0.0)
+                near, far, shift = places[k]
+                terms = (
+                    probe_real * back_real + probe_imag * back_imag,
+                    probe_real * back_imag - probe_imag * back_real,
+                    jnp.where(alive, probe_power, 0.0),
+                )
+                inside = lane >= shift
+                for plane in range(3):
+                    turned = pltpu.roll(terms[plane], shift, 1)
+                    sums[plane, near, pl.ds(rows[k], PATCH), :] += jnp.where(inside, turned, 0.0)
+                    sums[plane, far, pl.ds(rows[k], PATCH), :] += jnp.where(inside, 0.0, turned)
             for plane in range(3):
-                turned = pltpu.roll(terms[plane], shift, 1)
-                inside = lane >= shift
-                sums[plane, near, pl.ds(rows[k], PATCH), :] += jnp.where(inside, turned, 0.0)
-                sums[plane, far, pl.ds(rows[k], PATCH), :] += jnp.where(inside, 0.0, turned)
-        for plane in range(3):
-            probe_sums_ref[plane] = totals[plane]
+                probe_sums_ref[plane] += totals[plane]
+
+        stages = (
+            cut,
+            lambda pair: right(pair, 0),
+            lambda pair: left(pair, 2),
+            rescale,
+            lambda pair: left(pair, 6),
+            lambda pair: right(pair, 4),
+            collect,
+        )
+        pairs = GROUP // 2
+        for stage in stages:
+            for pair in range(pairs):
+                stage(pair)
         return carry
 
     def skip(step, carry):
@@ -237,47 +253,59 @@
         if from_strips:
             positions_kernel(True, *refs)
         else:
-            positions_kernel(False, *refs[:7], None, *refs[7:])
+            positions_kernel(False, *refs[:4], None, *refs[4:])
 
     pieces = (first, mine, other) if from_strips else (mine, other)
     return pl.pallas_call(
         kernel,
         out_shape=(quarter,) * 4 + (jax.ShapeDtypeStruct((3, PATCH, PATCH), jnp.float32),),
-        in_specs=[SMEM] * 4 + [VMEM] + [ANY] * (2 + len(pieces)),
+        in_specs=[ANY, VMEM] + [ANY] * (2 + len(pieces)),
         out_specs=(ANY,) * 4 + (VMEM,),
         scratch_shapes=[
             pltpu.VMEM((2, BLOCKS, BAND, PATCH), jnp.float32),
             pltpu.VMEM((3, BLOCKS, BAND, PATCH), jnp.float32),
             pltpu.VMEM(amps.shape, jnp.float32),
             pltpu.VMEM(tables.shape, tables.dtype),
-            pltpu.SemaphoreType.DMA((2 * BLOCKS + 1,)),
+            pltpu.SMEM(scalars.shape, jnp.int32),
+            pltpu.SemaphoreType.DMA((2 * BLOCKS + 2,)),
             pltpu.SemaphoreType.DMA((amps.shape[0] // GROUP,)),
         ],
-        compiler_params=pltpu.CompilerParams(vmem_limit_bytes=40 * 2**20),
+        compiler_params=pltpu.CompilerParams(vmem_limit_bytes=60 * 2**20),
         cost_estimate=pl.CostEstimate(
             flops=13 * 10**9, bytes_accessed=8 * 2**20, transcendentals=2**19
         ),
         name="positions",
-    )(*scalars, probe, amps, tables, *pieces)
-
-
-def probe_sum_everywhere(value):
+    )(scalars, probe, amps, tables, *pieces)
+
+
+def halved_over_cores(value):
     core = lax.axis_index("pos")
     lines = value.reshape(2, -1, PATCH)
     mine = lax.dynamic_index_in_dim(lines, core, 0, False)
     other = lax.dynamic_index_in_dim(lines, 1 - core, 0, False)
-    part = mine + swapped(other)
-    for axis in TILE[::-1]:
-        count = lax.axis_size(axis)
-        stride = 1
-        while stride < count:
-            fan = 4 if count % (stride * 4) == 0 else 2
-            part = shifts_among(part, axis, stride, fan)
-            stride *= fan
+    return mine + swapped(other)
+
+
+def joined_over_cores(part):
+    first = lax.axis_index("pos") == 0
     other = swapped(part)
-    low = jnp.where(core == 0, part, other)
-    high = jnp.where(core == 0, other, part)
-    return jnp.concatenate([low, high]).reshape(value.shape)
+    low = jnp.where(first, part, other)
+    high = jnp.where(first, other, part)
+    return jnp.concatenate([low, high])
+
+
+def summed_over(part, axis):
+    count = lax.axis_size(axis)
+    stride = 1
+    while stride < count:
+        fan = 4 if count % (stride * 4) == 0 else 2
+        part = shifts_among(part, axis, stride, fan)
+        stride *= fan
+    return part
+
+
+def after(value, other):
+    return value + jnp.minimum(jnp.abs(other[0, 0]), 0.0)
 
 
 def shifts_among(value, axis, stride, fan):
@@ -301,12 +329,10 @@
     tables = dft_tables()
     core = lax.axis_index("pos")
     amps = amplitudes[0, 0]
-    scalars = (
-        core.reshape(1).astype(jnp.int32),
-        scan_rows[0, 0],
-        scan_cols[0, 0],
-        live_count[0],
-    )
+    last = jnp.concatenate([live_count[0], core.astype(jnp.int32)[None]])
+    lines = [scan_rows[0, 0], scan_cols[0, 0], last]
+    scalars = jnp.stack([jnp.pad(line, (0, PATCH - line.shape[0])) for line in lines])
+    scalars = jnp.pad(scalars, ((0, 8 - len(lines)), (0, 0)))
     probe_relax = amps.shape[0] * lax.axis_size(TILE) * lax.axis_size("pos") / 4.0
     own_half = lax.dynamic_slice_in_dim(object_field, core * (COLS // 2), COLS // 2, 2)
     halo = from_tile(own_half, 1)
@@ -315,28 +341,32 @@
         scalars, probe_field, amps, tables, object_field, halo, halo_other
     )
 
-    def next_probe(sums, probe):
-        total = probe_sum_everywhere(sums)
+    def next_probe(part, probe):
+        for axis in TILE[1::-1]:
+            part = summed_over(part, axis)
+        total = joined_over_cores(part).reshape(3, PATCH, PATCH)
         return (total[:2] + probe_relax * probe) / (total[2] + probe_relax)[None]
 
     def updated(sums, field):
         return (sums[:2] + OBJECT_RELAX * field) / (sums[2] + OBJECT_RELAX)[None]
 
-    low = low + swapped(give_low)
-    up = up + swapped(give_up)
+    part = summed_over(halved_over_cores(probe_sums), TILE[2])
+    low = after(low + swapped(give_low), part)
+    up = after(up + swapped(give_up), part)
     above = from_tile(low, -1)
     below = from_tile(up, 1)
-    probe_field = next_probe(probe_sums, probe_field)
+    probe_field = next_probe(part, probe_field)
     own_half = updated(up + above, in_blocks(own_half))
     mine = jnp.concatenate([own_half, updated(low + below, in_blocks(halo))], axis=2)
     other = swapped(mine)
     up, low, give_up, give_low, probe_sums = run_positions(
         scalars, probe_field, amps, tables, None, mine, other
     )
-    low = low + swapped(give_low)
+    part = summed_over(halved_over_cores(probe_sums), TILE[2])
+    low = after(low + swapped(give_low), part)
     up = up + swapped(give_up)
     above = from_tile(low, -1)
-    probe_out = next_probe(probe_sums, probe_field)
+    probe_out = next_probe(part, probe_field)
     mine = updated(up + above, own_half).transpose(0, 2, 1, 3).reshape(2, STRIP, COLS // 2)
     other = swapped(mine)
     left = jnp.where(core == 0, mine, other)

time: 203 us -> 198 us (0.975)
  the two profiles are of different devices: /device:TPU:63 before, /device:TPU:223 now
where the time goes in v3:
time: 198 us
  waiting for transfers between devices  103 us (52%)
  starting transfers between devices  39.5 us (20%)
  Pallas kernels  32.6 us (16%)
  other arithmetic  9.82 us (5%)
  local copies, waits for them, and re-layouts  9.6 us (5%)
  between operations  3.04 us (2%)
    ppermute x20, waiting for transfers between devices, shifts_among(): total = total + lax.ppermute(value, axis, route)  50.1 us
    ppermute x4, waiting for transfers between devices, from_tile(): lax.ppermute(value, TILE, [((i + distance) % count, i) for i in range(cou...  48.1 us
    pallas_call x2, Pallas kernels, run_positions(): pl.pallas_call(kernel, out_shape=(quarter,) * 4 + (jax.ShapeDtypeStruct((...  32.6 us
    ppermute x11, starting transfers between devices, swapped(): return lax.ppermute(value, 'pos', [(0, 1), (1, 0)])  22.5 us
    ppermute x20, starting transfers between devices, shifts_among(): total = total + lax.ppermute(value, axis, route)  16 us
    ppermute x11, waiting for transfers between devices, swapped(): return lax.ppermute(value, 'pos', [(0, 1), (1, 0)])  4.78 us
  transfers between devices with their start and end apart: 35, of which 19 were waited for; matrix products, arithmetic and copies ran while one was open for 8% of the time, Pallas kernels for 0%

profile of v3, /device:TPU:223, one launch (start us, length us, event | category | flops | bytes accessed | tf_op | source)
XLA Modules:
  0.0 197.5 jit_solution(12809532571004106319)
XLA Ops:
  0.6 1.1 constant_dynamic-slice_fusion
  1.7 0.5 collective-permute-start
  2.3 16.5 %collective-permute-done.refs_5_ = f32[2,128,512]{2,1,0:T(8,128)S(1)} collective-permute-done((f32[2,128,512]{2,1,0:T(8,128)S(1)}, f32[2,128,512]{2,1,0:T(8,128)S(1)}, u32[]{:S(2)}, u32[]{:S(2)}) %collective-permute-start) | collective-permute-done | bytes 524320 | tf_op jit(solution)/shard_map/ppermute | solution.py:33
  18.8 1.5 collective-permute-start.1
  21.1 0.7 pad_bitcast_fusion.1
  21.8 0.6 pad.18.refs_0_
  22.4 0.8 copy-done.6
  23.2 16.3 %positions.2 = (f32[3,4,128,128]{3,2,1,0:T(8,128)}, f32[3,4,128,128]{3,2,1,0:T(8,128)}, f32[3,4,128,128]{3,2,1,0:T(8,128)}, f32[3,4,128,128]{3,2,1,0:T(8,128)}, f32[3,128,128]{2,1,0:T(8,128)}) custom-call(s32[8,128]{1,0:T(8,128)} %pad.18.refs_0_, f32[2,128,128]{2,1,0:T(8,128)} %refs_1_.1, f32[32,128,128]{2,1,0:T(8,128)} %bitcast.54, ...), custom_call_target="tpu_custom_call" | custom-call | flops 12999999488 | bytes 8388608 | tf_op jit(solution)/shard_map/positions/pallas_call | solution.py:259
  39.6 1.0 dynamic-slice_bitcast_fusion.1
  40.5 0.4 collective-permute-start.2
  41.0 1.0 collective-permute-done.2
  42.0 0.9 bitcast_add_fusion.1
  43.1 2.6 %collective-permute-start.3 = (f32[192,128]{1,0:T(8,128)S(1)}, f32[192,128]{1,0:T(8,128)S(1)}, u32[]{:S(2)}, u32[]{:S(2)}) collective-permute-start(f32[192,128]{1,0:T(8,128)S(1)} %bitcast_add_fusion.1), channel_id=1, source_target_pairs={{0,2},{2,4},{4,6},{6,0},{1,3},{3,5},{5,7},{7,1},{8,10},{10,12},{12... | collective-permute-start | bytes 294920 | tf_op jit(solution)/shard_map/ppermute | solution.py:319
  45.7 0.8 collective-permute-start.15
  46.5 4.2 %collective-permute-done.5 = f32[192,128]{1,0:T(8,128)S(1)} collective-permute-done((f32[192,128]{1,0:T(8,128)S(1)}, f32[192,128]{1,0:T(8,128)S(1)}, u32[]{:S(2)}, u32[]{:S(2)}) %collective-permute-start.5) | collective-permute-done | bytes 98336 | tf_op jit(solution)/shard_map/ppermute | solution.py:319
  50.8 0.6 slice.62
  52.1 1.2 add_add_fusion.3
  53.3 0.4 collective-permute-start.17
  53.7 2.7 %collective-permute-start.6 = (f32[192,128]{1,0:T(8,128)S(1)}, f32[192,128]{1,0:T(8,128)}, u32[]{:S(2)}, u32[]{:S(2)}) collective-permute-start(f32[192,128]{1,0:T(8,128)S(1)} %add_add_fusion.9), channel_id=1, source_target_pairs={{0,8},{8,16},{16,24},{24,0},{1,9},{9,17},{17,25},{25,1},{2,10},{10... | collective-permute-start | bytes 294920 | tf_op jit(solution)/shard_map/ppermute | solution.py:319
  56.3 20.2 %collective-permute-done.17 = f32[3,4,128,128]{3,2,1,0:T(8,128)S(1)} collective-permute-done((f32[3,4,128,128]{3,2,1,0:T(8,128)S(1)}, f32[3,4,128,128]{3,2,1,0:T(8,128)S(1)}, u32[]{:S(2)}, u32[]{:S(2)}) %collective-permute-start.17) | collective-permute-done | bytes 786464 | tf_op jit(solution)/shard_map/ppermute | solution.py:33
  76.6 1.1 fusion.7
  77.7 0.2 copy.9
  77.9 0.2 copy.10
  78.1 1.2 copy.11
  79.3 0.2 copy.12
  79.5 1.0 add_add_fusion.8
  80.6 0.5 collective-permute-start.11
  81.1 1.3 collective-permute-start.9
  82.5 11.3 %collective-permute-done.16 = f32[3,4,128,128]{3,2,1,0:T(8,128)} collective-permute-done((f32[3,4,128,128]{3,2,1,0:T(8,128)}, f32[3,4,128,128]{3,2,1,0:T(8,128)}, u32[]{:S(2)}, u32[]{:S(2)}) %collective-permute-start.16) | collective-permute-done | bytes 786464 | tf_op jit(solution)/shard_map/ppermute | solution.py:33
  93.8 1.2 add.182
  95.3 7.3 %collective-permute-start.18 = (f32[2,4,256,128]{3,2,1,0:T(8,128)S(1)}, f32[2,4,256,128]{3,2,1,0:T(8,128)}, u32[]{:S(2)}, u32[]{:S(2)}) collective-permute-start(f32[2,4,256,128]{3,2,1,0:T(8,128)S(1)} %pad_maximum_fusion.refs_4_), channel_id=1, source_target_pairs={{0,1},{1,0},{2,3},{3,2},{4,5},{5,4},{6,7},{7,6},{8,9},{9,8},{10,11... | collective-permute-start | bytes 3145736 | tf_op jit(solution)/shard_map/ppermute | solution.py:28
  102.6 0.4 collective-permute-done.9
  103.1 7.4 %collective-permute-done.12 = f32[192,128]{1,0:T(8,128)S(1)} collective-permute-done((f32[192,128]{1,0:T(8,128)S(1)}, f32[192,128]{1,0:T(8,128)S(1)}, u32[]{:S(2)}, u32[]{:S(2)}) %collective-permute-start.12) | collective-permute-done | bytes 98336 | tf_op jit(solution)/shard_map/ppermute | solution.py:319
  110.5 5.7 %collective-permute-start.13 = (f32[192,128]{1,0:T(8,128)S(1)}, f32[192,128]{1,0:T(8,128)S(1)}, u32[]{:S(2)}, u32[]{:S(2)}) collective-permute-start(f32[192,128]{1,0:T(8,128)S(1)} %add.174), channel_id=1, source_target_pairs={{0,1},{1,0},{2,3},{3,2},{4,5},{5,4},{6,7},{7,6},{8,9},{9,8},{10,11... | collective-permute-start | bytes 294920 | tf_op jit(solution)/shard_map/ppermute | solution.py:28
  116.1 0.9 collective-permute-done.13
  117.2 0.7 add_divide_fusion.1.refs_1_
  117.8 16.3 %positions.3 = (f32[3,4,128,128]{3,2,1,0:T(8,128)}, f32[3,4,128,128]{3,2,1,0:T(8,128)}, f32[3,4,128,128]{3,2,1,0:T(8,128)}, f32[3,4,128,128]{3,2,1,0:T(8,128)}, f32[3,128,128]{2,1,0:T(8,128)}) custom-call(s32[8,128]{1,0:T(8,128)} %pad.18.refs_0_, f32[2,128,128]{2,1,0:T(8,128)} %add_divide_fusion.1.refs_1_, f32[32,128,128]{2,1,0:T(8,128)} %bitcast.55, ...), custom_call_target="tpu_custom_call" | custom-call | flops 12999999488 | bytes 8388608 | tf_op jit(solution)/shard_map/positions/pallas_call | solution.py:259
  134.1 0.4 collective-permute-start.20
  134.6 0.9 dynamic-slice_bitcast_fusion
  135.5 0.2 collective-permute-start.21
  135.6 1.1 collective-permute-done.21
  136.8 0.9 bitcast_add_fusion
  137.9 2.6 %collective-permute-start.22 = (f32[192,128]{1,0:T(8,128)S(1)}, f32[192,128]{1,0:T(8,128)S(1)}, u32[]{:S(2)}, u32[]{:S(2)}) collective-permute-start(f32[192,128]{1,0:T(8,128)S(1)} %bitcast_add_fusion), channel_id=1, source_target_pairs={{0,2},{2,4},{4,6},{6,0},{1,3},{3,5},{5,7},{7,1},{8,10},{10,12},{12... | collective-permute-start | bytes 294920 | tf_op jit(solution)/shard_map/ppermute | solution.py:319
  140.4 0.8 collective-permute-start.19
  141.2 4.2 %collective-permute-done.24 = f32[192,128]{1,0:T(8,128)S(1)} collective-permute-done((f32[192,128]{1,0:T(8,128)S(1)}, f32[192,128]{1,0:T(8,128)S(1)}, u32[]{:S(2)}, u32[]{:S(2)}) %collective-permute-start.24) | collective-permute-done | bytes 98336 | tf_op jit(solution)/shard_map/ppermute | solution.py:319
  145.6 0.5 slice.67
  146.1 2.7 %collective-permute-start.27 = (f32[192,128]{1,0:T(8,128)S(1)}, f32[192,128]{1,0:T(8,128)S(1)}, u32[]{:S(2)}, u32[]{:S(2)}) collective-permute-start(f32[192,128]{1,0:T(8,128)S(1)} %add_add_fusion.6), channel_id=1, source_target_pairs={{0,8},{8,16},{16,24},{24,0},{1,9},{9,17},{17,25},{25,1},{2,10},{10... | collective-permute-start | bytes 294920 | tf_op jit(solution)/shard_map/ppermute | solution.py:319
  149.4 1.2 add_add_fusion
  150.7 2.6 %collective-permute-done.29 = f32[192,128]{1,0:T(8,128)S(1)} collective-permute-done((f32[192,128]{1,0:T(8,128)S(1)}, f32[192,128]{1,0:T(8,128)S(1)}, u32[]{:S(2)}, u32[]{:S(2)}) %collective-permute-start.29) | collective-permute-done | bytes 98336 | tf_op jit(solution)/shard_map/ppermute | solution.py:319
  153.4 1.5 collective-permute-start.32
  155.0 1.3 collective-permute-start.30
  156.2 1.0 collective-permute-done.32
  157.3 16.8 %collective-permute-done.31 = f32[192,128]{1,0:T(8,128)S(1)} collective-permute-done((f32[192,128]{1,0:T(8,128)S(1)}, f32[192,128]{1,0:T(8,128)S(1)}, u32[]{:S(2)}, u32[]{:S(2)}) %collective-permute-start.31) | collective-permute-done | bytes 98336 | tf_op jit(solution)/shard_map/ppermute | solution.py:319
  174.1 6.2 %collective-permute-done.30 = f32[192,128]{1,0:T(8,128)S(1)} collective-permute-done((f32[192,128]{1,0:T(8,128)S(1)}, f32[192,128]{1,0:T(8,128)S(1)}, u32[]{:S(2)}, u32[]{:S(2)}) %collective-permute-start.30) | collective-permute-done | bytes 98336 | tf_op jit(solution)/shard_map/ppermute | solution.py:319
  180.3 0.4 collective-permute-start.33
  180.7 7.0 %collective-permute-done.33 = f32[192,128]{1,0:T(8,128)S(1)} collective-permute-done((f32[192,128]{1,0:T(8,128)S(1)}, f32[192,128]{1,0:T(8,128)S(1)}, u32[]{:S(2)}, u32[]{:S(2)}) %collective-permute-start.33) | collective-permute-done | bytes 98336 | tf_op jit(solution)/shard_map/ppermute | solution.py:319
  187.8 4.8 %collective-permute-start.34 = (f32[192,128]{1,0:T(8,128)S(1)}, f32[192,128]{1,0:T(8,128)S(1)}, u32[]{:S(2)}, u32[]{:S(2)}) collective-permute-start(f32[192,128]{1,0:T(8,128)S(1)} %add.205), channel_id=1, source_target_pairs={{0,1},{1,0},{2,3},{3,2},{4,5},{5,4},{6,7},{7,6},{8,9},{9,8},{10,11... | collective-permute-start | bytes 294920 | tf_op jit(solution)/shard_map/ppermute | solution.py:28
  192.6 0.9 collective-permute-done.34
  193.6 0.1 add_add_fusion.1
  193.9 0.2 copy.13
  194.1 0.4 collective-permute-start.26
  194.6 0.7 add_divide_fusion
  195.3 0.7 collective-permute-done.26
  196.2 1.3 copy.14
  (70 shorter events, 1.8 us)
Async XLA Ops:
  1.7 17.1 %collective-permute-start = (f32[2,128,512]{2,1,0:T(8,128)S(1)}, f32[2,128,512]{2,1,0:T(8,128)S(1)}, u32[]{:S(2)}, u32[]{:S(2)}) collective-permute-start(f32[2,128,512]{2,1,0:T(8,128)S(1)} %constant_dynamic-slice_fusion), channel_id=1, source_target_pairs={{2,0},{4,2},{6,4},{8,6},{10,8},{12,10},{14,12},{16,14},{18,16},{20... | collective-permute-start | bytes 1572872 | tf_op jit(solution)/shard_map/ppermute | solution.py:33
  18.8 3.6 %copy-start.4 = (f32[2,128,512]{2,1,0:T(8,128)}, f32[2,128,512]{2,1,0:T(8,128)S(1)}, u32[]{:S(2)}) copy-start(f32[2,128,512]{2,1,0:T(8,128)S(1)} %collective-permute-done.refs_5_) | copy-start | bytes 1572868
  18.8 3.6 %collective-permute-start.1 = (f32[2,128,512]{2,1,0:T(8,128)S(1)}, f32[2,128,512]{2,1,0:T(8,128)S(1)}, u32[]{:S(2)}, u32[]{:S(2)}) collective-permute-start(f32[2,128,512]{2,1,0:T(8,128)S(1)} %collective-permute-done.refs_5_), channel_id=1, source_target_pairs={{0,1},{1,0},{2,3},{3,2},{4,5},{5,4},{6,7},{7,6},{8,9},{9,8},{10,11... | collective-permute-start | bytes 1572872 | tf_op jit(solution)/shard_map/ppermute | solution.py:28
  22.4 0.8 copy-start.6
  39.5 37.1 %copy-start.2 = (f32[3,4,128,128]{3,2,1,0:T(8,128)S(1)}, f32[3,4,128,128]{3,2,1,0:T(8,128)}, u32[]{:S(2)}) copy-start(f32[3,4,128,128]{3,2,1,0:T(8,128)} %get-tuple-element.15) | copy-start | bytes 2359300
  39.5 12.6 %collective-permute-start.14 = (f32[3,4,128,128]{3,2,1,0:T(8,128)}, f32[3,4,128,128]{3,2,1,0:T(8,128)S(1)}, u32[]{:S(2)}, u32[]{:S(2)}) collective-permute-start(f32[3,4,128,128]{3,2,1,0:T(8,128)} %get-tuple-element.14), channel_id=1, source_target_pairs={{0,1},{1,0},{2,3},{3,2},{4,5},{5,4},{6,7},{7,6},{8,9},{9,8},{10,11... | collective-permute-start | bytes 2359304 | tf_op jit(solution)/shard_map/ppermute | solution.py:28
  40.5 1.5 collective-permute-start.2
  42.9 7.8 %collective-permute-start.5 = (f32[192,128]{1,0:T(8,128)S(1)}, f32[192,128]{1,0:T(8,128)S(1)}, u32[]{:S(2)}, u32[]{:S(2)}) collective-permute-start(f32[192,128]{1,0:T(8,128)S(1)} %bitcast_add_fusion.1), channel_id=1, source_target_pairs={{0,6},{2,0},{4,2},{6,4},{1,7},{3,1},{5,3},{7,5},{8,14},{10,8},{12,... | collective-permute-start | bytes 294920 | tf_op jit(solution)/shard_map/ppermute | solution.py:319
  43.0 7.7 %collective-permute-start.4 = (f32[192,128]{1,0:T(8,128)S(1)}, f32[192,128]{1,0:T(8,128)S(1)}, u32[]{:S(2)}, u32[]{:S(2)}) collective-permute-start(f32[192,128]{1,0:T(8,128)S(1)} %bitcast_add_fusion.1), channel_id=1, source_target_pairs={{0,4},{2,6},{4,0},{6,2},{1,5},{3,7},{5,1},{7,3},{8,12},{10,14},{12... | collective-permute-start | bytes 294920 | tf_op jit(solution)/shard_map/ppermute | solution.py:319
  43.1 7.7 %collective-permute-start.3 = (f32[192,128]{1,0:T(8,128)S(1)}, f32[192,128]{1,0:T(8,128)S(1)}, u32[]{:S(2)}, u32[]{:S(2)}) collective-permute-start(f32[192,128]{1,0:T(8,128)S(1)} %bitcast_add_fusion.1), channel_id=1, source_target_pairs={{0,2},{2,4},{4,6},{6,0},{1,3},{3,5},{5,7},{7,1},{8,10},{10,12},{12... | collective-permute-start | bytes 294920 | tf_op jit(solution)/shard_map/ppermute | solution.py:319
  45.7 10.7 %collective-permute-start.15 = (f32[3,4,128,128]{3,2,1,0:T(8,128)}, f32[3,4,128,128]{3,2,1,0:T(8,128)S(1)}, u32[]{:S(2)}, u32[]{:S(2)}) collective-permute-start(f32[3,4,128,128]{3,2,1,0:T(8,128)} %get-tuple-element.16), channel_id=1, source_target_pairs={{0,1},{1,0},{2,3},{3,2},{4,5},{5,4},{6,7},{7,6},{8,9},{9,8},{10,11... | collective-permute-start | bytes 2359304 | tf_op jit(solution)/shard_map/ppermute | solution.py:28
  53.3 23.3 %collective-permute-start.17 = (f32[3,4,128,128]{3,2,1,0:T(8,128)S(1)}, f32[3,4,128,128]{3,2,1,0:T(8,128)S(1)}, u32[]{:S(2)}, u32[]{:S(2)}) collective-permute-start(f32[3,4,128,128]{3,2,1,0:T(8,128)S(1)} %add_add_fusion.3), channel_id=1, source_target_pairs={{2,0},{4,2},{6,4},{8,6},{10,8},{12,10},{14,12},{16,14},{18,16},{20... | collective-permute-start | bytes 2359304 | tf_op jit(solution)/shard_map/ppermute | solution.py:33
  53.7 25.9 %collective-permute-start.8 = (f32[192,128]{1,0:T(8,128)S(1)}, f32[192,128]{1,0:T(8,128)}, u32[]{:S(2)}, u32[]{:S(2)}) collective-permute-start(f32[192,128]{1,0:T(8,128)S(1)} %add_add_fusion.9), channel_id=1, source_target_pairs={{0,24},{8,0},{16,8},{24,16},{1,25},{9,1},{17,9},{25,17},{2,26},{10... | collective-permute-start | bytes 294920 | tf_op jit(solution)/shard_map/ppermute | solution.py:319
  53.7 25.9 %collective-permute-start.7 = (f32[192,128]{1,0:T(8,128)S(1)}, f32[192,128]{1,0:T(8,128)}, u32[]{:S(2)}, u32[]{:S(2)}) collective-permute-start(f32[192,128]{1,0:T(8,128)S(1)} %add_add_fusion.9), channel_id=1, source_target_pairs={{0,16},{8,24},{16,0},{24,8},{1,17},{9,25},{17,1},{25,9},{2,18},{10... | collective-permute-start | bytes 294920 | tf_op jit(solution)/shard_map/ppermute | solution.py:319
  53.7 25.9 %collective-permute-start.6 = (f32[192,128]{1,0:T(8,128)S(1)}, f32[192,128]{1,0:T(8,128)}, u32[]{:S(2)}, u32[]{:S(2)}) collective-permute-start(f32[192,128]{1,0:T(8,128)S(1)} %add_add_fusion.9), channel_id=1, source_target_pairs={{0,8},{8,16},{16,24},{24,0},{1,9},{9,17},{17,25},{25,1},{2,10},{10... | collective-permute-start | bytes 294920 | tf_op jit(solution)/shard_map/ppermute | solution.py:319
  77.7 16.2 %collective-permute-start.16 = (f32[3,4,128,128]{3,2,1,0:T(8,128)}, f32[3,4,128,128]{3,2,1,0:T(8,128)}, u32[]{:S(2)}, u32[]{:S(2)}) collective-permute-start(f32[3,4,128,128]{3,2,1,0:T(8,128)} %get-tuple-element.25), channel_id=1, source_target_pairs={{254,0},{0,2},{2,4},{4,6},{6,8},{8,10},{10,12},{12,14},{14,16},{16... | collective-permute-start | bytes 2359304 | tf_op jit(solution)/shard_map/ppermute | solution.py:33
  80.6 22.0 %collective-permute-start.11 = (f32[192,128]{1,0:T(8,128)S(1)}, f32[192,128]{1,0:T(8,128)S(1)}, u32[]{:S(2)}, u32[]{:S(2)}) collective-permute-start(f32[192,128]{1,0:T(8,128)S(1)} %add_add_fusion.8), channel_id=1, source_target_pairs={{0,96},{32,0},{64,32},{96,64},{128,224},{160,128},{192,160},{224,1... | collective-permute-start | bytes 294920 | tf_op jit(solution)/shard_map/ppermute | solution.py:319
  81.1 21.5 %collective-permute-start.10 = (f32[192,128]{1,0:T(8,128)S(1)}, f32[192,128]{1,0:T(8,128)S(1)}, u32[]{:S(2)}, u32[]{:S(2)}) collective-permute-start(f32[192,128]{1,0:T(8,128)S(1)} %add_add_fusion.8), channel_id=1, source_target_pairs={{0,64},{32,96},{64,0},{96,32},{128,192},{160,224},{192,128},{224,1... | collective-permute-start | bytes 294920 | tf_op jit(solution)/shard_map/ppermute | solution.py:319
  81.1 21.9 %collective-permute-start.9 = (f32[192,128]{1,0:T(8,128)S(1)}, f32[192,128]{1,0:T(8,128)S(1)}, u32[]{:S(2)}, u32[]{:S(2)}) collective-permute-start(f32[192,128]{1,0:T(8,128)S(1)} %add_add_fusion.8), channel_id=1, source_target_pairs={{0,32},{32,64},{64,96},{96,0},{128,160},{160,192},{192,224},{224,1... | collective-permute-start | bytes 294920 | tf_op jit(solution)/shard_map/ppermute | solution.py:319
  95.2 22.0 %copy-start.5 = (f32[2,128,128]{2,1,0:T(8,128)S(1)}, f32[2,128,128]{2,1,0:T(8,128)}, u32[]{:S(2)}) copy-start(f32[2,128,128]{2,1,0:T(8,128)} %refs_1_.1) | copy-start | bytes 393220
  95.3 22.6 %copy-start = (f32[2,4,256,128]{3,2,1,0:T(8,128)}, f32[2,4,256,128]{3,2,1,0:T(8,128)S(1)}, u32[]{:S(2)}) copy-start(f32[2,4,256,128]{3,2,1,0:T(8,128)S(1)} %pad_maximum_fusion.refs_4_) | copy-start | bytes 3145732
  95.3 22.6 %collective-permute-start.18 = (f32[2,4,256,128]{3,2,1,0:T(8,128)S(1)}, f32[2,4,256,128]{3,2,1,0:T(8,128)}, u32[]{:S(2)}, u32[]{:S(2)}) collective-permute-start(f32[2,4,256,128]{3,2,1,0:T(8,128)S(1)} %pad_maximum_fusion.refs_4_), channel_id=1, source_target_pairs={{0,1},{1,0},{2,3},{3,2},{4,5},{5,4},{6,7},{7,6},{8,9},{9,8},{10,11... | collective-permute-start | bytes 3145736 | tf_op jit(solution)/shard_map/ppermute | solution.py:28
  103.0 7.5 %collective-permute-start.12 = (f32[192,128]{1,0:T(8,128)S(1)}, f32[192,128]{1,0:T(8,128)S(1)}, u32[]{:S(2)}, u32[]{:S(2)}) collective-permute-start(f32[192,128]{1,0:T(8,128)S(1)} %add_add_fusion.7), channel_id=1, source_target_pairs={{0,128},{32,160},{64,192},{96,224},{128,0},{160,32},{192,64},{224,... | collective-permute-start | bytes 294920 | tf_op jit(solution)/shard_map/ppermute | solution.py:319
  110.5 6.6 %collective-permute-start.13 = (f32[192,128]{1,0:T(8,128)S(1)}, f32[192,128]{1,0:T(8,128)S(1)}, u32[]{:S(2)}, u32[]{:S(2)}) collective-permute-start(f32[192,128]{1,0:T(8,128)S(1)} %add.174), channel_id=1, source_target_pairs={{0,1},{1,0},{2,3},{3,2},{4,5},{5,4},{6,7},{7,6},{8,9},{9,8},{10,11... | collective-permute-start | bytes 294920 | tf_op jit(solution)/shard_map/ppermute | solution.py:28
  134.1 15.3 %collective-permute-start.20 = (f32[3,4,128,128]{3,2,1,0:T(8,128)}, f32[3,4,128,128]{3,2,1,0:T(8,128)S(1)}, u32[]{:S(2)}, u32[]{:S(2)}) collective-permute-start(f32[3,4,128,128]{3,2,1,0:T(8,128)} %get-tuple-element.20), channel_id=1, source_target_pairs={{0,1},{1,0},{2,3},{3,2},{4,5},{5,4},{6,7},{7,6},{8,9},{9,8},{10,11... | collective-permute-start | bytes 2359304 | tf_op jit(solution)/shard_map/ppermute | solution.py:28
  135.5 1.3 collective-permute-start.21
  137.7 7.8 %collective-permute-start.24 = (f32[192,128]{1,0:T(8,128)S(1)}, f32[192,128]{1,0:T(8,128)S(1)}, u32[]{:S(2)}, u32[]{:S(2)}) collective-permute-start(f32[192,128]{1,0:T(8,128)S(1)} %bitcast_add_fusion), channel_id=1, source_target_pairs={{0,6},{2,0},{4,2},{6,4},{1,7},{3,1},{5,3},{7,5},{8,14},{10,8},{12,... | collective-permute-start | bytes 294920 | tf_op jit(solution)/shard_map/ppermute | solution.py:319
  137.8 7.7 %collective-permute-start.23 = (f32[192,128]{1,0:T(8,128)S(1)}, f32[192,128]{1,0:T(8,128)S(1)}, u32[]{:S(2)}, u32[]{:S(2)}) collective-permute-start(f32[192,128]{1,0:T(8,128)S(1)} %bitcast_add_fusion), channel_id=1, source_target_pairs={{0,4},{2,6},{4,0},{6,2},{1,5},{3,7},{5,1},{7,3},{8,12},{10,14},{12... | collective-permute-start | bytes 294920 | tf_op jit(solution)/shard_map/ppermute | solution.py:319
  137.9 7.7 %collective-permute-start.22 = (f32[192,128]{1,0:T(8,128)S(1)}, f32[192,128]{1,0:T(8,128)S(1)}, u32[]{:S(2)}, u32[]{:S(2)}) collective-permute-start(f32[192,128]{1,0:T(8,128)S(1)} %bitcast_add_fusion), channel_id=1, source_target_pairs={{0,2},{2,4},{4,6},{6,0},{1,3},{3,5},{5,7},{7,1},{8,10},{10,12},{12... | collective-permute-start | bytes 294920 | tf_op jit(solution)/shard_map/ppermute | solution.py:319
  140.4 53.1 %collective-permute-start.19 = (f32[3,4,128,128]{3,2,1,0:T(8,128)}, f32[3,4,128,128]{3,2,1,0:T(8,128)S(1)}, u32[]{:S(2)}, u32[]{:S(2)}) collective-permute-start(f32[3,4,128,128]{3,2,1,0:T(8,128)} %get-tuple-element.18), channel_id=1, source_target_pairs={{0,1},{1,0},{2,3},{3,2},{4,5},{5,4},{6,7},{7,6},{8,9},{9,8},{10,11... | collective-permute-start | bytes 2359304 | tf_op jit(solution)/shard_map/ppermute | solution.py:28
  145.6 48.0 %copy-start.1 = (f32[3,4,128,128]{3,2,1,0:T(8,128)S(1)}, f32[3,4,128,128]{3,2,1,0:T(8,128)}, u32[]{:S(2)}) copy-start(f32[3,4,128,128]{3,2,1,0:T(8,128)} %get-tuple-element.17) | copy-start | bytes 2359300
  146.1 7.3 %collective-permute-start.29 = (f32[192,128]{1,0:T(8,128)S(1)}, f32[192,128]{1,0:T(8,128)S(1)}, u32[]{:S(2)}, u32[]{:S(2)}) collective-permute-start(f32[192,128]{1,0:T(8,128)S(1)} %add_add_fusion.6), channel_id=1, source_target_pairs={{0,24},{8,0},{16,8},{24,16},{1,25},{9,1},{17,9},{25,17},{2,26},{10... | collective-permute-start | bytes 294920 | tf_op jit(solution)/shard_map/ppermute | solution.py:319
  146.1 7.3 %collective-permute-start.28 = (f32[192,128]{1,0:T(8,128)S(1)}, f32[192,128]{1,0:T(8,128)S(1)}, u32[]{:S(2)}, u32[]{:S(2)}) collective-permute-start(f32[192,128]{1,0:T(8,128)S(1)} %add_add_fusion.6), channel_id=1, source_target_pairs={{0,16},{8,24},{16,0},{24,8},{1,17},{9,25},{17,1},{25,9},{2,18},{10... | collective-permute-start | bytes 294920 | tf_op jit(solution)/shard_map/ppermute | solution.py:319
  146.1 7.3 %collective-permute-start.27 = (f32[192,128]{1,0:T(8,128)S(1)}, f32[192,128]{1,0:T(8,128)S(1)}, u32[]{:S(2)}, u32[]{:S(2)}) collective-permute-start(f32[192,128]{1,0:T(8,128)S(1)} %add_add_fusion.6), channel_id=1, source_target_pairs={{0,8},{8,16},{16,24},{24,0},{1,9},{9,17},{17,25},{25,1},{2,10},{10... | collective-permute-start | bytes 294920 | tf_op jit(solution)/shard_map/ppermute | solution.py:319
  150.7 42.9 %collective-permute-start.25 = (f32[3,4,128,128]{3,2,1,0:T(8,128)S(1)}, f32[3,4,128,128]{3,2,1,0:T(8,128)S(1)}, u32[]{:S(2)}, u32[]{:S(2)}) collective-permute-start(f32[3,4,128,128]{3,2,1,0:T(8,128)S(1)} %add_add_fusion), channel_id=1, source_target_pairs={{254,0},{0,2},{2,4},{4,6},{6,8},{8,10},{10,12},{12,14},{14,16},{16... | collective-permute-start | bytes 2359304 | tf_op jit(solution)/shard_map/ppermute | solution.py:33
  153.4 3.8 %collective-permute-start.32 = (f32[192,128]{1,0:T(8,128)S(1)}, f32[192,128]{1,0:T(8,128)S(1)}, u32[]{:S(2)}, u32[]{:S(2)}) collective-permute-start(f32[192,128]{1,0:T(8,128)S(1)} %add_add_fusion.5), channel_id=1, source_target_pairs={{0,96},{32,0},{64,32},{96,64},{128,224},{160,128},{192,160},{224,1... | collective-permute-start | bytes 294920 | tf_op jit(solution)/shard_map/ppermute | solution.py:319
  155.0 19.1 %collective-permute-start.31 = (f32[192,128]{1,0:T(8,128)S(1)}, f32[192,128]{1,0:T(8,128)S(1)}, u32[]{:S(2)}, u32[]{:S(2)}) collective-permute-start(f32[192,128]{1,0:T(8,128)S(1)} %add_add_fusion.5), channel_id=1, source_target_pairs={{0,64},{32,96},{64,0},{96,32},{128,192},{160,224},{192,128},{224,1... | collective-permute-start | bytes 294920 | tf_op jit(solution)/shard_map/ppermute | solution.py:319
  155.0 25.3 %collective-permute-start.30 = (f32[192,128]{1,0:T(8,128)S(1)}, f32[192,128]{1,0:T(8,128)S(1)}, u32[]{:S(2)}, u32[]{:S(2)}) collective-permute-start(f32[192,128]{1,0:T(8,128)S(1)} %add_add_fusion.5), channel_id=1, source_target_pairs={{0,32},{32,64},{64,96},{96,0},{128,160},{160,192},{192,224},{224,1... | collective-permute-start | bytes 294920 | tf_op jit(solution)/shard_map/ppermute | solution.py:319
  180.3 7.5 %collective-permute-start.33 = (f32[192,128]{1,0:T(8,128)S(1)}, f32[192,128]{1,0:T(8,128)S(1)}, u32[]{:S(2)}, u32[]{:S(2)}) collective-permute-start(f32[192,128]{1,0:T(8,128)S(1)} %add_add_fusion.4), channel_id=1, source_target_pairs={{0,128},{32,160},{64,192},{96,224},{128,0},{160,32},{192,64},{224,... | collective-permute-start | bytes 294920 | tf_op jit(solution)/shard_map/ppermute | solution.py:319
  187.8 5.8 %collective-permute-start.34 = (f32[192,128]{1,0:T(8,128)S(1)}, f32[192,128]{1,0:T(8,128)S(1)}, u32[]{:S(2)}, u32[]{:S(2)}) collective-permute-start(f32[192,128]{1,0:T(8,128)S(1)} %add.205), channel_id=1, source_target_pairs={{0,1},{1,0},{2,3},{3,2},{4,5},{5,4},{6,7},{7,6},{8,9},{9,8},{10,11... | collective-permute-start | bytes 294920 | tf_op jit(solution)/shard_map/ppermute | solution.py:28
  193.7 0.9 copy-start.3
  194.1 2.0 %collective-permute-start.26 = (f32[2,128,512]{1,2,0:T(8,128)S(1)}, f32[2,128,512]{1,2,0:T(8,128)S(1)}, u32[]{:S(2)}, u32[]{:S(2)}) collective-permute-start(f32[2,128,512]{1,2,0:T(8,128)S(1)} %bitcast.43), channel_id=1, source_target_pairs={{0,1},{1,0},{2,3},{3,2},{4,5},{5,4},{6,7},{7,6},{8,9},{9,8},{10,11... | collective-permute-start | bytes 1572872 | tf_op jit(solution)/shard_map/ppermute | solution.py:28

commit v4 on v3

--- a/solution.py
+++ b/solution.py
@@ -91,7 +91,9 @@
 
 def positions_kernel(
     from_strips,
-    scalars_hbm,
+    rows_hbm,
+    cols_hbm,
+    live_hbm,
     probe_ref,
     amps_hbm,
     tables_hbm,
@@ -102,30 +104,33 @@
     keep_low_ref,
     give_up_ref,
     give_low_ref,
+    keep_probe_ref,
+    give_probe_ref,
     probe_sums_ref,
     band,
     sums,
     amps_ref,
     tables,
-    scalars,
+    rows_ref,
+    cols_ref,
+    live_ref,
     sems,
     amp_sems,
 ):
-    groups = amps_ref.shape[0] // GROUP
-    fetch = pltpu.make_async_copy(scalars_hbm, scalars, sems.at[2 * BLOCKS + 1])
-    fetch.start()
+    core = lax.axis_index("pos").astype(jnp.int32)
+    here = lax.axis_index(TILE[2]).astype(jnp.int32)
+    own_first = core * HALF
 
     def amp_copy(group):
         place = pl.ds(group * GROUP, GROUP)
         return pltpu.make_async_copy(amps_hbm.at[place], amps_ref.at[place], amp_sems.at[group])
 
-    for group in range(groups):
-        amp_copy(group).start()
-    sums[...] = jnp.zeros_like(sums)
-    probe_sums_ref[...] = jnp.zeros_like(probe_sums_ref)
-    fetch.wait()
-    own_first = scalars[2, 1] * HALF
-    copies = [(tables_hbm, tables)]
+    copies = [
+        (tables_hbm, tables),
+        (rows_hbm, rows_ref),
+        (cols_hbm, cols_ref),
+        (live_hbm, live_ref),
+    ]
     if from_strips:
         for k in range(BLOCKS):
             start = pl.multiple_of((k ^ own_first) * PATCH, PATCH)
@@ -139,16 +144,26 @@
     started = [pltpu.make_async_copy(a, b, sems.at[n]) for n, (a, b) in enumerate(copies)]
     for copy in started:
         copy.start()
+    amp_copy(0).start()
+    sums[...] = jnp.zeros_like(sums)
+    probe_sums_ref[...] = jnp.zeros_like(probe_sums_ref)
     for copy in started:
         copy.wait()
-    live = scalars[2, 0]
+    live = live_ref[0, 0]
     lane = lax.broadcasted_iota(jnp.int32, (PATCH, PATCH), 1)
+
+    steps = (live + GROUP - 1) // GROUP
 
     def visit(step, carry):
         amp_copy(step).wait()
+
+        @pl.when(step + 1 < steps)
+        def _():
+            amp_copy(step + 1).start()
+
         slots = [step * GROUP + k for k in range(GROUP)]
-        places = [column_place(scalars[1, s], own_first) for s in slots]
-        rows = [scalars[0, s] for s in slots]
+        places = [column_place(cols_ref[0, 0, s], own_first) for s in slots]
+        rows = [rows_ref[0, 0, s] for s in slots]
         patches = {}
         waves = {}
 
@@ -208,7 +223,7 @@
                     sums[plane, near, pl.ds(rows[k], PATCH), :] += jnp.where(inside, turned, 0.0)
                     sums[plane, far, pl.ds(rows[k], PATCH), :] += jnp.where(inside, 0.0, turned)
             for plane in range(3):
-                probe_sums_ref[plane] += totals[plane]
+                probe_sums_ref[pl.ds(plane * PATCH, PATCH), :] += totals[plane]
 
         stages = (
             cut,
@@ -225,22 +240,21 @@
                 stage(pair)
         return carry
 
-    def skip(step, carry):
-        amp_copy(step).wait()
-        return carry
-
-    steps = (live + GROUP - 1) // GROUP
     lax.fori_loop(0, steps, visit, 0)
-    outs = (
+    outs = [
         (sums.at[:, HALF:, STRIP:, :], give_low_ref),
         (sums.at[:, HALF:, :STRIP, :], give_up_ref),
         (sums.at[:, :HALF, STRIP:, :], keep_low_ref),
         (sums.at[:, :HALF, :STRIP, :], keep_up_ref),
-    )
+    ]
+    count, height, _ = keep_probe_ref.shape
+    for half, out in ((core, keep_probe_ref), (1 - core, give_probe_ref)):
+        for k in range(count):
+            start = (half * count + (here + k) % count) * height
+            outs.append((probe_sums_ref.at[pl.ds(pl.multiple_of(start, 8), height)], out.at[k]))
     started = [pltpu.make_async_copy(a, b, sems.at[n]) for n, (a, b) in enumerate(outs)]
     for copy in started:
         copy.start()
-    lax.fori_loop(steps, groups, skip, 0)
     for copy in started:
         copy.wait()
 
@@ -248,26 +262,29 @@
 def run_positions(scalars, probe, amps, tables, first, mine, other):
     from_strips = first is not None
     quarter = jax.ShapeDtypeStruct((3, HALF, STRIP, PATCH), jnp.float32)
+    count = lax.axis_size(TILE[2])
+    pieces_of = jax.ShapeDtypeStruct((count, 3 * PATCH // (2 * count), PATCH), jnp.float32)
 
     def kernel(*refs):
         if from_strips:
             positions_kernel(True, *refs)
         else:
-            positions_kernel(False, *refs[:4], None, *refs[4:])
+            positions_kernel(False, *refs[:6], None, *refs[6:])
 
     pieces = (first, mine, other) if from_strips else (mine, other)
     return pl.pallas_call(
         kernel,
-        out_shape=(quarter,) * 4 + (jax.ShapeDtypeStruct((3, PATCH, PATCH), jnp.float32),),
-        in_specs=[ANY, VMEM] + [ANY] * (2 + len(pieces)),
-        out_specs=(ANY,) * 4 + (VMEM,),
+        out_shape=(quarter,) * 4 + (pieces_of,) * 2,
+        in_specs=[ANY] * 3 + [VMEM] + [ANY] * (2 + len(pieces)),
+        out_specs=(ANY,) * 6,
         scratch_shapes=[
+            pltpu.VMEM((3 * PATCH, PATCH), jnp.float32),
             pltpu.VMEM((2, BLOCKS, BAND, PATCH), jnp.float32),
             pltpu.VMEM((3, BLOCKS, BAND, PATCH), jnp.float32),
             pltpu.VMEM(amps.shape, jnp.float32),
             pltpu.VMEM(tables.shape, tables.dtype),
-            pltpu.SMEM(scalars.shape, jnp.int32),
-            pltpu.SemaphoreType.DMA((2 * BLOCKS + 2,)),
+            *(pltpu.SMEM(s.shape, jnp.int32) for s in scalars),
+            pltpu.SemaphoreType.DMA((2 * BLOCKS + 4,)),
             pltpu.SemaphoreType.DMA((amps.shape[0] // GROUP,)),
         ],
         compiler_params=pltpu.CompilerParams(vmem_limit_bytes=60 * 2**20),
@@ -275,15 +292,7 @@
             flops=13 * 10**9, bytes_accessed=8 * 2**20, transcendentals=2**19
         ),
         name="positions",
-    )(scalars, probe, amps, tables, *pieces)
-
-
-def halved_over_cores(value):
-    core = lax.axis_index("pos")
-    lines = value.reshape(2, -1, PATCH)
-    mine = lax.dynamic_index_in_dim(lines, core, 0, False)
-    other = lax.dynamic_index_in_dim(lines, 1 - core, 0, False)
-    return mine + swapped(other)
+    )(*scalars, probe, amps, tables, *pieces)
 
 
 def joined_over_cores(part):
@@ -294,18 +303,50 @@
     return jnp.concatenate([low, high])
 
 
-def summed_over(part, axis):
-    count = lax.axis_size(axis)
+def fans_of(count):
+    fans = []
     stride = 1
     while stride < count:
-        fan = 4 if count % (stride * 4) == 0 else 2
+        fans.append((stride, 4 if count % (stride * 4) == 0 else 2))
+        stride *= fans[-1][1]
+    return fans
+
+
+def summed_over(part, axis):
+    for stride, fan in fans_of(lax.axis_size(axis)):
         part = shifts_among(part, axis, stride, fan)
-        stride *= fan
     return part
 
 
+def scattered_over(pieces, axis):
+    count = lax.axis_size(axis)
+    arrived = []
+    for step in range(1, count):
+        route = [(i, (i + step) % count) for i in range(count)]
+        arrived.append(lax.ppermute(pieces[step], axis, route))
+    total = pieces[0]
+    for piece in arrived:
+        total = total + piece
+    return total
+
+
+def gathered_over(piece, axis):
+    count = lax.axis_size(axis)
+    here = lax.axis_index(axis)
+    pieces = [piece]
+    for step in range(1, count):
+        pieces.append(lax.ppermute(piece, axis, [((i + step) % count, i) for i in range(count)]))
+    rows = []
+    for place in range(count):
+        row = pieces[0]
+        for step in range(1, count):
+            row = jnp.where((place - here) % count == step, pieces[step], row)
+        rows.append(row)
+    return jnp.concatenate(rows)
+
+
 def after(value, other):
-    return value + jnp.minimum(jnp.abs(other[0, 0]), 0.0)
+    return value + jnp.minimum(jnp.abs(other[(0,) * other.ndim]), 0.0)
 
 
 def shifts_among(value, axis, stride, fan):
@@ -329,49 +370,52 @@
     tables = dft_tables()
     core = lax.axis_index("pos")
     amps = amplitudes[0, 0]
-    last = jnp.concatenate([live_count[0], core.astype(jnp.int32)[None]])
-    lines = [scan_rows[0, 0], scan_cols[0, 0], last]
-    scalars = jnp.stack([jnp.pad(line, (0, PATCH - line.shape[0])) for line in lines])
-    scalars = jnp.pad(scalars, ((0, 8 - len(lines)), (0, 0)))
+    scalars = (scan_rows, scan_cols, live_count)
     probe_relax = amps.shape[0] * lax.axis_size(TILE) * lax.axis_size("pos") / 4.0
     own_half = lax.dynamic_slice_in_dim(object_field, core * (COLS // 2), COLS // 2, 2)
     halo = from_tile(own_half, 1)
     halo_other = swapped(halo)
-    up, low, give_up, give_low, probe_sums = run_positions(
+    up, low, give_up, give_low, keep_sums, give_sums = run_positions(
         scalars, probe_field, amps, tables, object_field, halo, halo_other
     )
 
-    def next_probe(part, probe):
-        for axis in TILE[1::-1]:
-            part = summed_over(part, axis)
+    def next_probe(part, earlier, probe):
+        part = gathered_over(part, TILE[2])
+        if earlier is not None:
+            part = after(part, earlier)
         total = joined_over_cores(part).reshape(3, PATCH, PATCH)
         return (total[:2] + probe_relax * probe) / (total[2] + probe_relax)[None]
 
     def updated(sums, field):
         return (sums[:2] + OBJECT_RELAX * field) / (sums[2] + OBJECT_RELAX)[None]
 
-    part = summed_over(halved_over_cores(probe_sums), TILE[2])
+    part = scattered_over(keep_sums + swapped(give_sums), TILE[2])
     low = after(low + swapped(give_low), part)
     up = after(up + swapped(give_up), part)
     above = from_tile(low, -1)
     below = from_tile(up, 1)
-    probe_field = next_probe(part, probe_field)
+    part = summed_over(summed_over(part, TILE[1]), TILE[0])
+    up, low, above, below = lax.optimization_barrier((up, low, above, below))
     own_half = updated(up + above, in_blocks(own_half))
     mine = jnp.concatenate([own_half, updated(low + below, in_blocks(halo))], axis=2)
     other = swapped(mine)
-    up, low, give_up, give_low, probe_sums = run_positions(
+    probe_field = next_probe(part, None, probe_field)
+    up, low, give_up, give_low, keep_sums, give_sums = run_positions(
         scalars, probe_field, amps, tables, None, mine, other
     )
-    part = summed_over(halved_over_cores(probe_sums), TILE[2])
+    part = scattered_over(keep_sums + swapped(give_sums), TILE[2])
     low = after(low + swapped(give_low), part)
     up = up + swapped(give_up)
     above = from_tile(low, -1)
-    probe_out = next_probe(part, probe_field)
+    part = summed_over(summed_over(part, TILE[1]), TILE[0])
+    up = after(up, part)
     mine = updated(up + above, own_half).transpose(0, 2, 1, 3).reshape(2, STRIP, COLS // 2)
     other = swapped(mine)
     left = jnp.where(core == 0, mine, other)
     right = jnp.where(core == 0, other, mine)
-    return jnp.concatenate([left, right], axis=2), probe_out
+    object_out = jnp.concatenate([left, right], axis=2)
+    probe_out = next_probe(part, object_out, probe_field)
+    return object_out, probe_out
 
 
 def torus_of(mesh):

time: 198 us -> 187 us (0.944)
  the two profiles are of different devices: /device:TPU:223 before, /device:TPU:1 now
where the time goes in v4:
time: 187 us; the launch traced here: 186 us
  starting transfers between devices  82.6 us (44%)
  waiting for transfers between devices  62.2 us (33%)
  Pallas kernels  19.5 us (10%)
  other arithmetic  9.02 us (5%)
  local copies, waits for them, and re-layouts  8.31 us (4%)
  between operations  4.34 us (2%)
    ppermute x14, waiting for transfers between devices, shifts_among(): total = total + lax.ppermute(value, axis, route)  31.5 us
    ppermute x11, starting transfers between devices, swapped(): return lax.ppermute(value, 'pos', [(0, 1), (1, 0)])  25.8 us
    ppermute x6, starting transfers between devices, gathered_over(): lax.ppermute(piece, axis, [((i + step) % count, i) for i in range(count)])  24.9 us
    pallas_call x2, Pallas kernels, run_positions(): pl.pallas_call(kernel, out_shape=(quarter,) * 4 + (pieces_of,) * 2, in_sp...  19.5 us
    ppermute x4, waiting for transfers between devices, from_tile(): lax.ppermute(value, TILE, [((i + distance) % count, i) for i in range(cou...  14.1 us
    ppermute x14, starting transfers between devices, shifts_among(): total = total + lax.ppermute(value, axis, route)  13.1 us
    ppermute x4, starting transfers between devices, from_tile(): lax.ppermute(value, TILE, [((i + distance) % count, i) for i in range(cou...  12.8 us
    ppermute x6, waiting for transfers between devices, scattered_over(): arrived.append(lax.ppermute(pieces[step], axis, route))  7.22 us
  transfers between devices with their start and end apart: 41, of which 24 were waited for; matrix products, arithmetic and copies ran while one was open for 7% of the time, Pallas kernels for 0%

profile of v4, /device:TPU:1, one launch (start us, length us, event | category | flops | bytes accessed | tf_op | source)
XLA Modules:
  0.0 186.0 jit_solution(17870223462985150373)
XLA Ops:
  0.6 1.1 constant_dynamic-slice_fusion
  1.7 11.1 %collective-permute-start = (f32[2,128,512]{2,1,0:T(8,128)S(1)}, f32[2,128,512]{2,1,0:T(8,128)S(1)}, u32[]{:S(2)}, u32[]{:S(2)}) collective-permute-start(f32[2,128,512]{2,1,0:T(8,128)S(1)} %constant_dynamic-slice_fusion), channel_id=1, source_target_pairs={{2,0},{4,2},{6,4},{8,6},{10,8},{12,10},{14,12},{16,14},{18,16},{20... | collective-permute-start | bytes 1572872 | tf_op jit(solution)/shard_map/ppermute | solution.py:33
  12.8 10.6 %collective-permute-done.refs_7_ = f32[2,128,512]{2,1,0:T(8,128)S(1)} collective-permute-done((f32[2,128,512]{2,1,0:T(8,128)S(1)}, f32[2,128,512]{2,1,0:T(8,128)S(1)}, u32[]{:S(2)}, u32[]{:S(2)}) %collective-permute-start) | collective-permute-done | bytes 524320 | tf_op jit(solution)/shard_map/ppermute | solution.py:33
  23.4 1.5 collective-permute-start.1
  25.6 0.9 collective-permute-done.1.refs_8_
  26.5 0.8 copy-done.7
  27.3 9.8 %positions.2 = (f32[3,4,128,128]{3,2,1,0:T(8,128)}, f32[3,4,128,128]{3,2,1,0:T(8,128)}, f32[3,4,128,128]{3,2,1,0:T(8,128)}, f32[3,4,128,128]{3,2,1,0:T(8,128)}, ...) custom-call(s32[1,1,32]{2,1,0:T(1,128)} %refs_0_.3, s32[1,1,32]{2,1,0:T(1,128)} %refs_1_.3, s32[1,1]{1,0:T(1,128)S(6)} %copy.15.refs_2_, ...), custom_call_target="tpu_custom_call" | custom-call | flops 12999999488 | bytes 8388608 | tf_op jit(solution)/shard_map/positions/pallas_call | solution.py:275
  37.1 5.4 %collective-permute-start.17 = (f32[3,4,128,128]{3,2,1,0:T(8,128)}, f32[3,4,128,128]{3,2,1,0:T(8,128)S(1)}, u32[]{:S(2)}, u32[]{:S(2)}) collective-permute-start(f32[3,4,128,128]{3,2,1,0:T(8,128)} %get-tuple-element.21), channel_id=1, source_target_pairs={{0,1},{1,0},{2,3},{3,2},{4,5},{5,4},{6,7},{7,6},{8,9},{9,8},{10,11... | collective-permute-start | bytes 2359304 | tf_op jit(solution)/shard_map/ppermute | solution.py:28
  43.0 1.8 collective-permute-done.2
  44.7 0.9 add.190
  45.8 2.7 %collective-permute-start.5 = (f32[48,128]{1,0:T(8,128)S(1)}, f32[48,128]{1,0:T(8,128)S(1)}, u32[]{:S(2)}, u32[]{:S(2)}) collective-permute-start(f32[48,128]{1,0:T(8,128)S(1)} %get-tuple-element.54), channel_id=1, source_target_pairs={{0,6},{2,0},{4,2},{6,4},{1,7},{3,1},{5,3},{7,5},{8,14},{10,8},{12,... | collective-permute-start | bytes 73736 | tf_op jit(solution)/shard_map/ppermute | solution.py:326
  48.4 1.2 collective-permute-done.3
  49.6 3.0 %collective-permute-done.4 = f32[48,128]{1,0:T(8,128)S(1)} collective-permute-done((f32[48,128]{1,0:T(8,128)S(1)}, f32[48,128]{1,0:T(8,128)S(1)}, u32[]{:S(2)}, u32[]{:S(2)}) %collective-permute-start.4) | collective-permute-done | bytes 24608 | tf_op jit(solution)/shard_map/ppermute | solution.py:326
  52.6 0.5 slice.106
  53.8 1.2 add_add_fusion.3
  55.0 1.5 collective-permute-start.20
  56.8 1.5 collective-permute-start.7
  58.3 14.3 %collective-permute-done.8 = f32[48,128]{1,0:T(8,128)S(1)} collective-permute-done((f32[48,128]{1,0:T(8,128)S(1)}, f32[48,128]{1,0:T(8,128)S(1)}, u32[]{:S(2)}, u32[]{:S(2)}) %collective-permute-start.8) | collective-permute-done | bytes 24608 | tf_op jit(solution)/shard_map/ppermute | solution.py:360
  73.1 1.4 collective-permute-start.9
  74.4 1.6 collective-permute-done.11
  76.0 1.0 collective-permute-done.10
  77.0 1.3 collective-permute-done.9
  78.4 3.9 %collective-permute-start.12 = (f32[48,128]{1,0:T(8,128)S(1)}, f32[48,128]{1,0:T(8,128)S(1)}, u32[]{:S(2)}, u32[]{:S(2)}) collective-permute-start(f32[48,128]{1,0:T(8,128)S(1)} %add_add_fusion.6), channel_id=1, source_target_pairs={{0,128},{32,160},{64,192},{96,224},{128,0},{160,32},{192,64},{224,... | collective-permute-start | bytes 73736 | tf_op jit(solution)/shard_map/ppermute | solution.py:360
  82.7 1.2 copy.11
  84.2 0.9 collective-permute-done.12
  85.1 7.4 %collective-permute-start.15 = (f32[48,128]{1,0:T(8,128)S(1)}, f32[48,128]{1,0:T(8,128)S(1)}, u32[]{:S(2)}, u32[]{:S(2)}) collective-permute-start(f32[48,128]{1,0:T(8,128)S(1)} %add.200), channel_id=1, source_target_pairs={{2,0},{4,2},{6,4},{0,6},{3,1},{5,3},{7,5},{1,7},{10,8},{12,10},{14... | collective-permute-start | bytes 73736 | tf_op jit(solution)/shard_map/ppermute | solution.py:338
  92.5 0.7 collective-permute-start.13
  93.1 1.2 add.211
  94.4 1.2 add.214
  96.0 5.9 %collective-permute-start.21 = (f32[2,4,256,128]{3,2,1,0:T(8,128)S(1)}, f32[2,4,256,128]{3,2,1,0:T(8,128)S(1)}, u32[]{:S(2)}, u32[]{:S(2)}) collective-permute-start(f32[2,4,256,128]{3,2,1,0:T(8,128)S(1)} %pad_maximum_fusion.refs_6_), channel_id=1, source_target_pairs={{0,1},{1,0},{2,3},{3,2},{4,5},{5,4},{6,7},{7,6},{8,9},{9,8},{10,11... | collective-permute-start | bytes 3145736 | tf_op jit(solution)/shard_map/ppermute | solution.py:28
  101.9 1.5 collective-permute-start.16
  103.5 0.9 collective-permute-done.16
  104.5 0.7 add_divide_fusion.1.refs_3_
  105.2 1.0 copy-done.6
  106.2 9.7 %positions.3 = (f32[3,4,128,128]{3,2,1,0:T(8,128)}, f32[3,4,128,128]{3,2,1,0:T(8,128)}, f32[3,4,128,128]{3,2,1,0:T(8,128)}, f32[3,4,128,128]{3,2,1,0:T(8,128)}, ...) custom-call(s32[1,1,32]{2,1,0:T(1,128)} %refs_0_.3, s32[1,1,32]{2,1,0:T(1,128)} %refs_1_.3, s32[1,1]{1,0:T(1,128)S(6)} %copy.15.refs_2_, ...), custom_call_target="tpu_custom_call" | custom-call | flops 12999999488 | bytes 8388608 | tf_op jit(solution)/shard_map/positions/pallas_call | solution.py:275
  116.0 5.4 %collective-permute-start.34 = (f32[3,4,128,128]{3,2,1,0:T(8,128)}, f32[3,4,128,128]{3,2,1,0:T(8,128)S(1)}, u32[]{:S(2)}, u32[]{:S(2)}) collective-permute-start(f32[3,4,128,128]{3,2,1,0:T(8,128)} %get-tuple-element.33), channel_id=1, source_target_pairs={{0,1},{1,0},{2,3},{3,2},{4,5},{5,4},{6,7},{7,6},{8,9},{9,8},{10,11... | collective-permute-start | bytes 2359304 | tf_op jit(solution)/shard_map/ppermute | solution.py:28
  121.4 2.2 %collective-permute-done.23 = f32[4,48,128]{2,1,0:T(8,128)S(1)} collective-permute-done((f32[4,48,128]{2,1,0:T(8,128)}, f32[4,48,128]{2,1,0:T(8,128)S(1)}, u32[]{:S(2)}, u32[]{:S(2)}) %collective-permute-start.23) | collective-permute-done | bytes 98336 | tf_op jit(solution)/shard_map/ppermute | solution.py:28
  123.6 0.9 add.218
  124.6 2.7 %collective-permute-start.26 = (f32[48,128]{1,0:T(8,128)S(1)}, f32[48,128]{1,0:T(8,128)S(1)}, u32[]{:S(2)}, u32[]{:S(2)}) collective-permute-start(f32[48,128]{1,0:T(8,128)S(1)} %get-tuple-element.47), channel_id=1, source_target_pairs={{0,6},{2,0},{4,2},{6,4},{1,7},{3,1},{5,3},{7,5},{8,14},{10,8},{12,... | collective-permute-start | bytes 73736 | tf_op jit(solution)/shard_map/ppermute | solution.py:326
  127.3 0.4 collective-permute-start.25
  127.7 0.7 collective-permute-start.22
  128.5 3.0 %collective-permute-done.25 = f32[48,128]{1,0:T(8,128)S(1)} collective-permute-done((f32[48,128]{1,0:T(8,128)S(1)}, f32[48,128]{1,0:T(8,128)S(1)}, u32[]{:S(2)}, u32[]{:S(2)}) %collective-permute-start.25) | collective-permute-done | bytes 24608 | tf_op jit(solution)/shard_map/ppermute | solution.py:326
  131.5 0.5 slice.116
  132.6 1.2 add_add_fusion
  134.2 1.4 collective-permute-start.27
  135.5 1.2 collective-permute-done.29
  136.7 1.6 collective-permute-done.28
  138.3 0.8 collective-permute-done.27
  139.2 1.3 collective-permute-start.31
  140.8 1.3 collective-permute-done.32
  142.2 0.7 collective-permute-done.31
  142.9 2.4 %collective-permute-done.30 = f32[48,128]{1,0:T(8,128)S(1)} collective-permute-done((f32[48,128]{1,0:T(8,128)S(1)}, f32[48,128]{1,0:T(8,128)S(1)}, u32[]{:S(2)}, u32[]{:S(2)}) %collective-permute-start.30) | collective-permute-done | bytes 24608 | tf_op jit(solution)/shard_map/ppermute | solution.py:360
  145.3 2.6 %collective-permute-start.33 = (f32[48,128]{1,0:T(8,128)S(1)}, f32[48,128]{1,0:T(8,128)S(1)}, u32[]{:S(2)}, u32[]{:S(2)}) collective-permute-start(f32[48,128]{1,0:T(8,128)S(1)} %add_add_fusion.4), channel_id=1, source_target_pairs={{0,128},{32,160},{64,192},{96,224},{128,0},{160,32},{192,64},{224,... | collective-permute-start | bytes 73736 | tf_op jit(solution)/shard_map/ppermute | solution.py:360
  147.9 4.3 %collective-permute-done.33 = f32[48,128]{1,0:T(8,128)S(1)} collective-permute-done((f32[48,128]{1,0:T(8,128)S(1)}, f32[48,128]{1,0:T(8,128)S(1)}, u32[]{:S(2)}, u32[]{:S(2)}) %collective-permute-start.33) | collective-permute-done | bytes 24608 | tf_op jit(solution)/shard_map/ppermute | solution.py:360
  152.2 0.5 slice.115
  153.4 3.5 %collective-permute-done.35 = f32[3,4,128,128]{3,2,1,0:T(8,128)S(1)} collective-permute-done((f32[3,4,128,128]{3,2,1,0:T(8,128)S(1)}, f32[3,4,128,128]{3,2,1,0:T(8,128)S(1)}, u32[]{:S(2)}, u32[]{:S(2)}) %collective-permute-start.35) | collective-permute-done | bytes 786464 | tf_op jit(solution)/shard_map/ppermute | solution.py:33
  157.4 3.2 %collective-permute-start.36 = (f32[2,128,512]{1,2,0:T(8,128)S(1)}, f32[2,128,512]{1,2,0:T(8,128)S(1)}, u32[]{:S(2)}, u32[]{:S(2)}) collective-permute-start(f32[2,128,512]{1,2,0:T(8,128)S(1)} %bitcast.52), channel_id=1, source_target_pairs={{0,1},{1,0},{2,3},{3,2},{4,5},{5,4},{6,7},{7,6},{8,9},{9,8},{10,11... | collective-permute-start | bytes 1572872 | tf_op jit(solution)/shard_map/ppermute | solution.py:28
  160.5 16.3 %collective-permute-start.39 = (f32[48,128]{1,0:T(8,128)S(1)}, f32[48,128]{1,0:T(8,128)S(1)}, u32[]{:S(2)}, u32[]{:S(2)}) collective-permute-start(f32[48,128]{1,0:T(8,128)S(1)} %add.228), channel_id=1, source_target_pairs={{2,0},{4,2},{6,4},{0,6},{3,1},{5,3},{7,5},{1,7},{10,8},{12,10},{14... | collective-permute-start | bytes 73736 | tf_op jit(solution)/shard_map/ppermute | solution.py:338
  176.8 0.6 collective-permute-start.37
  177.8 3.2 %collective-permute-done.38 = f32[48,128]{1,0:T(8,128)S(1)} collective-permute-done((f32[48,128]{1,0:T(8,128)S(1)}, f32[48,128]{1,0:T(8,128)S(1)}, u32[]{:S(2)}, u32[]{:S(2)}) %collective-permute-start.38) | collective-permute-done | bytes 24608 | tf_op jit(solution)/shard_map/ppermute | solution.py:338
  181.1 0.5 slice.119
  182.3 1.6 collective-permute-start.40
  184.0 1.3 copy.14
  185.3 0.7 add_divide_fusion
  (85 shorter events, 4.3 us)
Async XLA Ops:
  1.7 21.7 %collective-permute-start = (f32[2,128,512]{2,1,0:T(8,128)S(1)}, f32[2,128,512]{2,1,0:T(8,128)S(1)}, u32[]{:S(2)}, u32[]{:S(2)}) collective-permute-start(f32[2,128,512]{2,1,0:T(8,128)S(1)} %constant_dynamic-slice_fusion), channel_id=1, source_target_pairs={{2,0},{4,2},{6,4},{8,6},{10,8},{12,10},{14,12},{16,14},{18,16},{20... | collective-permute-start | bytes 1572872 | tf_op jit(solution)/shard_map/ppermute | solution.py:33
  23.4 3.1 %copy-start.4 = (f32[2,128,512]{2,1,0:T(8,128)}, f32[2,128,512]{2,1,0:T(8,128)S(1)}, u32[]{:S(2)}) copy-start(f32[2,128,512]{2,1,0:T(8,128)S(1)} %collective-permute-done.refs_7_) | copy-start | bytes 1572868
  23.4 3.1 %collective-permute-start.1 = (f32[2,128,512]{2,1,0:T(8,128)S(1)}, f32[2,128,512]{2,1,0:T(8,128)S(1)}, u32[]{:S(2)}, u32[]{:S(2)}) collective-permute-start(f32[2,128,512]{2,1,0:T(8,128)S(1)} %collective-permute-done.refs_7_), channel_id=1, source_target_pairs={{0,1},{1,0},{2,3},{3,2},{4,5},{5,4},{6,7},{7,6},{8,9},{9,8},{10,11... | collective-permute-start | bytes 1572872 | tf_op jit(solution)/shard_map/ppermute | solution.py:28
  26.5 0.8 copy-start.7
  37.1 19.5 %copy-start.1 = (f32[3,4,128,128]{3,2,1,0:T(8,128)S(1)}, f32[3,4,128,128]{3,2,1,0:T(8,128)}, u32[]{:S(2)}) copy-start(f32[3,4,128,128]{3,2,1,0:T(8,128)} %get-tuple-element.22) | copy-start | bytes 2359300
  37.1 16.7 %collective-permute-start.17 = (f32[3,4,128,128]{3,2,1,0:T(8,128)}, f32[3,4,128,128]{3,2,1,0:T(8,128)S(1)}, u32[]{:S(2)}, u32[]{:S(2)}) collective-permute-start(f32[3,4,128,128]{3,2,1,0:T(8,128)} %get-tuple-element.21), channel_id=1, source_target_pairs={{0,1},{1,0},{2,3},{3,2},{4,5},{5,4},{6,7},{7,6},{8,9},{9,8},{10,11... | collective-permute-start | bytes 2359304 | tf_op jit(solution)/shard_map/ppermute | solution.py:28
  42.5 2.3 %collective-permute-start.2 = (f32[4,48,128]{2,1,0:T(8,128)}, f32[4,48,128]{2,1,0:T(8,128)S(1)}, u32[]{:S(2)}, u32[]{:S(2)}) collective-permute-start(f32[4,48,128]{2,1,0:T(8,128)} %get-tuple-element.19), channel_id=1, source_target_pairs={{0,1},{1,0},{2,3},{3,2},{4,5},{5,4},{6,7},{7,6},{8,9},{9,8},{10,11... | collective-permute-start | bytes 294920 | tf_op jit(solution)/shard_map/ppermute | solution.py:28
  42.6 14.0 %collective-permute-start.18 = (f32[3,4,128,128]{3,2,1,0:T(8,128)}, f32[3,4,128,128]{3,2,1,0:T(8,128)S(1)}, u32[]{:S(2)}, u32[]{:S(2)}) collective-permute-start(f32[3,4,128,128]{3,2,1,0:T(8,128)} %get-tuple-element.23), channel_id=1, source_target_pairs={{0,1},{1,0},{2,3},{3,2},{4,5},{5,4},{6,7},{7,6},{8,9},{9,8},{10,11... | collective-permute-start | bytes 2359304 | tf_op jit(solution)/shard_map/ppermute | solution.py:28
  45.7 4.0 %collective-permute-start.3 = (f32[48,128]{1,0:T(8,128)S(1)}, f32[48,128]{1,0:T(8,128)S(1)}, u32[]{:S(2)}, u32[]{:S(2)}) collective-permute-start(f32[48,128]{1,0:T(8,128)S(1)} %get-tuple-element.53), channel_id=1, source_target_pairs={{0,2},{2,4},{4,6},{6,0},{1,3},{3,5},{5,7},{7,1},{8,10},{10,12},{12... | collective-permute-start | bytes 73736 | tf_op jit(solution)/shard_map/ppermute | solution.py:326
  45.8 3.9 %collective-permute-start.5 = (f32[48,128]{1,0:T(8,128)S(1)}, f32[48,128]{1,0:T(8,128)S(1)}, u32[]{:S(2)}, u32[]{:S(2)}) collective-permute-start(f32[48,128]{1,0:T(8,128)S(1)} %get-tuple-element.54), channel_id=1, source_target_pairs={{0,6},{2,0},{4,2},{6,4},{1,7},{3,1},{5,3},{7,5},{8,14},{10,8},{12,... | collective-permute-start | bytes 73736 | tf_op jit(solution)/shard_map/ppermute | solution.py:326
  48.4 4.2 %collective-permute-start.4 = (f32[48,128]{1,0:T(8,128)S(1)}, f32[48,128]{1,0:T(8,128)S(1)}, u32[]{:S(2)}, u32[]{:S(2)}) collective-permute-start(f32[48,128]{1,0:T(8,128)S(1)} %get-tuple-element.55), channel_id=1, source_target_pairs={{0,4},{2,6},{4,0},{6,2},{1,5},{3,7},{5,1},{7,3},{8,12},{10,14},{12... | collective-permute-start | bytes 73736 | tf_op jit(solution)/shard_map/ppermute | solution.py:326
  55.0 38.1 %collective-permute-start.20 = (f32[3,4,128,128]{3,2,1,0:T(8,128)S(1)}, f32[3,4,128,128]{3,2,1,0:T(8,128)}, u32[]{:S(2)}, u32[]{:S(2)}) collective-permute-start(f32[3,4,128,128]{3,2,1,0:T(8,128)S(1)} %add_add_fusion.3), channel_id=1, source_target_pairs={{2,0},{4,2},{6,4},{8,6},{10,8},{12,10},{14,12},{16,14},{18,16},{20... | collective-permute-start | bytes 2359304 | tf_op jit(solution)/shard_map/ppermute | solution.py:33
  56.6 36.5 %collective-permute-start.19 = (f32[3,4,128,128]{3,2,1,0:T(8,128)S(1)}, f32[3,4,128,128]{3,2,1,0:T(8,128)}, u32[]{:S(2)}, u32[]{:S(2)}) collective-permute-start(f32[3,4,128,128]{3,2,1,0:T(8,128)S(1)} %add_add_fusion.2), channel_id=1, source_target_pairs={{254,0},{0,2},{2,4},{4,6},{6,8},{8,10},{10,12},{12,14},{14,16},{16... | collective-permute-start | bytes 2359304 | tf_op jit(solution)/shard_map/ppermute | solution.py:33
  56.7 15.9 %collective-permute-start.8 = (f32[48,128]{1,0:T(8,128)S(1)}, f32[48,128]{1,0:T(8,128)S(1)}, u32[]{:S(2)}, u32[]{:S(2)}) collective-permute-start(f32[48,128]{1,0:T(8,128)S(1)} %fusion.12), channel_id=1, source_target_pairs={{0,24},{8,0},{16,8},{24,16},{1,25},{9,1},{17,9},{25,17},{2,26},{10... | collective-permute-start | bytes 73736 | tf_op jit(solution)/shard_map/ppermute | solution.py:360
  56.8 15.8 %collective-permute-start.7 = (f32[48,128]{1,0:T(8,128)S(1)}, f32[48,128]{1,0:T(8,128)S(1)}, u32[]{:S(2)}, u32[]{:S(2)}) collective-permute-start(f32[48,128]{1,0:T(8,128)S(1)} %fusion.12), channel_id=1, source_target_pairs={{0,16},{8,24},{16,0},{24,8},{1,17},{9,25},{17,1},{25,9},{2,18},{10... | collective-permute-start | bytes 73736 | tf_op jit(solution)/shard_map/ppermute | solution.py:360
  58.3 14.3 %collective-permute-start.6 = (f32[48,128]{1,0:T(8,128)S(1)}, f32[48,128]{1,0:T(8,128)S(1)}, u32[]{:S(2)}, u32[]{:S(2)}) collective-permute-start(f32[48,128]{1,0:T(8,128)S(1)} %fusion.12), channel_id=1, source_target_pairs={{0,8},{8,16},{16,24},{24,0},{1,9},{9,17},{17,25},{25,1},{2,10},{10... | collective-permute-start | bytes 73736 | tf_op jit(solution)/shard_map/ppermute | solution.py:360
  72.7 3.3 %collective-permute-start.11 = (f32[48,128]{1,0:T(8,128)S(1)}, f32[48,128]{1,0:T(8,128)S(1)}, u32[]{:S(2)}, u32[]{:S(2)}) collective-permute-start(f32[48,128]{1,0:T(8,128)S(1)} %add_add_fusion.7), channel_id=1, source_target_pairs={{0,96},{32,0},{64,32},{96,64},{128,224},{160,128},{192,160},{224,1... | collective-permute-start | bytes 73736 | tf_op jit(solution)/shard_map/ppermute | solution.py:360
  73.0 4.1 %collective-permute-start.10 = (f32[48,128]{1,0:T(8,128)S(1)}, f32[48,128]{1,0:T(8,128)S(1)}, u32[]{:S(2)}, u32[]{:S(2)}) collective-permute-start(f32[48,128]{1,0:T(8,128)S(1)} %add_add_fusion.7), channel_id=1, source_target_pairs={{0,64},{32,96},{64,0},{96,32},{128,192},{160,224},{192,128},{224,1... | collective-permute-start | bytes 73736 | tf_op jit(solution)/shard_map/ppermute | solution.py:360
  73.1 5.3 %collective-permute-start.9 = (f32[48,128]{1,0:T(8,128)S(1)}, f32[48,128]{1,0:T(8,128)S(1)}, u32[]{:S(2)}, u32[]{:S(2)}) collective-permute-start(f32[48,128]{1,0:T(8,128)S(1)} %add_add_fusion.7), channel_id=1, source_target_pairs={{0,32},{32,64},{64,96},{96,0},{128,160},{160,192},{192,224},{224,1... | collective-permute-start | bytes 73736 | tf_op jit(solution)/shard_map/ppermute | solution.py:360
  78.4 6.7 %collective-permute-start.12 = (f32[48,128]{1,0:T(8,128)S(1)}, f32[48,128]{1,0:T(8,128)S(1)}, u32[]{:S(2)}, u32[]{:S(2)}) collective-permute-start(f32[48,128]{1,0:T(8,128)S(1)} %add_add_fusion.6), channel_id=1, source_target_pairs={{0,128},{32,160},{64,192},{96,224},{128,0},{160,32},{192,64},{224,... | collective-permute-start | bytes 73736 | tf_op jit(solution)/shard_map/ppermute | solution.py:360
  85.1 16.8 %collective-permute-start.15 = (f32[48,128]{1,0:T(8,128)S(1)}, f32[48,128]{1,0:T(8,128)S(1)}, u32[]{:S(2)}, u32[]{:S(2)}) collective-permute-start(f32[48,128]{1,0:T(8,128)S(1)} %add.200), channel_id=1, source_target_pairs={{2,0},{4,2},{6,4},{0,6},{3,1},{5,3},{7,5},{1,7},{10,8},{12,10},{14... | collective-permute-start | bytes 73736 | tf_op jit(solution)/shard_map/ppermute | solution.py:338
  92.5 9.4 %collective-permute-start.14 = (f32[48,128]{1,0:T(8,128)S(1)}, f32[48,128]{1,0:T(8,128)S(1)}, u32[]{:S(2)}, u32[]{:S(2)}) collective-permute-start(f32[48,128]{1,0:T(8,128)S(1)} %add.200), channel_id=1, source_target_pairs={{4,0},{6,2},{0,4},{2,6},{5,1},{7,3},{1,5},{3,7},{12,8},{14,10},{8,... | collective-permute-start | bytes 73736 | tf_op jit(solution)/shard_map/ppermute | solution.py:338
  92.5 9.4 %collective-permute-start.13 = (f32[48,128]{1,0:T(8,128)S(1)}, f32[48,128]{1,0:T(8,128)S(1)}, u32[]{:S(2)}, u32[]{:S(2)}) collective-permute-start(f32[48,128]{1,0:T(8,128)S(1)} %add.200), channel_id=1, source_target_pairs={{6,0},{0,2},{2,4},{4,6},{7,1},{1,3},{3,5},{5,7},{14,8},{8,10},{10,... | collective-permute-start | bytes 73736 | tf_op jit(solution)/shard_map/ppermute | solution.py:338
  95.9 8.6 %copy-start.5 = (f32[2,128,128]{2,1,0:T(8,128)S(1)}, f32[2,128,128]{2,1,0:T(8,128)}, u32[]{:S(2)}) copy-start(f32[2,128,128]{2,1,0:T(8,128)} %refs_3_.1) | copy-start | bytes 393220
  95.9 9.2 %copy-start = (f32[2,4,256,128]{3,2,1,0:T(8,128)}, f32[2,4,256,128]{3,2,1,0:T(8,128)S(1)}, u32[]{:S(2)}) copy-start(f32[2,4,256,128]{3,2,1,0:T(8,128)S(1)} %pad_maximum_fusion.refs_6_) | copy-start | bytes 3145732
  96.0 9.2 %collective-permute-start.21 = (f32[2,4,256,128]{3,2,1,0:T(8,128)S(1)}, f32[2,4,256,128]{3,2,1,0:T(8,128)S(1)}, u32[]{:S(2)}, u32[]{:S(2)}) collective-permute-start(f32[2,4,256,128]{3,2,1,0:T(8,128)S(1)} %pad_maximum_fusion.refs_6_), channel_id=1, source_target_pairs={{0,1},{1,0},{2,3},{3,2},{4,5},{5,4},{6,7},{7,6},{8,9},{9,8},{10,11... | collective-permute-start | bytes 3145736 | tf_op jit(solution)/shard_map/ppermute | solution.py:28
  101.9 2.5 %collective-permute-start.16 = (f32[192,128]{1,0:T(8,128)S(1)}, f32[192,128]{1,0:T(8,128)S(1)}, u32[]{:S(2)}, u32[]{:S(2)}) collective-permute-start(f32[192,128]{1,0:T(8,128)S(1)} %pad_maximum_fusion.4), channel_id=1, source_target_pairs={{0,1},{1,0},{2,3},{3,2},{4,5},{5,4},{6,7},{7,6},{8,9},{9,8},{10,11... | collective-permute-start | bytes 294920 | tf_op jit(solution)/shard_map/ppermute | solution.py:28
  105.2 1.0 copy-start.6
  116.0 40.9 %copy-start.2 = (f32[3,4,128,128]{3,2,1,0:T(8,128)S(1)}, f32[3,4,128,128]{3,2,1,0:T(8,128)}, u32[]{:S(2)}) copy-start(f32[3,4,128,128]{3,2,1,0:T(8,128)} %get-tuple-element.28) | copy-start | bytes 2359300
  116.0 16.7 %collective-permute-start.34 = (f32[3,4,128,128]{3,2,1,0:T(8,128)}, f32[3,4,128,128]{3,2,1,0:T(8,128)S(1)}, u32[]{:S(2)}, u32[]{:S(2)}) collective-permute-start(f32[3,4,128,128]{3,2,1,0:T(8,128)} %get-tuple-element.33), channel_id=1, source_target_pairs={{0,1},{1,0},{2,3},{3,2},{4,5},{5,4},{6,7},{7,6},{8,9},{9,8},{10,11... | collective-permute-start | bytes 2359304 | tf_op jit(solution)/shard_map/ppermute | solution.py:28
  121.3 2.3 %collective-permute-start.23 = (f32[4,48,128]{2,1,0:T(8,128)}, f32[4,48,128]{2,1,0:T(8,128)S(1)}, u32[]{:S(2)}, u32[]{:S(2)}) collective-permute-start(f32[4,48,128]{2,1,0:T(8,128)} %get-tuple-element.31), channel_id=1, source_target_pairs={{0,1},{1,0},{2,3},{3,2},{4,5},{5,4},{6,7},{7,6},{8,9},{9,8},{10,11... | collective-permute-start | bytes 294920 | tf_op jit(solution)/shard_map/ppermute | solution.py:28
  124.5 4.0 %collective-permute-start.24 = (f32[48,128]{1,0:T(8,128)S(1)}, f32[48,128]{1,0:T(8,128)S(1)}, u32[]{:S(2)}, u32[]{:S(2)}) collective-permute-start(f32[48,128]{1,0:T(8,128)S(1)} %get-tuple-element.46), channel_id=1, source_target_pairs={{0,2},{2,4},{4,6},{6,0},{1,3},{3,5},{5,7},{7,1},{8,10},{10,12},{12... | collective-permute-start | bytes 73736 | tf_op jit(solution)/shard_map/ppermute | solution.py:326
  124.6 3.9 %collective-permute-start.26 = (f32[48,128]{1,0:T(8,128)S(1)}, f32[48,128]{1,0:T(8,128)S(1)}, u32[]{:S(2)}, u32[]{:S(2)}) collective-permute-start(f32[48,128]{1,0:T(8,128)S(1)} %get-tuple-element.47), channel_id=1, source_target_pairs={{0,6},{2,0},{4,2},{6,4},{1,7},{3,1},{5,3},{7,5},{8,14},{10,8},{12,... | collective-permute-start | bytes 73736 | tf_op jit(solution)/shard_map/ppermute | solution.py:326
  127.3 4.2 %collective-permute-start.25 = (f32[48,128]{1,0:T(8,128)S(1)}, f32[48,128]{1,0:T(8,128)S(1)}, u32[]{:S(2)}, u32[]{:S(2)}) collective-permute-start(f32[48,128]{1,0:T(8,128)S(1)} %get-tuple-element.48), channel_id=1, source_target_pairs={{0,4},{2,6},{4,0},{6,2},{1,5},{3,7},{5,1},{7,3},{8,12},{10,14},{12... | collective-permute-start | bytes 73736 | tf_op jit(solution)/shard_map/ppermute | solution.py:326
  127.7 25.7 %collective-permute-start.22 = (f32[3,4,128,128]{3,2,1,0:T(8,128)}, f32[3,4,128,128]{3,2,1,0:T(8,128)S(1)}, u32[]{:S(2)}, u32[]{:S(2)}) collective-permute-start(f32[3,4,128,128]{3,2,1,0:T(8,128)} %get-tuple-element.29), channel_id=1, source_target_pairs={{0,1},{1,0},{2,3},{3,2},{4,5},{5,4},{6,7},{7,6},{8,9},{9,8},{10,11... | collective-permute-start | bytes 2359304 | tf_op jit(solution)/shard_map/ppermute | solution.py:28
  133.9 23.0 %collective-permute-start.35 = (f32[3,4,128,128]{3,2,1,0:T(8,128)S(1)}, f32[3,4,128,128]{3,2,1,0:T(8,128)S(1)}, u32[]{:S(2)}, u32[]{:S(2)}) collective-permute-start(f32[3,4,128,128]{3,2,1,0:T(8,128)S(1)} %add_add_fusion), channel_id=1, source_target_pairs={{254,0},{0,2},{2,4},{4,6},{6,8},{8,10},{10,12},{12,14},{14,16},{16... | collective-permute-start | bytes 2359304 | tf_op jit(solution)/shard_map/ppermute | solution.py:33
  134.0 2.8 %collective-permute-start.29 = (f32[48,128]{1,0:T(8,128)S(1)}, f32[48,128]{1,0:T(8,128)S(1)}, u32[]{:S(2)}, u32[]{:S(2)}) collective-permute-start(f32[48,128]{1,0:T(8,128)S(1)} %fusion.9), channel_id=1, source_target_pairs={{0,24},{8,0},{16,8},{24,16},{1,25},{9,1},{17,9},{25,17},{2,26},{10... | collective-permute-start | bytes 73736 | tf_op jit(solution)/shard_map/ppermute | solution.py:360
  134.1 4.3 %collective-permute-start.28 = (f32[48,128]{1,0:T(8,128)S(1)}, f32[48,128]{1,0:T(8,128)S(1)}, u32[]{:S(2)}, u32[]{:S(2)}) collective-permute-start(f32[48,128]{1,0:T(8,128)S(1)} %fusion.9), channel_id=1, source_target_pairs={{0,16},{8,24},{16,0},{24,8},{1,17},{9,25},{17,1},{25,9},{2,18},{10... | collective-permute-start | bytes 73736 | tf_op jit(solution)/shard_map/ppermute | solution.py:360
  134.2 5.0 %collective-permute-start.27 = (f32[48,128]{1,0:T(8,128)S(1)}, f32[48,128]{1,0:T(8,128)S(1)}, u32[]{:S(2)}, u32[]{:S(2)}) collective-permute-start(f32[48,128]{1,0:T(8,128)S(1)} %fusion.9), channel_id=1, source_target_pairs={{0,8},{8,16},{16,24},{24,0},{1,9},{9,17},{17,25},{25,1},{2,10},{10... | collective-permute-start | bytes 73736 | tf_op jit(solution)/shard_map/ppermute | solution.py:360
  139.1 3.0 %collective-permute-start.32 = (f32[48,128]{1,0:T(8,128)S(1)}, f32[48,128]{1,0:T(8,128)S(1)}, u32[]{:S(2)}, u32[]{:S(2)}) collective-permute-start(f32[48,128]{1,0:T(8,128)S(1)} %add_add_fusion.5), channel_id=1, source_target_pairs={{0,96},{32,0},{64,32},{96,64},{128,224},{160,128},{192,160},{224,1... | collective-permute-start | bytes 73736 | tf_op jit(solution)/shard_map/ppermute | solution.py:360
  139.2 3.7 %collective-permute-start.31 = (f32[48,128]{1,0:T(8,128)S(1)}, f32[48,128]{1,0:T(8,128)S(1)}, u32[]{:S(2)}, u32[]{:S(2)}) collective-permute-start(f32[48,128]{1,0:T(8,128)S(1)} %add_add_fusion.5), channel_id=1, source_target_pairs={{0,64},{32,96},{64,0},{96,32},{128,192},{160,224},{192,128},{224,1... | collective-permute-start | bytes 73736 | tf_op jit(solution)/shard_map/ppermute | solution.py:360
  140.5 4.8 %collective-permute-start.30 = (f32[48,128]{1,0:T(8,128)S(1)}, f32[48,128]{1,0:T(8,128)S(1)}, u32[]{:S(2)}, u32[]{:S(2)}) collective-permute-start(f32[48,128]{1,0:T(8,128)S(1)} %add_add_fusion.5), channel_id=1, source_target_pairs={{0,32},{32,64},{64,96},{96,0},{128,160},{160,192},{192,224},{224,1... | collective-permute-start | bytes 73736 | tf_op jit(solution)/shard_map/ppermute | solution.py:360
  145.3 7.0 %collective-permute-start.33 = (f32[48,128]{1,0:T(8,128)S(1)}, f32[48,128]{1,0:T(8,128)S(1)}, u32[]{:S(2)}, u32[]{:S(2)}) collective-permute-start(f32[48,128]{1,0:T(8,128)S(1)} %add_add_fusion.4), channel_id=1, source_target_pairs={{0,128},{32,160},{64,192},{96,224},{128,0},{160,32},{192,64},{224,... | collective-permute-start | bytes 73736 | tf_op jit(solution)/shard_map/ppermute | solution.py:360
  157.4 23.7 %collective-permute-start.36 = (f32[2,128,512]{1,2,0:T(8,128)S(1)}, f32[2,128,512]{1,2,0:T(8,128)S(1)}, u32[]{:S(2)}, u32[]{:S(2)}) collective-permute-start(f32[2,128,512]{1,2,0:T(8,128)S(1)} %bitcast.52), channel_id=1, source_target_pairs={{0,1},{1,0},{2,3},{3,2},{4,5},{5,4},{6,7},{7,6},{8,9},{9,8},{10,11... | collective-permute-start | bytes 1572872 | tf_op jit(solution)/shard_map/ppermute | solution.py:28
  160.5 17.2 %collective-permute-start.39 = (f32[48,128]{1,0:T(8,128)S(1)}, f32[48,128]{1,0:T(8,128)S(1)}, u32[]{:S(2)}, u32[]{:S(2)}) collective-permute-start(f32[48,128]{1,0:T(8,128)S(1)} %add.228), channel_id=1, source_target_pairs={{2,0},{4,2},{6,4},{0,6},{3,1},{5,3},{7,5},{1,7},{10,8},{12,10},{14... | collective-permute-start | bytes 73736 | tf_op jit(solution)/shard_map/ppermute | solution.py:338
  176.8 4.2 %collective-permute-start.38 = (f32[48,128]{1,0:T(8,128)S(1)}, f32[48,128]{1,0:T(8,128)S(1)}, u32[]{:S(2)}, u32[]{:S(2)}) collective-permute-start(f32[48,128]{1,0:T(8,128)S(1)} %add.228), channel_id=1, source_target_pairs={{4,0},{6,2},{0,4},{2,6},{5,1},{7,3},{1,5},{3,7},{12,8},{14,10},{8,... | collective-permute-start | bytes 73736 | tf_op jit(solution)/shard_map/ppermute | solution.py:338
  176.8 4.2 %collective-permute-start.37 = (f32[48,128]{1,0:T(8,128)S(1)}, f32[48,128]{1,0:T(8,128)S(1)}, u32[]{:S(2)}, u32[]{:S(2)}) collective-permute-start(f32[48,128]{1,0:T(8,128)S(1)} %add.228), channel_id=1, source_target_pairs={{6,0},{0,2},{2,4},{4,6},{7,1},{1,3},{3,5},{5,7},{14,8},{8,10},{10,... | collective-permute-start | bytes 73736 | tf_op jit(solution)/shard_map/ppermute | solution.py:338
  182.3 3.0 %collective-permute-start.40 = (f32[192,128]{1,0:T(8,128)S(1)}, f32[192,128]{1,0:T(8,128)S(1)}, u32[]{:S(2)}, u32[]{:S(2)}) collective-permute-start(f32[192,128]{1,0:T(8,128)S(1)} %maximum_add_fusion), channel_id=1, source_target_pairs={{0,1},{1,0},{2,3},{3,2},{4,5},{5,4},{6,7},{7,6},{8,9},{9,8},{10,11... | collective-permute-start | bytes 294920 | tf_op jit(solution)/shard_map/ppermute | solution.py:28
  183.9 1.4 copy-start.3

commit v5 on v4

--- a/solution.py
+++ b/solution.py
@@ -394,7 +394,7 @@
     up = after(up + swapped(give_up), part)
     above = from_tile(low, -1)
     below = from_tile(up, 1)
-    part = summed_over(summed_over(part, TILE[1]), TILE[0])
+    part = summed_over(summed_over(part, TILE[0]), TILE[1])
     up, low, above, below = lax.optimization_barrier((up, low, above, below))
     own_half = updated(up + above, in_blocks(own_half))
     mine = jnp.concatenate([own_half, updated(low + below, in_blocks(halo))], axis=2)
@@ -407,7 +407,7 @@
     low = after(low + swapped(give_low), part)
     up = up + swapped(give_up)
     above = from_tile(low, -1)
-    part = summed_over(summed_over(part, TILE[1]), TILE[0])
+    part = summed_over(summed_over(part, TILE[0]), TILE[1])
     up = after(up, part)
     mine = updated(up + above, own_half).transpose(0, 2, 1, 3).reshape(2, STRIP, COLS // 2)
     other = swapped(mine)

time: 187 us -> 181 us (0.968)
  waiting for transfers between devices: 62.2 us -> 50.8 us
  Pallas kernels: 19.5 us -> 24.4 us
    ppermute x14, starting transfers between devices: 13.1 us -> 24 us  [shifts_among(): total = total + lax.ppermute(value, axis, route)]
    ppermute x6, starting transfers between devices: 24.9 us -> 15 us  [gathered_over(): lax.ppermute(piece, axis, [((i + step) % count, i) for i in range(count)])]
    ppermute x14, waiting for transfers between devices: 31.5 us -> 23.4 us  [shifts_among(): total = total + lax.ppermute(value, axis, route)]
    pallas_call x2, Pallas kernels: 19.5 us -> 24.4 us  [run_positions(): pl.pallas_call(kernel, out_shape=(quarter,) * 4 + (pieces_of,) * 2, in_sp...]
    ppermute x4, waiting for transfers between devices: 14.1 us -> 10.6 us  [from_tile(): lax.ppermute(value, TILE, [((i + distance) % count, i) for i in range(cou...]
    ppermute x4, starting transfers between devices: 12.8 us -> 15.3 us  [from_tile(): lax.ppermute(value, TILE, [((i + distance) % count, i) for i in range(cou...]
    ppermute x11, starting transfers between devices: 25.8 us -> 23.5 us  [swapped(): return lax.ppermute(value, 'pos', [(0, 1), (1, 0)])]
  transfers between devices with their start and end apart: 41 -> 41, of which waited for: 24 -> 21; matrix products, arithmetic and copies ran while one was open for 7% -> 7% of each run, Pallas kernels for 0% -> 0%
where the time goes in v5:
time: 181 us; the launch traced here: 180 us
  starting transfers between devices  83.3 us (46%)
  waiting for transfers between devices  50.8 us (28%)
  Pallas kernels  24.4 us (13%)
  other arithmetic  9.02 us (5%)
  local copies, waits for them, and re-layouts  8.31 us (5%)
  between operations  4.34 us (2%)
    pallas_call x2, Pallas kernels, run_positions(): pl.pallas_call(kernel, out_shape=(quarter,) * 4 + (pieces_of,) * 2, in_sp...  24.4 us
    ppermute x14, starting transfers between devices, shifts_among(): total = total + lax.ppermute(value, axis, route)  24 us
    ppermute x11, starting transfers between devices, swapped(): return lax.ppermute(value, 'pos', [(0, 1), (1, 0)])  23.5 us
    ppermute x14, waiting for transfers between devices, shifts_among(): total = total + lax.ppermute(value, axis, route)  23.4 us
    ppermute x4, starting transfers between devices, from_tile(): lax.ppermute(value, TILE, [((i + distance) % count, i) for i in range(cou...  15.3 us
    ppermute x6, starting transfers between devices, gathered_over(): lax.ppermute(piece, axis, [((i + step) % count, i) for i in range(count)])  15 us
    ppermute x4, waiting for transfers between devices, from_tile(): lax.ppermute(value, TILE, [((i + distance) % count, i) for i in range(cou...  10.6 us
    ppermute x6, waiting for transfers between devices, scattered_over(): arrived.append(lax.ppermute(pieces[step], axis, route))  7.42 us
  transfers between devices with their start and end apart: 41, of which 21 were waited for; matrix products, arithmetic and copies ran while one was open for 7% of the time, Pallas kernels for 0%

profile of v5, /device:TPU:1, one launch (start us, length us, event | category | flops | bytes accessed | tf_op | source)
XLA Modules:
  0.0 180.3 jit_solution(8806999849881683085)
XLA Ops:
  0.6 1.1 constant_dynamic-slice_fusion
  1.7 11.1 %collective-permute-start = (f32[2,128,512]{2,1,0:T(8,128)S(1)}, f32[2,128,512]{2,1,0:T(8,128)S(1)}, u32[]{:S(2)}, u32[]{:S(2)}) collective-permute-start(f32[2,128,512]{2,1,0:T(8,128)S(1)} %constant_dynamic-slice_fusion), channel_id=1, source_target_pairs={{2,0},{4,2},{6,4},{8,6},{10,8},{12,10},{14,12},{16,14},{18,16},{20... | collective-permute-start | bytes 1572872 | tf_op jit(solution)/shard_map/ppermute | solution.py:33
  12.8 10.6 %collective-permute-done.refs_7_ = f32[2,128,512]{2,1,0:T(8,128)S(1)} collective-permute-done((f32[2,128,512]{2,1,0:T(8,128)S(1)}, f32[2,128,512]{2,1,0:T(8,128)S(1)}, u32[]{:S(2)}, u32[]{:S(2)}) %collective-permute-start) | collective-permute-done | bytes 524320 | tf_op jit(solution)/shard_map/ppermute | solution.py:33
  23.4 1.5 collective-permute-start.1
  25.6 0.9 collective-permute-done.1.refs_8_
  26.5 0.8 copy-done.7
  27.3 12.2 %positions.2 = (f32[3,4,128,128]{3,2,1,0:T(8,128)}, f32[3,4,128,128]{3,2,1,0:T(8,128)}, f32[3,4,128,128]{3,2,1,0:T(8,128)}, f32[3,4,128,128]{3,2,1,0:T(8,128)}, ...) custom-call(s32[1,1,32]{2,1,0:T(1,128)} %refs_0_.3, s32[1,1,32]{2,1,0:T(1,128)} %refs_1_.3, s32[1,1]{1,0:T(1,128)S(6)} %copy.15.refs_2_, ...), custom_call_target="tpu_custom_call" | custom-call | flops 12999999488 | bytes 8388608 | tf_op jit(solution)/shard_map/positions/pallas_call | solution.py:275
  39.6 2.9 %collective-permute-start.17 = (f32[3,4,128,128]{3,2,1,0:T(8,128)}, f32[3,4,128,128]{3,2,1,0:T(8,128)S(1)}, u32[]{:S(2)}, u32[]{:S(2)}) collective-permute-start(f32[3,4,128,128]{3,2,1,0:T(8,128)} %get-tuple-element.21), channel_id=1, source_target_pairs={{0,1},{1,0},{2,3},{3,2},{4,5},{5,4},{6,7},{7,6},{8,9},{9,8},{10,11... | collective-permute-start | bytes 2359304 | tf_op jit(solution)/shard_map/ppermute | solution.py:28
  42.6 0.4 collective-permute-start.18
  43.0 1.8 collective-permute-done.2
  44.7 0.9 add.190
  45.7 2.7 %collective-permute-start.5 = (f32[48,128]{1,0:T(8,128)S(1)}, f32[48,128]{1,0:T(8,128)S(1)}, u32[]{:S(2)}, u32[]{:S(2)}) collective-permute-start(f32[48,128]{1,0:T(8,128)S(1)} %get-tuple-element.54), channel_id=1, source_target_pairs={{0,6},{2,0},{4,2},{6,4},{1,7},{3,1},{5,3},{7,5},{8,14},{10,8},{12,... | collective-permute-start | bytes 73736 | tf_op jit(solution)/shard_map/ppermute | solution.py:326
  48.4 1.2 collective-permute-done.3
  49.6 3.0 %collective-permute-done.4 = f32[48,128]{1,0:T(8,128)S(1)} collective-permute-done((f32[48,128]{1,0:T(8,128)S(1)}, f32[48,128]{1,0:T(8,128)S(1)}, u32[]{:S(2)}, u32[]{:S(2)}) %collective-permute-start.4) | collective-permute-done | bytes 24608 | tf_op jit(solution)/shard_map/ppermute | solution.py:326
  52.6 0.5 slice.106
  53.8 1.2 add_add_fusion.3
  55.0 4.0 %collective-permute-start.20 = (f32[3,4,128,128]{3,2,1,0:T(8,128)S(1)}, f32[3,4,128,128]{3,2,1,0:T(8,128)}, u32[]{:S(2)}, u32[]{:S(2)}) collective-permute-start(f32[3,4,128,128]{3,2,1,0:T(8,128)S(1)} %add_add_fusion.3), channel_id=1, source_target_pairs={{2,0},{4,2},{6,4},{8,6},{10,8},{12,10},{14,12},{16,14},{18,16},{20... | collective-permute-start | bytes 2359304 | tf_op jit(solution)/shard_map/ppermute | solution.py:33
  59.4 1.4 collective-permute-start.6
  60.8 9.4 %collective-permute-done.8 = f32[48,128]{1,0:T(8,128)S(1)} collective-permute-done((f32[48,128]{1,0:T(8,128)S(1)}, f32[48,128]{1,0:T(8,128)S(1)}, u32[]{:S(2)}, u32[]{:S(2)}) %collective-permute-start.8) | collective-permute-done | bytes 24608 | tf_op jit(solution)/shard_map/ppermute | solution.py:360
  70.2 1.0 collective-permute-done.6
  71.2 7.9 %collective-permute-start.9 = (f32[48,128]{1,0:T(8,128)S(1)}, f32[48,128]{1,0:T(8,128)S(1)}, u32[]{:S(2)}, u32[]{:S(2)}) collective-permute-start(f32[48,128]{1,0:T(8,128)S(1)} %add_add_fusion.7), channel_id=1, source_target_pairs={{0,128},{32,160},{64,192},{96,224},{128,0},{160,32},{192,64},{224,... | collective-permute-start | bytes 73736 | tf_op jit(solution)/shard_map/ppermute | solution.py:360
  79.1 1.6 collective-permute-done.9
  80.8 1.4 collective-permute-start.10
  82.6 1.2 copy.11
  84.0 0.9 collective-permute-done.11
  85.0 0.8 collective-permute-done.10
  85.8 2.3 %collective-permute-start.15 = (f32[48,128]{1,0:T(8,128)S(1)}, f32[48,128]{1,0:T(8,128)S(1)}, u32[]{:S(2)}, u32[]{:S(2)}) collective-permute-start(f32[48,128]{1,0:T(8,128)S(1)} %add_add_fusion.6), channel_id=1, source_target_pairs={{2,0},{4,2},{6,4},{0,6},{3,1},{5,3},{7,5},{1,7},{10,8},{12,10},{14... | collective-permute-start | bytes 73736 | tf_op jit(solution)/shard_map/ppermute | solution.py:338
  88.0 0.7 collective-permute-start.13
  88.7 1.2 add.211
  90.0 1.2 add.214
  91.5 5.9 %collective-permute-start.21 = (f32[2,4,256,128]{3,2,1,0:T(8,128)S(1)}, f32[2,4,256,128]{3,2,1,0:T(8,128)S(1)}, u32[]{:S(2)}, u32[]{:S(2)}) collective-permute-start(f32[2,4,256,128]{3,2,1,0:T(8,128)S(1)} %pad_maximum_fusion.refs_6_), channel_id=1, source_target_pairs={{0,1},{1,0},{2,3},{3,2},{4,5},{5,4},{6,7},{7,6},{8,9},{9,8},{10,11... | collective-permute-start | bytes 3145736 | tf_op jit(solution)/shard_map/ppermute | solution.py:28
  97.5 1.5 collective-permute-start.16
  99.1 0.9 collective-permute-done.16
  100.1 0.7 add_divide_fusion.1.refs_3_
  100.8 1.0 copy-done.6
  101.8 12.2 %positions.3 = (f32[3,4,128,128]{3,2,1,0:T(8,128)}, f32[3,4,128,128]{3,2,1,0:T(8,128)}, f32[3,4,128,128]{3,2,1,0:T(8,128)}, f32[3,4,128,128]{3,2,1,0:T(8,128)}, ...) custom-call(s32[1,1,32]{2,1,0:T(1,128)} %refs_0_.3, s32[1,1,32]{2,1,0:T(1,128)} %refs_1_.3, s32[1,1]{1,0:T(1,128)S(6)} %copy.15.refs_2_, ...), custom_call_target="tpu_custom_call" | custom-call | flops 12999999488 | bytes 8388608 | tf_op jit(solution)/shard_map/positions/pallas_call | solution.py:275
  114.0 2.9 %collective-permute-start.34 = (f32[3,4,128,128]{3,2,1,0:T(8,128)}, f32[3,4,128,128]{3,2,1,0:T(8,128)S(1)}, u32[]{:S(2)}, u32[]{:S(2)}) collective-permute-start(f32[3,4,128,128]{3,2,1,0:T(8,128)} %get-tuple-element.33), channel_id=1, source_target_pairs={{0,1},{1,0},{2,3},{3,2},{4,5},{5,4},{6,7},{7,6},{8,9},{9,8},{10,11... | collective-permute-start | bytes 2359304 | tf_op jit(solution)/shard_map/ppermute | solution.py:28
  117.0 2.2 %collective-permute-done.23 = f32[4,48,128]{2,1,0:T(8,128)S(1)} collective-permute-done((f32[4,48,128]{2,1,0:T(8,128)}, f32[4,48,128]{2,1,0:T(8,128)S(1)}, u32[]{:S(2)}, u32[]{:S(2)}) %collective-permute-start.23) | collective-permute-done | bytes 98336 | tf_op jit(solution)/shard_map/ppermute | solution.py:28
  119.2 0.9 add.218
  120.2 2.7 %collective-permute-start.26 = (f32[48,128]{1,0:T(8,128)S(1)}, f32[48,128]{1,0:T(8,128)S(1)}, u32[]{:S(2)}, u32[]{:S(2)}) collective-permute-start(f32[48,128]{1,0:T(8,128)S(1)} %get-tuple-element.47), channel_id=1, source_target_pairs={{0,6},{2,0},{4,2},{6,4},{1,7},{3,1},{5,3},{7,5},{8,14},{10,8},{12,... | collective-permute-start | bytes 73736 | tf_op jit(solution)/shard_map/ppermute | solution.py:326
  122.8 0.9 collective-permute-start.22
  124.0 3.0 %collective-permute-done.25 = f32[48,128]{1,0:T(8,128)S(1)} collective-permute-done((f32[48,128]{1,0:T(8,128)S(1)}, f32[48,128]{1,0:T(8,128)S(1)}, u32[]{:S(2)}, u32[]{:S(2)}) %collective-permute-start.25) | collective-permute-done | bytes 24608 | tf_op jit(solution)/shard_map/ppermute | solution.py:326
  127.0 0.5 slice.116
  128.2 1.2 add_add_fusion
  129.5 3.3 %collective-permute-start.29 = (f32[48,128]{1,0:T(8,128)S(1)}, f32[48,128]{1,0:T(8,128)S(1)}, u32[]{:S(2)}, u32[]{:S(2)}) collective-permute-start(f32[48,128]{1,0:T(8,128)S(1)} %fusion.9), channel_id=1, source_target_pairs={{0,96},{32,0},{64,32},{96,64},{128,224},{160,128},{192,160},{224,1... | collective-permute-start | bytes 73736 | tf_op jit(solution)/shard_map/ppermute | solution.py:360
  132.9 1.0 collective-permute-start.28
  133.9 2.6 %collective-permute-done.28 = f32[48,128]{1,0:T(8,128)S(1)} collective-permute-done((f32[48,128]{1,0:T(8,128)S(1)}, f32[48,128]{1,0:T(8,128)S(1)}, u32[]{:S(2)}, u32[]{:S(2)}) %collective-permute-start.28) | collective-permute-done | bytes 24608 | tf_op jit(solution)/shard_map/ppermute | solution.py:360
  136.5 1.9 %collective-permute-done.27 = f32[48,128]{1,0:T(8,128)S(1)} collective-permute-done((f32[48,128]{1,0:T(8,128)S(1)}, f32[48,128]{1,0:T(8,128)S(1)}, u32[]{:S(2)}, u32[]{:S(2)}) %collective-permute-start.27) | collective-permute-done | bytes 24608 | tf_op jit(solution)/shard_map/ppermute | solution.py:360
  138.4 5.1 %collective-permute-start.30 = (f32[48,128]{1,0:T(8,128)S(1)}, f32[48,128]{1,0:T(8,128)S(1)}, u32[]{:S(2)}, u32[]{:S(2)}) collective-permute-start(f32[48,128]{1,0:T(8,128)S(1)} %add_add_fusion.5), channel_id=1, source_target_pairs={{0,128},{32,160},{64,192},{96,224},{128,0},{160,32},{192,64},{224,... | collective-permute-start | bytes 73736 | tf_op jit(solution)/shard_map/ppermute | solution.py:360
  143.5 1.8 %collective-permute-done.30 = f32[48,128]{1,0:T(8,128)S(1)} collective-permute-done((f32[48,128]{1,0:T(8,128)S(1)}, f32[48,128]{1,0:T(8,128)S(1)}, u32[]{:S(2)}, u32[]{:S(2)}) %collective-permute-start.30) | collective-permute-done | bytes 24608 | tf_op jit(solution)/shard_map/ppermute | solution.py:360
  145.3 2.8 %collective-permute-start.32 = (f32[48,128]{1,0:T(8,128)S(1)}, f32[48,128]{1,0:T(8,128)S(1)}, u32[]{:S(2)}, u32[]{:S(2)}) collective-permute-start(f32[48,128]{1,0:T(8,128)S(1)} %add.225), channel_id=1, source_target_pairs={{0,16},{8,24},{16,0},{24,8},{1,17},{9,25},{17,1},{25,9},{2,18},{10... | collective-permute-start | bytes 73736 | tf_op jit(solution)/shard_map/ppermute | solution.py:360
  148.2 0.8 collective-permute-start.31
  149.0 1.0 collective-permute-done.32
  149.9 2.5 %collective-permute-done.31 = f32[48,128]{1,0:T(8,128)S(1)} collective-permute-done((f32[48,128]{1,0:T(8,128)S(1)}, f32[48,128]{1,0:T(8,128)S(1)}, u32[]{:S(2)}, u32[]{:S(2)}) %collective-permute-start.31) | collective-permute-done | bytes 24608 | tf_op jit(solution)/shard_map/ppermute | solution.py:360
  152.4 0.5 slice.115
  154.0 5.6 %collective-permute-start.36 = (f32[2,128,512]{1,2,0:T(8,128)S(1)}, f32[2,128,512]{1,2,0:T(8,128)S(1)}, u32[]{:S(2)}, u32[]{:S(2)}) collective-permute-start(f32[2,128,512]{1,2,0:T(8,128)S(1)} %bitcast.52), channel_id=1, source_target_pairs={{0,1},{1,0},{2,3},{3,2},{4,5},{5,4},{6,7},{7,6},{8,9},{9,8},{10,11... | collective-permute-start | bytes 1572872 | tf_op jit(solution)/shard_map/ppermute | solution.py:28
  159.6 11.5 %collective-permute-start.39 = (f32[48,128]{1,0:T(8,128)S(1)}, f32[48,128]{1,0:T(8,128)S(1)}, u32[]{:S(2)}, u32[]{:S(2)}) collective-permute-start(f32[48,128]{1,0:T(8,128)S(1)} %add_add_fusion.4), channel_id=1, source_target_pairs={{2,0},{4,2},{6,4},{0,6},{3,1},{5,3},{7,5},{1,7},{10,8},{12,10},{14... | collective-permute-start | bytes 73736 | tf_op jit(solution)/shard_map/ppermute | solution.py:338
  171.1 0.6 collective-permute-start.37
  171.6 0.4 collective-permute-done.39
  172.0 3.2 %collective-permute-done.38 = f32[48,128]{1,0:T(8,128)S(1)} collective-permute-done((f32[48,128]{1,0:T(8,128)S(1)}, f32[48,128]{1,0:T(8,128)S(1)}, u32[]{:S(2)}, u32[]{:S(2)}) %collective-permute-start.38) | collective-permute-done | bytes 24608 | tf_op jit(solution)/shard_map/ppermute | solution.py:338
  175.4 0.5 slice.119
  176.6 1.6 collective-permute-start.40
  178.2 1.3 copy.14
  179.6 0.7 add_divide_fusion
  (85 shorter events, 3.0 us)
Async XLA Ops:
  1.7 21.7 %collective-permute-start = (f32[2,128,512]{2,1,0:T(8,128)S(1)}, f32[2,128,512]{2,1,0:T(8,128)S(1)}, u32[]{:S(2)}, u32[]{:S(2)}) collective-permute-start(f32[2,128,512]{2,1,0:T(8,128)S(1)} %constant_dynamic-slice_fusion), channel_id=1, source_target_pairs={{2,0},{4,2},{6,4},{8,6},{10,8},{12,10},{14,12},{16,14},{18,16},{20... | collective-permute-start | bytes 1572872 | tf_op jit(solution)/shard_map/ppermute | solution.py:33
  23.4 3.1 %copy-start.4 = (f32[2,128,512]{2,1,0:T(8,128)}, f32[2,128,512]{2,1,0:T(8,128)S(1)}, u32[]{:S(2)}) copy-start(f32[2,128,512]{2,1,0:T(8,128)S(1)} %collective-permute-done.refs_7_) | copy-start | bytes 1572868
  23.4 3.1 %collective-permute-start.1 = (f32[2,128,512]{2,1,0:T(8,128)S(1)}, f32[2,128,512]{2,1,0:T(8,128)S(1)}, u32[]{:S(2)}, u32[]{:S(2)}) collective-permute-start(f32[2,128,512]{2,1,0:T(8,128)S(1)} %collective-permute-done.refs_7_), channel_id=1, source_target_pairs={{0,1},{1,0},{2,3},{3,2},{4,5},{5,4},{6,7},{7,6},{8,9},{9,8},{10,11... | collective-permute-start | bytes 1572872 | tf_op jit(solution)/shard_map/ppermute | solution.py:28
  26.5 0.8 copy-start.7
  39.5 19.5 %copy-start.1 = (f32[3,4,128,128]{3,2,1,0:T(8,128)S(1)}, f32[3,4,128,128]{3,2,1,0:T(8,128)}, u32[]{:S(2)}) copy-start(f32[3,4,128,128]{3,2,1,0:T(8,128)} %get-tuple-element.22) | copy-start | bytes 2359300
  39.6 14.2 %collective-permute-start.17 = (f32[3,4,128,128]{3,2,1,0:T(8,128)}, f32[3,4,128,128]{3,2,1,0:T(8,128)S(1)}, u32[]{:S(2)}, u32[]{:S(2)}) collective-permute-start(f32[3,4,128,128]{3,2,1,0:T(8,128)} %get-tuple-element.21), channel_id=1, source_target_pairs={{0,1},{1,0},{2,3},{3,2},{4,5},{5,4},{6,7},{7,6},{8,9},{9,8},{10,11... | collective-permute-start | bytes 2359304 | tf_op jit(solution)/shard_map/ppermute | solution.py:28
  42.5 2.3 %collective-permute-start.2 = (f32[4,48,128]{2,1,0:T(8,128)}, f32[4,48,128]{2,1,0:T(8,128)S(1)}, u32[]{:S(2)}, u32[]{:S(2)}) collective-permute-start(f32[4,48,128]{2,1,0:T(8,128)} %get-tuple-element.19), channel_id=1, source_target_pairs={{0,1},{1,0},{2,3},{3,2},{4,5},{5,4},{6,7},{7,6},{8,9},{9,8},{10,11... | collective-permute-start | bytes 294920 | tf_op jit(solution)/shard_map/ppermute | solution.py:28
  42.6 16.5 %collective-permute-start.18 = (f32[3,4,128,128]{3,2,1,0:T(8,128)}, f32[3,4,128,128]{3,2,1,0:T(8,128)S(1)}, u32[]{:S(2)}, u32[]{:S(2)}) collective-permute-start(f32[3,4,128,128]{3,2,1,0:T(8,128)} %get-tuple-element.23), channel_id=1, source_target_pairs={{0,1},{1,0},{2,3},{3,2},{4,5},{5,4},{6,7},{7,6},{8,9},{9,8},{10,11... | collective-permute-start | bytes 2359304 | tf_op jit(solution)/shard_map/ppermute | solution.py:28
  45.6 4.0 %collective-permute-start.3 = (f32[48,128]{1,0:T(8,128)S(1)}, f32[48,128]{1,0:T(8,128)S(1)}, u32[]{:S(2)}, u32[]{:S(2)}) collective-permute-start(f32[48,128]{1,0:T(8,128)S(1)} %get-tuple-element.53), channel_id=1, source_target_pairs={{0,2},{2,4},{4,6},{6,0},{1,3},{3,5},{5,7},{7,1},{8,10},{10,12},{12... | collective-permute-start | bytes 73736 | tf_op jit(solution)/shard_map/ppermute | solution.py:326
  45.7 3.9 %collective-permute-start.5 = (f32[48,128]{1,0:T(8,128)S(1)}, f32[48,128]{1,0:T(8,128)S(1)}, u32[]{:S(2)}, u32[]{:S(2)}) collective-permute-start(f32[48,128]{1,0:T(8,128)S(1)} %get-tuple-element.54), channel_id=1, source_target_pairs={{0,6},{2,0},{4,2},{6,4},{1,7},{3,1},{5,3},{7,5},{8,14},{10,8},{12,... | collective-permute-start | bytes 73736 | tf_op jit(solution)/shard_map/ppermute | solution.py:326
  48.4 4.2 %collective-permute-start.4 = (f32[48,128]{1,0:T(8,128)S(1)}, f32[48,128]{1,0:T(8,128)S(1)}, u32[]{:S(2)}, u32[]{:S(2)}) collective-permute-start(f32[48,128]{1,0:T(8,128)S(1)} %get-tuple-element.55), channel_id=1, source_target_pairs={{0,4},{2,6},{4,0},{6,2},{1,5},{3,7},{5,1},{7,3},{8,12},{10,14},{12... | collective-permute-start | bytes 73736 | tf_op jit(solution)/shard_map/ppermute | solution.py:326
  55.0 33.7 %collective-permute-start.20 = (f32[3,4,128,128]{3,2,1,0:T(8,128)S(1)}, f32[3,4,128,128]{3,2,1,0:T(8,128)}, u32[]{:S(2)}, u32[]{:S(2)}) collective-permute-start(f32[3,4,128,128]{3,2,1,0:T(8,128)S(1)} %add_add_fusion.3), channel_id=1, source_target_pairs={{2,0},{4,2},{6,4},{8,6},{10,8},{12,10},{14,12},{16,14},{18,16},{20... | collective-permute-start | bytes 2359304 | tf_op jit(solution)/shard_map/ppermute | solution.py:33
  59.1 29.6 %collective-permute-start.19 = (f32[3,4,128,128]{3,2,1,0:T(8,128)S(1)}, f32[3,4,128,128]{3,2,1,0:T(8,128)}, u32[]{:S(2)}, u32[]{:S(2)}) collective-permute-start(f32[3,4,128,128]{3,2,1,0:T(8,128)S(1)} %add_add_fusion.2), channel_id=1, source_target_pairs={{254,0},{0,2},{2,4},{4,6},{6,8},{8,10},{10,12},{12,14},{14,16},{16... | collective-permute-start | bytes 2359304 | tf_op jit(solution)/shard_map/ppermute | solution.py:33
  59.2 10.9 %collective-permute-start.8 = (f32[48,128]{1,0:T(8,128)S(1)}, f32[48,128]{1,0:T(8,128)S(1)}, u32[]{:S(2)}, u32[]{:S(2)}) collective-permute-start(f32[48,128]{1,0:T(8,128)S(1)} %fusion.12), channel_id=1, source_target_pairs={{0,96},{32,0},{64,32},{96,64},{128,224},{160,128},{192,160},{224,1... | collective-permute-start | bytes 73736 | tf_op jit(solution)/shard_map/ppermute | solution.py:360
  59.3 10.8 %collective-permute-start.7 = (f32[48,128]{1,0:T(8,128)S(1)}, f32[48,128]{1,0:T(8,128)S(1)}, u32[]{:S(2)}, u32[]{:S(2)}) collective-permute-start(f32[48,128]{1,0:T(8,128)S(1)} %fusion.12), channel_id=1, source_target_pairs={{0,64},{32,96},{64,0},{96,32},{128,192},{160,224},{192,128},{224,1... | collective-permute-start | bytes 73736 | tf_op jit(solution)/shard_map/ppermute | solution.py:360
  59.4 11.7 %collective-permute-start.6 = (f32[48,128]{1,0:T(8,128)S(1)}, f32[48,128]{1,0:T(8,128)S(1)}, u32[]{:S(2)}, u32[]{:S(2)}) collective-permute-start(f32[48,128]{1,0:T(8,128)S(1)} %fusion.12), channel_id=1, source_target_pairs={{0,32},{32,64},{64,96},{96,0},{128,160},{160,192},{192,224},{224,1... | collective-permute-start | bytes 73736 | tf_op jit(solution)/shard_map/ppermute | solution.py:360
  71.2 9.5 %collective-permute-start.9 = (f32[48,128]{1,0:T(8,128)S(1)}, f32[48,128]{1,0:T(8,128)S(1)}, u32[]{:S(2)}, u32[]{:S(2)}) collective-permute-start(f32[48,128]{1,0:T(8,128)S(1)} %add_add_fusion.7), channel_id=1, source_target_pairs={{0,128},{32,160},{64,192},{96,224},{128,0},{160,32},{192,64},{224,... | collective-permute-start | bytes 73736 | tf_op jit(solution)/shard_map/ppermute | solution.py:360
  80.7 3.3 %collective-permute-start.12 = (f32[48,128]{1,0:T(8,128)S(1)}, f32[48,128]{1,0:T(8,128)S(1)}, u32[]{:S(2)}, u32[]{:S(2)}) collective-permute-start(f32[48,128]{1,0:T(8,128)S(1)} %add.197), channel_id=1, source_target_pairs={{0,24},{8,0},{16,8},{24,16},{1,25},{9,1},{17,9},{25,17},{2,26},{10... | collective-permute-start | bytes 73736 | tf_op jit(solution)/shard_map/ppermute | solution.py:360
  80.7 4.3 %collective-permute-start.11 = (f32[48,128]{1,0:T(8,128)S(1)}, f32[48,128]{1,0:T(8,128)S(1)}, u32[]{:S(2)}, u32[]{:S(2)}) collective-permute-start(f32[48,128]{1,0:T(8,128)S(1)} %add.197), channel_id=1, source_target_pairs={{0,16},{8,24},{16,0},{24,8},{1,17},{9,25},{17,1},{25,9},{2,18},{10... | collective-permute-start | bytes 73736 | tf_op jit(solution)/shard_map/ppermute | solution.py:360
  80.8 5.0 %collective-permute-start.10 = (f32[48,128]{1,0:T(8,128)S(1)}, f32[48,128]{1,0:T(8,128)S(1)}, u32[]{:S(2)}, u32[]{:S(2)}) collective-permute-start(f32[48,128]{1,0:T(8,128)S(1)} %add.197), channel_id=1, source_target_pairs={{0,8},{8,16},{16,24},{24,0},{1,9},{9,17},{17,25},{25,1},{2,10},{10... | collective-permute-start | bytes 73736 | tf_op jit(solution)/shard_map/ppermute | solution.py:360
  85.8 11.7 %collective-permute-start.15 = (f32[48,128]{1,0:T(8,128)S(1)}, f32[48,128]{1,0:T(8,128)S(1)}, u32[]{:S(2)}, u32[]{:S(2)}) collective-permute-start(f32[48,128]{1,0:T(8,128)S(1)} %add_add_fusion.6), channel_id=1, source_target_pairs={{2,0},{4,2},{6,4},{0,6},{3,1},{5,3},{7,5},{1,7},{10,8},{12,10},{14... | collective-permute-start | bytes 73736 | tf_op jit(solution)/shard_map/ppermute | solution.py:338
  88.0 9.4 %collective-permute-start.14 = (f32[48,128]{1,0:T(8,128)S(1)}, f32[48,128]{1,0:T(8,128)S(1)}, u32[]{:S(2)}, u32[]{:S(2)}) collective-permute-start(f32[48,128]{1,0:T(8,128)S(1)} %add_add_fusion.6), channel_id=1, source_target_pairs={{4,0},{6,2},{0,4},{2,6},{5,1},{7,3},{1,5},{3,7},{12,8},{14,10},{8,... | collective-permute-start | bytes 73736 | tf_op jit(solution)/shard_map/ppermute | solution.py:338
  88.0 9.4 %collective-permute-start.13 = (f32[48,128]{1,0:T(8,128)S(1)}, f32[48,128]{1,0:T(8,128)S(1)}, u32[]{:S(2)}, u32[]{:S(2)}) collective-permute-start(f32[48,128]{1,0:T(8,128)S(1)} %add_add_fusion.6), channel_id=1, source_target_pairs={{6,0},{0,2},{2,4},{4,6},{7,1},{1,3},{3,5},{5,7},{14,8},{8,10},{10,... | collective-permute-start | bytes 73736 | tf_op jit(solution)/shard_map/ppermute | solution.py:338
  91.4 8.6 %copy-start.5 = (f32[2,128,128]{2,1,0:T(8,128)S(1)}, f32[2,128,128]{2,1,0:T(8,128)}, u32[]{:S(2)}) copy-start(f32[2,128,128]{2,1,0:T(8,128)} %refs_3_.1) | copy-start | bytes 393220
  91.5 9.2 %copy-start = (f32[2,4,256,128]{3,2,1,0:T(8,128)}, f32[2,4,256,128]{3,2,1,0:T(8,128)S(1)}, u32[]{:S(2)}) copy-start(f32[2,4,256,128]{3,2,1,0:T(8,128)S(1)} %pad_maximum_fusion.refs_6_) | copy-start | bytes 3145732
  91.5 9.2 %collective-permute-start.21 = (f32[2,4,256,128]{3,2,1,0:T(8,128)S(1)}, f32[2,4,256,128]{3,2,1,0:T(8,128)S(1)}, u32[]{:S(2)}, u32[]{:S(2)}) collective-permute-start(f32[2,4,256,128]{3,2,1,0:T(8,128)S(1)} %pad_maximum_fusion.refs_6_), channel_id=1, source_target_pairs={{0,1},{1,0},{2,3},{3,2},{4,5},{5,4},{6,7},{7,6},{8,9},{9,8},{10,11... | collective-permute-start | bytes 3145736 | tf_op jit(solution)/shard_map/ppermute | solution.py:28
  97.5 2.5 %collective-permute-start.16 = (f32[192,128]{1,0:T(8,128)S(1)}, f32[192,128]{1,0:T(8,128)S(1)}, u32[]{:S(2)}, u32[]{:S(2)}) collective-permute-start(f32[192,128]{1,0:T(8,128)S(1)} %pad_maximum_fusion.4), channel_id=1, source_target_pairs={{0,1},{1,0},{2,3},{3,2},{4,5},{5,4},{6,7},{7,6},{8,9},{9,8},{10,11... | collective-permute-start | bytes 294920 | tf_op jit(solution)/shard_map/ppermute | solution.py:28
  100.8 1.0 copy-start.6
  114.0 39.6 %copy-start.2 = (f32[3,4,128,128]{3,2,1,0:T(8,128)S(1)}, f32[3,4,128,128]{3,2,1,0:T(8,128)}, u32[]{:S(2)}) copy-start(f32[3,4,128,128]{3,2,1,0:T(8,128)} %get-tuple-element.28) | copy-start | bytes 2359300
  114.0 14.2 %collective-permute-start.34 = (f32[3,4,128,128]{3,2,1,0:T(8,128)}, f32[3,4,128,128]{3,2,1,0:T(8,128)S(1)}, u32[]{:S(2)}, u32[]{:S(2)}) collective-permute-start(f32[3,4,128,128]{3,2,1,0:T(8,128)} %get-tuple-element.33), channel_id=1, source_target_pairs={{0,1},{1,0},{2,3},{3,2},{4,5},{5,4},{6,7},{7,6},{8,9},{9,8},{10,11... | collective-permute-start | bytes 2359304 | tf_op jit(solution)/shard_map/ppermute | solution.py:28
  116.9 2.3 %collective-permute-start.23 = (f32[4,48,128]{2,1,0:T(8,128)}, f32[4,48,128]{2,1,0:T(8,128)S(1)}, u32[]{:S(2)}, u32[]{:S(2)}) collective-permute-start(f32[4,48,128]{2,1,0:T(8,128)} %get-tuple-element.31), channel_id=1, source_target_pairs={{0,1},{1,0},{2,3},{3,2},{4,5},{5,4},{6,7},{7,6},{8,9},{9,8},{10,11... | collective-permute-start | bytes 294920 | tf_op jit(solution)/shard_map/ppermute | solution.py:28
  120.1 4.0 %collective-permute-start.24 = (f32[48,128]{1,0:T(8,128)S(1)}, f32[48,128]{1,0:T(8,128)S(1)}, u32[]{:S(2)}, u32[]{:S(2)}) collective-permute-start(f32[48,128]{1,0:T(8,128)S(1)} %get-tuple-element.46), channel_id=1, source_target_pairs={{0,2},{2,4},{4,6},{6,0},{1,3},{3,5},{5,7},{7,1},{8,10},{10,12},{12... | collective-permute-start | bytes 73736 | tf_op jit(solution)/shard_map/ppermute | solution.py:326
  120.2 3.9 %collective-permute-start.26 = (f32[48,128]{1,0:T(8,128)S(1)}, f32[48,128]{1,0:T(8,128)S(1)}, u32[]{:S(2)}, u32[]{:S(2)}) collective-permute-start(f32[48,128]{1,0:T(8,128)S(1)} %get-tuple-element.47), channel_id=1, source_target_pairs={{0,6},{2,0},{4,2},{6,4},{1,7},{3,1},{5,3},{7,5},{8,14},{10,8},{12,... | collective-permute-start | bytes 73736 | tf_op jit(solution)/shard_map/ppermute | solution.py:326
  122.8 4.2 %collective-permute-start.25 = (f32[48,128]{1,0:T(8,128)S(1)}, f32[48,128]{1,0:T(8,128)S(1)}, u32[]{:S(2)}, u32[]{:S(2)}) collective-permute-start(f32[48,128]{1,0:T(8,128)S(1)} %get-tuple-element.48), channel_id=1, source_target_pairs={{0,4},{2,6},{4,0},{6,2},{1,5},{3,7},{5,1},{7,3},{8,12},{10,14},{12... | collective-permute-start | bytes 73736 | tf_op jit(solution)/shard_map/ppermute | solution.py:326
  122.8 30.7 %collective-permute-start.22 = (f32[3,4,128,128]{3,2,1,0:T(8,128)}, f32[3,4,128,128]{3,2,1,0:T(8,128)S(1)}, u32[]{:S(2)}, u32[]{:S(2)}) collective-permute-start(f32[3,4,128,128]{3,2,1,0:T(8,128)} %get-tuple-element.29), channel_id=1, source_target_pairs={{0,1},{1,0},{2,3},{3,2},{4,5},{5,4},{6,7},{7,6},{8,9},{9,8},{10,11... | collective-permute-start | bytes 2359304 | tf_op jit(solution)/shard_map/ppermute | solution.py:28
  129.4 24.1 %collective-permute-start.35 = (f32[3,4,128,128]{3,2,1,0:T(8,128)S(1)}, f32[3,4,128,128]{3,2,1,0:T(8,128)S(1)}, u32[]{:S(2)}, u32[]{:S(2)}) collective-permute-start(f32[3,4,128,128]{3,2,1,0:T(8,128)S(1)} %add_add_fusion), channel_id=1, source_target_pairs={{254,0},{0,2},{2,4},{4,6},{6,8},{8,10},{10,12},{12,14},{14,16},{16... | collective-permute-start | bytes 2359304 | tf_op jit(solution)/shard_map/ppermute | solution.py:33
  129.5 4.4 %collective-permute-start.29 = (f32[48,128]{1,0:T(8,128)S(1)}, f32[48,128]{1,0:T(8,128)S(1)}, u32[]{:S(2)}, u32[]{:S(2)}) collective-permute-start(f32[48,128]{1,0:T(8,128)S(1)} %fusion.9), channel_id=1, source_target_pairs={{0,96},{32,0},{64,32},{96,64},{128,224},{160,128},{192,160},{224,1... | collective-permute-start | bytes 73736 | tf_op jit(solution)/shard_map/ppermute | solution.py:360
  132.9 3.6 %collective-permute-start.28 = (f32[48,128]{1,0:T(8,128)S(1)}, f32[48,128]{1,0:T(8,128)S(1)}, u32[]{:S(2)}, u32[]{:S(2)}) collective-permute-start(f32[48,128]{1,0:T(8,128)S(1)} %fusion.9), channel_id=1, source_target_pairs={{0,64},{32,96},{64,0},{96,32},{128,192},{160,224},{192,128},{224,1... | collective-permute-start | bytes 73736 | tf_op jit(solution)/shard_map/ppermute | solution.py:360
  133.9 4.5 %collective-permute-start.27 = (f32[48,128]{1,0:T(8,128)S(1)}, f32[48,128]{1,0:T(8,128)S(1)}, u32[]{:S(2)}, u32[]{:S(2)}) collective-permute-start(f32[48,128]{1,0:T(8,128)S(1)} %fusion.9), channel_id=1, source_target_pairs={{0,32},{32,64},{64,96},{96,0},{128,160},{160,192},{192,224},{224,1... | collective-permute-start | bytes 73736 | tf_op jit(solution)/shard_map/ppermute | solution.py:360
  138.4 7.0 %collective-permute-start.30 = (f32[48,128]{1,0:T(8,128)S(1)}, f32[48,128]{1,0:T(8,128)S(1)}, u32[]{:S(2)}, u32[]{:S(2)}) collective-permute-start(f32[48,128]{1,0:T(8,128)S(1)} %add_add_fusion.5), channel_id=1, source_target_pairs={{0,128},{32,160},{64,192},{96,224},{128,0},{160,32},{192,64},{224,... | collective-permute-start | bytes 73736 | tf_op jit(solution)/shard_map/ppermute | solution.py:360
  145.3 3.6 %collective-permute-start.33 = (f32[48,128]{1,0:T(8,128)S(1)}, f32[48,128]{1,0:T(8,128)S(1)}, u32[]{:S(2)}, u32[]{:S(2)}) collective-permute-start(f32[48,128]{1,0:T(8,128)S(1)} %add.225), channel_id=1, source_target_pairs={{0,24},{8,0},{16,8},{24,16},{1,25},{9,1},{17,9},{25,17},{2,26},{10... | collective-permute-start | bytes 73736 | tf_op jit(solution)/shard_map/ppermute | solution.py:360
  145.3 4.6 %collective-permute-start.32 = (f32[48,128]{1,0:T(8,128)S(1)}, f32[48,128]{1,0:T(8,128)S(1)}, u32[]{:S(2)}, u32[]{:S(2)}) collective-permute-start(f32[48,128]{1,0:T(8,128)S(1)} %add.225), channel_id=1, source_target_pairs={{0,16},{8,24},{16,0},{24,8},{1,17},{9,25},{17,1},{25,9},{2,18},{10... | collective-permute-start | bytes 73736 | tf_op jit(solution)/shard_map/ppermute | solution.py:360
  148.2 4.2 %collective-permute-start.31 = (f32[48,128]{1,0:T(8,128)S(1)}, f32[48,128]{1,0:T(8,128)S(1)}, u32[]{:S(2)}, u32[]{:S(2)}) collective-permute-start(f32[48,128]{1,0:T(8,128)S(1)} %add.225), channel_id=1, source_target_pairs={{0,8},{8,16},{16,24},{24,0},{1,9},{9,17},{17,25},{25,1},{2,10},{10... | collective-permute-start | bytes 73736 | tf_op jit(solution)/shard_map/ppermute | solution.py:360
  154.0 21.3 %collective-permute-start.36 = (f32[2,128,512]{1,2,0:T(8,128)S(1)}, f32[2,128,512]{1,2,0:T(8,128)S(1)}, u32[]{:S(2)}, u32[]{:S(2)}) collective-permute-start(f32[2,128,512]{1,2,0:T(8,128)S(1)} %bitcast.52), channel_id=1, source_target_pairs={{0,1},{1,0},{2,3},{3,2},{4,5},{5,4},{6,7},{7,6},{8,9},{9,8},{10,11... | collective-permute-start | bytes 1572872 | tf_op jit(solution)/shard_map/ppermute | solution.py:28
  159.6 12.4 %collective-permute-start.39 = (f32[48,128]{1,0:T(8,128)S(1)}, f32[48,128]{1,0:T(8,128)S(1)}, u32[]{:S(2)}, u32[]{:S(2)}) collective-permute-start(f32[48,128]{1,0:T(8,128)S(1)} %add_add_fusion.4), channel_id=1, source_target_pairs={{2,0},{4,2},{6,4},{0,6},{3,1},{5,3},{7,5},{1,7},{10,8},{12,10},{14... | collective-permute-start | bytes 73736 | tf_op jit(solution)/shard_map/ppermute | solution.py:338
  171.1 4.2 %collective-permute-start.38 = (f32[48,128]{1,0:T(8,128)S(1)}, f32[48,128]{1,0:T(8,128)S(1)}, u32[]{:S(2)}, u32[]{:S(2)}) collective-permute-start(f32[48,128]{1,0:T(8,128)S(1)} %add_add_fusion.4), channel_id=1, source_target_pairs={{4,0},{6,2},{0,4},{2,6},{5,1},{7,3},{1,5},{3,7},{12,8},{14,10},{8,... | collective-permute-start | bytes 73736 | tf_op jit(solution)/shard_map/ppermute | solution.py:338
  171.1 4.2 %collective-permute-start.37 = (f32[48,128]{1,0:T(8,128)S(1)}, f32[48,128]{1,0:T(8,128)S(1)}, u32[]{:S(2)}, u32[]{:S(2)}) collective-permute-start(f32[48,128]{1,0:T(8,128)S(1)} %add_add_fusion.4), channel_id=1, source_target_pairs={{6,0},{0,2},{2,4},{4,6},{7,1},{1,3},{3,5},{5,7},{14,8},{8,10},{10,... | collective-permute-start | bytes 73736 | tf_op jit(solution)/shard_map/ppermute | solution.py:338
  176.6 3.0 %collective-permute-start.40 = (f32[192,128]{1,0:T(8,128)S(1)}, f32[192,128]{1,0:T(8,128)S(1)}, u32[]{:S(2)}, u32[]{:S(2)}) collective-permute-start(f32[192,128]{1,0:T(8,128)S(1)} %maximum_add_fusion), channel_id=1, source_target_pairs={{0,1},{1,0},{2,3},{3,2},{4,5},{5,4},{6,7},{7,6},{8,9},{9,8},{10,11... | collective-permute-start | bytes 294920 | tf_op jit(solution)/shard_map/ppermute | solution.py:28
  178.2 1.4 copy-start.3

commit v6 on v5

--- a/solution.py
+++ b/solution.py
@@ -318,6 +318,29 @@
     return part
 
 
+def moved_along(value, shift):
+    depth, wide, high = (lax.axis_size(axis) for axis in TILE)
+    route = []
+    for place in range(depth * wide * high):
+        line = place % (wide * high)
+        step = shift if line == 0 else -shift
+        route.append((place, (place // (wide * high) + step) % depth * wide * high + line))
+    return lax.ppermute(value, TILE, route)
+
+
+def summed_one_way(part):
+    count = lax.axis_size(TILE[0])
+    stride = 1
+    while stride < count:
+        arrived = part
+        hops = 2 if stride > 2 else 1
+        for _ in range(hops):
+            arrived = moved_along(arrived, stride // hops)
+        part = part + arrived
+        stride *= 2
+    return part
+
+
 def scattered_over(pieces, axis):
     count = lax.axis_size(axis)
     arrived = []
@@ -394,7 +417,7 @@
     up = after(up + swapped(give_up), part)
     above = from_tile(low, -1)
     below = from_tile(up, 1)
-    part = summed_over(summed_over(part, TILE[0]), TILE[1])
+    part = summed_over(summed_one_way(part), TILE[1])
     up, low, above, below = lax.optimization_barrier((up, low, above, below))
     own_half = updated(up + above, in_blocks(own_half))
     mine = jnp.concatenate([own_half, updated(low + below, in_blocks(halo))], axis=2)
@@ -407,7 +430,7 @@
     low = after(low + swapped(give_low), part)
     up = up + swapped(give_up)
     above = from_tile(low, -1)
-    part = summed_over(summed_over(part, TILE[0]), TILE[1])
+    part = summed_over(summed_one_way(part), TILE[1])
     up = after(up, part)
     mine = updated(up + above, own_half).transpose(0, 2, 1, 3).reshape(2, STRIP, COLS // 2)
     other = swapped(mine)

time: 181 us -> 176 us (0.972); the launches traced: 180 us -> 173 us
  starting transfers between devices: 83.3 us -> 62.7 us
  waiting for transfers between devices: 50.8 us -> 63.9 us
    ppermute x0 -> x8, waiting for transfers between devices: none -> 31.6 us  [moved_along(): return lax.ppermute(value, TILE, route)]
    ppermute x14 -> x6, starting transfers between devices: 24 us -> 2.97 us  [shifts_among(): total = total + lax.ppermute(value, axis, route)]
    ppermute x14 -> x6, waiting for transfers between devices: 23.4 us -> 6.22 us  [shifts_among(): total = total + lax.ppermute(value, axis, route)]
    ppermute x6, starting transfers between devices: 15 us -> 5.3 us  [gathered_over(): lax.ppermute(piece, axis, [((i + step) % count, i) for i in range(count)])]
    ppermute x0 -> x8, starting transfers between devices: none -> 6.68 us  [moved_along(): return lax.ppermute(value, TILE, route)]
    ppermute x11, starting transfers between devices: 23.5 us -> 27.3 us  [swapped(): return lax.ppermute(value, 'pos', [(0, 1), (1, 0)])]
  transfers between devices with their start and end apart: 41 -> 41, of which waited for: 21 -> 23; matrix products, arithmetic and copies ran while one was open for 7% -> 7% of each run, Pallas kernels for 0% -> 0%
where the time goes in v6:
time: 176 us; the launch traced here: 173 us
  waiting for transfers between devices  63.9 us (36%)
  starting transfers between devices  62.7 us (36%)
  Pallas kernels  24.4 us (14%)
  other arithmetic  9.02 us (5%)
  local copies, waits for them, and re-layouts  8.31 us (5%)
  between operations  4.33 us (2%)
    ppermute x8, waiting for transfers between devices, moved_along(): return lax.ppermute(value, TILE, route)  31.6 us
    ppermute x11, starting transfers between devices, swapped(): return lax.ppermute(value, 'pos', [(0, 1), (1, 0)])  27.3 us
    pallas_call x2, Pallas kernels, run_positions(): pl.pallas_call(kernel, out_shape=(quarter,) * 4 + (pieces_of,) * 2, in_sp...  24.4 us
    ppermute x4, starting transfers between devices, from_tile(): lax.ppermute(value, TILE, [((i + distance) % count, i) for i in range(cou...  13.5 us
    ppermute x4, waiting for transfers between devices, from_tile(): lax.ppermute(value, TILE, [((i + distance) % count, i) for i in range(cou...  10.6 us
    ppermute x6, starting transfers between devices, scattered_over(): arrived.append(lax.ppermute(pieces[step], axis, route))  6.85 us
    ppermute x8, starting transfers between devices, moved_along(): return lax.ppermute(value, TILE, route)  6.68 us
    ppermute x6, waiting for transfers between devices, shifts_among(): total = total + lax.ppermute(value, axis, route)  6.22 us
  transfers between devices with their start and end apart: 41, of which 23 were waited for; matrix products, arithmetic and copies ran while one was open for 7% of the time, Pallas kernels for 0%

profile of v6, /device:TPU:1, one launch (start us, length us, event | category | flops | bytes accessed | tf_op | source)
XLA Modules:
  0.0 172.7 jit_solution(15963189194398309088)
XLA Ops:
  0.6 1.1 constant_dynamic-slice_fusion
  1.7 11.1 %collective-permute-start = (f32[2,128,512]{2,1,0:T(8,128)S(1)}, f32[2,128,512]{2,1,0:T(8,128)S(1)}, u32[]{:S(2)}, u32[]{:S(2)}) collective-permute-start(f32[2,128,512]{2,1,0:T(8,128)S(1)} %constant_dynamic-slice_fusion), channel_id=1, source_target_pairs={{2,0},{4,2},{6,4},{8,6},{10,8},{12,10},{14,12},{16,14},{18,16},{20... | collective-permute-start | bytes 1572872 | tf_op jit(solution)/shard_map/ppermute | solution.py:33
  12.8 10.6 %collective-permute-done.refs_7_ = f32[2,128,512]{2,1,0:T(8,128)S(1)} collective-permute-done((f32[2,128,512]{2,1,0:T(8,128)S(1)}, f32[2,128,512]{2,1,0:T(8,128)S(1)}, u32[]{:S(2)}, u32[]{:S(2)}) %collective-permute-start) | collective-permute-done | bytes 524320 | tf_op jit(solution)/shard_map/ppermute | solution.py:33
  23.4 1.5 collective-permute-start.1
  25.6 0.9 collective-permute-done.1.refs_8_
  26.5 0.8 copy-done.7
  27.3 12.2 %positions.2 = (f32[3,4,128,128]{3,2,1,0:T(8,128)}, f32[3,4,128,128]{3,2,1,0:T(8,128)}, f32[3,4,128,128]{3,2,1,0:T(8,128)}, f32[3,4,128,128]{3,2,1,0:T(8,128)}, ...) custom-call(s32[1,1,32]{2,1,0:T(1,128)} %refs_0_.3, s32[1,1,32]{2,1,0:T(1,128)} %refs_1_.3, s32[1,1]{1,0:T(1,128)S(6)} %copy.15.refs_2_, ...), custom_call_target="tpu_custom_call" | custom-call | flops 12999999488 | bytes 8388608 | tf_op jit(solution)/shard_map/positions/pallas_call | solution.py:275
  39.5 2.9 %collective-permute-start.17 = (f32[3,4,128,128]{3,2,1,0:T(8,128)}, f32[3,4,128,128]{3,2,1,0:T(8,128)S(1)}, u32[]{:S(2)}, u32[]{:S(2)}) collective-permute-start(f32[3,4,128,128]{3,2,1,0:T(8,128)} %get-tuple-element.21), channel_id=1, source_target_pairs={{0,1},{1,0},{2,3},{3,2},{4,5},{5,4},{6,7},{7,6},{8,9},{9,8},{10,11... | collective-permute-start | bytes 2359304 | tf_op jit(solution)/shard_map/ppermute | solution.py:28
  43.0 1.8 %collective-permute-done.2 = f32[4,48,128]{2,1,0:T(8,128)S(1)} collective-permute-done((f32[4,48,128]{2,1,0:T(8,128)}, f32[4,48,128]{2,1,0:T(8,128)S(1)}, u32[]{:S(2)}, u32[]{:S(2)}) %collective-permute-start.2) | collective-permute-done | bytes 98336 | tf_op jit(solution)/shard_map/ppermute | solution.py:28
  44.8 0.9 add.184
  45.8 2.7 %collective-permute-start.5 = (f32[48,128]{1,0:T(8,128)S(1)}, f32[48,128]{1,0:T(8,128)S(1)}, u32[]{:S(2)}, u32[]{:S(2)}) collective-permute-start(f32[48,128]{1,0:T(8,128)S(1)} %get-tuple-element.54), channel_id=1, source_target_pairs={{0,6},{2,0},{4,2},{6,4},{1,7},{3,1},{5,3},{7,5},{8,14},{10,8},{12,... | collective-permute-start | bytes 73736 | tf_op jit(solution)/shard_map/ppermute | solution.py:349
  48.4 1.2 collective-permute-done.3
  49.6 3.0 %collective-permute-done.4 = f32[48,128]{1,0:T(8,128)S(1)} collective-permute-done((f32[48,128]{1,0:T(8,128)S(1)}, f32[48,128]{1,0:T(8,128)S(1)}, u32[]{:S(2)}, u32[]{:S(2)}) %collective-permute-start.4) | collective-permute-done | bytes 24608 | tf_op jit(solution)/shard_map/ppermute | solution.py:349
  52.6 0.5 slice.106
  53.8 1.2 add_add_fusion.3
  55.0 1.5 collective-permute-start.20
  56.9 3.9 %collective-permute-done.6 = f32[48,128]{1,0:T(8,128)S(1)} collective-permute-done((f32[48,128]{1,0:T(8,128)S(1)}, f32[48,128]{1,0:T(8,128)S(1)}, u32[]{:S(2)}, u32[]{:S(2)}) %collective-permute-start.6) | collective-permute-done | bytes 24608 | tf_op jit(solution)/shard_map/ppermute | solution.py:328
  60.7 4.8 %collective-permute-done.7 = f32[48,128]{1,0:T(8,128)S(1)} collective-permute-done((f32[48,128]{1,0:T(8,128)S(1)}, f32[48,128]{1,0:T(8,128)S(1)}, u32[]{:S(2)}, u32[]{:S(2)}) %collective-permute-start.7) | collective-permute-done | bytes 24608 | tf_op jit(solution)/shard_map/ppermute | solution.py:328
  65.5 5.2 %collective-permute-done.8 = f32[48,128]{1,0:T(8,128)S(1)} collective-permute-done((f32[48,128]{1,0:T(8,128)S(1)}, f32[48,128]{1,0:T(8,128)S(1)}, u32[]{:S(2)}, u32[]{:S(2)}) %collective-permute-start.8) | collective-permute-done | bytes 24608 | tf_op jit(solution)/shard_map/ppermute | solution.py:328
  70.7 5.3 %collective-permute-done.9 = f32[48,128]{1,0:T(8,128)S(1)} collective-permute-done((f32[48,128]{1,0:T(8,128)S(1)}, f32[48,128]{1,0:T(8,128)S(1)}, u32[]{:S(2)}, u32[]{:S(2)}) %collective-permute-start.9) | collective-permute-done | bytes 24608 | tf_op jit(solution)/shard_map/ppermute | solution.py:328
  76.1 1.4 collective-permute-start.10
  77.9 1.2 copy.11
  79.3 1.3 collective-permute-done.11
  80.7 0.8 collective-permute-done.10
  81.5 1.1 collective-permute-start.15
  82.6 0.7 collective-permute-start.13
  83.3 1.2 add.204
  84.6 1.2 add.207
  86.1 7.8 %collective-permute-start.21 = (f32[2,4,256,128]{3,2,1,0:T(8,128)S(1)}, f32[2,4,256,128]{3,2,1,0:T(8,128)S(1)}, u32[]{:S(2)}, u32[]{:S(2)}) collective-permute-start(f32[2,4,256,128]{3,2,1,0:T(8,128)S(1)} %pad_maximum_fusion.refs_6_), channel_id=1, source_target_pairs={{0,1},{1,0},{2,3},{3,2},{4,5},{5,4},{6,7},{7,6},{8,9},{9,8},{10,11... | collective-permute-start | bytes 3145736 | tf_op jit(solution)/shard_map/ppermute | solution.py:28
  94.0 1.6 collective-permute-start.16
  95.6 0.9 collective-permute-done.16
  96.6 0.7 add_divide_fusion.1.refs_3_
  97.3 1.0 copy-done.6
  98.3 12.2 %positions.3 = (f32[3,4,128,128]{3,2,1,0:T(8,128)}, f32[3,4,128,128]{3,2,1,0:T(8,128)}, f32[3,4,128,128]{3,2,1,0:T(8,128)}, f32[3,4,128,128]{3,2,1,0:T(8,128)}, ...) custom-call(s32[1,1,32]{2,1,0:T(1,128)} %refs_0_.3, s32[1,1,32]{2,1,0:T(1,128)} %refs_1_.3, s32[1,1]{1,0:T(1,128)S(6)} %copy.15.refs_2_, ...), custom_call_target="tpu_custom_call" | custom-call | flops 12999999488 | bytes 8388608 | tf_op jit(solution)/shard_map/positions/pallas_call | solution.py:275
  110.6 2.9 %collective-permute-start.34 = (f32[3,4,128,128]{3,2,1,0:T(8,128)}, f32[3,4,128,128]{3,2,1,0:T(8,128)S(1)}, u32[]{:S(2)}, u32[]{:S(2)}) collective-permute-start(f32[3,4,128,128]{3,2,1,0:T(8,128)} %get-tuple-element.33), channel_id=1, source_target_pairs={{0,1},{1,0},{2,3},{3,2},{4,5},{5,4},{6,7},{7,6},{8,9},{9,8},{10,11... | collective-permute-start | bytes 2359304 | tf_op jit(solution)/shard_map/ppermute | solution.py:28
  113.6 2.2 %collective-permute-done.23 = f32[4,48,128]{2,1,0:T(8,128)S(1)} collective-permute-done((f32[4,48,128]{2,1,0:T(8,128)}, f32[4,48,128]{2,1,0:T(8,128)S(1)}, u32[]{:S(2)}, u32[]{:S(2)}) %collective-permute-start.23) | collective-permute-done | bytes 98336 | tf_op jit(solution)/shard_map/ppermute | solution.py:28
  115.8 0.9 add.211
  116.7 2.0 %collective-permute-start.24 = (f32[48,128]{1,0:T(8,128)S(1)}, f32[48,128]{1,0:T(8,128)S(1)}, u32[]{:S(2)}, u32[]{:S(2)}) collective-permute-start(f32[48,128]{1,0:T(8,128)S(1)} %get-tuple-element.46), channel_id=1, source_target_pairs={{0,2},{2,4},{4,6},{6,0},{1,3},{3,5},{5,7},{7,1},{8,10},{10,12},{12... | collective-permute-start | bytes 73736 | tf_op jit(solution)/shard_map/ppermute | solution.py:349
  118.7 0.8 collective-permute-start.26
  119.4 1.3 collective-permute-start.25
  120.8 0.9 collective-permute-start.22
  121.7 1.9 %collective-permute-done.25 = f32[48,128]{1,0:T(8,128)S(1)} collective-permute-done((f32[48,128]{1,0:T(8,128)S(1)}, f32[48,128]{1,0:T(8,128)S(1)}, u32[]{:S(2)}, u32[]{:S(2)}) %collective-permute-start.25) | collective-permute-done | bytes 24608 | tf_op jit(solution)/shard_map/ppermute | solution.py:349
  123.6 0.5 slice.116
  124.8 1.2 add_add_fusion
  126.0 0.8 collective-permute-start.35
  126.8 2.8 %collective-permute-start.27 = (f32[48,128]{1,0:T(8,128)S(1)}, f32[48,128]{1,0:T(8,128)S(1)}, u32[]{:S(2)}, u32[]{:S(2)}) collective-permute-start(f32[48,128]{1,0:T(8,128)S(1)} %fusion.9), channel_id=1, source_target_pairs={{0,32},{2,226},{4,228},{6,230},{8,232},{10,234},{12,236},{14,238},... | collective-permute-start | bytes 73736 | tf_op jit(solution)/shard_map/ppermute | solution.py:328
  129.6 1.1 collective-permute-done.27
  130.7 2.0 %collective-permute-start.28 = (f32[48,128]{1,0:T(8,128)S(1)}, f32[48,128]{1,0:T(8,128)S(1)}, u32[]{:S(2)}, u32[]{:S(2)}) collective-permute-start(f32[48,128]{1,0:T(8,128)S(1)} %add.215), channel_id=1, source_target_pairs={{0,64},{2,194},{4,196},{6,198},{8,200},{10,202},{12,204},{14,206},... | collective-permute-start | bytes 73736 | tf_op jit(solution)/shard_map/ppermute | solution.py:328
  132.7 2.8 %collective-permute-done.28 = f32[48,128]{1,0:T(8,128)S(1)} collective-permute-done((f32[48,128]{1,0:T(8,128)S(1)}, f32[48,128]{1,0:T(8,128)S(1)}, u32[]{:S(2)}, u32[]{:S(2)}) %collective-permute-start.28) | collective-permute-done | bytes 24608 | tf_op jit(solution)/shard_map/ppermute | solution.py:328
  135.5 0.8 collective-permute-start.29
  136.3 4.3 %collective-permute-done.29 = f32[48,128]{1,0:T(8,128)S(1)} collective-permute-done((f32[48,128]{1,0:T(8,128)S(1)}, f32[48,128]{1,0:T(8,128)S(1)}, u32[]{:S(2)}, u32[]{:S(2)}) %collective-permute-start.29) | collective-permute-done | bytes 24608 | tf_op jit(solution)/shard_map/ppermute | solution.py:328
  140.6 1.0 collective-permute-start.30
  141.6 4.3 %collective-permute-done.30 = f32[48,128]{1,0:T(8,128)S(1)} collective-permute-done((f32[48,128]{1,0:T(8,128)S(1)}, f32[48,128]{1,0:T(8,128)S(1)}, u32[]{:S(2)}, u32[]{:S(2)}) %collective-permute-start.30) | collective-permute-done | bytes 24608 | tf_op jit(solution)/shard_map/ppermute | solution.py:328
  145.9 0.9 collective-permute-start.33
  146.8 0.7 collective-permute-start.31
  147.4 1.5 collective-permute-done.33
  148.9 2.2 %collective-permute-done.32 = f32[48,128]{1,0:T(8,128)S(1)} collective-permute-done((f32[48,128]{1,0:T(8,128)S(1)}, f32[48,128]{1,0:T(8,128)S(1)}, u32[]{:S(2)}, u32[]{:S(2)}) %collective-permute-start.32) | collective-permute-done | bytes 24608 | tf_op jit(solution)/shard_map/ppermute | solution.py:383
  153.2 7.4 %collective-permute-start.36 = (f32[2,128,512]{1,2,0:T(8,128)S(1)}, f32[2,128,512]{1,2,0:T(8,128)S(1)}, u32[]{:S(2)}, u32[]{:S(2)}) collective-permute-start(f32[2,128,512]{1,2,0:T(8,128)S(1)} %bitcast.52), channel_id=1, source_target_pairs={{0,1},{1,0},{2,3},{3,2},{4,5},{5,4},{6,7},{7,6},{8,9},{9,8},{10,11... | collective-permute-start | bytes 1572872 | tf_op jit(solution)/shard_map/ppermute | solution.py:28
  160.5 2.9 %collective-permute-start.39 = (f32[48,128]{1,0:T(8,128)S(1)}, f32[48,128]{1,0:T(8,128)S(1)}, u32[]{:S(2)}, u32[]{:S(2)}) collective-permute-start(f32[48,128]{1,0:T(8,128)S(1)} %add_add_fusion.4), channel_id=1, source_target_pairs={{2,0},{4,2},{6,4},{0,6},{3,1},{5,3},{7,5},{1,7},{10,8},{12,10},{14... | collective-permute-start | bytes 73736 | tf_op jit(solution)/shard_map/ppermute | solution.py:361
  163.5 0.6 collective-permute-start.37
  164.4 3.2 %collective-permute-done.38 = f32[48,128]{1,0:T(8,128)S(1)} collective-permute-done((f32[48,128]{1,0:T(8,128)S(1)}, f32[48,128]{1,0:T(8,128)S(1)}, u32[]{:S(2)}, u32[]{:S(2)}) %collective-permute-start.38) | collective-permute-done | bytes 24608 | tf_op jit(solution)/shard_map/ppermute | solution.py:361
  168.9 1.6 collective-permute-start.40
  170.6 1.3 copy.14
  172.0 0.7 add_divide_fusion
  (87 shorter events, 4.6 us)
Async XLA Ops:
  1.7 21.7 %collective-permute-start = (f32[2,128,512]{2,1,0:T(8,128)S(1)}, f32[2,128,512]{2,1,0:T(8,128)S(1)}, u32[]{:S(2)}, u32[]{:S(2)}) collective-permute-start(f32[2,128,512]{2,1,0:T(8,128)S(1)} %constant_dynamic-slice_fusion), channel_id=1, source_target_pairs={{2,0},{4,2},{6,4},{8,6},{10,8},{12,10},{14,12},{16,14},{18,16},{20... | collective-permute-start | bytes 1572872 | tf_op jit(solution)/shard_map/ppermute | solution.py:33
  23.4 3.1 %copy-start.4 = (f32[2,128,512]{2,1,0:T(8,128)}, f32[2,128,512]{2,1,0:T(8,128)S(1)}, u32[]{:S(2)}) copy-start(f32[2,128,512]{2,1,0:T(8,128)S(1)} %collective-permute-done.refs_7_) | copy-start | bytes 1572868
  23.4 3.1 %collective-permute-start.1 = (f32[2,128,512]{2,1,0:T(8,128)S(1)}, f32[2,128,512]{2,1,0:T(8,128)S(1)}, u32[]{:S(2)}, u32[]{:S(2)}) collective-permute-start(f32[2,128,512]{2,1,0:T(8,128)S(1)} %collective-permute-done.refs_7_), channel_id=1, source_target_pairs={{0,1},{1,0},{2,3},{3,2},{4,5},{5,4},{6,7},{7,6},{8,9},{9,8},{10,11... | collective-permute-start | bytes 1572872 | tf_op jit(solution)/shard_map/ppermute | solution.py:28
  26.5 0.8 copy-start.7
  39.5 17.0 %copy-start.1 = (f32[3,4,128,128]{3,2,1,0:T(8,128)S(1)}, f32[3,4,128,128]{3,2,1,0:T(8,128)}, u32[]{:S(2)}) copy-start(f32[3,4,128,128]{3,2,1,0:T(8,128)} %get-tuple-element.22) | copy-start | bytes 2359300
  39.5 14.2 %collective-permute-start.17 = (f32[3,4,128,128]{3,2,1,0:T(8,128)}, f32[3,4,128,128]{3,2,1,0:T(8,128)S(1)}, u32[]{:S(2)}, u32[]{:S(2)}) collective-permute-start(f32[3,4,128,128]{3,2,1,0:T(8,128)} %get-tuple-element.21), channel_id=1, source_target_pairs={{0,1},{1,0},{2,3},{3,2},{4,5},{5,4},{6,7},{7,6},{8,9},{9,8},{10,11... | collective-permute-start | bytes 2359304 | tf_op jit(solution)/shard_map/ppermute | solution.py:28
  42.5 2.3 %collective-permute-start.2 = (f32[4,48,128]{2,1,0:T(8,128)}, f32[4,48,128]{2,1,0:T(8,128)S(1)}, u32[]{:S(2)}, u32[]{:S(2)}) collective-permute-start(f32[4,48,128]{2,1,0:T(8,128)} %get-tuple-element.19), channel_id=1, source_target_pairs={{0,1},{1,0},{2,3},{3,2},{4,5},{5,4},{6,7},{7,6},{8,9},{9,8},{10,11... | collective-permute-start | bytes 294920 | tf_op jit(solution)/shard_map/ppermute | solution.py:28
  42.6 14.0 %collective-permute-start.18 = (f32[3,4,128,128]{3,2,1,0:T(8,128)}, f32[3,4,128,128]{3,2,1,0:T(8,128)S(1)}, u32[]{:S(2)}, u32[]{:S(2)}) collective-permute-start(f32[3,4,128,128]{3,2,1,0:T(8,128)} %get-tuple-element.23), channel_id=1, source_target_pairs={{0,1},{1,0},{2,3},{3,2},{4,5},{5,4},{6,7},{7,6},{8,9},{9,8},{10,11... | collective-permute-start | bytes 2359304 | tf_op jit(solution)/shard_map/ppermute | solution.py:28
  45.7 4.0 %collective-permute-start.3 = (f32[48,128]{1,0:T(8,128)S(1)}, f32[48,128]{1,0:T(8,128)S(1)}, u32[]{:S(2)}, u32[]{:S(2)}) collective-permute-start(f32[48,128]{1,0:T(8,128)S(1)} %get-tuple-element.53), channel_id=1, source_target_pairs={{0,2},{2,4},{4,6},{6,0},{1,3},{3,5},{5,7},{7,1},{8,10},{10,12},{12... | collective-permute-start | bytes 73736 | tf_op jit(solution)/shard_map/ppermute | solution.py:349
  45.8 3.9 %collective-permute-start.5 = (f32[48,128]{1,0:T(8,128)S(1)}, f32[48,128]{1,0:T(8,128)S(1)}, u32[]{:S(2)}, u32[]{:S(2)}) collective-permute-start(f32[48,128]{1,0:T(8,128)S(1)} %get-tuple-element.54), channel_id=1, source_target_pairs={{0,6},{2,0},{4,2},{6,4},{1,7},{3,1},{5,3},{7,5},{8,14},{10,8},{12,... | collective-permute-start | bytes 73736 | tf_op jit(solution)/shard_map/ppermute | solution.py:349
  48.4 4.2 %collective-permute-start.4 = (f32[48,128]{1,0:T(8,128)S(1)}, f32[48,128]{1,0:T(8,128)S(1)}, u32[]{:S(2)}, u32[]{:S(2)}) collective-permute-start(f32[48,128]{1,0:T(8,128)S(1)} %get-tuple-element.55), channel_id=1, source_target_pairs={{0,4},{2,6},{4,0},{6,2},{1,5},{3,7},{5,1},{7,3},{8,12},{10,14},{12... | collective-permute-start | bytes 73736 | tf_op jit(solution)/shard_map/ppermute | solution.py:349
  55.0 28.3 %collective-permute-start.20 = (f32[3,4,128,128]{3,2,1,0:T(8,128)S(1)}, f32[3,4,128,128]{3,2,1,0:T(8,128)}, u32[]{:S(2)}, u32[]{:S(2)}) collective-permute-start(f32[3,4,128,128]{3,2,1,0:T(8,128)S(1)} %add_add_fusion.3), channel_id=1, source_target_pairs={{2,0},{4,2},{6,4},{8,6},{10,8},{12,10},{14,12},{16,14},{18,16},{20... | collective-permute-start | bytes 2359304 | tf_op jit(solution)/shard_map/ppermute | solution.py:33
  56.7 26.6 %collective-permute-start.19 = (f32[3,4,128,128]{3,2,1,0:T(8,128)S(1)}, f32[3,4,128,128]{3,2,1,0:T(8,128)}, u32[]{:S(2)}, u32[]{:S(2)}) collective-permute-start(f32[3,4,128,128]{3,2,1,0:T(8,128)S(1)} %add_add_fusion.2), channel_id=1, source_target_pairs={{254,0},{0,2},{2,4},{4,6},{6,8},{8,10},{10,12},{12,14},{14,16},{16... | collective-permute-start | bytes 2359304 | tf_op jit(solution)/shard_map/ppermute | solution.py:33
  56.8 4.0 %collective-permute-start.6 = (f32[48,128]{1,0:T(8,128)S(1)}, f32[48,128]{1,0:T(8,128)S(1)}, u32[]{:S(2)}, u32[]{:S(2)}) collective-permute-start(f32[48,128]{1,0:T(8,128)S(1)} %fusion.12), channel_id=1, source_target_pairs={{0,32},{2,226},{4,228},{6,230},{8,232},{10,234},{12,236},{14,238},... | collective-permute-start | bytes 73736 | tf_op jit(solution)/shard_map/ppermute | solution.py:328
  60.7 4.8 %collective-permute-start.7 = (f32[48,128]{1,0:T(8,128)S(1)}, f32[48,128]{1,0:T(8,128)S(1)}, u32[]{:S(2)}, u32[]{:S(2)}) collective-permute-start(f32[48,128]{1,0:T(8,128)S(1)} %add.188), channel_id=1, source_target_pairs={{0,64},{2,194},{4,196},{6,198},{8,200},{10,202},{12,204},{14,206},... | collective-permute-start | bytes 73736 | tf_op jit(solution)/shard_map/ppermute | solution.py:328
  65.5 5.2 %collective-permute-start.8 = (f32[48,128]{1,0:T(8,128)S(1)}, f32[48,128]{1,0:T(8,128)S(1)}, u32[]{:S(2)}, u32[]{:S(2)}) collective-permute-start(f32[48,128]{1,0:T(8,128)S(1)} %add.189), channel_id=1, source_target_pairs={{0,64},{2,194},{4,196},{6,198},{8,200},{10,202},{12,204},{14,206},... | collective-permute-start | bytes 73736 | tf_op jit(solution)/shard_map/ppermute | solution.py:328
  70.7 5.3 %collective-permute-start.9 = (f32[48,128]{1,0:T(8,128)S(1)}, f32[48,128]{1,0:T(8,128)S(1)}, u32[]{:S(2)}, u32[]{:S(2)}) collective-permute-start(f32[48,128]{1,0:T(8,128)S(1)} %collective-permute-done.8), channel_id=1, source_target_pairs={{0,64},{2,194},{4,196},{6,198},{8,200},{10,202},{12,204},{14,206},... | collective-permute-start | bytes 73736 | tf_op jit(solution)/shard_map/ppermute | solution.py:328
  76.0 3.3 %collective-permute-start.12 = (f32[48,128]{1,0:T(8,128)S(1)}, f32[48,128]{1,0:T(8,128)S(1)}, u32[]{:S(2)}, u32[]{:S(2)}) collective-permute-start(f32[48,128]{1,0:T(8,128)S(1)} %add.190), channel_id=1, source_target_pairs={{0,24},{8,0},{16,8},{24,16},{1,25},{9,1},{17,9},{25,17},{2,26},{10... | collective-permute-start | bytes 73736 | tf_op jit(solution)/shard_map/ppermute | solution.py:383
  76.0 4.7 %collective-permute-start.11 = (f32[48,128]{1,0:T(8,128)S(1)}, f32[48,128]{1,0:T(8,128)S(1)}, u32[]{:S(2)}, u32[]{:S(2)}) collective-permute-start(f32[48,128]{1,0:T(8,128)S(1)} %add.190), channel_id=1, source_target_pairs={{0,16},{8,24},{16,0},{24,8},{1,17},{9,25},{17,1},{25,9},{2,18},{10... | collective-permute-start | bytes 73736 | tf_op jit(solution)/shard_map/ppermute | solution.py:383
  76.1 5.4 %collective-permute-start.10 = (f32[48,128]{1,0:T(8,128)S(1)}, f32[48,128]{1,0:T(8,128)S(1)}, u32[]{:S(2)}, u32[]{:S(2)}) collective-permute-start(f32[48,128]{1,0:T(8,128)S(1)} %add.190), channel_id=1, source_target_pairs={{0,8},{8,16},{16,24},{24,0},{1,9},{9,17},{17,25},{25,1},{2,10},{10... | collective-permute-start | bytes 73736 | tf_op jit(solution)/shard_map/ppermute | solution.py:383
  81.5 12.5 %collective-permute-start.15 = (f32[48,128]{1,0:T(8,128)S(1)}, f32[48,128]{1,0:T(8,128)S(1)}, u32[]{:S(2)}, u32[]{:S(2)}) collective-permute-start(f32[48,128]{1,0:T(8,128)S(1)} %add_add_fusion.5), channel_id=1, source_target_pairs={{2,0},{4,2},{6,4},{0,6},{3,1},{5,3},{7,5},{1,7},{10,8},{12,10},{14... | collective-permute-start | bytes 73736 | tf_op jit(solution)/shard_map/ppermute | solution.py:361
  82.6 11.3 %collective-permute-start.14 = (f32[48,128]{1,0:T(8,128)S(1)}, f32[48,128]{1,0:T(8,128)S(1)}, u32[]{:S(2)}, u32[]{:S(2)}) collective-permute-start(f32[48,128]{1,0:T(8,128)S(1)} %add_add_fusion.5), channel_id=1, source_target_pairs={{4,0},{6,2},{0,4},{2,6},{5,1},{7,3},{1,5},{3,7},{12,8},{14,10},{8,... | collective-permute-start | bytes 73736 | tf_op jit(solution)/shard_map/ppermute | solution.py:361
  82.6 11.3 %collective-permute-start.13 = (f32[48,128]{1,0:T(8,128)S(1)}, f32[48,128]{1,0:T(8,128)S(1)}, u32[]{:S(2)}, u32[]{:S(2)}) collective-permute-start(f32[48,128]{1,0:T(8,128)S(1)} %add_add_fusion.5), channel_id=1, source_target_pairs={{6,0},{0,2},{2,4},{4,6},{7,1},{1,3},{3,5},{5,7},{14,8},{8,10},{10,... | collective-permute-start | bytes 73736 | tf_op jit(solution)/shard_map/ppermute | solution.py:361
  86.0 10.6 %copy-start.5 = (f32[2,128,128]{2,1,0:T(8,128)S(1)}, f32[2,128,128]{2,1,0:T(8,128)}, u32[]{:S(2)}) copy-start(f32[2,128,128]{2,1,0:T(8,128)} %refs_3_.1) | copy-start | bytes 393220
  86.1 11.2 %copy-start = (f32[2,4,256,128]{3,2,1,0:T(8,128)}, f32[2,4,256,128]{3,2,1,0:T(8,128)S(1)}, u32[]{:S(2)}) copy-start(f32[2,4,256,128]{3,2,1,0:T(8,128)S(1)} %pad_maximum_fusion.refs_6_) | copy-start | bytes 3145732
  86.1 11.2 %collective-permute-start.21 = (f32[2,4,256,128]{3,2,1,0:T(8,128)S(1)}, f32[2,4,256,128]{3,2,1,0:T(8,128)S(1)}, u32[]{:S(2)}, u32[]{:S(2)}) collective-permute-start(f32[2,4,256,128]{3,2,1,0:T(8,128)S(1)} %pad_maximum_fusion.refs_6_), channel_id=1, source_target_pairs={{0,1},{1,0},{2,3},{3,2},{4,5},{5,4},{6,7},{7,6},{8,9},{9,8},{10,11... | collective-permute-start | bytes 3145736 | tf_op jit(solution)/shard_map/ppermute | solution.py:28
  94.0 2.6 %collective-permute-start.16 = (f32[192,128]{1,0:T(8,128)S(1)}, f32[192,128]{1,0:T(8,128)S(1)}, u32[]{:S(2)}, u32[]{:S(2)}) collective-permute-start(f32[192,128]{1,0:T(8,128)S(1)} %pad_maximum_fusion.4), channel_id=1, source_target_pairs={{0,1},{1,0},{2,3},{3,2},{4,5},{5,4},{6,7},{7,6},{8,9},{9,8},{10,11... | collective-permute-start | bytes 294920 | tf_op jit(solution)/shard_map/ppermute | solution.py:28
  97.3 1.0 copy-start.6
  110.6 42.2 %copy-start.2 = (f32[3,4,128,128]{3,2,1,0:T(8,128)S(1)}, f32[3,4,128,128]{3,2,1,0:T(8,128)}, u32[]{:S(2)}) copy-start(f32[3,4,128,128]{3,2,1,0:T(8,128)} %get-tuple-element.28) | copy-start | bytes 2359300
  110.6 14.2 %collective-permute-start.34 = (f32[3,4,128,128]{3,2,1,0:T(8,128)}, f32[3,4,128,128]{3,2,1,0:T(8,128)S(1)}, u32[]{:S(2)}, u32[]{:S(2)}) collective-permute-start(f32[3,4,128,128]{3,2,1,0:T(8,128)} %get-tuple-element.33), channel_id=1, source_target_pairs={{0,1},{1,0},{2,3},{3,2},{4,5},{5,4},{6,7},{7,6},{8,9},{9,8},{10,11... | collective-permute-start | bytes 2359304 | tf_op jit(solution)/shard_map/ppermute | solution.py:28
  113.5 2.3 %collective-permute-start.23 = (f32[4,48,128]{2,1,0:T(8,128)}, f32[4,48,128]{2,1,0:T(8,128)S(1)}, u32[]{:S(2)}, u32[]{:S(2)}) collective-permute-start(f32[4,48,128]{2,1,0:T(8,128)} %get-tuple-element.31), channel_id=1, source_target_pairs={{0,1},{1,0},{2,3},{3,2},{4,5},{5,4},{6,7},{7,6},{8,9},{9,8},{10,11... | collective-permute-start | bytes 294920 | tf_op jit(solution)/shard_map/ppermute | solution.py:28
  116.7 5.0 %collective-permute-start.24 = (f32[48,128]{1,0:T(8,128)S(1)}, f32[48,128]{1,0:T(8,128)S(1)}, u32[]{:S(2)}, u32[]{:S(2)}) collective-permute-start(f32[48,128]{1,0:T(8,128)S(1)} %get-tuple-element.46), channel_id=1, source_target_pairs={{0,2},{2,4},{4,6},{6,0},{1,3},{3,5},{5,7},{7,1},{8,10},{10,12},{12... | collective-permute-start | bytes 73736 | tf_op jit(solution)/shard_map/ppermute | solution.py:349
  118.7 3.0 %collective-permute-start.26 = (f32[48,128]{1,0:T(8,128)S(1)}, f32[48,128]{1,0:T(8,128)S(1)}, u32[]{:S(2)}, u32[]{:S(2)}) collective-permute-start(f32[48,128]{1,0:T(8,128)S(1)} %get-tuple-element.47), channel_id=1, source_target_pairs={{0,6},{2,0},{4,2},{6,4},{1,7},{3,1},{5,3},{7,5},{8,14},{10,8},{12,... | collective-permute-start | bytes 73736 | tf_op jit(solution)/shard_map/ppermute | solution.py:349
  119.4 4.2 %collective-permute-start.25 = (f32[48,128]{1,0:T(8,128)S(1)}, f32[48,128]{1,0:T(8,128)S(1)}, u32[]{:S(2)}, u32[]{:S(2)}) collective-permute-start(f32[48,128]{1,0:T(8,128)S(1)} %get-tuple-element.48), channel_id=1, source_target_pairs={{0,4},{2,6},{4,0},{6,2},{1,5},{3,7},{5,1},{7,3},{8,12},{10,14},{12... | collective-permute-start | bytes 73736 | tf_op jit(solution)/shard_map/ppermute | solution.py:349
  120.8 31.9 %collective-permute-start.22 = (f32[3,4,128,128]{3,2,1,0:T(8,128)}, f32[3,4,128,128]{3,2,1,0:T(8,128)S(1)}, u32[]{:S(2)}, u32[]{:S(2)}) collective-permute-start(f32[3,4,128,128]{3,2,1,0:T(8,128)} %get-tuple-element.29), channel_id=1, source_target_pairs={{0,1},{1,0},{2,3},{3,2},{4,5},{5,4},{6,7},{7,6},{8,9},{9,8},{10,11... | collective-permute-start | bytes 2359304 | tf_op jit(solution)/shard_map/ppermute | solution.py:28
  126.0 26.7 %collective-permute-start.35 = (f32[3,4,128,128]{3,2,1,0:T(8,128)S(1)}, f32[3,4,128,128]{3,2,1,0:T(8,128)S(1)}, u32[]{:S(2)}, u32[]{:S(2)}) collective-permute-start(f32[3,4,128,128]{3,2,1,0:T(8,128)S(1)} %add_add_fusion), channel_id=1, source_target_pairs={{254,0},{0,2},{2,4},{4,6},{6,8},{8,10},{10,12},{12,14},{14,16},{16... | collective-permute-start | bytes 2359304 | tf_op jit(solution)/shard_map/ppermute | solution.py:33
  126.8 3.9 %collective-permute-start.27 = (f32[48,128]{1,0:T(8,128)S(1)}, f32[48,128]{1,0:T(8,128)S(1)}, u32[]{:S(2)}, u32[]{:S(2)}) collective-permute-start(f32[48,128]{1,0:T(8,128)S(1)} %fusion.9), channel_id=1, source_target_pairs={{0,32},{2,226},{4,228},{6,230},{8,232},{10,234},{12,236},{14,238},... | collective-permute-start | bytes 73736 | tf_op jit(solution)/shard_map/ppermute | solution.py:328
  130.7 4.8 %collective-permute-start.28 = (f32[48,128]{1,0:T(8,128)S(1)}, f32[48,128]{1,0:T(8,128)S(1)}, u32[]{:S(2)}, u32[]{:S(2)}) collective-permute-start(f32[48,128]{1,0:T(8,128)S(1)} %add.215), channel_id=1, source_target_pairs={{0,64},{2,194},{4,196},{6,198},{8,200},{10,202},{12,204},{14,206},... | collective-permute-start | bytes 73736 | tf_op jit(solution)/shard_map/ppermute | solution.py:328
  135.5 5.1 %collective-permute-start.29 = (f32[48,128]{1,0:T(8,128)S(1)}, f32[48,128]{1,0:T(8,128)S(1)}, u32[]{:S(2)}, u32[]{:S(2)}) collective-permute-start(f32[48,128]{1,0:T(8,128)S(1)} %add.216), channel_id=1, source_target_pairs={{0,64},{2,194},{4,196},{6,198},{8,200},{10,202},{12,204},{14,206},... | collective-permute-start | bytes 73736 | tf_op jit(solution)/shard_map/ppermute | solution.py:328
  140.6 5.3 %collective-permute-start.30 = (f32[48,128]{1,0:T(8,128)S(1)}, f32[48,128]{1,0:T(8,128)S(1)}, u32[]{:S(2)}, u32[]{:S(2)}) collective-permute-start(f32[48,128]{1,0:T(8,128)S(1)} %collective-permute-done.29), channel_id=1, source_target_pairs={{0,64},{2,194},{4,196},{6,198},{8,200},{10,202},{12,204},{14,206},... | collective-permute-start | bytes 73736 | tf_op jit(solution)/shard_map/ppermute | solution.py:328
  145.9 3.0 %collective-permute-start.33 = (f32[48,128]{1,0:T(8,128)S(1)}, f32[48,128]{1,0:T(8,128)S(1)}, u32[]{:S(2)}, u32[]{:S(2)}) collective-permute-start(f32[48,128]{1,0:T(8,128)S(1)} %add.217), channel_id=1, source_target_pairs={{0,24},{8,0},{16,8},{24,16},{1,25},{9,1},{17,9},{25,17},{2,26},{10... | collective-permute-start | bytes 73736 | tf_op jit(solution)/shard_map/ppermute | solution.py:383
  146.8 4.3 %collective-permute-start.32 = (f32[48,128]{1,0:T(8,128)S(1)}, f32[48,128]{1,0:T(8,128)S(1)}, u32[]{:S(2)}, u32[]{:S(2)}) collective-permute-start(f32[48,128]{1,0:T(8,128)S(1)} %add.217), channel_id=1, source_target_pairs={{0,16},{8,24},{16,0},{24,8},{1,17},{9,25},{17,1},{25,9},{2,18},{10... | collective-permute-start | bytes 73736 | tf_op jit(solution)/shard_map/ppermute | solution.py:383
  146.8 4.7 %collective-permute-start.31 = (f32[48,128]{1,0:T(8,128)S(1)}, f32[48,128]{1,0:T(8,128)S(1)}, u32[]{:S(2)}, u32[]{:S(2)}) collective-permute-start(f32[48,128]{1,0:T(8,128)S(1)} %add.217), channel_id=1, source_target_pairs={{0,8},{8,16},{16,24},{24,0},{1,9},{9,17},{17,25},{25,1},{2,10},{10... | collective-permute-start | bytes 73736 | tf_op jit(solution)/shard_map/ppermute | solution.py:383
  153.2 14.5 %collective-permute-start.36 = (f32[2,128,512]{1,2,0:T(8,128)S(1)}, f32[2,128,512]{1,2,0:T(8,128)S(1)}, u32[]{:S(2)}, u32[]{:S(2)}) collective-permute-start(f32[2,128,512]{1,2,0:T(8,128)S(1)} %bitcast.52), channel_id=1, source_target_pairs={{0,1},{1,0},{2,3},{3,2},{4,5},{5,4},{6,7},{7,6},{8,9},{9,8},{10,11... | collective-permute-start | bytes 1572872 | tf_op jit(solution)/shard_map/ppermute | solution.py:28
  160.5 3.9 %collective-permute-start.39 = (f32[48,128]{1,0:T(8,128)S(1)}, f32[48,128]{1,0:T(8,128)S(1)}, u32[]{:S(2)}, u32[]{:S(2)}) collective-permute-start(f32[48,128]{1,0:T(8,128)S(1)} %add_add_fusion.4), channel_id=1, source_target_pairs={{2,0},{4,2},{6,4},{0,6},{3,1},{5,3},{7,5},{1,7},{10,8},{12,10},{14... | collective-permute-start | bytes 73736 | tf_op jit(solution)/shard_map/ppermute | solution.py:361
  163.5 4.2 %collective-permute-start.38 = (f32[48,128]{1,0:T(8,128)S(1)}, f32[48,128]{1,0:T(8,128)S(1)}, u32[]{:S(2)}, u32[]{:S(2)}) collective-permute-start(f32[48,128]{1,0:T(8,128)S(1)} %add_add_fusion.4), channel_id=1, source_target_pairs={{4,0},{6,2},{0,4},{2,6},{5,1},{7,3},{1,5},{3,7},{12,8},{14,10},{8,... | collective-permute-start | bytes 73736 | tf_op jit(solution)/shard_map/ppermute | solution.py:361
  163.5 4.2 %collective-permute-start.37 = (f32[48,128]{1,0:T(8,128)S(1)}, f32[48,128]{1,0:T(8,128)S(1)}, u32[]{:S(2)}, u32[]{:S(2)}) collective-permute-start(f32[48,128]{1,0:T(8,128)S(1)} %add_add_fusion.4), channel_id=1, source_target_pairs={{6,0},{0,2},{2,4},{4,6},{7,1},{1,3},{3,5},{5,7},{14,8},{8,10},{10,... | collective-permute-start | bytes 73736 | tf_op jit(solution)/shard_map/ppermute | solution.py:361
  168.9 3.0 %collective-permute-start.40 = (f32[192,128]{1,0:T(8,128)S(1)}, f32[192,128]{1,0:T(8,128)S(1)}, u32[]{:S(2)}, u32[]{:S(2)}) collective-permute-start(f32[192,128]{1,0:T(8,128)S(1)} %maximum_add_fusion), channel_id=1, source_target_pairs={{0,1},{1,0},{2,3},{3,2},{4,5},{5,4},{6,7},{7,6},{8,9},{9,8},{10,11... | collective-permute-start | bytes 294920 | tf_op jit(solution)/shard_map/ppermute | solution.py:28
  170.5 1.4 copy-start.3

commit v7 on v6

--- a/solution.py
+++ b/solution.py
@@ -332,11 +332,7 @@
     count = lax.axis_size(TILE[0])
     stride = 1
     while stride < count:
-        arrived = part
-        hops = 2 if stride > 2 else 1
-        for _ in range(hops):
-            arrived = moved_along(arrived, stride // hops)
-        part = part + arrived
+        part = part + moved_along(part, stride)
         stride *= 2
     return part
 
@@ -369,7 +365,8 @@
 
 
 def after(value, other):
-    return value + jnp.minimum(jnp.abs(other[(0,) * other.ndim]), 0.0)
+    line = other[(0,) * (other.ndim - 1)][:PATCH]
+    return value + jnp.minimum(jnp.abs(line), 0.0)
 
 
 def shifts_among(value, axis, stride, fan):

time: 176 us -> 162 us (0.920); the launches traced: 173 us -> 162 us
  Pallas kernels: 24.4 us -> 19.5 us
  between operations: 4.33 us -> 1.74 us
  waiting for transfers between devices: 63.9 us -> 61.7 us
  local copies, waits for them, and re-layouts: 8.31 us -> 6.23 us
    pallas_call x2, Pallas kernels: 24.4 us -> 19.5 us  [run_positions(): pl.pallas_call(kernel, out_shape=(quarter,) * 4 + (pieces_of,) * 2, in_sp...]
    ppermute x4, starting transfers between devices: 13.5 us -> 18.2 us  [from_tile(): lax.ppermute(value, TILE, [((i + distance) % count, i) for i in range(cou...]
    ppermute x8 -> x6, starting transfers between devices: 6.68 us -> 2.4 us  [moved_along(): return lax.ppermute(value, TILE, route)]
    ppermute x11, waiting for transfers between devices: 5.76 us -> 3.55 us  [swapped(): return lax.ppermute(value, 'pos', [(0, 1), (1, 0)])]
    slice x4 -> x0, local copies, waits for them, and re-layouts: 2.05 us -> none  [after(): return value + jnp.minimum(jnp.abs(other[(0,) * other.ndim]), 0.0)]
    ppermute x8 -> x6, waiting for transfers between devices: 31.6 us -> 29.7 us  [moved_along(): return lax.ppermute(value, TILE, route)]
    ppermute x4, waiting for transfers between devices: 10.6 us -> 12.5 us  [from_tile(): lax.ppermute(value, TILE, [((i + distance) % count, i) for i in range(cou...]
  transfers between devices with their start and end apart: 41 -> 39, of which waited for: 23 -> 22; matrix products, arithmetic and copies ran while one was open for 7% -> 6% of each run, Pallas kernels for 0% -> 0%
where the time goes in v7:
time: 162 us
  starting transfers between devices  63.4 us (39%)
  waiting for transfers between devices  61.7 us (38%)
  Pallas kernels  19.5 us (12%)
  other arithmetic  9.5 us (6%)
  local copies, waits for them, and re-layouts  6.23 us (4%)
  between operations  1.74 us (1%)
    ppermute x6, waiting for transfers between devices, moved_along(): return lax.ppermute(value, TILE, route)  29.7 us
    ppermute x11, starting transfers between devices, swapped(): return lax.ppermute(value, 'pos', [(0, 1), (1, 0)])  29.1 us
    pallas_call x2, Pallas kernels, run_positions(): pl.pallas_call(kernel, out_shape=(quarter,) * 4 + (pieces_of,) * 2, in_sp...  19.5 us
    ppermute x4, starting transfers between devices, from_tile(): lax.ppermute(value, TILE, [((i + distance) % count, i) for i in range(cou...  18.2 us
    ppermute x4, waiting for transfers between devices, from_tile(): lax.ppermute(value, TILE, [((i + distance) % count, i) for i in range(cou...  12.5 us
    ppermute x6, waiting for transfers between devices, scattered_over(): arrived.append(lax.ppermute(pieces[step], axis, route))  6.8 us
    ppermute x6, starting transfers between devices, scattered_over(): arrived.append(lax.ppermute(pieces[step], axis, route))  6.14 us
    ppermute x6, waiting for transfers between devices, shifts_among(): total = total + lax.ppermute(value, axis, route)  5.64 us
  transfers between devices with their start and end apart: 39, of which 22 were waited for; matrix products, arithmetic and copies ran while one was open for 6% of the time, Pallas kernels for 0%

profile of v7, /device:TPU:1, one launch (start us, length us, event | category | flops | bytes accessed | tf_op | source)
XLA Modules:
  0.0 162.1 jit_solution(7240299274447097810)
XLA Ops:
  0.6 1.1 constant_dynamic-slice_fusion
  1.7 11.1 %collective-permute-start = (f32[2,128,512]{2,1,0:T(8,128)S(1)}, f32[2,128,512]{2,1,0:T(8,128)S(1)}, u32[]{:S(2)}, u32[]{:S(2)}) collective-permute-start(f32[2,128,512]{2,1,0:T(8,128)S(1)} %constant_dynamic-slice_fusion), channel_id=1, source_target_pairs={{2,0},{4,2},{6,4},{8,6},{10,8},{12,10},{14,12},{16,14},{18,16},{20... | collective-permute-start | bytes 1572872 | tf_op jit(solution)/shard_map/ppermute | solution.py:33
  12.8 10.6 %collective-permute-done.refs_7_ = f32[2,128,512]{2,1,0:T(8,128)S(1)} collective-permute-done((f32[2,128,512]{2,1,0:T(8,128)S(1)}, f32[2,128,512]{2,1,0:T(8,128)S(1)}, u32[]{:S(2)}, u32[]{:S(2)}) %collective-permute-start) | collective-permute-done | bytes 524320 | tf_op jit(solution)/shard_map/ppermute | solution.py:33
  23.4 1.5 collective-permute-start.1
  25.6 0.9 collective-permute-done.1.refs_8_
  26.5 0.8 copy-done.6
  27.3 9.8 %positions.2 = (f32[3,4,128,128]{3,2,1,0:T(8,128)}, f32[3,4,128,128]{3,2,1,0:T(8,128)}, f32[3,4,128,128]{3,2,1,0:T(8,128)}, f32[3,4,128,128]{3,2,1,0:T(8,128)}, ...) custom-call(s32[1,1,32]{2,1,0:T(1,128)} %refs_0_.3, s32[1,1,32]{2,1,0:T(1,128)} %refs_1_.3, s32[1,1]{1,0:T(1,128)S(6)} %copy.21.refs_2_, ...), custom_call_target="tpu_custom_call" | custom-call | flops 12999999488 | bytes 8388608 | tf_op jit(solution)/shard_map/positions/pallas_call | solution.py:275
  37.1 5.5 %collective-permute-start.2 = (f32[4,48,128]{2,1,0:T(8,128)}, f32[4,48,128]{2,1,0:T(8,128)S(1)}, u32[]{:S(2)}, u32[]{:S(2)}) collective-permute-start(f32[4,48,128]{2,1,0:T(8,128)} %get-tuple-element.19), channel_id=1, source_target_pairs={{0,1},{1,0},{2,3},{3,2},{4,5},{5,4},{6,7},{7,6},{8,9},{9,8},{10,11... | collective-permute-start | bytes 294920 | tf_op jit(solution)/shard_map/ppermute | solution.py:28
  42.6 0.4 collective-permute-start.17
  43.1 0.6 collective-permute-done.2
  43.7 0.9 add.194
  44.7 2.7 %collective-permute-start.5 = (f32[48,128]{1,0:T(8,128)S(1)}, f32[48,128]{1,0:T(8,128)S(1)}, u32[]{:S(2)}, u32[]{:S(2)}) collective-permute-start(f32[48,128]{1,0:T(8,128)S(1)} %get-tuple-element.56), channel_id=1, source_target_pairs={{0,6},{2,0},{4,2},{6,4},{1,7},{3,1},{5,3},{7,5},{8,14},{10,8},{12,... | collective-permute-start | bytes 73736 | tf_op jit(solution)/shard_map/ppermute | solution.py:345
  47.4 1.2 collective-permute-done.3
  48.6 3.0 %collective-permute-done.4 = f32[48,128]{1,0:T(8,128)S(1)} collective-permute-done((f32[48,128]{1,0:T(8,128)S(1)}, f32[48,128]{1,0:T(8,128)S(1)}, u32[]{:S(2)}, u32[]{:S(2)}) %collective-permute-start.4) | collective-permute-done | bytes 24608 | tf_op jit(solution)/shard_map/ppermute | solution.py:345
  51.6 1.6 %add_add_fusion.2 = (f32[3,4,128,128]{3,2,1,0:T(8,128)S(1)}, f32[3,4,128,128]{3,2,1,0:T(8,128)S(1)}) fusion(f32[3,4,128,128]{3,2,1,0:T(8,128)} %get-tuple-element.22, f32[3,4,128,128]{3,2,1,0:T(8,128)S(1)} %collective-permute-done.17, f32[128]{0:T(128)S(1)} %fusion.20, f32[3,4,128,128]{3,2,1,0:T(8,128)} %get-tuple-element.20, ...), kind=kLoop, calls=%fused_computation.4 | loop fusion | flops 786432 | bytes 4719104 | tf_op jit(solution)/shard_map/add | solution.py:369
  53.3 6.9 %collective-permute-start.19 = (f32[3,4,128,128]{3,2,1,0:T(8,128)S(1)}, f32[3,4,128,128]{3,2,1,0:T(8,128)}, u32[]{:S(2)}, u32[]{:S(2)}) collective-permute-start(f32[3,4,128,128]{3,2,1,0:T(8,128)S(1)} %get-tuple-element.24), channel_id=1, source_target_pairs={{2,0},{4,2},{6,4},{8,6},{10,8},{12,10},{14,12},{16,14},{18,16},{20... | collective-permute-start | bytes 2359304 | tf_op jit(solution)/shard_map/ppermute | solution.py:33
  60.2 4.3 %collective-permute-done.6 = f32[48,128]{1,0:T(8,128)S(1)} collective-permute-done((f32[48,128]{1,0:T(8,128)S(1)}, f32[48,128]{1,0:T(8,128)S(1)}, u32[]{:S(2)}, u32[]{:S(2)}) %collective-permute-start.6) | collective-permute-done | bytes 24608 | tf_op jit(solution)/shard_map/ppermute | solution.py:328
  64.5 5.2 %collective-permute-done.7 = f32[48,128]{1,0:T(8,128)S(1)} collective-permute-done((f32[48,128]{1,0:T(8,128)S(1)}, f32[48,128]{1,0:T(8,128)S(1)}, u32[]{:S(2)}, u32[]{:S(2)}) %collective-permute-start.7) | collective-permute-done | bytes 24608 | tf_op jit(solution)/shard_map/ppermute | solution.py:328
  69.7 1.1 collective-permute-start.8
  70.8 5.8 %collective-permute-done.8 = f32[48,128]{1,0:T(8,128)S(1)} collective-permute-done((f32[48,128]{1,0:T(8,128)S(1)}, f32[48,128]{1,0:T(8,128)S(1)}, u32[]{:S(2)}, u32[]{:S(2)}) %collective-permute-start.8) | collective-permute-done | bytes 24608 | tf_op jit(solution)/shard_map/ppermute | solution.py:328
  76.8 1.4 collective-permute-start.9
  78.1 0.2 copy.15
  78.3 0.2 copy.16
  78.6 1.2 copy.17
  79.8 0.2 copy.18
  80.0 1.2 collective-permute-done.10
  81.2 0.5 collective-permute-done.9
  82.0 1.4 collective-permute-start.12
  83.3 1.2 add.214
  84.6 1.2 add.217
  85.8 0.2 fusion.2
  86.1 7.1 %collective-permute-start.20 = (f32[2,4,256,128]{3,2,1,0:T(8,128)S(1)}, f32[2,4,256,128]{3,2,1,0:T(8,128)S(1)}, u32[]{:S(2)}, u32[]{:S(2)}) collective-permute-start(f32[2,4,256,128]{3,2,1,0:T(8,128)S(1)} %pad_maximum_fusion.refs_6_), channel_id=1, source_target_pairs={{0,1},{1,0},{2,3},{3,2},{4,5},{5,4},{6,7},{7,6},{8,9},{9,8},{10,11... | collective-permute-start | bytes 3145736 | tf_op jit(solution)/shard_map/ppermute | solution.py:28
  93.3 1.6 %collective-permute-start.15 = (f32[192,128]{1,0:T(8,128)S(1)}, f32[192,128]{1,0:T(8,128)S(1)}, u32[]{:S(2)}, u32[]{:S(2)}) collective-permute-start(f32[192,128]{1,0:T(8,128)S(1)} %pad_maximum_fusion.4), channel_id=1, source_target_pairs={{0,1},{1,0},{2,3},{3,2},{4,5},{5,4},{6,7},{7,6},{8,9},{9,8},{10,11... | collective-permute-start | bytes 294920 | tf_op jit(solution)/shard_map/ppermute | solution.py:28
  94.9 0.9 collective-permute-done.15
  95.9 0.7 add_divide_fusion.1.refs_3_
  96.6 1.0 copy-done.5
  97.6 9.8 %positions.3 = (f32[3,4,128,128]{3,2,1,0:T(8,128)}, f32[3,4,128,128]{3,2,1,0:T(8,128)}, f32[3,4,128,128]{3,2,1,0:T(8,128)}, f32[3,4,128,128]{3,2,1,0:T(8,128)}, ...) custom-call(s32[1,1,32]{2,1,0:T(1,128)} %refs_0_.3, s32[1,1,32]{2,1,0:T(1,128)} %refs_1_.3, s32[1,1]{1,0:T(1,128)S(6)} %copy.21.refs_2_, ...), custom_call_target="tpu_custom_call" | custom-call | flops 12999999488 | bytes 8388608 | tf_op jit(solution)/shard_map/positions/pallas_call | solution.py:275
  107.4 5.4 %collective-permute-start.22 = (f32[4,48,128]{2,1,0:T(8,128)}, f32[4,48,128]{2,1,0:T(8,128)S(1)}, u32[]{:S(2)}, u32[]{:S(2)}) collective-permute-start(f32[4,48,128]{2,1,0:T(8,128)} %get-tuple-element.31), channel_id=1, source_target_pairs={{0,1},{1,0},{2,3},{3,2},{4,5},{5,4},{6,7},{7,6},{8,9},{9,8},{10,11... | collective-permute-start | bytes 294920 | tf_op jit(solution)/shard_map/ppermute | solution.py:28
  112.9 1.1 collective-permute-done.22
  114.0 0.9 add.221
  114.9 1.1 collective-permute-start.23
  116.0 1.7 %collective-permute-start.25 = (f32[48,128]{1,0:T(8,128)S(1)}, f32[48,128]{1,0:T(8,128)S(1)}, u32[]{:S(2)}, u32[]{:S(2)}) collective-permute-start(f32[48,128]{1,0:T(8,128)S(1)} %get-tuple-element.49), channel_id=1, source_target_pairs={{0,6},{2,0},{4,2},{6,4},{1,7},{3,1},{5,3},{7,5},{8,14},{10,8},{12,... | collective-permute-start | bytes 73736 | tf_op jit(solution)/shard_map/ppermute | solution.py:345
  117.6 0.6 collective-permute-start.24
  118.3 0.9 collective-permute-start.21
  119.2 2.6 %collective-permute-done.24 = f32[48,128]{1,0:T(8,128)S(1)} collective-permute-done((f32[48,128]{1,0:T(8,128)S(1)}, f32[48,128]{1,0:T(8,128)S(1)}, u32[]{:S(2)}, u32[]{:S(2)}) %collective-permute-start.24) | collective-permute-done | bytes 24608 | tf_op jit(solution)/shard_map/ppermute | solution.py:345
  121.9 1.2 add_add_fusion
  123.3 3.9 %collective-permute-done.26 = f32[48,128]{1,0:T(8,128)S(1)} collective-permute-done((f32[48,128]{1,0:T(8,128)S(1)}, f32[48,128]{1,0:T(8,128)S(1)}, u32[]{:S(2)}, u32[]{:S(2)}) %collective-permute-start.26) | collective-permute-done | bytes 24608 | tf_op jit(solution)/shard_map/ppermute | solution.py:328
  127.2 4.8 %collective-permute-done.27 = f32[48,128]{1,0:T(8,128)S(1)} collective-permute-done((f32[48,128]{1,0:T(8,128)S(1)}, f32[48,128]{1,0:T(8,128)S(1)}, u32[]{:S(2)}, u32[]{:S(2)}) %collective-permute-start.27) | collective-permute-done | bytes 24608 | tf_op jit(solution)/shard_map/ppermute | solution.py:328
  131.9 1.2 collective-permute-start.28
  133.1 5.7 %collective-permute-done.28 = f32[48,128]{1,0:T(8,128)S(1)} collective-permute-done((f32[48,128]{1,0:T(8,128)S(1)}, f32[48,128]{1,0:T(8,128)S(1)}, u32[]{:S(2)}, u32[]{:S(2)}) %collective-permute-start.28) | collective-permute-done | bytes 24608 | tf_op jit(solution)/shard_map/ppermute | solution.py:328
  138.9 1.4 collective-permute-start.29
  140.3 1.5 collective-permute-done.31
  141.8 1.6 collective-permute-done.30
  143.4 0.8 collective-permute-done.29
  144.2 1.9 %collective-permute-done.33 = f32[3,4,128,128]{3,2,1,0:T(8,128)S(1)} collective-permute-done((f32[3,4,128,128]{3,2,1,0:T(8,128)S(1)}, f32[3,4,128,128]{3,2,1,0:T(8,128)S(1)}, u32[]{:S(2)}, u32[]{:S(2)}) %collective-permute-start.33) | collective-permute-done | bytes 786464 | tf_op jit(solution)/shard_map/ppermute | solution.py:33
  146.4 0.2 copy.19
  146.6 4.8 %collective-permute-start.34 = (f32[2,128,512]{1,2,0:T(8,128)S(1)}, f32[2,128,512]{1,2,0:T(8,128)S(1)}, u32[]{:S(2)}, u32[]{:S(2)}) collective-permute-start(f32[2,128,512]{1,2,0:T(8,128)S(1)} %bitcast.54), channel_id=1, source_target_pairs={{0,1},{1,0},{2,3},{3,2},{4,5},{5,4},{6,7},{7,6},{8,9},{9,8},{10,11... | collective-permute-start | bytes 1572872 | tf_op jit(solution)/shard_map/ppermute | solution.py:28
  151.4 2.6 %collective-permute-start.37 = (f32[48,128]{1,0:T(8,128)S(1)}, f32[48,128]{1,0:T(8,128)S(1)}, u32[]{:S(2)}, u32[]{:S(2)}) collective-permute-start(f32[48,128]{1,0:T(8,128)S(1)} %add_add_fusion.4), channel_id=1, source_target_pairs={{2,0},{4,2},{6,4},{0,6},{3,1},{5,3},{7,5},{1,7},{10,8},{12,10},{14... | collective-permute-start | bytes 73736 | tf_op jit(solution)/shard_map/ppermute | solution.py:357
  154.0 0.6 collective-permute-start.35
  154.5 0.4 collective-permute-done.37
  154.9 3.2 %collective-permute-done.36 = f32[48,128]{1,0:T(8,128)S(1)} collective-permute-done((f32[48,128]{1,0:T(8,128)S(1)}, f32[48,128]{1,0:T(8,128)S(1)}, u32[]{:S(2)}, u32[]{:S(2)}) %collective-permute-start.36) | collective-permute-done | bytes 24608 | tf_op jit(solution)/shard_map/ppermute | solution.py:357
  158.4 1.6 collective-permute-start.38
  160.0 1.3 copy.20
  161.4 0.7 add_divide_fusion
  (80 shorter events, 1.8 us)
Async XLA Ops:
  1.7 21.7 %collective-permute-start = (f32[2,128,512]{2,1,0:T(8,128)S(1)}, f32[2,128,512]{2,1,0:T(8,128)S(1)}, u32[]{:S(2)}, u32[]{:S(2)}) collective-permute-start(f32[2,128,512]{2,1,0:T(8,128)S(1)} %constant_dynamic-slice_fusion), channel_id=1, source_target_pairs={{2,0},{4,2},{6,4},{8,6},{10,8},{12,10},{14,12},{16,14},{18,16},{20... | collective-permute-start | bytes 1572872 | tf_op jit(solution)/shard_map/ppermute | solution.py:33
  23.4 3.1 %copy-start.3 = (f32[2,128,512]{2,1,0:T(8,128)}, f32[2,128,512]{2,1,0:T(8,128)S(1)}, u32[]{:S(2)}) copy-start(f32[2,128,512]{2,1,0:T(8,128)S(1)} %collective-permute-done.refs_7_) | copy-start | bytes 1572868
  23.4 3.1 %collective-permute-start.1 = (f32[2,128,512]{2,1,0:T(8,128)S(1)}, f32[2,128,512]{2,1,0:T(8,128)S(1)}, u32[]{:S(2)}, u32[]{:S(2)}) collective-permute-start(f32[2,128,512]{2,1,0:T(8,128)S(1)} %collective-permute-done.refs_7_), channel_id=1, source_target_pairs={{0,1},{1,0},{2,3},{3,2},{4,5},{5,4},{6,7},{7,6},{8,9},{9,8},{10,11... | collective-permute-start | bytes 1572872 | tf_op jit(solution)/shard_map/ppermute | solution.py:28
  26.5 0.8 copy-start.6
  37.1 6.6 %collective-permute-start.2 = (f32[4,48,128]{2,1,0:T(8,128)}, f32[4,48,128]{2,1,0:T(8,128)S(1)}, u32[]{:S(2)}, u32[]{:S(2)}) collective-permute-start(f32[4,48,128]{2,1,0:T(8,128)} %get-tuple-element.19), channel_id=1, source_target_pairs={{0,1},{1,0},{2,3},{3,2},{4,5},{5,4},{6,7},{7,6},{8,9},{9,8},{10,11... | collective-permute-start | bytes 294920 | tf_op jit(solution)/shard_map/ppermute | solution.py:28
  42.5 9.0 %collective-permute-start.16 = (f32[3,4,128,128]{3,2,1,0:T(8,128)}, f32[3,4,128,128]{3,2,1,0:T(8,128)S(1)}, u32[]{:S(2)}, u32[]{:S(2)}) collective-permute-start(f32[3,4,128,128]{3,2,1,0:T(8,128)} %get-tuple-element.21), channel_id=1, source_target_pairs={{0,1},{1,0},{2,3},{3,2},{4,5},{5,4},{6,7},{7,6},{8,9},{9,8},{10,11... | collective-permute-start | bytes 2359304 | tf_op jit(solution)/shard_map/ppermute | solution.py:28
  42.6 9.0 %collective-permute-start.17 = (f32[3,4,128,128]{3,2,1,0:T(8,128)}, f32[3,4,128,128]{3,2,1,0:T(8,128)S(1)}, u32[]{:S(2)}, u32[]{:S(2)}) collective-permute-start(f32[3,4,128,128]{3,2,1,0:T(8,128)} %get-tuple-element.23), channel_id=1, source_target_pairs={{0,1},{1,0},{2,3},{3,2},{4,5},{5,4},{6,7},{7,6},{8,9},{9,8},{10,11... | collective-permute-start | bytes 2359304 | tf_op jit(solution)/shard_map/ppermute | solution.py:28
  44.6 4.0 %collective-permute-start.3 = (f32[48,128]{1,0:T(8,128)S(1)}, f32[48,128]{1,0:T(8,128)S(1)}, u32[]{:S(2)}, u32[]{:S(2)}) collective-permute-start(f32[48,128]{1,0:T(8,128)S(1)} %get-tuple-element.55), channel_id=1, source_target_pairs={{0,2},{2,4},{4,6},{6,0},{1,3},{3,5},{5,7},{7,1},{8,10},{10,12},{12... | collective-permute-start | bytes 73736 | tf_op jit(solution)/shard_map/ppermute | solution.py:345
  44.7 3.9 %collective-permute-start.5 = (f32[48,128]{1,0:T(8,128)S(1)}, f32[48,128]{1,0:T(8,128)S(1)}, u32[]{:S(2)}, u32[]{:S(2)}) collective-permute-start(f32[48,128]{1,0:T(8,128)S(1)} %get-tuple-element.56), channel_id=1, source_target_pairs={{0,6},{2,0},{4,2},{6,4},{1,7},{3,1},{5,3},{7,5},{8,14},{10,8},{12,... | collective-permute-start | bytes 73736 | tf_op jit(solution)/shard_map/ppermute | solution.py:345
  47.4 4.2 %collective-permute-start.4 = (f32[48,128]{1,0:T(8,128)S(1)}, f32[48,128]{1,0:T(8,128)S(1)}, u32[]{:S(2)}, u32[]{:S(2)}) collective-permute-start(f32[48,128]{1,0:T(8,128)S(1)} %get-tuple-element.57), channel_id=1, source_target_pairs={{0,4},{2,6},{4,0},{6,2},{1,5},{3,7},{5,1},{7,3},{8,12},{10,14},{12... | collective-permute-start | bytes 73736 | tf_op jit(solution)/shard_map/ppermute | solution.py:345
  53.2 30.1 %collective-permute-start.18 = (f32[3,4,128,128]{3,2,1,0:T(8,128)S(1)}, f32[3,4,128,128]{3,2,1,0:T(8,128)}, u32[]{:S(2)}, u32[]{:S(2)}) collective-permute-start(f32[3,4,128,128]{3,2,1,0:T(8,128)S(1)} %get-tuple-element.26), channel_id=1, source_target_pairs={{254,0},{0,2},{2,4},{4,6},{6,8},{8,10},{10,12},{12,14},{14,16},{16... | collective-permute-start | bytes 2359304 | tf_op jit(solution)/shard_map/ppermute | solution.py:33
  53.3 30.0 %collective-permute-start.19 = (f32[3,4,128,128]{3,2,1,0:T(8,128)S(1)}, f32[3,4,128,128]{3,2,1,0:T(8,128)}, u32[]{:S(2)}, u32[]{:S(2)}) collective-permute-start(f32[3,4,128,128]{3,2,1,0:T(8,128)S(1)} %get-tuple-element.24), channel_id=1, source_target_pairs={{2,0},{4,2},{6,4},{8,6},{10,8},{12,10},{14,12},{16,14},{18,16},{20... | collective-permute-start | bytes 2359304 | tf_op jit(solution)/shard_map/ppermute | solution.py:33
  60.2 4.3 %collective-permute-start.6 = (f32[48,128]{1,0:T(8,128)S(1)}, f32[48,128]{1,0:T(8,128)S(1)}, u32[]{:S(2)}, u32[]{:S(2)}) collective-permute-start(f32[48,128]{1,0:T(8,128)S(1)} %fusion.14), channel_id=1, source_target_pairs={{0,32},{2,226},{4,228},{6,230},{8,232},{10,234},{12,236},{14,238},... | collective-permute-start | bytes 73736 | tf_op jit(solution)/shard_map/ppermute | solution.py:328
  64.5 5.2 %collective-permute-start.7 = (f32[48,128]{1,0:T(8,128)S(1)}, f32[48,128]{1,0:T(8,128)S(1)}, u32[]{:S(2)}, u32[]{:S(2)}) collective-permute-start(f32[48,128]{1,0:T(8,128)S(1)} %add.198), channel_id=1, source_target_pairs={{0,64},{2,194},{4,196},{6,198},{8,200},{10,202},{12,204},{14,206},... | collective-permute-start | bytes 73736 | tf_op jit(solution)/shard_map/ppermute | solution.py:328
  69.7 7.0 %collective-permute-start.8 = (f32[48,128]{1,0:T(8,128)S(1)}, f32[48,128]{1,0:T(8,128)S(1)}, u32[]{:S(2)}, u32[]{:S(2)}) collective-permute-start(f32[48,128]{1,0:T(8,128)S(1)} %add.199), channel_id=1, source_target_pairs={{0,128},{2,130},{4,132},{6,134},{8,136},{10,138},{12,140},{14,142}... | collective-permute-start | bytes 73736 | tf_op jit(solution)/shard_map/ppermute | solution.py:328
  76.7 3.3 %collective-permute-start.11 = (f32[48,128]{1,0:T(8,128)S(1)}, f32[48,128]{1,0:T(8,128)S(1)}, u32[]{:S(2)}, u32[]{:S(2)}) collective-permute-start(f32[48,128]{1,0:T(8,128)S(1)} %add.200), channel_id=1, source_target_pairs={{0,24},{8,0},{16,8},{24,16},{1,25},{9,1},{17,9},{25,17},{2,26},{10... | collective-permute-start | bytes 73736 | tf_op jit(solution)/shard_map/ppermute | solution.py:380
  76.7 4.6 %collective-permute-start.10 = (f32[48,128]{1,0:T(8,128)S(1)}, f32[48,128]{1,0:T(8,128)S(1)}, u32[]{:S(2)}, u32[]{:S(2)}) collective-permute-start(f32[48,128]{1,0:T(8,128)S(1)} %add.200), channel_id=1, source_target_pairs={{0,16},{8,24},{16,0},{24,8},{1,17},{9,25},{17,1},{25,9},{2,18},{10... | collective-permute-start | bytes 73736 | tf_op jit(solution)/shard_map/ppermute | solution.py:380
  76.8 5.0 %collective-permute-start.9 = (f32[48,128]{1,0:T(8,128)S(1)}, f32[48,128]{1,0:T(8,128)S(1)}, u32[]{:S(2)}, u32[]{:S(2)}) collective-permute-start(f32[48,128]{1,0:T(8,128)S(1)} %add.200), channel_id=1, source_target_pairs={{0,8},{8,16},{16,24},{24,0},{1,9},{9,17},{17,25},{25,1},{2,10},{10... | collective-permute-start | bytes 73736 | tf_op jit(solution)/shard_map/ppermute | solution.py:380
  81.8 11.4 %collective-permute-start.14 = (f32[48,128]{1,0:T(8,128)S(1)}, f32[48,128]{1,0:T(8,128)S(1)}, u32[]{:S(2)}, u32[]{:S(2)}) collective-permute-start(f32[48,128]{1,0:T(8,128)S(1)} %add_add_fusion.5), channel_id=1, source_target_pairs={{2,0},{4,2},{6,4},{0,6},{3,1},{5,3},{7,5},{1,7},{10,8},{12,10},{14... | collective-permute-start | bytes 73736 | tf_op jit(solution)/shard_map/ppermute | solution.py:357
  81.9 11.4 %collective-permute-start.13 = (f32[48,128]{1,0:T(8,128)S(1)}, f32[48,128]{1,0:T(8,128)S(1)}, u32[]{:S(2)}, u32[]{:S(2)}) collective-permute-start(f32[48,128]{1,0:T(8,128)S(1)} %add_add_fusion.5), channel_id=1, source_target_pairs={{4,0},{6,2},{0,4},{2,6},{5,1},{7,3},{1,5},{3,7},{12,8},{14,10},{8,... | collective-permute-start | bytes 73736 | tf_op jit(solution)/shard_map/ppermute | solution.py:357
  82.0 11.3 %collective-permute-start.12 = (f32[48,128]{1,0:T(8,128)S(1)}, f32[48,128]{1,0:T(8,128)S(1)}, u32[]{:S(2)}, u32[]{:S(2)}) collective-permute-start(f32[48,128]{1,0:T(8,128)S(1)} %add_add_fusion.5), channel_id=1, source_target_pairs={{6,0},{0,2},{2,4},{4,6},{7,1},{1,3},{3,5},{5,7},{14,8},{8,10},{10,... | collective-permute-start | bytes 73736 | tf_op jit(solution)/shard_map/ppermute | solution.py:357
  86.0 9.9 %copy-start.4 = (f32[2,128,128]{2,1,0:T(8,128)S(1)}, f32[2,128,128]{2,1,0:T(8,128)}, u32[]{:S(2)}) copy-start(f32[2,128,128]{2,1,0:T(8,128)} %refs_3_.1) | copy-start | bytes 393220
  86.1 10.5 %copy-start = (f32[2,4,256,128]{3,2,1,0:T(8,128)}, f32[2,4,256,128]{3,2,1,0:T(8,128)S(1)}, u32[]{:S(2)}) copy-start(f32[2,4,256,128]{3,2,1,0:T(8,128)S(1)} %pad_maximum_fusion.refs_6_) | copy-start | bytes 3145732
  86.1 10.5 %collective-permute-start.20 = (f32[2,4,256,128]{3,2,1,0:T(8,128)S(1)}, f32[2,4,256,128]{3,2,1,0:T(8,128)S(1)}, u32[]{:S(2)}, u32[]{:S(2)}) collective-permute-start(f32[2,4,256,128]{3,2,1,0:T(8,128)S(1)} %pad_maximum_fusion.refs_6_), channel_id=1, source_target_pairs={{0,1},{1,0},{2,3},{3,2},{4,5},{5,4},{6,7},{7,6},{8,9},{9,8},{10,11... | collective-permute-start | bytes 3145736 | tf_op jit(solution)/shard_map/ppermute | solution.py:28
  93.3 2.6 %collective-permute-start.15 = (f32[192,128]{1,0:T(8,128)S(1)}, f32[192,128]{1,0:T(8,128)S(1)}, u32[]{:S(2)}, u32[]{:S(2)}) collective-permute-start(f32[192,128]{1,0:T(8,128)S(1)} %pad_maximum_fusion.4), channel_id=1, source_target_pairs={{0,1},{1,0},{2,3},{3,2},{4,5},{5,4},{6,7},{7,6},{8,9},{9,8},{10,11... | collective-permute-start | bytes 294920 | tf_op jit(solution)/shard_map/ppermute | solution.py:28
  96.6 1.0 copy-start.5
  107.4 38.7 %copy-start.1 = (f32[3,4,128,128]{3,2,1,0:T(8,128)S(1)}, f32[3,4,128,128]{3,2,1,0:T(8,128)}, u32[]{:S(2)}) copy-start(f32[3,4,128,128]{3,2,1,0:T(8,128)} %get-tuple-element.28) | copy-start | bytes 2359300
  107.4 6.6 %collective-permute-start.22 = (f32[4,48,128]{2,1,0:T(8,128)}, f32[4,48,128]{2,1,0:T(8,128)S(1)}, u32[]{:S(2)}, u32[]{:S(2)}) collective-permute-start(f32[4,48,128]{2,1,0:T(8,128)} %get-tuple-element.31), channel_id=1, source_target_pairs={{0,1},{1,0},{2,3},{3,2},{4,5},{5,4},{6,7},{7,6},{8,9},{9,8},{10,11... | collective-permute-start | bytes 294920 | tf_op jit(solution)/shard_map/ppermute | solution.py:28
  112.8 9.0 %collective-permute-start.32 = (f32[3,4,128,128]{3,2,1,0:T(8,128)}, f32[3,4,128,128]{3,2,1,0:T(8,128)S(1)}, u32[]{:S(2)}, u32[]{:S(2)}) collective-permute-start(f32[3,4,128,128]{3,2,1,0:T(8,128)} %get-tuple-element.33), channel_id=1, source_target_pairs={{0,1},{1,0},{2,3},{3,2},{4,5},{5,4},{6,7},{7,6},{8,9},{9,8},{10,11... | collective-permute-start | bytes 2359304 | tf_op jit(solution)/shard_map/ppermute | solution.py:28
  114.9 4.3 %collective-permute-start.23 = (f32[48,128]{1,0:T(8,128)S(1)}, f32[48,128]{1,0:T(8,128)S(1)}, u32[]{:S(2)}, u32[]{:S(2)}) collective-permute-start(f32[48,128]{1,0:T(8,128)S(1)} %get-tuple-element.48), channel_id=1, source_target_pairs={{0,2},{2,4},{4,6},{6,0},{1,3},{3,5},{5,7},{7,1},{8,10},{10,12},{12... | collective-permute-start | bytes 73736 | tf_op jit(solution)/shard_map/ppermute | solution.py:345
  116.0 3.2 %collective-permute-start.25 = (f32[48,128]{1,0:T(8,128)S(1)}, f32[48,128]{1,0:T(8,128)S(1)}, u32[]{:S(2)}, u32[]{:S(2)}) collective-permute-start(f32[48,128]{1,0:T(8,128)S(1)} %get-tuple-element.49), channel_id=1, source_target_pairs={{0,6},{2,0},{4,2},{6,4},{1,7},{3,1},{5,3},{7,5},{8,14},{10,8},{12,... | collective-permute-start | bytes 73736 | tf_op jit(solution)/shard_map/ppermute | solution.py:345
  117.6 4.2 %collective-permute-start.24 = (f32[48,128]{1,0:T(8,128)S(1)}, f32[48,128]{1,0:T(8,128)S(1)}, u32[]{:S(2)}, u32[]{:S(2)}) collective-permute-start(f32[48,128]{1,0:T(8,128)S(1)} %get-tuple-element.50), channel_id=1, source_target_pairs={{0,4},{2,6},{4,0},{6,2},{1,5},{3,7},{5,1},{7,3},{8,12},{10,14},{12... | collective-permute-start | bytes 73736 | tf_op jit(solution)/shard_map/ppermute | solution.py:345
  118.3 25.9 %collective-permute-start.21 = (f32[3,4,128,128]{3,2,1,0:T(8,128)}, f32[3,4,128,128]{3,2,1,0:T(8,128)S(1)}, u32[]{:S(2)}, u32[]{:S(2)}) collective-permute-start(f32[3,4,128,128]{3,2,1,0:T(8,128)} %get-tuple-element.29), channel_id=1, source_target_pairs={{0,1},{1,0},{2,3},{3,2},{4,5},{5,4},{6,7},{7,6},{8,9},{9,8},{10,11... | collective-permute-start | bytes 2359304 | tf_op jit(solution)/shard_map/ppermute | solution.py:28
  123.1 23.0 %collective-permute-start.33 = (f32[3,4,128,128]{3,2,1,0:T(8,128)S(1)}, f32[3,4,128,128]{3,2,1,0:T(8,128)S(1)}, u32[]{:S(2)}, u32[]{:S(2)}) collective-permute-start(f32[3,4,128,128]{3,2,1,0:T(8,128)S(1)} %add_add_fusion), channel_id=1, source_target_pairs={{254,0},{0,2},{2,4},{4,6},{6,8},{8,10},{10,12},{12,14},{14,16},{16... | collective-permute-start | bytes 2359304 | tf_op jit(solution)/shard_map/ppermute | solution.py:33
  123.2 4.0 %collective-permute-start.26 = (f32[48,128]{1,0:T(8,128)S(1)}, f32[48,128]{1,0:T(8,128)S(1)}, u32[]{:S(2)}, u32[]{:S(2)}) collective-permute-start(f32[48,128]{1,0:T(8,128)S(1)} %fusion.11), channel_id=1, source_target_pairs={{0,32},{2,226},{4,228},{6,230},{8,232},{10,234},{12,236},{14,238},... | collective-permute-start | bytes 73736 | tf_op jit(solution)/shard_map/ppermute | solution.py:328
  127.1 4.8 %collective-permute-start.27 = (f32[48,128]{1,0:T(8,128)S(1)}, f32[48,128]{1,0:T(8,128)S(1)}, u32[]{:S(2)}, u32[]{:S(2)}) collective-permute-start(f32[48,128]{1,0:T(8,128)S(1)} %add.225), channel_id=1, source_target_pairs={{0,64},{2,194},{4,196},{6,198},{8,200},{10,202},{12,204},{14,206},... | collective-permute-start | bytes 73736 | tf_op jit(solution)/shard_map/ppermute | solution.py:328
  131.9 6.9 %collective-permute-start.28 = (f32[48,128]{1,0:T(8,128)S(1)}, f32[48,128]{1,0:T(8,128)S(1)}, u32[]{:S(2)}, u32[]{:S(2)}) collective-permute-start(f32[48,128]{1,0:T(8,128)S(1)} %add.226), channel_id=1, source_target_pairs={{0,128},{2,130},{4,132},{6,134},{8,136},{10,138},{12,140},{14,142}... | collective-permute-start | bytes 73736 | tf_op jit(solution)/shard_map/ppermute | solution.py:328
  138.8 3.0 %collective-permute-start.31 = (f32[48,128]{1,0:T(8,128)S(1)}, f32[48,128]{1,0:T(8,128)S(1)}, u32[]{:S(2)}, u32[]{:S(2)}) collective-permute-start(f32[48,128]{1,0:T(8,128)S(1)} %add.227), channel_id=1, source_target_pairs={{0,24},{8,0},{16,8},{24,16},{1,25},{9,1},{17,9},{25,17},{2,26},{10... | collective-permute-start | bytes 73736 | tf_op jit(solution)/shard_map/ppermute | solution.py:380
  138.8 4.6 %collective-permute-start.30 = (f32[48,128]{1,0:T(8,128)S(1)}, f32[48,128]{1,0:T(8,128)S(1)}, u32[]{:S(2)}, u32[]{:S(2)}) collective-permute-start(f32[48,128]{1,0:T(8,128)S(1)} %add.227), channel_id=1, source_target_pairs={{0,16},{8,24},{16,0},{24,8},{1,17},{9,25},{17,1},{25,9},{2,18},{10... | collective-permute-start | bytes 73736 | tf_op jit(solution)/shard_map/ppermute | solution.py:380
  138.9 5.3 %collective-permute-start.29 = (f32[48,128]{1,0:T(8,128)S(1)}, f32[48,128]{1,0:T(8,128)S(1)}, u32[]{:S(2)}, u32[]{:S(2)}) collective-permute-start(f32[48,128]{1,0:T(8,128)S(1)} %add.227), channel_id=1, source_target_pairs={{0,8},{8,16},{16,24},{24,0},{1,9},{9,17},{17,25},{25,1},{2,10},{10... | collective-permute-start | bytes 73736 | tf_op jit(solution)/shard_map/ppermute | solution.py:380
  146.6 11.6 %collective-permute-start.34 = (f32[2,128,512]{1,2,0:T(8,128)S(1)}, f32[2,128,512]{1,2,0:T(8,128)S(1)}, u32[]{:S(2)}, u32[]{:S(2)}) collective-permute-start(f32[2,128,512]{1,2,0:T(8,128)S(1)} %bitcast.54), channel_id=1, source_target_pairs={{0,1},{1,0},{2,3},{3,2},{4,5},{5,4},{6,7},{7,6},{8,9},{9,8},{10,11... | collective-permute-start | bytes 1572872 | tf_op jit(solution)/shard_map/ppermute | solution.py:28
  151.4 3.5 %collective-permute-start.37 = (f32[48,128]{1,0:T(8,128)S(1)}, f32[48,128]{1,0:T(8,128)S(1)}, u32[]{:S(2)}, u32[]{:S(2)}) collective-permute-start(f32[48,128]{1,0:T(8,128)S(1)} %add_add_fusion.4), channel_id=1, source_target_pairs={{2,0},{4,2},{6,4},{0,6},{3,1},{5,3},{7,5},{1,7},{10,8},{12,10},{14... | collective-permute-start | bytes 73736 | tf_op jit(solution)/shard_map/ppermute | solution.py:357
  153.9 4.2 %collective-permute-start.36 = (f32[48,128]{1,0:T(8,128)S(1)}, f32[48,128]{1,0:T(8,128)S(1)}, u32[]{:S(2)}, u32[]{:S(2)}) collective-permute-start(f32[48,128]{1,0:T(8,128)S(1)} %add_add_fusion.4), channel_id=1, source_target_pairs={{4,0},{6,2},{0,4},{2,6},{5,1},{7,3},{1,5},{3,7},{12,8},{14,10},{8,... | collective-permute-start | bytes 73736 | tf_op jit(solution)/shard_map/ppermute | solution.py:357
  154.0 4.2 %collective-permute-start.35 = (f32[48,128]{1,0:T(8,128)S(1)}, f32[48,128]{1,0:T(8,128)S(1)}, u32[]{:S(2)}, u32[]{:S(2)}) collective-permute-start(f32[48,128]{1,0:T(8,128)S(1)} %add_add_fusion.4), channel_id=1, source_target_pairs={{6,0},{0,2},{2,4},{4,6},{7,1},{1,3},{3,5},{5,7},{14,8},{8,10},{10,... | collective-permute-start | bytes 73736 | tf_op jit(solution)/shard_map/ppermute | solution.py:357
  158.4 3.0 %collective-permute-start.38 = (f32[192,128]{1,0:T(8,128)S(1)}, f32[192,128]{1,0:T(8,128)S(1)}, u32[]{:S(2)}, u32[]{:S(2)}) collective-permute-start(f32[192,128]{1,0:T(8,128)S(1)} %maximum_add_fusion), channel_id=1, source_target_pairs={{0,1},{1,0},{2,3},{3,2},{4,5},{5,4},{6,7},{7,6},{8,9},{9,8},{10,11... | collective-permute-start | bytes 294920 | tf_op jit(solution)/shard_map/ppermute | solution.py:28
  160.0 1.4 copy-start.2

commit v8 on v7

--- a/solution.py
+++ b/solution.py
@@ -21,7 +21,6 @@
 MODULUS_FLOOR = 0.2
 OBJECT_RELAX = 1.0
 ANY = pl.BlockSpec(memory_space=pl.ANY)
-VMEM = pl.BlockSpec(memory_space=pltpu.VMEM)
 
 
 def swapped(value):
@@ -46,11 +45,10 @@
     sine = np.sin(angle) / math.sqrt(PATCH)
     tables = []
     for sign in (1.0, -1.0):
-        for turn in (1.0, -1.0):
-            cross = sign * turn * sine
-            table = np.block([[cosine, -cross], [cross, cosine]]).astype(np.float32)
-            high = table.astype(jnp.bfloat16)
-            tables += [high, (table - high.astype(np.float32)).astype(jnp.bfloat16)]
+        cross = sign * sine
+        table = np.block([[cosine, -cross], [cross, cosine]]).astype(np.float32)
+        high = table.astype(jnp.bfloat16)
+        tables += [high, (table - high.astype(np.float32)).astype(jnp.bfloat16)]
     return jnp.asarray(np.stack(tables))
 
 
@@ -94,7 +92,7 @@
     rows_hbm,
     cols_hbm,
     live_hbm,
-    probe_ref,
+    probe_hbm,
     amps_hbm,
     tables_hbm,
     first_ref,
@@ -110,6 +108,7 @@
     band,
     sums,
     amps_ref,
+    probe_ref,
     tables,
     rows_ref,
     cols_ref,
@@ -127,6 +126,7 @@
 
     copies = [
         (tables_hbm, tables),
+        (probe_hbm, probe_ref),
         (rows_hbm, rows_ref),
         (cols_hbm, cols_ref),
         (live_hbm, live_ref),
@@ -230,8 +230,8 @@
             lambda pair: right(pair, 0),
             lambda pair: left(pair, 2),
             rescale,
-            lambda pair: left(pair, 6),
-            lambda pair: right(pair, 4),
+            lambda pair: left(pair, 0),
+            lambda pair: right(pair, 2),
             collect,
         )
         pairs = GROUP // 2
@@ -275,16 +275,17 @@
     return pl.pallas_call(
         kernel,
         out_shape=(quarter,) * 4 + (pieces_of,) * 2,
-        in_specs=[ANY] * 3 + [VMEM] + [ANY] * (2 + len(pieces)),
+        in_specs=[ANY] * (6 + len(pieces)),
         out_specs=(ANY,) * 6,
         scratch_shapes=[
             pltpu.VMEM((3 * PATCH, PATCH), jnp.float32),
             pltpu.VMEM((2, BLOCKS, BAND, PATCH), jnp.float32),
             pltpu.VMEM((3, BLOCKS, BAND, PATCH), jnp.float32),
             pltpu.VMEM(amps.shape, jnp.float32),
+            pltpu.VMEM(probe.shape, jnp.float32),
             pltpu.VMEM(tables.shape, tables.dtype),
             *(pltpu.SMEM(s.shape, jnp.int32) for s in scalars),
-            pltpu.SemaphoreType.DMA((2 * BLOCKS + 4,)),
+            pltpu.SemaphoreType.DMA((2 * BLOCKS + 5,)),
             pltpu.SemaphoreType.DMA((amps.shape[0] // GROUP,)),
         ],
         compiler_params=pltpu.CompilerParams(vmem_limit_bytes=60 * 2**20),

time: 162 us -> 160 us (0.988)
  Pallas kernels: 19.5 us -> 17.6 us
  starting transfers between devices: 63.4 us -> 61.5 us
  waiting for transfers between devices: 61.7 us -> 63.6 us
    pallas_call x2, Pallas kernels: 19.5 us -> 17.6 us  [run_positions(): pl.pallas_call(kernel, out_shape=(quarter,) * 4 + (pieces_of,) * 2, in_sp...]
  transfers between devices with their start and end apart: 39 -> 39, of which waited for: 22 -> 23; matrix products, arithmetic and copies ran while one was open for 6% -> 6% of each run, Pallas kernels for 0% -> 0%
where the time goes in v8:
time: 160 us
  waiting for transfers between devices  63.6 us (40%)
  starting transfers between devices  61.5 us (38%)
  Pallas kernels  17.6 us (11%)
  other arithmetic  9.5 us (6%)
  local copies, waits for them, and re-layouts  6.23 us (4%)
  between operations  1.75 us (1%)
    ppermute x6, waiting for transfers between devices, moved_along(): return lax.ppermute(value, TILE, route)  30.2 us
    ppermute x11, starting transfers between devices, swapped(): return lax.ppermute(value, 'pos', [(0, 1), (1, 0)])  28.7 us
    ppermute x4, starting transfers between devices, from_tile(): lax.ppermute(value, TILE, [((i + distance) % count, i) for i in range(cou...  18.2 us
    pallas_call x2, Pallas kernels, run_positions(): pl.pallas_call(kernel, out_shape=(quarter,) * 4 + (pieces_of,) * 2, in_sp...  17.6 us
    ppermute x4, waiting for transfers between devices, from_tile(): lax.ppermute(value, TILE, [((i + distance) % count, i) for i in range(cou...  13 us
    ppermute x6, waiting for transfers between devices, scattered_over(): arrived.append(lax.ppermute(pieces[step], axis, route))  7.44 us
    ppermute x6, waiting for transfers between devices, shifts_among(): total = total + lax.ppermute(value, axis, route)  5.64 us
    ppermute x6, starting transfers between devices, scattered_over(): arrived.append(lax.ppermute(pieces[step], axis, route))  5.5 us
  transfers between devices with their start and end apart: 39, of which 23 were waited for; matrix products, arithmetic and copies ran while one was open for 6% of the time, Pallas kernels for 0%

profile of v8, /device:TPU:1, one launch (start us, length us, event | category | flops | bytes accessed | tf_op | source)
XLA Modules:
  0.0 160.2 jit_solution(8196101500012558484)
XLA Ops:
  0.6 1.1 constant_dynamic-slice_fusion
  1.7 11.1 %collective-permute-start = (f32[2,128,512]{2,1,0:T(8,128)S(1)}, f32[2,128,512]{2,1,0:T(8,128)S(1)}, u32[]{:S(2)}, u32[]{:S(2)}) collective-permute-start(f32[2,128,512]{2,1,0:T(8,128)S(1)} %constant_dynamic-slice_fusion), channel_id=1, source_target_pairs={{2,0},{4,2},{6,4},{8,6},{10,8},{12,10},{14,12},{16,14},{18,16},{20... | collective-permute-start | bytes 1572872 | tf_op jit(solution)/shard_map/ppermute | solution.py:32
  12.8 10.6 %collective-permute-done.refs_7_ = f32[2,128,512]{2,1,0:T(8,128)S(1)} collective-permute-done((f32[2,128,512]{2,1,0:T(8,128)S(1)}, f32[2,128,512]{2,1,0:T(8,128)S(1)}, u32[]{:S(2)}, u32[]{:S(2)}) %collective-permute-start) | collective-permute-done | bytes 524320 | tf_op jit(solution)/shard_map/ppermute | solution.py:32
  23.4 1.5 collective-permute-start.1
  25.6 0.9 collective-permute-done.1.refs_8_
  26.5 0.8 copy-done.6
  27.3 8.8 %positions.2 = (f32[3,4,128,128]{3,2,1,0:T(8,128)}, f32[3,4,128,128]{3,2,1,0:T(8,128)}, f32[3,4,128,128]{3,2,1,0:T(8,128)}, f32[3,4,128,128]{3,2,1,0:T(8,128)}, ...) custom-call(s32[1,1,32]{2,1,0:T(1,128)} %refs_0_.3, s32[1,1,32]{2,1,0:T(1,128)} %refs_1_.3, s32[1,1]{1,0:T(1,128)S(6)} %copy.21.refs_2_, ...), custom_call_target="tpu_custom_call" | custom-call | flops 12999999488 | bytes 8388608 | tf_op jit(solution)/shard_map/positions/pallas_call | solution.py:275
  36.1 5.5 %collective-permute-start.2 = (f32[4,48,128]{2,1,0:T(8,128)}, f32[4,48,128]{2,1,0:T(8,128)S(1)}, u32[]{:S(2)}, u32[]{:S(2)}) collective-permute-start(f32[4,48,128]{2,1,0:T(8,128)} %get-tuple-element.19), channel_id=1, source_target_pairs={{0,1},{1,0},{2,3},{3,2},{4,5},{5,4},{6,7},{7,6},{8,9},{9,8},{10,11... | collective-permute-start | bytes 294920 | tf_op jit(solution)/shard_map/ppermute | solution.py:27
  41.7 0.4 collective-permute-start.17
  42.1 0.6 collective-permute-done.2
  42.8 0.9 add.194
  43.8 2.7 %collective-permute-start.5 = (f32[48,128]{1,0:T(8,128)S(1)}, f32[48,128]{1,0:T(8,128)S(1)}, u32[]{:S(2)}, u32[]{:S(2)}) collective-permute-start(f32[48,128]{1,0:T(8,128)S(1)} %get-tuple-element.56), channel_id=1, source_target_pairs={{0,6},{2,0},{4,2},{6,4},{1,7},{3,1},{5,3},{7,5},{8,14},{10,8},{12,... | collective-permute-start | bytes 73736 | tf_op jit(solution)/shard_map/ppermute | solution.py:346
  46.5 1.2 collective-permute-done.3
  47.7 3.0 %collective-permute-done.4 = f32[48,128]{1,0:T(8,128)S(1)} collective-permute-done((f32[48,128]{1,0:T(8,128)S(1)}, f32[48,128]{1,0:T(8,128)S(1)}, u32[]{:S(2)}, u32[]{:S(2)}) %collective-permute-start.4) | collective-permute-done | bytes 24608 | tf_op jit(solution)/shard_map/ppermute | solution.py:346
  50.7 1.6 %add_add_fusion.2 = (f32[3,4,128,128]{3,2,1,0:T(8,128)S(1)}, f32[3,4,128,128]{3,2,1,0:T(8,128)S(1)}) fusion(f32[3,4,128,128]{3,2,1,0:T(8,128)} %get-tuple-element.22, f32[3,4,128,128]{3,2,1,0:T(8,128)S(1)} %collective-permute-done.17, f32[128]{0:T(128)S(1)} %fusion.20, f32[3,4,128,128]{3,2,1,0:T(8,128)} %get-tuple-element.20, ...), kind=kLoop, calls=%fused_computation.4 | loop fusion | flops 786432 | bytes 4719104 | tf_op jit(solution)/shard_map/add | solution.py:370
  52.4 6.9 %collective-permute-start.19 = (f32[3,4,128,128]{3,2,1,0:T(8,128)S(1)}, f32[3,4,128,128]{3,2,1,0:T(8,128)}, u32[]{:S(2)}, u32[]{:S(2)}) collective-permute-start(f32[3,4,128,128]{3,2,1,0:T(8,128)S(1)} %get-tuple-element.24), channel_id=1, source_target_pairs={{2,0},{4,2},{6,4},{8,6},{10,8},{12,10},{14,12},{16,14},{18,16},{20... | collective-permute-start | bytes 2359304 | tf_op jit(solution)/shard_map/ppermute | solution.py:32
  59.3 4.3 %collective-permute-done.6 = f32[48,128]{1,0:T(8,128)S(1)} collective-permute-done((f32[48,128]{1,0:T(8,128)S(1)}, f32[48,128]{1,0:T(8,128)S(1)}, u32[]{:S(2)}, u32[]{:S(2)}) %collective-permute-start.6) | collective-permute-done | bytes 24608 | tf_op jit(solution)/shard_map/ppermute | solution.py:329
  63.6 5.2 %collective-permute-done.7 = f32[48,128]{1,0:T(8,128)S(1)} collective-permute-done((f32[48,128]{1,0:T(8,128)S(1)}, f32[48,128]{1,0:T(8,128)S(1)}, u32[]{:S(2)}, u32[]{:S(2)}) %collective-permute-start.7) | collective-permute-done | bytes 24608 | tf_op jit(solution)/shard_map/ppermute | solution.py:329
  68.8 1.1 collective-permute-start.8
  69.9 5.8 %collective-permute-done.8 = f32[48,128]{1,0:T(8,128)S(1)} collective-permute-done((f32[48,128]{1,0:T(8,128)S(1)}, f32[48,128]{1,0:T(8,128)S(1)}, u32[]{:S(2)}, u32[]{:S(2)}) %collective-permute-start.8) | collective-permute-done | bytes 24608 | tf_op jit(solution)/shard_map/ppermute | solution.py:329
  75.9 1.4 collective-permute-start.9
  77.2 0.2 copy.15
  77.4 0.2 copy.16
  77.6 1.2 copy.17
  78.9 0.2 copy.18
  79.1 1.2 collective-permute-done.10
  80.3 0.5 collective-permute-done.9
  81.0 1.4 collective-permute-start.12
  82.4 1.2 add.214
  83.6 1.2 add.217
  84.9 0.2 fusion.2
  85.2 7.1 %collective-permute-start.20 = (f32[2,4,256,128]{3,2,1,0:T(8,128)S(1)}, f32[2,4,256,128]{3,2,1,0:T(8,128)S(1)}, u32[]{:S(2)}, u32[]{:S(2)}) collective-permute-start(f32[2,4,256,128]{3,2,1,0:T(8,128)S(1)} %pad_maximum_fusion.refs_6_), channel_id=1, source_target_pairs={{0,1},{1,0},{2,3},{3,2},{4,5},{5,4},{6,7},{7,6},{8,9},{9,8},{10,11... | collective-permute-start | bytes 3145736 | tf_op jit(solution)/shard_map/ppermute | solution.py:27
  92.4 1.6 %collective-permute-start.15 = (f32[192,128]{1,0:T(8,128)S(1)}, f32[192,128]{1,0:T(8,128)S(1)}, u32[]{:S(2)}, u32[]{:S(2)}) collective-permute-start(f32[192,128]{1,0:T(8,128)S(1)} %pad_maximum_fusion.4), channel_id=1, source_target_pairs={{0,1},{1,0},{2,3},{3,2},{4,5},{5,4},{6,7},{7,6},{8,9},{9,8},{10,11... | collective-permute-start | bytes 294920 | tf_op jit(solution)/shard_map/ppermute | solution.py:27
  94.0 0.9 collective-permute-done.15
  95.0 0.7 add_divide_fusion.1.refs_3_
  95.7 1.0 copy-done.5
  96.7 8.8 %positions.3 = (f32[3,4,128,128]{3,2,1,0:T(8,128)}, f32[3,4,128,128]{3,2,1,0:T(8,128)}, f32[3,4,128,128]{3,2,1,0:T(8,128)}, f32[3,4,128,128]{3,2,1,0:T(8,128)}, ...) custom-call(s32[1,1,32]{2,1,0:T(1,128)} %refs_0_.3, s32[1,1,32]{2,1,0:T(1,128)} %refs_1_.3, s32[1,1]{1,0:T(1,128)S(6)} %copy.21.refs_2_, ...), custom_call_target="tpu_custom_call" | custom-call | flops 12999999488 | bytes 8388608 | tf_op jit(solution)/shard_map/positions/pallas_call | solution.py:275
  105.5 5.5 %collective-permute-start.22 = (f32[4,48,128]{2,1,0:T(8,128)}, f32[4,48,128]{2,1,0:T(8,128)S(1)}, u32[]{:S(2)}, u32[]{:S(2)}) collective-permute-start(f32[4,48,128]{2,1,0:T(8,128)} %get-tuple-element.31), channel_id=1, source_target_pairs={{0,1},{1,0},{2,3},{3,2},{4,5},{5,4},{6,7},{7,6},{8,9},{9,8},{10,11... | collective-permute-start | bytes 294920 | tf_op jit(solution)/shard_map/ppermute | solution.py:27
  111.1 1.1 collective-permute-done.22
  112.1 0.9 add.221
  113.1 2.7 %collective-permute-start.25 = (f32[48,128]{1,0:T(8,128)S(1)}, f32[48,128]{1,0:T(8,128)S(1)}, u32[]{:S(2)}, u32[]{:S(2)}) collective-permute-start(f32[48,128]{1,0:T(8,128)S(1)} %get-tuple-element.49), channel_id=1, source_target_pairs={{0,6},{2,0},{4,2},{6,4},{1,7},{3,1},{5,3},{7,5},{8,14},{10,8},{12,... | collective-permute-start | bytes 73736 | tf_op jit(solution)/shard_map/ppermute | solution.py:346
  115.8 0.9 collective-permute-start.21
  116.7 0.3 collective-permute-done.23
  117.0 3.0 %collective-permute-done.24 = f32[48,128]{1,0:T(8,128)S(1)} collective-permute-done((f32[48,128]{1,0:T(8,128)S(1)}, f32[48,128]{1,0:T(8,128)S(1)}, u32[]{:S(2)}, u32[]{:S(2)}) %collective-permute-start.24) | collective-permute-done | bytes 24608 | tf_op jit(solution)/shard_map/ppermute | solution.py:346
  120.0 1.2 add_add_fusion
  121.4 3.9 %collective-permute-done.26 = f32[48,128]{1,0:T(8,128)S(1)} collective-permute-done((f32[48,128]{1,0:T(8,128)S(1)}, f32[48,128]{1,0:T(8,128)S(1)}, u32[]{:S(2)}, u32[]{:S(2)}) %collective-permute-start.26) | collective-permute-done | bytes 24608 | tf_op jit(solution)/shard_map/ppermute | solution.py:329
  125.3 4.8 %collective-permute-done.27 = f32[48,128]{1,0:T(8,128)S(1)} collective-permute-done((f32[48,128]{1,0:T(8,128)S(1)}, f32[48,128]{1,0:T(8,128)S(1)}, u32[]{:S(2)}, u32[]{:S(2)}) %collective-permute-start.27) | collective-permute-done | bytes 24608 | tf_op jit(solution)/shard_map/ppermute | solution.py:329
  130.1 0.6 collective-permute-start.28
  130.7 6.3 %collective-permute-done.28 = f32[48,128]{1,0:T(8,128)S(1)} collective-permute-done((f32[48,128]{1,0:T(8,128)S(1)}, f32[48,128]{1,0:T(8,128)S(1)}, u32[]{:S(2)}, u32[]{:S(2)}) %collective-permute-start.28) | collective-permute-done | bytes 24608 | tf_op jit(solution)/shard_map/ppermute | solution.py:329
  137.1 1.4 collective-permute-start.29
  138.5 1.5 collective-permute-done.31
  140.0 1.6 collective-permute-done.30
  141.6 0.8 collective-permute-done.29
  142.4 2.4 %collective-permute-done.33 = f32[3,4,128,128]{3,2,1,0:T(8,128)S(1)} collective-permute-done((f32[3,4,128,128]{3,2,1,0:T(8,128)S(1)}, f32[3,4,128,128]{3,2,1,0:T(8,128)S(1)}, u32[]{:S(2)}, u32[]{:S(2)}) %collective-permute-start.33) | collective-permute-done | bytes 786464 | tf_op jit(solution)/shard_map/ppermute | solution.py:32
  145.1 0.2 copy.19
  145.3 4.2 %collective-permute-start.34 = (f32[2,128,512]{1,2,0:T(8,128)S(1)}, f32[2,128,512]{1,2,0:T(8,128)S(1)}, u32[]{:S(2)}, u32[]{:S(2)}) collective-permute-start(f32[2,128,512]{1,2,0:T(8,128)S(1)} %bitcast.54), channel_id=1, source_target_pairs={{0,1},{1,0},{2,3},{3,2},{4,5},{5,4},{6,7},{7,6},{8,9},{9,8},{10,11... | collective-permute-start | bytes 1572872 | tf_op jit(solution)/shard_map/ppermute | solution.py:27
  149.5 2.3 %collective-permute-start.37 = (f32[48,128]{1,0:T(8,128)S(1)}, f32[48,128]{1,0:T(8,128)S(1)}, u32[]{:S(2)}, u32[]{:S(2)}) collective-permute-start(f32[48,128]{1,0:T(8,128)S(1)} %add_add_fusion.4), channel_id=1, source_target_pairs={{2,0},{4,2},{6,4},{0,6},{3,1},{5,3},{7,5},{1,7},{10,8},{12,10},{14... | collective-permute-start | bytes 73736 | tf_op jit(solution)/shard_map/ppermute | solution.py:358
  151.8 0.2 collective-permute-start.36
  151.9 0.4 collective-permute-start.35
  152.3 0.4 collective-permute-done.37
  152.7 3.3 %collective-permute-done.36 = f32[48,128]{1,0:T(8,128)S(1)} collective-permute-done((f32[48,128]{1,0:T(8,128)S(1)}, f32[48,128]{1,0:T(8,128)S(1)}, u32[]{:S(2)}, u32[]{:S(2)}) %collective-permute-start.36) | collective-permute-done | bytes 24608 | tf_op jit(solution)/shard_map/ppermute | solution.py:358
  156.3 1.7 %collective-permute-start.38 = (f32[192,128]{1,0:T(8,128)S(1)}, f32[192,128]{1,0:T(8,128)S(1)}, u32[]{:S(2)}, u32[]{:S(2)}) collective-permute-start(f32[192,128]{1,0:T(8,128)S(1)} %maximum_add_fusion), channel_id=1, source_target_pairs={{0,1},{1,0},{2,3},{3,2},{4,5},{5,4},{6,7},{7,6},{8,9},{9,8},{10,11... | collective-permute-start | bytes 294920 | tf_op jit(solution)/shard_map/ppermute | solution.py:27
  158.1 1.3 copy.20
  159.5 0.7 add_divide_fusion
  (80 shorter events, 1.9 us)
Async XLA Ops:
  1.7 21.7 %collective-permute-start = (f32[2,128,512]{2,1,0:T(8,128)S(1)}, f32[2,128,512]{2,1,0:T(8,128)S(1)}, u32[]{:S(2)}, u32[]{:S(2)}) collective-permute-start(f32[2,128,512]{2,1,0:T(8,128)S(1)} %constant_dynamic-slice_fusion), channel_id=1, source_target_pairs={{2,0},{4,2},{6,4},{8,6},{10,8},{12,10},{14,12},{16,14},{18,16},{20... | collective-permute-start | bytes 1572872 | tf_op jit(solution)/shard_map/ppermute | solution.py:32
  23.4 3.1 %copy-start.3 = (f32[2,128,512]{2,1,0:T(8,128)}, f32[2,128,512]{2,1,0:T(8,128)S(1)}, u32[]{:S(2)}) copy-start(f32[2,128,512]{2,1,0:T(8,128)S(1)} %collective-permute-done.refs_7_) | copy-start | bytes 1572868
  23.4 3.1 %collective-permute-start.1 = (f32[2,128,512]{2,1,0:T(8,128)S(1)}, f32[2,128,512]{2,1,0:T(8,128)S(1)}, u32[]{:S(2)}, u32[]{:S(2)}) collective-permute-start(f32[2,128,512]{2,1,0:T(8,128)S(1)} %collective-permute-done.refs_7_), channel_id=1, source_target_pairs={{0,1},{1,0},{2,3},{3,2},{4,5},{5,4},{6,7},{7,6},{8,9},{9,8},{10,11... | collective-permute-start | bytes 1572872 | tf_op jit(solution)/shard_map/ppermute | solution.py:27
  26.5 0.8 copy-start.6
  36.1 6.6 %collective-permute-start.2 = (f32[4,48,128]{2,1,0:T(8,128)}, f32[4,48,128]{2,1,0:T(8,128)S(1)}, u32[]{:S(2)}, u32[]{:S(2)}) collective-permute-start(f32[4,48,128]{2,1,0:T(8,128)} %get-tuple-element.19), channel_id=1, source_target_pairs={{0,1},{1,0},{2,3},{3,2},{4,5},{5,4},{6,7},{7,6},{8,9},{9,8},{10,11... | collective-permute-start | bytes 294920 | tf_op jit(solution)/shard_map/ppermute | solution.py:27
  41.6 9.0 %collective-permute-start.16 = (f32[3,4,128,128]{3,2,1,0:T(8,128)}, f32[3,4,128,128]{3,2,1,0:T(8,128)S(1)}, u32[]{:S(2)}, u32[]{:S(2)}) collective-permute-start(f32[3,4,128,128]{3,2,1,0:T(8,128)} %get-tuple-element.21), channel_id=1, source_target_pairs={{0,1},{1,0},{2,3},{3,2},{4,5},{5,4},{6,7},{7,6},{8,9},{9,8},{10,11... | collective-permute-start | bytes 2359304 | tf_op jit(solution)/shard_map/ppermute | solution.py:27
  41.7 9.0 %collective-permute-start.17 = (f32[3,4,128,128]{3,2,1,0:T(8,128)}, f32[3,4,128,128]{3,2,1,0:T(8,128)S(1)}, u32[]{:S(2)}, u32[]{:S(2)}) collective-permute-start(f32[3,4,128,128]{3,2,1,0:T(8,128)} %get-tuple-element.23), channel_id=1, source_target_pairs={{0,1},{1,0},{2,3},{3,2},{4,5},{5,4},{6,7},{7,6},{8,9},{9,8},{10,11... | collective-permute-start | bytes 2359304 | tf_op jit(solution)/shard_map/ppermute | solution.py:27
  43.7 4.0 %collective-permute-start.3 = (f32[48,128]{1,0:T(8,128)S(1)}, f32[48,128]{1,0:T(8,128)S(1)}, u32[]{:S(2)}, u32[]{:S(2)}) collective-permute-start(f32[48,128]{1,0:T(8,128)S(1)} %get-tuple-element.55), channel_id=1, source_target_pairs={{0,2},{2,4},{4,6},{6,0},{1,3},{3,5},{5,7},{7,1},{8,10},{10,12},{12... | collective-permute-start | bytes 73736 | tf_op jit(solution)/shard_map/ppermute | solution.py:346
  43.8 3.9 %collective-permute-start.5 = (f32[48,128]{1,0:T(8,128)S(1)}, f32[48,128]{1,0:T(8,128)S(1)}, u32[]{:S(2)}, u32[]{:S(2)}) collective-permute-start(f32[48,128]{1,0:T(8,128)S(1)} %get-tuple-element.56), channel_id=1, source_target_pairs={{0,6},{2,0},{4,2},{6,4},{1,7},{3,1},{5,3},{7,5},{8,14},{10,8},{12,... | collective-permute-start | bytes 73736 | tf_op jit(solution)/shard_map/ppermute | solution.py:346
  46.5 4.2 %collective-permute-start.4 = (f32[48,128]{1,0:T(8,128)S(1)}, f32[48,128]{1,0:T(8,128)S(1)}, u32[]{:S(2)}, u32[]{:S(2)}) collective-permute-start(f32[48,128]{1,0:T(8,128)S(1)} %get-tuple-element.57), channel_id=1, source_target_pairs={{0,4},{2,6},{4,0},{6,2},{1,5},{3,7},{5,1},{7,3},{8,12},{10,14},{12... | collective-permute-start | bytes 73736 | tf_op jit(solution)/shard_map/ppermute | solution.py:346
  52.3 30.1 %collective-permute-start.18 = (f32[3,4,128,128]{3,2,1,0:T(8,128)S(1)}, f32[3,4,128,128]{3,2,1,0:T(8,128)}, u32[]{:S(2)}, u32[]{:S(2)}) collective-permute-start(f32[3,4,128,128]{3,2,1,0:T(8,128)S(1)} %get-tuple-element.26), channel_id=1, source_target_pairs={{254,0},{0,2},{2,4},{4,6},{6,8},{8,10},{10,12},{12,14},{14,16},{16... | collective-permute-start | bytes 2359304 | tf_op jit(solution)/shard_map/ppermute | solution.py:32
  52.4 30.0 %collective-permute-start.19 = (f32[3,4,128,128]{3,2,1,0:T(8,128)S(1)}, f32[3,4,128,128]{3,2,1,0:T(8,128)}, u32[]{:S(2)}, u32[]{:S(2)}) collective-permute-start(f32[3,4,128,128]{3,2,1,0:T(8,128)S(1)} %get-tuple-element.24), channel_id=1, source_target_pairs={{2,0},{4,2},{6,4},{8,6},{10,8},{12,10},{14,12},{16,14},{18,16},{20... | collective-permute-start | bytes 2359304 | tf_op jit(solution)/shard_map/ppermute | solution.py:32
  59.3 4.3 %collective-permute-start.6 = (f32[48,128]{1,0:T(8,128)S(1)}, f32[48,128]{1,0:T(8,128)S(1)}, u32[]{:S(2)}, u32[]{:S(2)}) collective-permute-start(f32[48,128]{1,0:T(8,128)S(1)} %fusion.14), channel_id=1, source_target_pairs={{0,32},{2,226},{4,228},{6,230},{8,232},{10,234},{12,236},{14,238},... | collective-permute-start | bytes 73736 | tf_op jit(solution)/shard_map/ppermute | solution.py:329
  63.6 5.2 %collective-permute-start.7 = (f32[48,128]{1,0:T(8,128)S(1)}, f32[48,128]{1,0:T(8,128)S(1)}, u32[]{:S(2)}, u32[]{:S(2)}) collective-permute-start(f32[48,128]{1,0:T(8,128)S(1)} %add.198), channel_id=1, source_target_pairs={{0,64},{2,194},{4,196},{6,198},{8,200},{10,202},{12,204},{14,206},... | collective-permute-start | bytes 73736 | tf_op jit(solution)/shard_map/ppermute | solution.py:329
  68.8 7.0 %collective-permute-start.8 = (f32[48,128]{1,0:T(8,128)S(1)}, f32[48,128]{1,0:T(8,128)S(1)}, u32[]{:S(2)}, u32[]{:S(2)}) collective-permute-start(f32[48,128]{1,0:T(8,128)S(1)} %add.199), channel_id=1, source_target_pairs={{0,128},{2,130},{4,132},{6,134},{8,136},{10,138},{12,140},{14,142}... | collective-permute-start | bytes 73736 | tf_op jit(solution)/shard_map/ppermute | solution.py:329
  75.8 3.3 %collective-permute-start.11 = (f32[48,128]{1,0:T(8,128)S(1)}, f32[48,128]{1,0:T(8,128)S(1)}, u32[]{:S(2)}, u32[]{:S(2)}) collective-permute-start(f32[48,128]{1,0:T(8,128)S(1)} %add.200), channel_id=1, source_target_pairs={{0,24},{8,0},{16,8},{24,16},{1,25},{9,1},{17,9},{25,17},{2,26},{10... | collective-permute-start | bytes 73736 | tf_op jit(solution)/shard_map/ppermute | solution.py:381
  75.8 4.6 %collective-permute-start.10 = (f32[48,128]{1,0:T(8,128)S(1)}, f32[48,128]{1,0:T(8,128)S(1)}, u32[]{:S(2)}, u32[]{:S(2)}) collective-permute-start(f32[48,128]{1,0:T(8,128)S(1)} %add.200), channel_id=1, source_target_pairs={{0,16},{8,24},{16,0},{24,8},{1,17},{9,25},{17,1},{25,9},{2,18},{10... | collective-permute-start | bytes 73736 | tf_op jit(solution)/shard_map/ppermute | solution.py:381
  75.9 5.0 %collective-permute-start.9 = (f32[48,128]{1,0:T(8,128)S(1)}, f32[48,128]{1,0:T(8,128)S(1)}, u32[]{:S(2)}, u32[]{:S(2)}) collective-permute-start(f32[48,128]{1,0:T(8,128)S(1)} %add.200), channel_id=1, source_target_pairs={{0,8},{8,16},{16,24},{24,0},{1,9},{9,17},{17,25},{25,1},{2,10},{10... | collective-permute-start | bytes 73736 | tf_op jit(solution)/shard_map/ppermute | solution.py:381
  80.8 11.4 %collective-permute-start.14 = (f32[48,128]{1,0:T(8,128)S(1)}, f32[48,128]{1,0:T(8,128)S(1)}, u32[]{:S(2)}, u32[]{:S(2)}) collective-permute-start(f32[48,128]{1,0:T(8,128)S(1)} %add_add_fusion.5), channel_id=1, source_target_pairs={{2,0},{4,2},{6,4},{0,6},{3,1},{5,3},{7,5},{1,7},{10,8},{12,10},{14... | collective-permute-start | bytes 73736 | tf_op jit(solution)/shard_map/ppermute | solution.py:358
  80.9 11.4 %collective-permute-start.13 = (f32[48,128]{1,0:T(8,128)S(1)}, f32[48,128]{1,0:T(8,128)S(1)}, u32[]{:S(2)}, u32[]{:S(2)}) collective-permute-start(f32[48,128]{1,0:T(8,128)S(1)} %add_add_fusion.5), channel_id=1, source_target_pairs={{4,0},{6,2},{0,4},{2,6},{5,1},{7,3},{1,5},{3,7},{12,8},{14,10},{8,... | collective-permute-start | bytes 73736 | tf_op jit(solution)/shard_map/ppermute | solution.py:358
  81.0 11.3 %collective-permute-start.12 = (f32[48,128]{1,0:T(8,128)S(1)}, f32[48,128]{1,0:T(8,128)S(1)}, u32[]{:S(2)}, u32[]{:S(2)}) collective-permute-start(f32[48,128]{1,0:T(8,128)S(1)} %add_add_fusion.5), channel_id=1, source_target_pairs={{6,0},{0,2},{2,4},{4,6},{7,1},{1,3},{3,5},{5,7},{14,8},{8,10},{10,... | collective-permute-start | bytes 73736 | tf_op jit(solution)/shard_map/ppermute | solution.py:358
  85.1 9.9 %copy-start.4 = (f32[2,128,128]{2,1,0:T(8,128)S(1)}, f32[2,128,128]{2,1,0:T(8,128)}, u32[]{:S(2)}) copy-start(f32[2,128,128]{2,1,0:T(8,128)} %refs_3_.1) | copy-start | bytes 393220
  85.2 10.5 %copy-start = (f32[2,4,256,128]{3,2,1,0:T(8,128)}, f32[2,4,256,128]{3,2,1,0:T(8,128)S(1)}, u32[]{:S(2)}) copy-start(f32[2,4,256,128]{3,2,1,0:T(8,128)S(1)} %pad_maximum_fusion.refs_6_) | copy-start | bytes 3145732
  85.2 10.5 %collective-permute-start.20 = (f32[2,4,256,128]{3,2,1,0:T(8,128)S(1)}, f32[2,4,256,128]{3,2,1,0:T(8,128)S(1)}, u32[]{:S(2)}, u32[]{:S(2)}) collective-permute-start(f32[2,4,256,128]{3,2,1,0:T(8,128)S(1)} %pad_maximum_fusion.refs_6_), channel_id=1, source_target_pairs={{0,1},{1,0},{2,3},{3,2},{4,5},{5,4},{6,7},{7,6},{8,9},{9,8},{10,11... | collective-permute-start | bytes 3145736 | tf_op jit(solution)/shard_map/ppermute | solution.py:27
  92.4 2.6 %collective-permute-start.15 = (f32[192,128]{1,0:T(8,128)S(1)}, f32[192,128]{1,0:T(8,128)S(1)}, u32[]{:S(2)}, u32[]{:S(2)}) collective-permute-start(f32[192,128]{1,0:T(8,128)S(1)} %pad_maximum_fusion.4), channel_id=1, source_target_pairs={{0,1},{1,0},{2,3},{3,2},{4,5},{5,4},{6,7},{7,6},{8,9},{9,8},{10,11... | collective-permute-start | bytes 294920 | tf_op jit(solution)/shard_map/ppermute | solution.py:27
  95.7 1.0 copy-start.5
  105.5 39.3 %copy-start.1 = (f32[3,4,128,128]{3,2,1,0:T(8,128)S(1)}, f32[3,4,128,128]{3,2,1,0:T(8,128)}, u32[]{:S(2)}) copy-start(f32[3,4,128,128]{3,2,1,0:T(8,128)} %get-tuple-element.28) | copy-start | bytes 2359300
  105.5 6.6 %collective-permute-start.22 = (f32[4,48,128]{2,1,0:T(8,128)}, f32[4,48,128]{2,1,0:T(8,128)S(1)}, u32[]{:S(2)}, u32[]{:S(2)}) collective-permute-start(f32[4,48,128]{2,1,0:T(8,128)} %get-tuple-element.31), channel_id=1, source_target_pairs={{0,1},{1,0},{2,3},{3,2},{4,5},{5,4},{6,7},{7,6},{8,9},{9,8},{10,11... | collective-permute-start | bytes 294920 | tf_op jit(solution)/shard_map/ppermute | solution.py:27
  111.0 9.0 %collective-permute-start.32 = (f32[3,4,128,128]{3,2,1,0:T(8,128)}, f32[3,4,128,128]{3,2,1,0:T(8,128)S(1)}, u32[]{:S(2)}, u32[]{:S(2)}) collective-permute-start(f32[3,4,128,128]{3,2,1,0:T(8,128)} %get-tuple-element.33), channel_id=1, source_target_pairs={{0,1},{1,0},{2,3},{3,2},{4,5},{5,4},{6,7},{7,6},{8,9},{9,8},{10,11... | collective-permute-start | bytes 2359304 | tf_op jit(solution)/shard_map/ppermute | solution.py:27
  113.1 4.0 %collective-permute-start.23 = (f32[48,128]{1,0:T(8,128)S(1)}, f32[48,128]{1,0:T(8,128)S(1)}, u32[]{:S(2)}, u32[]{:S(2)}) collective-permute-start(f32[48,128]{1,0:T(8,128)S(1)} %get-tuple-element.48), channel_id=1, source_target_pairs={{0,2},{2,4},{4,6},{6,0},{1,3},{3,5},{5,7},{7,1},{8,10},{10,12},{12... | collective-permute-start | bytes 73736 | tf_op jit(solution)/shard_map/ppermute | solution.py:346
  113.1 3.9 %collective-permute-start.25 = (f32[48,128]{1,0:T(8,128)S(1)}, f32[48,128]{1,0:T(8,128)S(1)}, u32[]{:S(2)}, u32[]{:S(2)}) collective-permute-start(f32[48,128]{1,0:T(8,128)S(1)} %get-tuple-element.49), channel_id=1, source_target_pairs={{0,6},{2,0},{4,2},{6,4},{1,7},{3,1},{5,3},{7,5},{8,14},{10,8},{12,... | collective-permute-start | bytes 73736 | tf_op jit(solution)/shard_map/ppermute | solution.py:346
  115.8 4.2 %collective-permute-start.24 = (f32[48,128]{1,0:T(8,128)S(1)}, f32[48,128]{1,0:T(8,128)S(1)}, u32[]{:S(2)}, u32[]{:S(2)}) collective-permute-start(f32[48,128]{1,0:T(8,128)S(1)} %get-tuple-element.50), channel_id=1, source_target_pairs={{0,4},{2,6},{4,0},{6,2},{1,5},{3,7},{5,1},{7,3},{8,12},{10,14},{12... | collective-permute-start | bytes 73736 | tf_op jit(solution)/shard_map/ppermute | solution.py:346
  115.8 26.6 %collective-permute-start.21 = (f32[3,4,128,128]{3,2,1,0:T(8,128)}, f32[3,4,128,128]{3,2,1,0:T(8,128)S(1)}, u32[]{:S(2)}, u32[]{:S(2)}) collective-permute-start(f32[3,4,128,128]{3,2,1,0:T(8,128)} %get-tuple-element.29), channel_id=1, source_target_pairs={{0,1},{1,0},{2,3},{3,2},{4,5},{5,4},{6,7},{7,6},{8,9},{9,8},{10,11... | collective-permute-start | bytes 2359304 | tf_op jit(solution)/shard_map/ppermute | solution.py:27
  121.2 23.5 %collective-permute-start.33 = (f32[3,4,128,128]{3,2,1,0:T(8,128)S(1)}, f32[3,4,128,128]{3,2,1,0:T(8,128)S(1)}, u32[]{:S(2)}, u32[]{:S(2)}) collective-permute-start(f32[3,4,128,128]{3,2,1,0:T(8,128)S(1)} %add_add_fusion), channel_id=1, source_target_pairs={{254,0},{0,2},{2,4},{4,6},{6,8},{8,10},{10,12},{12,14},{14,16},{16... | collective-permute-start | bytes 2359304 | tf_op jit(solution)/shard_map/ppermute | solution.py:32
  121.3 4.0 %collective-permute-start.26 = (f32[48,128]{1,0:T(8,128)S(1)}, f32[48,128]{1,0:T(8,128)S(1)}, u32[]{:S(2)}, u32[]{:S(2)}) collective-permute-start(f32[48,128]{1,0:T(8,128)S(1)} %fusion.11), channel_id=1, source_target_pairs={{0,32},{2,226},{4,228},{6,230},{8,232},{10,234},{12,236},{14,238},... | collective-permute-start | bytes 73736 | tf_op jit(solution)/shard_map/ppermute | solution.py:329
  125.3 4.8 %collective-permute-start.27 = (f32[48,128]{1,0:T(8,128)S(1)}, f32[48,128]{1,0:T(8,128)S(1)}, u32[]{:S(2)}, u32[]{:S(2)}) collective-permute-start(f32[48,128]{1,0:T(8,128)S(1)} %add.225), channel_id=1, source_target_pairs={{0,64},{2,194},{4,196},{6,198},{8,200},{10,202},{12,204},{14,206},... | collective-permute-start | bytes 73736 | tf_op jit(solution)/shard_map/ppermute | solution.py:329
  130.1 6.9 %collective-permute-start.28 = (f32[48,128]{1,0:T(8,128)S(1)}, f32[48,128]{1,0:T(8,128)S(1)}, u32[]{:S(2)}, u32[]{:S(2)}) collective-permute-start(f32[48,128]{1,0:T(8,128)S(1)} %add.226), channel_id=1, source_target_pairs={{0,128},{2,130},{4,132},{6,134},{8,136},{10,138},{12,140},{14,142}... | collective-permute-start | bytes 73736 | tf_op jit(solution)/shard_map/ppermute | solution.py:329
  137.0 3.0 %collective-permute-start.31 = (f32[48,128]{1,0:T(8,128)S(1)}, f32[48,128]{1,0:T(8,128)S(1)}, u32[]{:S(2)}, u32[]{:S(2)}) collective-permute-start(f32[48,128]{1,0:T(8,128)S(1)} %add.227), channel_id=1, source_target_pairs={{0,24},{8,0},{16,8},{24,16},{1,25},{9,1},{17,9},{25,17},{2,26},{10... | collective-permute-start | bytes 73736 | tf_op jit(solution)/shard_map/ppermute | solution.py:381
  137.0 4.6 %collective-permute-start.30 = (f32[48,128]{1,0:T(8,128)S(1)}, f32[48,128]{1,0:T(8,128)S(1)}, u32[]{:S(2)}, u32[]{:S(2)}) collective-permute-start(f32[48,128]{1,0:T(8,128)S(1)} %add.227), channel_id=1, source_target_pairs={{0,16},{8,24},{16,0},{24,8},{1,17},{9,25},{17,1},{25,9},{2,18},{10... | collective-permute-start | bytes 73736 | tf_op jit(solution)/shard_map/ppermute | solution.py:381
  137.1 5.3 %collective-permute-start.29 = (f32[48,128]{1,0:T(8,128)S(1)}, f32[48,128]{1,0:T(8,128)S(1)}, u32[]{:S(2)}, u32[]{:S(2)}) collective-permute-start(f32[48,128]{1,0:T(8,128)S(1)} %add.227), channel_id=1, source_target_pairs={{0,8},{8,16},{16,24},{24,0},{1,9},{9,17},{17,25},{25,1},{2,10},{10... | collective-permute-start | bytes 73736 | tf_op jit(solution)/shard_map/ppermute | solution.py:381
  145.3 10.9 %collective-permute-start.34 = (f32[2,128,512]{1,2,0:T(8,128)S(1)}, f32[2,128,512]{1,2,0:T(8,128)S(1)}, u32[]{:S(2)}, u32[]{:S(2)}) collective-permute-start(f32[2,128,512]{1,2,0:T(8,128)S(1)} %bitcast.54), channel_id=1, source_target_pairs={{0,1},{1,0},{2,3},{3,2},{4,5},{5,4},{6,7},{7,6},{8,9},{9,8},{10,11... | collective-permute-start | bytes 1572872 | tf_op jit(solution)/shard_map/ppermute | solution.py:27
  149.5 3.2 %collective-permute-start.37 = (f32[48,128]{1,0:T(8,128)S(1)}, f32[48,128]{1,0:T(8,128)S(1)}, u32[]{:S(2)}, u32[]{:S(2)}) collective-permute-start(f32[48,128]{1,0:T(8,128)S(1)} %add_add_fusion.4), channel_id=1, source_target_pairs={{2,0},{4,2},{6,4},{0,6},{3,1},{5,3},{7,5},{1,7},{10,8},{12,10},{14... | collective-permute-start | bytes 73736 | tf_op jit(solution)/shard_map/ppermute | solution.py:358
  151.8 4.3 %collective-permute-start.36 = (f32[48,128]{1,0:T(8,128)S(1)}, f32[48,128]{1,0:T(8,128)S(1)}, u32[]{:S(2)}, u32[]{:S(2)}) collective-permute-start(f32[48,128]{1,0:T(8,128)S(1)} %add_add_fusion.4), channel_id=1, source_target_pairs={{4,0},{6,2},{0,4},{2,6},{5,1},{7,3},{1,5},{3,7},{12,8},{14,10},{8,... | collective-permute-start | bytes 73736 | tf_op jit(solution)/shard_map/ppermute | solution.py:358
  151.9 4.2 %collective-permute-start.35 = (f32[48,128]{1,0:T(8,128)S(1)}, f32[48,128]{1,0:T(8,128)S(1)}, u32[]{:S(2)}, u32[]{:S(2)}) collective-permute-start(f32[48,128]{1,0:T(8,128)S(1)} %add_add_fusion.4), channel_id=1, source_target_pairs={{6,0},{0,2},{2,4},{4,6},{7,1},{1,3},{3,5},{5,7},{14,8},{8,10},{10,... | collective-permute-start | bytes 73736 | tf_op jit(solution)/shard_map/ppermute | solution.py:358
  156.3 3.1 %collective-permute-start.38 = (f32[192,128]{1,0:T(8,128)S(1)}, f32[192,128]{1,0:T(8,128)S(1)}, u32[]{:S(2)}, u32[]{:S(2)}) collective-permute-start(f32[192,128]{1,0:T(8,128)S(1)} %maximum_add_fusion), channel_id=1, source_target_pairs={{0,1},{1,0},{2,3},{3,2},{4,5},{5,4},{6,7},{7,6},{8,9},{9,8},{10,11... | collective-permute-start | bytes 294920 | tf_op jit(solution)/shard_map/ppermute | solution.py:27
  158.1 1.4 copy-start.2

commit v9 on v8

--- a/solution.py
+++ b/solution.py
@@ -338,8 +338,9 @@
     return part
 
 
-def scattered_over(pieces, axis):
+def scattered_over(own, given, axis):
     count = lax.axis_size(axis)
+    pieces = [own[step] + given[step] for step in range(count)]
     arrived = []
     for step in range(1, count):
         route = [(i, (i + step) % count) for i in range(count)]
@@ -410,7 +411,7 @@
     def updated(sums, field):
         return (sums[:2] + OBJECT_RELAX * field) / (sums[2] + OBJECT_RELAX)[None]
 
-    part = scattered_over(keep_sums + swapped(give_sums), TILE[2])
+    part = scattered_over(keep_sums, swapped(give_sums), TILE[2])
     low = after(low + swapped(give_low), part)
     up = after(up + swapped(give_up), part)
     above = from_tile(low, -1)
@@ -424,7 +425,7 @@
     up, low, give_up, give_low, keep_sums, give_sums = run_positions(
         scalars, probe_field, amps, tables, None, mine, other
     )
-    part = scattered_over(keep_sums + swapped(give_sums), TILE[2])
+    part = scattered_over(keep_sums, swapped(give_sums), TILE[2])
     low = after(low + swapped(give_low), part)
     up = up + swapped(give_up)
     above = from_tile(low, -1)

time: 160 us -> 162 us (1.012)
  transfers between devices with their start and end apart: 39 -> 39, of which waited for: 23 -> 23; matrix products, arithmetic and copies ran while one was open for 6% -> 7% of each run, Pallas kernels for 0% -> 0%
where the time goes in v9:
time: 162 us; the launch traced here: 161 us
  waiting for transfers between devices  62.9 us (39%)
  starting transfers between devices  62.1 us (38%)
  Pallas kernels  17.6 us (11%)
  other arithmetic  10.7 us (7%)
  local copies, waits for them, and re-layouts  6.21 us (4%)
  between operations  1.73 us (1%)
    ppermute x6, waiting for transfers between devices, moved_along(): return lax.ppermute(value, TILE, route)  30.2 us
    ppermute x11, starting transfers between devices, swapped(): return lax.ppermute(value, 'pos', [(0, 1), (1, 0)])  29.1 us
    ppermute x4, starting transfers between devices, from_tile(): lax.ppermute(value, TILE, [((i + distance) % count, i) for i in range(cou...  18.2 us
    pallas_call x2, Pallas kernels, run_positions(): pl.pallas_call(kernel, out_shape=(quarter,) * 4 + (pieces_of,) * 2, in_sp...  17.6 us
    ppermute x4, waiting for transfers between devices, from_tile(): lax.ppermute(value, TILE, [((i + distance) % count, i) for i in range(cou...  12.5 us
    ppermute x6, waiting for transfers between devices, scattered_over(): arrived.append(lax.ppermute(pieces[step], axis, route))  7.41 us
    ppermute x6, waiting for transfers between devices, shifts_among(): total = total + lax.ppermute(value, axis, route)  5.64 us
    ppermute x6, starting transfers between devices, scattered_over(): arrived.append(lax.ppermute(pieces[step], axis, route))  5.5 us
  transfers between devices with their start and end apart: 39, of which 23 were waited for; matrix products, arithmetic and copies ran while one was open for 7% of the time, Pallas kernels for 0%

profile of v9, /device:TPU:1, one launch (start us, length us, event | category | flops | bytes accessed | tf_op | source)
XLA Modules:
  0.0 161.3 jit_solution(15663881437077995684)
XLA Ops:
  0.6 1.1 constant_dynamic-slice_fusion
  1.7 11.1 %collective-permute-start = (f32[2,128,512]{2,1,0:T(8,128)S(1)}, f32[2,128,512]{2,1,0:T(8,128)S(1)}, u32[]{:S(2)}, u32[]{:S(2)}) collective-permute-start(f32[2,128,512]{2,1,0:T(8,128)S(1)} %constant_dynamic-slice_fusion), channel_id=1, source_target_pairs={{2,0},{4,2},{6,4},{8,6},{10,8},{12,10},{14,12},{16,14},{18,16},{20... | collective-permute-start | bytes 1572872 | tf_op jit(solution)/shard_map/ppermute | solution.py:32
  12.8 10.6 %collective-permute-done.refs_7_ = f32[2,128,512]{2,1,0:T(8,128)S(1)} collective-permute-done((f32[2,128,512]{2,1,0:T(8,128)S(1)}, f32[2,128,512]{2,1,0:T(8,128)S(1)}, u32[]{:S(2)}, u32[]{:S(2)}) %collective-permute-start) | collective-permute-done | bytes 524320 | tf_op jit(solution)/shard_map/ppermute | solution.py:32
  23.4 1.5 collective-permute-start.1
  25.6 0.9 collective-permute-done.1.refs_8_
  26.5 0.8 copy-done.6
  27.3 8.8 %positions.2 = (f32[3,4,128,128]{3,2,1,0:T(8,128)}, f32[3,4,128,128]{3,2,1,0:T(8,128)}, f32[3,4,128,128]{3,2,1,0:T(8,128)}, f32[3,4,128,128]{3,2,1,0:T(8,128)}, ...) custom-call(s32[1,1,32]{2,1,0:T(1,128)} %refs_0_.3, s32[1,1,32]{2,1,0:T(1,128)} %refs_1_.3, s32[1,1]{1,0:T(1,128)S(6)} %copy.21.refs_2_, ...), custom_call_target="tpu_custom_call" | custom-call | flops 12999999488 | bytes 8388608 | tf_op jit(solution)/shard_map/positions/pallas_call | solution.py:275
  36.1 5.5 %collective-permute-start.2 = (f32[4,48,128]{2,1,0:T(8,128)}, f32[4,48,128]{2,1,0:T(8,128)S(1)}, u32[]{:S(2)}, u32[]{:S(2)}) collective-permute-start(f32[4,48,128]{2,1,0:T(8,128)} %get-tuple-element.19), channel_id=1, source_target_pairs={{0,1},{1,0},{2,3},{3,2},{4,5},{5,4},{6,7},{7,6},{8,9},{9,8},{10,11... | collective-permute-start | bytes 294920 | tf_op jit(solution)/shard_map/ppermute | solution.py:27
  41.7 0.4 collective-permute-start.17
  42.1 0.6 collective-permute-done.2
  42.8 0.8 fusion.18
  43.6 2.7 %collective-permute-start.5 = (f32[48,128]{1,0:T(8,128)S(1)}, f32[48,128]{1,0:T(8,128)S(1)}, u32[]{:S(2)}, u32[]{:S(2)}) collective-permute-start(f32[48,128]{1,0:T(8,128)S(1)} %get-tuple-element.48), channel_id=1, source_target_pairs={{0,6},{2,0},{4,2},{6,4},{1,7},{3,1},{5,3},{7,5},{8,14},{10,8},{12,... | collective-permute-start | bytes 73736 | tf_op jit(solution)/shard_map/ppermute | solution.py:347
  46.3 1.2 collective-permute-done.3
  47.5 3.0 %collective-permute-done.4 = f32[48,128]{1,0:T(8,128)S(1)} collective-permute-done((f32[48,128]{1,0:T(8,128)S(1)}, f32[48,128]{1,0:T(8,128)S(1)}, u32[]{:S(2)}, u32[]{:S(2)}) %collective-permute-start.4) | collective-permute-done | bytes 24608 | tf_op jit(solution)/shard_map/ppermute | solution.py:347
  50.5 0.7 fusion.22
  51.3 1.6 %add_add_fusion.2 = (f32[3,4,128,128]{3,2,1,0:T(8,128)S(1)}, f32[3,4,128,128]{3,2,1,0:T(8,128)S(1)}) fusion(f32[3,4,128,128]{3,2,1,0:T(8,128)} %get-tuple-element.22, f32[3,4,128,128]{3,2,1,0:T(8,128)S(1)} %collective-permute-done.17, f32[128]{0:T(128)S(1)} %fusion.28, f32[3,4,128,128]{3,2,1,0:T(8,128)} %get-tuple-element.20, ...), kind=kLoop, calls=%fused_computation.4 | loop fusion | flops 786432 | bytes 4719104 | tf_op jit(solution)/shard_map/add | solution.py:371
  53.0 6.9 %collective-permute-start.19 = (f32[3,4,128,128]{3,2,1,0:T(8,128)S(1)}, f32[3,4,128,128]{3,2,1,0:T(8,128)}, u32[]{:S(2)}, u32[]{:S(2)}) collective-permute-start(f32[3,4,128,128]{3,2,1,0:T(8,128)S(1)} %get-tuple-element.24), channel_id=1, source_target_pairs={{2,0},{4,2},{6,4},{8,6},{10,8},{12,10},{14,12},{16,14},{18,16},{20... | collective-permute-start | bytes 2359304 | tf_op jit(solution)/shard_map/ppermute | solution.py:32
  59.9 4.3 %collective-permute-done.6 = f32[48,128]{1,0:T(8,128)S(1)} collective-permute-done((f32[48,128]{1,0:T(8,128)S(1)}, f32[48,128]{1,0:T(8,128)S(1)}, u32[]{:S(2)}, u32[]{:S(2)}) %collective-permute-start.6) | collective-permute-done | bytes 24608 | tf_op jit(solution)/shard_map/ppermute | solution.py:329
  64.2 5.2 %collective-permute-done.7 = f32[48,128]{1,0:T(8,128)S(1)} collective-permute-done((f32[48,128]{1,0:T(8,128)S(1)}, f32[48,128]{1,0:T(8,128)S(1)}, u32[]{:S(2)}, u32[]{:S(2)}) %collective-permute-start.7) | collective-permute-done | bytes 24608 | tf_op jit(solution)/shard_map/ppermute | solution.py:329
  69.3 0.8 collective-permute-start.8
  70.1 6.2 %collective-permute-done.8 = f32[48,128]{1,0:T(8,128)S(1)} collective-permute-done((f32[48,128]{1,0:T(8,128)S(1)}, f32[48,128]{1,0:T(8,128)S(1)}, u32[]{:S(2)}, u32[]{:S(2)}) %collective-permute-start.8) | collective-permute-done | bytes 24608 | tf_op jit(solution)/shard_map/ppermute | solution.py:329
  76.4 1.4 collective-permute-start.9
  78.0 0.2 copy.16
  78.2 1.2 copy.17
  79.5 0.2 copy.18
  79.7 1.2 collective-permute-done.10
  80.9 0.5 collective-permute-done.9
  81.6 1.4 collective-permute-start.12
  83.0 1.2 add.263
  84.2 1.2 add.266
  85.5 0.2 fusion.2
  85.8 7.1 %collective-permute-start.20 = (f32[2,4,256,128]{3,2,1,0:T(8,128)S(1)}, f32[2,4,256,128]{3,2,1,0:T(8,128)S(1)}, u32[]{:S(2)}, u32[]{:S(2)}) collective-permute-start(f32[2,4,256,128]{3,2,1,0:T(8,128)S(1)} %pad_maximum_fusion.refs_6_), channel_id=1, source_target_pairs={{0,1},{1,0},{2,3},{3,2},{4,5},{5,4},{6,7},{7,6},{8,9},{9,8},{10,11... | collective-permute-start | bytes 3145736 | tf_op jit(solution)/shard_map/ppermute | solution.py:27
  92.9 1.6 %collective-permute-start.15 = (f32[192,128]{1,0:T(8,128)S(1)}, f32[192,128]{1,0:T(8,128)S(1)}, u32[]{:S(2)}, u32[]{:S(2)}) collective-permute-start(f32[192,128]{1,0:T(8,128)S(1)} %pad_maximum_fusion.4), channel_id=1, source_target_pairs={{0,1},{1,0},{2,3},{3,2},{4,5},{5,4},{6,7},{7,6},{8,9},{9,8},{10,11... | collective-permute-start | bytes 294920 | tf_op jit(solution)/shard_map/ppermute | solution.py:27
  94.6 0.9 collective-permute-done.15
  95.6 0.7 add_divide_fusion.1.refs_3_
  96.3 1.0 copy-done.5
  97.3 8.8 %positions.3 = (f32[3,4,128,128]{3,2,1,0:T(8,128)}, f32[3,4,128,128]{3,2,1,0:T(8,128)}, f32[3,4,128,128]{3,2,1,0:T(8,128)}, f32[3,4,128,128]{3,2,1,0:T(8,128)}, ...) custom-call(s32[1,1,32]{2,1,0:T(1,128)} %refs_0_.3, s32[1,1,32]{2,1,0:T(1,128)} %refs_1_.3, s32[1,1]{1,0:T(1,128)S(6)} %copy.21.refs_2_, ...), custom_call_target="tpu_custom_call" | custom-call | flops 12999999488 | bytes 8388608 | tf_op jit(solution)/shard_map/positions/pallas_call | solution.py:275
  106.1 5.4 %collective-permute-start.22 = (f32[4,48,128]{2,1,0:T(8,128)}, f32[4,48,128]{2,1,0:T(8,128)S(1)}, u32[]{:S(2)}, u32[]{:S(2)}) collective-permute-start(f32[4,48,128]{2,1,0:T(8,128)} %get-tuple-element.31), channel_id=1, source_target_pairs={{0,1},{1,0},{2,3},{3,2},{4,5},{5,4},{6,7},{7,6},{8,9},{9,8},{10,11... | collective-permute-start | bytes 294920 | tf_op jit(solution)/shard_map/ppermute | solution.py:27
  111.6 1.1 collective-permute-done.22
  112.7 0.8 fusion.11
  113.6 2.7 %collective-permute-start.25 = (f32[48,128]{1,0:T(8,128)S(1)}, f32[48,128]{1,0:T(8,128)S(1)}, u32[]{:S(2)}, u32[]{:S(2)}) collective-permute-start(f32[48,128]{1,0:T(8,128)S(1)} %get-tuple-element.43), channel_id=1, source_target_pairs={{0,6},{2,0},{4,2},{6,4},{1,7},{3,1},{5,3},{7,5},{8,14},{10,8},{12,... | collective-permute-start | bytes 73736 | tf_op jit(solution)/shard_map/ppermute | solution.py:347
  116.2 0.9 collective-permute-start.21
  117.2 0.3 collective-permute-done.23
  117.4 3.0 %collective-permute-done.24 = f32[48,128]{1,0:T(8,128)S(1)} collective-permute-done((f32[48,128]{1,0:T(8,128)S(1)}, f32[48,128]{1,0:T(8,128)S(1)}, u32[]{:S(2)}, u32[]{:S(2)}) %collective-permute-start.24) | collective-permute-done | bytes 24608 | tf_op jit(solution)/shard_map/ppermute | solution.py:347
  120.4 0.7 fusion.15
  121.2 1.2 add_add_fusion
  122.6 3.9 %collective-permute-done.26 = f32[48,128]{1,0:T(8,128)S(1)} collective-permute-done((f32[48,128]{1,0:T(8,128)S(1)}, f32[48,128]{1,0:T(8,128)S(1)}, u32[]{:S(2)}, u32[]{:S(2)}) %collective-permute-start.26) | collective-permute-done | bytes 24608 | tf_op jit(solution)/shard_map/ppermute | solution.py:329
  126.5 4.8 %collective-permute-done.27 = f32[48,128]{1,0:T(8,128)S(1)} collective-permute-done((f32[48,128]{1,0:T(8,128)S(1)}, f32[48,128]{1,0:T(8,128)S(1)}, u32[]{:S(2)}, u32[]{:S(2)}) %collective-permute-start.27) | collective-permute-done | bytes 24608 | tf_op jit(solution)/shard_map/ppermute | solution.py:329
  131.3 1.0 collective-permute-start.28
  132.3 5.9 %collective-permute-done.28 = f32[48,128]{1,0:T(8,128)S(1)} collective-permute-done((f32[48,128]{1,0:T(8,128)S(1)}, f32[48,128]{1,0:T(8,128)S(1)}, u32[]{:S(2)}, u32[]{:S(2)}) %collective-permute-start.28) | collective-permute-done | bytes 24608 | tf_op jit(solution)/shard_map/ppermute | solution.py:329
  138.2 1.4 collective-permute-start.29
  139.6 1.5 collective-permute-done.31
  141.1 1.6 collective-permute-done.30
  142.7 0.8 collective-permute-done.29
  143.5 1.9 %collective-permute-done.33 = f32[3,4,128,128]{3,2,1,0:T(8,128)S(1)} collective-permute-done((f32[3,4,128,128]{3,2,1,0:T(8,128)S(1)}, f32[3,4,128,128]{3,2,1,0:T(8,128)S(1)}, u32[]{:S(2)}, u32[]{:S(2)}) %collective-permute-start.33) | collective-permute-done | bytes 786464 | tf_op jit(solution)/shard_map/ppermute | solution.py:32
  145.7 0.2 copy.19
  145.9 4.7 %collective-permute-start.34 = (f32[2,128,512]{1,2,0:T(8,128)S(1)}, f32[2,128,512]{1,2,0:T(8,128)S(1)}, u32[]{:S(2)}, u32[]{:S(2)}) collective-permute-start(f32[2,128,512]{1,2,0:T(8,128)S(1)} %bitcast.54), channel_id=1, source_target_pairs={{0,1},{1,0},{2,3},{3,2},{4,5},{5,4},{6,7},{7,6},{8,9},{9,8},{10,11... | collective-permute-start | bytes 1572872 | tf_op jit(solution)/shard_map/ppermute | solution.py:27
  150.7 2.5 %collective-permute-start.37 = (f32[48,128]{1,0:T(8,128)S(1)}, f32[48,128]{1,0:T(8,128)S(1)}, u32[]{:S(2)}, u32[]{:S(2)}) collective-permute-start(f32[48,128]{1,0:T(8,128)S(1)} %add_add_fusion.4), channel_id=1, source_target_pairs={{2,0},{4,2},{6,4},{0,6},{3,1},{5,3},{7,5},{1,7},{10,8},{12,10},{14... | collective-permute-start | bytes 73736 | tf_op jit(solution)/shard_map/ppermute | solution.py:359
  153.2 0.6 collective-permute-start.35
  153.7 0.4 collective-permute-done.37
  154.1 3.2 %collective-permute-done.36 = f32[48,128]{1,0:T(8,128)S(1)} collective-permute-done((f32[48,128]{1,0:T(8,128)S(1)}, f32[48,128]{1,0:T(8,128)S(1)}, u32[]{:S(2)}, u32[]{:S(2)}) %collective-permute-start.36) | collective-permute-done | bytes 24608 | tf_op jit(solution)/shard_map/ppermute | solution.py:359
  157.6 1.6 collective-permute-start.38
  159.3 1.3 copy.20
  160.6 0.7 add_divide_fusion
  (78 shorter events, 2.1 us)
Async XLA Ops:
  1.7 21.7 %collective-permute-start = (f32[2,128,512]{2,1,0:T(8,128)S(1)}, f32[2,128,512]{2,1,0:T(8,128)S(1)}, u32[]{:S(2)}, u32[]{:S(2)}) collective-permute-start(f32[2,128,512]{2,1,0:T(8,128)S(1)} %constant_dynamic-slice_fusion), channel_id=1, source_target_pairs={{2,0},{4,2},{6,4},{8,6},{10,8},{12,10},{14,12},{16,14},{18,16},{20... | collective-permute-start | bytes 1572872 | tf_op jit(solution)/shard_map/ppermute | solution.py:32
  23.4 3.1 %copy-start.3 = (f32[2,128,512]{2,1,0:T(8,128)}, f32[2,128,512]{2,1,0:T(8,128)S(1)}, u32[]{:S(2)}) copy-start(f32[2,128,512]{2,1,0:T(8,128)S(1)} %collective-permute-done.refs_7_) | copy-start | bytes 1572868
  23.4 3.1 %collective-permute-start.1 = (f32[2,128,512]{2,1,0:T(8,128)S(1)}, f32[2,128,512]{2,1,0:T(8,128)S(1)}, u32[]{:S(2)}, u32[]{:S(2)}) collective-permute-start(f32[2,128,512]{2,1,0:T(8,128)S(1)} %collective-permute-done.refs_7_), channel_id=1, source_target_pairs={{0,1},{1,0},{2,3},{3,2},{4,5},{5,4},{6,7},{7,6},{8,9},{9,8},{10,11... | collective-permute-start | bytes 1572872 | tf_op jit(solution)/shard_map/ppermute | solution.py:27
  26.5 0.8 copy-start.6
  36.1 6.6 %collective-permute-start.2 = (f32[4,48,128]{2,1,0:T(8,128)}, f32[4,48,128]{2,1,0:T(8,128)S(1)}, u32[]{:S(2)}, u32[]{:S(2)}) collective-permute-start(f32[4,48,128]{2,1,0:T(8,128)} %get-tuple-element.19), channel_id=1, source_target_pairs={{0,1},{1,0},{2,3},{3,2},{4,5},{5,4},{6,7},{7,6},{8,9},{9,8},{10,11... | collective-permute-start | bytes 294920 | tf_op jit(solution)/shard_map/ppermute | solution.py:27
  41.6 9.6 %collective-permute-start.16 = (f32[3,4,128,128]{3,2,1,0:T(8,128)}, f32[3,4,128,128]{3,2,1,0:T(8,128)S(1)}, u32[]{:S(2)}, u32[]{:S(2)}) collective-permute-start(f32[3,4,128,128]{3,2,1,0:T(8,128)} %get-tuple-element.21), channel_id=1, source_target_pairs={{0,1},{1,0},{2,3},{3,2},{4,5},{5,4},{6,7},{7,6},{8,9},{9,8},{10,11... | collective-permute-start | bytes 2359304 | tf_op jit(solution)/shard_map/ppermute | solution.py:27
  41.7 9.6 %collective-permute-start.17 = (f32[3,4,128,128]{3,2,1,0:T(8,128)}, f32[3,4,128,128]{3,2,1,0:T(8,128)S(1)}, u32[]{:S(2)}, u32[]{:S(2)}) collective-permute-start(f32[3,4,128,128]{3,2,1,0:T(8,128)} %get-tuple-element.23), channel_id=1, source_target_pairs={{0,1},{1,0},{2,3},{3,2},{4,5},{5,4},{6,7},{7,6},{8,9},{9,8},{10,11... | collective-permute-start | bytes 2359304 | tf_op jit(solution)/shard_map/ppermute | solution.py:27
  43.5 4.0 %collective-permute-start.3 = (f32[48,128]{1,0:T(8,128)S(1)}, f32[48,128]{1,0:T(8,128)S(1)}, u32[]{:S(2)}, u32[]{:S(2)}) collective-permute-start(f32[48,128]{1,0:T(8,128)S(1)} %get-tuple-element.47), channel_id=1, source_target_pairs={{0,2},{2,4},{4,6},{6,0},{1,3},{3,5},{5,7},{7,1},{8,10},{10,12},{12... | collective-permute-start | bytes 73736 | tf_op jit(solution)/shard_map/ppermute | solution.py:347
  43.6 3.9 %collective-permute-start.5 = (f32[48,128]{1,0:T(8,128)S(1)}, f32[48,128]{1,0:T(8,128)S(1)}, u32[]{:S(2)}, u32[]{:S(2)}) collective-permute-start(f32[48,128]{1,0:T(8,128)S(1)} %get-tuple-element.48), channel_id=1, source_target_pairs={{0,6},{2,0},{4,2},{6,4},{1,7},{3,1},{5,3},{7,5},{8,14},{10,8},{12,... | collective-permute-start | bytes 73736 | tf_op jit(solution)/shard_map/ppermute | solution.py:347
  46.3 4.2 %collective-permute-start.4 = (f32[48,128]{1,0:T(8,128)S(1)}, f32[48,128]{1,0:T(8,128)S(1)}, u32[]{:S(2)}, u32[]{:S(2)}) collective-permute-start(f32[48,128]{1,0:T(8,128)S(1)} %get-tuple-element.49), channel_id=1, source_target_pairs={{0,4},{2,6},{4,0},{6,2},{1,5},{3,7},{5,1},{7,3},{8,12},{10,14},{12... | collective-permute-start | bytes 73736 | tf_op jit(solution)/shard_map/ppermute | solution.py:347
  52.9 30.1 %collective-permute-start.18 = (f32[3,4,128,128]{3,2,1,0:T(8,128)S(1)}, f32[3,4,128,128]{3,2,1,0:T(8,128)}, u32[]{:S(2)}, u32[]{:S(2)}) collective-permute-start(f32[3,4,128,128]{3,2,1,0:T(8,128)S(1)} %get-tuple-element.26), channel_id=1, source_target_pairs={{254,0},{0,2},{2,4},{4,6},{6,8},{8,10},{10,12},{12,14},{14,16},{16... | collective-permute-start | bytes 2359304 | tf_op jit(solution)/shard_map/ppermute | solution.py:32
  53.0 30.0 %collective-permute-start.19 = (f32[3,4,128,128]{3,2,1,0:T(8,128)S(1)}, f32[3,4,128,128]{3,2,1,0:T(8,128)}, u32[]{:S(2)}, u32[]{:S(2)}) collective-permute-start(f32[3,4,128,128]{3,2,1,0:T(8,128)S(1)} %get-tuple-element.24), channel_id=1, source_target_pairs={{2,0},{4,2},{6,4},{8,6},{10,8},{12,10},{14,12},{16,14},{18,16},{20... | collective-permute-start | bytes 2359304 | tf_op jit(solution)/shard_map/ppermute | solution.py:32
  59.9 4.3 %collective-permute-start.6 = (f32[48,128]{1,0:T(8,128)S(1)}, f32[48,128]{1,0:T(8,128)S(1)}, u32[]{:S(2)}, u32[]{:S(2)}) collective-permute-start(f32[48,128]{1,0:T(8,128)S(1)} %fusion.22), channel_id=1, source_target_pairs={{0,32},{2,226},{4,228},{6,230},{8,232},{10,234},{12,236},{14,238},... | collective-permute-start | bytes 73736 | tf_op jit(solution)/shard_map/ppermute | solution.py:329
  64.2 5.2 %collective-permute-start.7 = (f32[48,128]{1,0:T(8,128)S(1)}, f32[48,128]{1,0:T(8,128)S(1)}, u32[]{:S(2)}, u32[]{:S(2)}) collective-permute-start(f32[48,128]{1,0:T(8,128)S(1)} %add.247), channel_id=1, source_target_pairs={{0,64},{2,194},{4,196},{6,198},{8,200},{10,202},{12,204},{14,206},... | collective-permute-start | bytes 73736 | tf_op jit(solution)/shard_map/ppermute | solution.py:329
  69.3 7.0 %collective-permute-start.8 = (f32[48,128]{1,0:T(8,128)S(1)}, f32[48,128]{1,0:T(8,128)S(1)}, u32[]{:S(2)}, u32[]{:S(2)}) collective-permute-start(f32[48,128]{1,0:T(8,128)S(1)} %add.248), channel_id=1, source_target_pairs={{0,128},{2,130},{4,132},{6,134},{8,136},{10,138},{12,140},{14,142}... | collective-permute-start | bytes 73736 | tf_op jit(solution)/shard_map/ppermute | solution.py:329
  76.3 3.3 %collective-permute-start.11 = (f32[48,128]{1,0:T(8,128)S(1)}, f32[48,128]{1,0:T(8,128)S(1)}, u32[]{:S(2)}, u32[]{:S(2)}) collective-permute-start(f32[48,128]{1,0:T(8,128)S(1)} %add.249), channel_id=1, source_target_pairs={{0,24},{8,0},{16,8},{24,16},{1,25},{9,1},{17,9},{25,17},{2,26},{10... | collective-permute-start | bytes 73736 | tf_op jit(solution)/shard_map/ppermute | solution.py:382
  76.3 4.6 %collective-permute-start.10 = (f32[48,128]{1,0:T(8,128)S(1)}, f32[48,128]{1,0:T(8,128)S(1)}, u32[]{:S(2)}, u32[]{:S(2)}) collective-permute-start(f32[48,128]{1,0:T(8,128)S(1)} %add.249), channel_id=1, source_target_pairs={{0,16},{8,24},{16,0},{24,8},{1,17},{9,25},{17,1},{25,9},{2,18},{10... | collective-permute-start | bytes 73736 | tf_op jit(solution)/shard_map/ppermute | solution.py:382
  76.4 5.0 %collective-permute-start.9 = (f32[48,128]{1,0:T(8,128)S(1)}, f32[48,128]{1,0:T(8,128)S(1)}, u32[]{:S(2)}, u32[]{:S(2)}) collective-permute-start(f32[48,128]{1,0:T(8,128)S(1)} %add.249), channel_id=1, source_target_pairs={{0,8},{8,16},{16,24},{24,0},{1,9},{9,17},{17,25},{25,1},{2,10},{10... | collective-permute-start | bytes 73736 | tf_op jit(solution)/shard_map/ppermute | solution.py:382
  81.4 11.4 %collective-permute-start.14 = (f32[48,128]{1,0:T(8,128)S(1)}, f32[48,128]{1,0:T(8,128)S(1)}, u32[]{:S(2)}, u32[]{:S(2)}) collective-permute-start(f32[48,128]{1,0:T(8,128)S(1)} %add_add_fusion.5), channel_id=1, source_target_pairs={{2,0},{4,2},{6,4},{0,6},{3,1},{5,3},{7,5},{1,7},{10,8},{12,10},{14... | collective-permute-start | bytes 73736 | tf_op jit(solution)/shard_map/ppermute | solution.py:359
  81.5 11.4 %collective-permute-start.13 = (f32[48,128]{1,0:T(8,128)S(1)}, f32[48,128]{1,0:T(8,128)S(1)}, u32[]{:S(2)}, u32[]{:S(2)}) collective-permute-start(f32[48,128]{1,0:T(8,128)S(1)} %add_add_fusion.5), channel_id=1, source_target_pairs={{4,0},{6,2},{0,4},{2,6},{5,1},{7,3},{1,5},{3,7},{12,8},{14,10},{8,... | collective-permute-start | bytes 73736 | tf_op jit(solution)/shard_map/ppermute | solution.py:359
  81.6 11.3 %collective-permute-start.12 = (f32[48,128]{1,0:T(8,128)S(1)}, f32[48,128]{1,0:T(8,128)S(1)}, u32[]{:S(2)}, u32[]{:S(2)}) collective-permute-start(f32[48,128]{1,0:T(8,128)S(1)} %add_add_fusion.5), channel_id=1, source_target_pairs={{6,0},{0,2},{2,4},{4,6},{7,1},{1,3},{3,5},{5,7},{14,8},{8,10},{10,... | collective-permute-start | bytes 73736 | tf_op jit(solution)/shard_map/ppermute | solution.py:359
  85.7 9.9 %copy-start.4 = (f32[2,128,128]{2,1,0:T(8,128)S(1)}, f32[2,128,128]{2,1,0:T(8,128)}, u32[]{:S(2)}) copy-start(f32[2,128,128]{2,1,0:T(8,128)} %refs_3_.1) | copy-start | bytes 393220
  85.8 10.5 %copy-start = (f32[2,4,256,128]{3,2,1,0:T(8,128)}, f32[2,4,256,128]{3,2,1,0:T(8,128)S(1)}, u32[]{:S(2)}) copy-start(f32[2,4,256,128]{3,2,1,0:T(8,128)S(1)} %pad_maximum_fusion.refs_6_) | copy-start | bytes 3145732
  85.8 10.5 %collective-permute-start.20 = (f32[2,4,256,128]{3,2,1,0:T(8,128)S(1)}, f32[2,4,256,128]{3,2,1,0:T(8,128)S(1)}, u32[]{:S(2)}, u32[]{:S(2)}) collective-permute-start(f32[2,4,256,128]{3,2,1,0:T(8,128)S(1)} %pad_maximum_fusion.refs_6_), channel_id=1, source_target_pairs={{0,1},{1,0},{2,3},{3,2},{4,5},{5,4},{6,7},{7,6},{8,9},{9,8},{10,11... | collective-permute-start | bytes 3145736 | tf_op jit(solution)/shard_map/ppermute | solution.py:27
  92.9 2.6 %collective-permute-start.15 = (f32[192,128]{1,0:T(8,128)S(1)}, f32[192,128]{1,0:T(8,128)S(1)}, u32[]{:S(2)}, u32[]{:S(2)}) collective-permute-start(f32[192,128]{1,0:T(8,128)S(1)} %pad_maximum_fusion.4), channel_id=1, source_target_pairs={{0,1},{1,0},{2,3},{3,2},{4,5},{5,4},{6,7},{7,6},{8,9},{9,8},{10,11... | collective-permute-start | bytes 294920 | tf_op jit(solution)/shard_map/ppermute | solution.py:27
  96.3 1.0 copy-start.5
  106.1 39.4 %copy-start.1 = (f32[3,4,128,128]{3,2,1,0:T(8,128)S(1)}, f32[3,4,128,128]{3,2,1,0:T(8,128)}, u32[]{:S(2)}) copy-start(f32[3,4,128,128]{3,2,1,0:T(8,128)} %get-tuple-element.28) | copy-start | bytes 2359300
  106.1 6.6 %collective-permute-start.22 = (f32[4,48,128]{2,1,0:T(8,128)}, f32[4,48,128]{2,1,0:T(8,128)S(1)}, u32[]{:S(2)}, u32[]{:S(2)}) collective-permute-start(f32[4,48,128]{2,1,0:T(8,128)} %get-tuple-element.31), channel_id=1, source_target_pairs={{0,1},{1,0},{2,3},{3,2},{4,5},{5,4},{6,7},{7,6},{8,9},{9,8},{10,11... | collective-permute-start | bytes 294920 | tf_op jit(solution)/shard_map/ppermute | solution.py:27
  111.5 9.6 %collective-permute-start.32 = (f32[3,4,128,128]{3,2,1,0:T(8,128)}, f32[3,4,128,128]{3,2,1,0:T(8,128)S(1)}, u32[]{:S(2)}, u32[]{:S(2)}) collective-permute-start(f32[3,4,128,128]{3,2,1,0:T(8,128)} %get-tuple-element.33), channel_id=1, source_target_pairs={{0,1},{1,0},{2,3},{3,2},{4,5},{5,4},{6,7},{7,6},{8,9},{9,8},{10,11... | collective-permute-start | bytes 2359304 | tf_op jit(solution)/shard_map/ppermute | solution.py:27
  113.5 4.0 %collective-permute-start.23 = (f32[48,128]{1,0:T(8,128)S(1)}, f32[48,128]{1,0:T(8,128)S(1)}, u32[]{:S(2)}, u32[]{:S(2)}) collective-permute-start(f32[48,128]{1,0:T(8,128)S(1)} %get-tuple-element.42), channel_id=1, source_target_pairs={{0,2},{2,4},{4,6},{6,0},{1,3},{3,5},{5,7},{7,1},{8,10},{10,12},{12... | collective-permute-start | bytes 73736 | tf_op jit(solution)/shard_map/ppermute | solution.py:347
  113.6 3.9 %collective-permute-start.25 = (f32[48,128]{1,0:T(8,128)S(1)}, f32[48,128]{1,0:T(8,128)S(1)}, u32[]{:S(2)}, u32[]{:S(2)}) collective-permute-start(f32[48,128]{1,0:T(8,128)S(1)} %get-tuple-element.43), channel_id=1, source_target_pairs={{0,6},{2,0},{4,2},{6,4},{1,7},{3,1},{5,3},{7,5},{8,14},{10,8},{12,... | collective-permute-start | bytes 73736 | tf_op jit(solution)/shard_map/ppermute | solution.py:347
  116.2 4.2 %collective-permute-start.24 = (f32[48,128]{1,0:T(8,128)S(1)}, f32[48,128]{1,0:T(8,128)S(1)}, u32[]{:S(2)}, u32[]{:S(2)}) collective-permute-start(f32[48,128]{1,0:T(8,128)S(1)} %get-tuple-element.44), channel_id=1, source_target_pairs={{0,4},{2,6},{4,0},{6,2},{1,5},{3,7},{5,1},{7,3},{8,12},{10,14},{12... | collective-permute-start | bytes 73736 | tf_op jit(solution)/shard_map/ppermute | solution.py:347
  116.2 27.3 %collective-permute-start.21 = (f32[3,4,128,128]{3,2,1,0:T(8,128)}, f32[3,4,128,128]{3,2,1,0:T(8,128)S(1)}, u32[]{:S(2)}, u32[]{:S(2)}) collective-permute-start(f32[3,4,128,128]{3,2,1,0:T(8,128)} %get-tuple-element.29), channel_id=1, source_target_pairs={{0,1},{1,0},{2,3},{3,2},{4,5},{5,4},{6,7},{7,6},{8,9},{9,8},{10,11... | collective-permute-start | bytes 2359304 | tf_op jit(solution)/shard_map/ppermute | solution.py:27
  122.4 23.0 %collective-permute-start.33 = (f32[3,4,128,128]{3,2,1,0:T(8,128)S(1)}, f32[3,4,128,128]{3,2,1,0:T(8,128)S(1)}, u32[]{:S(2)}, u32[]{:S(2)}) collective-permute-start(f32[3,4,128,128]{3,2,1,0:T(8,128)S(1)} %add_add_fusion), channel_id=1, source_target_pairs={{254,0},{0,2},{2,4},{4,6},{6,8},{8,10},{10,12},{12,14},{14,16},{16... | collective-permute-start | bytes 2359304 | tf_op jit(solution)/shard_map/ppermute | solution.py:32
  122.5 4.0 %collective-permute-start.26 = (f32[48,128]{1,0:T(8,128)S(1)}, f32[48,128]{1,0:T(8,128)S(1)}, u32[]{:S(2)}, u32[]{:S(2)}) collective-permute-start(f32[48,128]{1,0:T(8,128)S(1)} %fusion.15), channel_id=1, source_target_pairs={{0,32},{2,226},{4,228},{6,230},{8,232},{10,234},{12,236},{14,238},... | collective-permute-start | bytes 73736 | tf_op jit(solution)/shard_map/ppermute | solution.py:329
  126.5 4.8 %collective-permute-start.27 = (f32[48,128]{1,0:T(8,128)S(1)}, f32[48,128]{1,0:T(8,128)S(1)}, u32[]{:S(2)}, u32[]{:S(2)}) collective-permute-start(f32[48,128]{1,0:T(8,128)S(1)} %add.281), channel_id=1, source_target_pairs={{0,64},{2,194},{4,196},{6,198},{8,200},{10,202},{12,204},{14,206},... | collective-permute-start | bytes 73736 | tf_op jit(solution)/shard_map/ppermute | solution.py:329
  131.3 6.9 %collective-permute-start.28 = (f32[48,128]{1,0:T(8,128)S(1)}, f32[48,128]{1,0:T(8,128)S(1)}, u32[]{:S(2)}, u32[]{:S(2)}) collective-permute-start(f32[48,128]{1,0:T(8,128)S(1)} %add.282), channel_id=1, source_target_pairs={{0,128},{2,130},{4,132},{6,134},{8,136},{10,138},{12,140},{14,142}... | collective-permute-start | bytes 73736 | tf_op jit(solution)/shard_map/ppermute | solution.py:329
  138.1 3.0 %collective-permute-start.31 = (f32[48,128]{1,0:T(8,128)S(1)}, f32[48,128]{1,0:T(8,128)S(1)}, u32[]{:S(2)}, u32[]{:S(2)}) collective-permute-start(f32[48,128]{1,0:T(8,128)S(1)} %add.283), channel_id=1, source_target_pairs={{0,24},{8,0},{16,8},{24,16},{1,25},{9,1},{17,9},{25,17},{2,26},{10... | collective-permute-start | bytes 73736 | tf_op jit(solution)/shard_map/ppermute | solution.py:382
  138.1 4.6 %collective-permute-start.30 = (f32[48,128]{1,0:T(8,128)S(1)}, f32[48,128]{1,0:T(8,128)S(1)}, u32[]{:S(2)}, u32[]{:S(2)}) collective-permute-start(f32[48,128]{1,0:T(8,128)S(1)} %add.283), channel_id=1, source_target_pairs={{0,16},{8,24},{16,0},{24,8},{1,17},{9,25},{17,1},{25,9},{2,18},{10... | collective-permute-start | bytes 73736 | tf_op jit(solution)/shard_map/ppermute | solution.py:382
  138.2 5.3 %collective-permute-start.29 = (f32[48,128]{1,0:T(8,128)S(1)}, f32[48,128]{1,0:T(8,128)S(1)}, u32[]{:S(2)}, u32[]{:S(2)}) collective-permute-start(f32[48,128]{1,0:T(8,128)S(1)} %add.283), channel_id=1, source_target_pairs={{0,8},{8,16},{16,24},{24,0},{1,9},{9,17},{17,25},{25,1},{2,10},{10... | collective-permute-start | bytes 73736 | tf_op jit(solution)/shard_map/ppermute | solution.py:382
  145.9 11.4 %collective-permute-start.34 = (f32[2,128,512]{1,2,0:T(8,128)S(1)}, f32[2,128,512]{1,2,0:T(8,128)S(1)}, u32[]{:S(2)}, u32[]{:S(2)}) collective-permute-start(f32[2,128,512]{1,2,0:T(8,128)S(1)} %bitcast.54), channel_id=1, source_target_pairs={{0,1},{1,0},{2,3},{3,2},{4,5},{5,4},{6,7},{7,6},{8,9},{9,8},{10,11... | collective-permute-start | bytes 1572872 | tf_op jit(solution)/shard_map/ppermute | solution.py:27
  150.7 3.4 %collective-permute-start.37 = (f32[48,128]{1,0:T(8,128)S(1)}, f32[48,128]{1,0:T(8,128)S(1)}, u32[]{:S(2)}, u32[]{:S(2)}) collective-permute-start(f32[48,128]{1,0:T(8,128)S(1)} %add_add_fusion.4), channel_id=1, source_target_pairs={{2,0},{4,2},{6,4},{0,6},{3,1},{5,3},{7,5},{1,7},{10,8},{12,10},{14... | collective-permute-start | bytes 73736 | tf_op jit(solution)/shard_map/ppermute | solution.py:359
  153.2 4.2 %collective-permute-start.36 = (f32[48,128]{1,0:T(8,128)S(1)}, f32[48,128]{1,0:T(8,128)S(1)}, u32[]{:S(2)}, u32[]{:S(2)}) collective-permute-start(f32[48,128]{1,0:T(8,128)S(1)} %add_add_fusion.4), channel_id=1, source_target_pairs={{4,0},{6,2},{0,4},{2,6},{5,1},{7,3},{1,5},{3,7},{12,8},{14,10},{8,... | collective-permute-start | bytes 73736 | tf_op jit(solution)/shard_map/ppermute | solution.py:359
  153.2 4.2 %collective-permute-start.35 = (f32[48,128]{1,0:T(8,128)S(1)}, f32[48,128]{1,0:T(8,128)S(1)}, u32[]{:S(2)}, u32[]{:S(2)}) collective-permute-start(f32[48,128]{1,0:T(8,128)S(1)} %add_add_fusion.4), channel_id=1, source_target_pairs={{6,0},{0,2},{2,4},{4,6},{7,1},{1,3},{3,5},{5,7},{14,8},{8,10},{10,... | collective-permute-start | bytes 73736 | tf_op jit(solution)/shard_map/ppermute | solution.py:359
  157.6 3.0 %collective-permute-start.38 = (f32[192,128]{1,0:T(8,128)S(1)}, f32[192,128]{1,0:T(8,128)S(1)}, u32[]{:S(2)}, u32[]{:S(2)}) collective-permute-start(f32[192,128]{1,0:T(8,128)S(1)} %maximum_add_fusion), channel_id=1, source_target_pairs={{0,1},{1,0},{2,3},{3,2},{4,5},{5,4},{6,7},{7,6},{8,9},{9,8},{10,11... | collective-permute-start | bytes 294920 | tf_op jit(solution)/shard_map/ppermute | solution.py:27
  159.2 1.4 copy-start.2

commit v10 on v8

--- a/solution.py
+++ b/solution.py
@@ -420,7 +420,7 @@
     own_half = updated(up + above, in_blocks(own_half))
     mine = jnp.concatenate([own_half, updated(low + below, in_blocks(halo))], axis=2)
     other = swapped(mine)
-    probe_field = next_probe(part, None, probe_field)
+    probe_field = next_probe(after(part, mine), None, probe_field)
     up, low, give_up, give_low, keep_sums, give_sums = run_positions(
         scalars, probe_field, amps, tables, None, mine, other
     )

time: 160 us -> 160 us (level)
    ppermute x6, starting transfers between devices: 1.83 us -> 0.1 us  [moved_along(): return lax.ppermute(value, TILE, route)]
where the time goes in v10:
time: 160 us
  waiting for transfers between devices  62.7 us (39%)
  starting transfers between devices  62 us (39%)
  Pallas kernels  17.6 us (11%)
  other arithmetic  9.45 us (6%)
  local copies, waits for them, and re-layouts  6.24 us (4%)
  between operations  1.85 us (1%)
    ppermute x6, waiting for transfers between devices, moved_along(): return lax.ppermute(value, TILE, route)  30 us
    ppermute x11, starting transfers between devices, swapped(): return lax.ppermute(value, 'pos', [(0, 1), (1, 0)])  29.9 us
    ppermute x4, starting transfers between devices, from_tile(): lax.ppermute(value, TILE, [((i + distance) % count, i) for i in range(cou...  18.2 us
    pallas_call x2, Pallas kernels, run_positions(): pl.pallas_call(kernel, out_shape=(quarter,) * 4 + (pieces_of,) * 2, in_sp...  17.6 us
    ppermute x4, waiting for transfers between devices, from_tile(): lax.ppermute(value, TILE, [((i + distance) % count, i) for i in range(cou...  13 us
    ppermute x6, starting transfers between devices, scattered_over(): arrived.append(lax.ppermute(pieces[step], axis, route))  6.44 us
    ppermute x6, waiting for transfers between devices, scattered_over(): arrived.append(lax.ppermute(pieces[step], axis, route))  6.41 us
    ppermute x6, waiting for transfers between devices, shifts_among(): total = total + lax.ppermute(value, axis, route)  6.15 us
  transfers between devices with their start and end apart: 39, of which 23 were waited for; matrix products, arithmetic and copies ran while one was open for 6% of the time, Pallas kernels for 0%

profile of v10, /device:TPU:1, one launch (start us, length us, event | category | flops | bytes accessed | tf_op | source)
XLA Modules:
  0.0 159.8 jit_solution(14219454275875789541)
XLA Ops:
  0.6 1.1 constant_dynamic-slice_fusion
  1.7 11.1 %collective-permute-start = (f32[2,128,512]{2,1,0:T(8,128)S(1)}, f32[2,128,512]{2,1,0:T(8,128)S(1)}, u32[]{:S(2)}, u32[]{:S(2)}) collective-permute-start(f32[2,128,512]{2,1,0:T(8,128)S(1)} %constant_dynamic-slice_fusion), channel_id=1, source_target_pairs={{2,0},{4,2},{6,4},{8,6},{10,8},{12,10},{14,12},{16,14},{18,16},{20... | collective-permute-start | bytes 1572872 | tf_op jit(solution)/shard_map/ppermute | solution.py:32
  12.8 10.6 %collective-permute-done.refs_7_ = f32[2,128,512]{2,1,0:T(8,128)S(1)} collective-permute-done((f32[2,128,512]{2,1,0:T(8,128)S(1)}, f32[2,128,512]{2,1,0:T(8,128)S(1)}, u32[]{:S(2)}, u32[]{:S(2)}) %collective-permute-start) | collective-permute-done | bytes 524320 | tf_op jit(solution)/shard_map/ppermute | solution.py:32
  23.4 1.5 collective-permute-start.1
  25.6 0.9 collective-permute-done.1.refs_8_
  26.5 0.8 copy-done.6
  27.3 8.8 %positions.2 = (f32[3,4,128,128]{3,2,1,0:T(8,128)}, f32[3,4,128,128]{3,2,1,0:T(8,128)}, f32[3,4,128,128]{3,2,1,0:T(8,128)}, f32[3,4,128,128]{3,2,1,0:T(8,128)}, ...) custom-call(s32[1,1,32]{2,1,0:T(1,128)} %refs_0_.3, s32[1,1,32]{2,1,0:T(1,128)} %refs_1_.3, s32[1,1]{1,0:T(1,128)S(6)} %copy.21.refs_2_, ...), custom_call_target="tpu_custom_call" | custom-call | flops 12999999488 | bytes 8388608 | tf_op jit(solution)/shard_map/positions/pallas_call | solution.py:275
  36.1 5.4 %collective-permute-start.2 = (f32[4,48,128]{2,1,0:T(8,128)}, f32[4,48,128]{2,1,0:T(8,128)S(1)}, u32[]{:S(2)}, u32[]{:S(2)}) collective-permute-start(f32[4,48,128]{2,1,0:T(8,128)} %get-tuple-element.19), channel_id=1, source_target_pairs={{0,1},{1,0},{2,3},{3,2},{4,5},{5,4},{6,7},{7,6},{8,9},{9,8},{10,11... | collective-permute-start | bytes 294920 | tf_op jit(solution)/shard_map/ppermute | solution.py:27
  41.7 0.4 collective-permute-start.13
  42.1 0.6 collective-permute-done.2
  42.7 0.9 add.202
  43.8 2.7 %collective-permute-start.5 = (f32[48,128]{1,0:T(8,128)S(1)}, f32[48,128]{1,0:T(8,128)S(1)}, u32[]{:S(2)}, u32[]{:S(2)}) collective-permute-start(f32[48,128]{1,0:T(8,128)S(1)} %get-tuple-element.56), channel_id=1, source_target_pairs={{0,6},{2,0},{4,2},{6,4},{1,7},{3,1},{5,3},{7,5},{8,14},{10,8},{12,... | collective-permute-start | bytes 73736 | tf_op jit(solution)/shard_map/ppermute | solution.py:346
  46.4 1.2 collective-permute-done.3
  47.6 3.0 %collective-permute-done.4 = f32[48,128]{1,0:T(8,128)S(1)} collective-permute-done((f32[48,128]{1,0:T(8,128)S(1)}, f32[48,128]{1,0:T(8,128)S(1)}, u32[]{:S(2)}, u32[]{:S(2)}) %collective-permute-start.4) | collective-permute-done | bytes 24608 | tf_op jit(solution)/shard_map/ppermute | solution.py:346
  50.6 1.6 %add_add_fusion.2 = (f32[3,4,128,128]{3,2,1,0:T(8,128)S(1)}, f32[3,4,128,128]{3,2,1,0:T(8,128)S(1)}) fusion(f32[3,4,128,128]{3,2,1,0:T(8,128)} %get-tuple-element.22, f32[3,4,128,128]{3,2,1,0:T(8,128)S(1)} %collective-permute-done.13, f32[128]{0:T(128)S(1)} %fusion.22, f32[3,4,128,128]{3,2,1,0:T(8,128)} %get-tuple-element.20, ...), kind=kLoop, calls=%fused_computation.4 | loop fusion | flops 786432 | bytes 4719104 | tf_op jit(solution)/shard_map/add | solution.py:370
  52.4 6.9 %collective-permute-start.15 = (f32[3,4,128,128]{3,2,1,0:T(8,128)S(1)}, f32[3,4,128,128]{3,2,1,0:T(8,128)}, u32[]{:S(2)}, u32[]{:S(2)}) collective-permute-start(f32[3,4,128,128]{3,2,1,0:T(8,128)S(1)} %get-tuple-element.24), channel_id=1, source_target_pairs={{2,0},{4,2},{6,4},{8,6},{10,8},{12,10},{14,12},{16,14},{18,16},{20... | collective-permute-start | bytes 2359304 | tf_op jit(solution)/shard_map/ppermute | solution.py:32
  59.2 4.3 %collective-permute-done.6 = f32[48,128]{1,0:T(8,128)S(1)} collective-permute-done((f32[48,128]{1,0:T(8,128)S(1)}, f32[48,128]{1,0:T(8,128)S(1)}, u32[]{:S(2)}, u32[]{:S(2)}) %collective-permute-start.6) | collective-permute-done | bytes 24608 | tf_op jit(solution)/shard_map/ppermute | solution.py:329
  63.5 5.2 %collective-permute-done.7 = f32[48,128]{1,0:T(8,128)S(1)} collective-permute-done((f32[48,128]{1,0:T(8,128)S(1)}, f32[48,128]{1,0:T(8,128)S(1)}, u32[]{:S(2)}, u32[]{:S(2)}) %collective-permute-start.7) | collective-permute-done | bytes 24608 | tf_op jit(solution)/shard_map/ppermute | solution.py:329
  68.8 0.2 copy.15
  69.0 0.2 copy.16
  69.2 1.2 copy.17
  70.5 0.2 copy.18
  70.7 5.0 %collective-permute-done.8 = f32[48,128]{1,0:T(8,128)S(1)} collective-permute-done((f32[48,128]{1,0:T(8,128)S(1)}, f32[48,128]{1,0:T(8,128)S(1)}, u32[]{:S(2)}, u32[]{:S(2)}) %collective-permute-start.8) | collective-permute-done | bytes 24608 | tf_op jit(solution)/shard_map/ppermute | solution.py:329
  75.8 1.4 collective-permute-start.9
  77.2 1.2 add.217
  78.5 0.1 collective-permute-done.11
  78.7 1.6 collective-permute-done.10
  80.3 0.5 collective-permute-done.9
  81.0 1.4 collective-permute-start.16
  82.4 1.2 add.227
  83.8 7.1 %collective-permute-start.20 = (f32[2,4,256,128]{3,2,1,0:T(8,128)S(1)}, f32[2,4,256,128]{3,2,1,0:T(8,128)S(1)}, u32[]{:S(2)}, u32[]{:S(2)}) collective-permute-start(f32[2,4,256,128]{3,2,1,0:T(8,128)S(1)} %pad_maximum_fusion.refs_6_), channel_id=1, source_target_pairs={{0,1},{1,0},{2,3},{3,2},{4,5},{5,4},{6,7},{7,6},{8,9},{9,8},{10,11... | collective-permute-start | bytes 3145736 | tf_op jit(solution)/shard_map/ppermute | solution.py:27
  90.9 3.0 %collective-permute-start.19 = (f32[192,128]{1,0:T(8,128)S(1)}, f32[192,128]{1,0:T(8,128)S(1)}, u32[]{:S(2)}, u32[]{:S(2)}) collective-permute-start(f32[192,128]{1,0:T(8,128)S(1)} %pad_maximum_fusion.4), channel_id=1, source_target_pairs={{0,1},{1,0},{2,3},{3,2},{4,5},{5,4},{6,7},{7,6},{8,9},{9,8},{10,11... | collective-permute-start | bytes 294920 | tf_op jit(solution)/shard_map/ppermute | solution.py:27
  93.9 0.9 collective-permute-done.19
  95.0 0.7 add_divide_fusion.1.refs_3_
  95.6 1.0 copy-done.5
  96.6 8.8 %positions.3 = (f32[3,4,128,128]{3,2,1,0:T(8,128)}, f32[3,4,128,128]{3,2,1,0:T(8,128)}, f32[3,4,128,128]{3,2,1,0:T(8,128)}, f32[3,4,128,128]{3,2,1,0:T(8,128)}, ...) custom-call(s32[1,1,32]{2,1,0:T(1,128)} %refs_0_.3, s32[1,1,32]{2,1,0:T(1,128)} %refs_1_.3, s32[1,1]{1,0:T(1,128)S(6)} %copy.21.refs_2_, ...), custom_call_target="tpu_custom_call" | custom-call | flops 12999999488 | bytes 8388608 | tf_op jit(solution)/shard_map/positions/pallas_call | solution.py:275
  105.5 5.4 %collective-permute-start.22 = (f32[4,48,128]{2,1,0:T(8,128)}, f32[4,48,128]{2,1,0:T(8,128)S(1)}, u32[]{:S(2)}, u32[]{:S(2)}) collective-permute-start(f32[4,48,128]{2,1,0:T(8,128)} %get-tuple-element.31), channel_id=1, source_target_pairs={{0,1},{1,0},{2,3},{3,2},{4,5},{5,4},{6,7},{7,6},{8,9},{9,8},{10,11... | collective-permute-start | bytes 294920 | tf_op jit(solution)/shard_map/ppermute | solution.py:27
  111.0 1.1 collective-permute-done.22
  112.0 0.9 add.231
  113.1 2.7 %collective-permute-start.25 = (f32[48,128]{1,0:T(8,128)S(1)}, f32[48,128]{1,0:T(8,128)S(1)}, u32[]{:S(2)}, u32[]{:S(2)}) collective-permute-start(f32[48,128]{1,0:T(8,128)S(1)} %get-tuple-element.49), channel_id=1, source_target_pairs={{0,6},{2,0},{4,2},{6,4},{1,7},{3,1},{5,3},{7,5},{8,14},{10,8},{12,... | collective-permute-start | bytes 73736 | tf_op jit(solution)/shard_map/ppermute | solution.py:346
  115.7 0.9 collective-permute-start.24
  116.7 1.0 collective-permute-start.21
  117.7 2.2 %collective-permute-done.24 = f32[48,128]{1,0:T(8,128)S(1)} collective-permute-done((f32[48,128]{1,0:T(8,128)S(1)}, f32[48,128]{1,0:T(8,128)S(1)}, u32[]{:S(2)}, u32[]{:S(2)}) %collective-permute-start.24) | collective-permute-done | bytes 24608 | tf_op jit(solution)/shard_map/ppermute | solution.py:346
  119.9 1.2 add_add_fusion
  121.3 3.9 %collective-permute-done.26 = f32[48,128]{1,0:T(8,128)S(1)} collective-permute-done((f32[48,128]{1,0:T(8,128)S(1)}, f32[48,128]{1,0:T(8,128)S(1)}, u32[]{:S(2)}, u32[]{:S(2)}) %collective-permute-start.26) | collective-permute-done | bytes 24608 | tf_op jit(solution)/shard_map/ppermute | solution.py:329
  125.2 4.8 %collective-permute-done.27 = f32[48,128]{1,0:T(8,128)S(1)} collective-permute-done((f32[48,128]{1,0:T(8,128)S(1)}, f32[48,128]{1,0:T(8,128)S(1)}, u32[]{:S(2)}, u32[]{:S(2)}) %collective-permute-start.27) | collective-permute-done | bytes 24608 | tf_op jit(solution)/shard_map/ppermute | solution.py:329
  130.0 6.9 %collective-permute-done.28 = f32[48,128]{1,0:T(8,128)S(1)} collective-permute-done((f32[48,128]{1,0:T(8,128)S(1)}, f32[48,128]{1,0:T(8,128)S(1)}, u32[]{:S(2)}, u32[]{:S(2)}) %collective-permute-start.28) | collective-permute-done | bytes 24608 | tf_op jit(solution)/shard_map/ppermute | solution.py:329
  137.0 1.4 collective-permute-start.29
  138.4 1.5 collective-permute-done.31
  139.9 1.6 collective-permute-done.30
  141.5 0.8 collective-permute-done.29
  142.3 2.4 %collective-permute-done.33 = f32[3,4,128,128]{3,2,1,0:T(8,128)S(1)} collective-permute-done((f32[3,4,128,128]{3,2,1,0:T(8,128)S(1)}, f32[3,4,128,128]{3,2,1,0:T(8,128)S(1)}, u32[]{:S(2)}, u32[]{:S(2)}) %collective-permute-start.33) | collective-permute-done | bytes 786464 | tf_op jit(solution)/shard_map/ppermute | solution.py:32
  144.7 0.1 add_add_fusion.1
  144.9 0.1 fusion.1
  145.0 0.2 copy.19
  145.2 4.2 %collective-permute-start.34 = (f32[2,128,512]{1,2,0:T(8,128)S(1)}, f32[2,128,512]{1,2,0:T(8,128)S(1)}, u32[]{:S(2)}, u32[]{:S(2)}) collective-permute-start(f32[2,128,512]{1,2,0:T(8,128)S(1)} %bitcast.56), channel_id=1, source_target_pairs={{0,1},{1,0},{2,3},{3,2},{4,5},{5,4},{6,7},{7,6},{8,9},{9,8},{10,11... | collective-permute-start | bytes 1572872 | tf_op jit(solution)/shard_map/ppermute | solution.py:27
  149.4 2.3 %collective-permute-start.37 = (f32[48,128]{1,0:T(8,128)S(1)}, f32[48,128]{1,0:T(8,128)S(1)}, u32[]{:S(2)}, u32[]{:S(2)}) collective-permute-start(f32[48,128]{1,0:T(8,128)S(1)} %add_add_fusion.4), channel_id=1, source_target_pairs={{2,0},{4,2},{6,4},{0,6},{3,1},{5,3},{7,5},{1,7},{10,8},{12,10},{14... | collective-permute-start | bytes 73736 | tf_op jit(solution)/shard_map/ppermute | solution.py:358
  151.7 0.6 collective-permute-start.35
  152.3 0.4 collective-permute-done.37
  152.6 3.2 %collective-permute-done.36 = f32[48,128]{1,0:T(8,128)S(1)} collective-permute-done((f32[48,128]{1,0:T(8,128)S(1)}, f32[48,128]{1,0:T(8,128)S(1)}, u32[]{:S(2)}, u32[]{:S(2)}) %collective-permute-start.36) | collective-permute-done | bytes 24608 | tf_op jit(solution)/shard_map/ppermute | solution.py:358
  156.0 0.1 fusion.8
  156.1 1.6 collective-permute-start.38
  157.8 1.3 copy.20
  159.2 0.7 add_divide_fusion
  (82 shorter events, 1.7 us)
Async XLA Ops:
  1.7 21.7 %collective-permute-start = (f32[2,128,512]{2,1,0:T(8,128)S(1)}, f32[2,128,512]{2,1,0:T(8,128)S(1)}, u32[]{:S(2)}, u32[]{:S(2)}) collective-permute-start(f32[2,128,512]{2,1,0:T(8,128)S(1)} %constant_dynamic-slice_fusion), channel_id=1, source_target_pairs={{2,0},{4,2},{6,4},{8,6},{10,8},{12,10},{14,12},{16,14},{18,16},{20... | collective-permute-start | bytes 1572872 | tf_op jit(solution)/shard_map/ppermute | solution.py:32
  23.4 3.1 %copy-start.3 = (f32[2,128,512]{2,1,0:T(8,128)}, f32[2,128,512]{2,1,0:T(8,128)S(1)}, u32[]{:S(2)}) copy-start(f32[2,128,512]{2,1,0:T(8,128)S(1)} %collective-permute-done.refs_7_) | copy-start | bytes 1572868
  23.4 3.1 %collective-permute-start.1 = (f32[2,128,512]{2,1,0:T(8,128)S(1)}, f32[2,128,512]{2,1,0:T(8,128)S(1)}, u32[]{:S(2)}, u32[]{:S(2)}) collective-permute-start(f32[2,128,512]{2,1,0:T(8,128)S(1)} %collective-permute-done.refs_7_), channel_id=1, source_target_pairs={{0,1},{1,0},{2,3},{3,2},{4,5},{5,4},{6,7},{7,6},{8,9},{9,8},{10,11... | collective-permute-start | bytes 1572872 | tf_op jit(solution)/shard_map/ppermute | solution.py:27
  26.5 0.8 copy-start.6
  36.1 6.6 %collective-permute-start.2 = (f32[4,48,128]{2,1,0:T(8,128)}, f32[4,48,128]{2,1,0:T(8,128)S(1)}, u32[]{:S(2)}, u32[]{:S(2)}) collective-permute-start(f32[4,48,128]{2,1,0:T(8,128)} %get-tuple-element.19), channel_id=1, source_target_pairs={{0,1},{1,0},{2,3},{3,2},{4,5},{5,4},{6,7},{7,6},{8,9},{9,8},{10,11... | collective-permute-start | bytes 294920 | tf_op jit(solution)/shard_map/ppermute | solution.py:27
  41.6 9.0 %collective-permute-start.12 = (f32[3,4,128,128]{3,2,1,0:T(8,128)}, f32[3,4,128,128]{3,2,1,0:T(8,128)S(1)}, u32[]{:S(2)}, u32[]{:S(2)}) collective-permute-start(f32[3,4,128,128]{3,2,1,0:T(8,128)} %get-tuple-element.21), channel_id=1, source_target_pairs={{0,1},{1,0},{2,3},{3,2},{4,5},{5,4},{6,7},{7,6},{8,9},{9,8},{10,11... | collective-permute-start | bytes 2359304 | tf_op jit(solution)/shard_map/ppermute | solution.py:27
  41.7 9.0 %collective-permute-start.13 = (f32[3,4,128,128]{3,2,1,0:T(8,128)}, f32[3,4,128,128]{3,2,1,0:T(8,128)S(1)}, u32[]{:S(2)}, u32[]{:S(2)}) collective-permute-start(f32[3,4,128,128]{3,2,1,0:T(8,128)} %get-tuple-element.23), channel_id=1, source_target_pairs={{0,1},{1,0},{2,3},{3,2},{4,5},{5,4},{6,7},{7,6},{8,9},{9,8},{10,11... | collective-permute-start | bytes 2359304 | tf_op jit(solution)/shard_map/ppermute | solution.py:27
  43.7 4.0 %collective-permute-start.3 = (f32[48,128]{1,0:T(8,128)S(1)}, f32[48,128]{1,0:T(8,128)S(1)}, u32[]{:S(2)}, u32[]{:S(2)}) collective-permute-start(f32[48,128]{1,0:T(8,128)S(1)} %get-tuple-element.55), channel_id=1, source_target_pairs={{0,2},{2,4},{4,6},{6,0},{1,3},{3,5},{5,7},{7,1},{8,10},{10,12},{12... | collective-permute-start | bytes 73736 | tf_op jit(solution)/shard_map/ppermute | solution.py:346
  43.8 3.9 %collective-permute-start.5 = (f32[48,128]{1,0:T(8,128)S(1)}, f32[48,128]{1,0:T(8,128)S(1)}, u32[]{:S(2)}, u32[]{:S(2)}) collective-permute-start(f32[48,128]{1,0:T(8,128)S(1)} %get-tuple-element.56), channel_id=1, source_target_pairs={{0,6},{2,0},{4,2},{6,4},{1,7},{3,1},{5,3},{7,5},{8,14},{10,8},{12,... | collective-permute-start | bytes 73736 | tf_op jit(solution)/shard_map/ppermute | solution.py:346
  46.4 4.2 %collective-permute-start.4 = (f32[48,128]{1,0:T(8,128)S(1)}, f32[48,128]{1,0:T(8,128)S(1)}, u32[]{:S(2)}, u32[]{:S(2)}) collective-permute-start(f32[48,128]{1,0:T(8,128)S(1)} %get-tuple-element.57), channel_id=1, source_target_pairs={{0,4},{2,6},{4,0},{6,2},{1,5},{3,7},{5,1},{7,3},{8,12},{10,14},{12... | collective-permute-start | bytes 73736 | tf_op jit(solution)/shard_map/ppermute | solution.py:346
  52.3 24.9 %collective-permute-start.14 = (f32[3,4,128,128]{3,2,1,0:T(8,128)S(1)}, f32[3,4,128,128]{3,2,1,0:T(8,128)}, u32[]{:S(2)}, u32[]{:S(2)}) collective-permute-start(f32[3,4,128,128]{3,2,1,0:T(8,128)S(1)} %get-tuple-element.26), channel_id=1, source_target_pairs={{254,0},{0,2},{2,4},{4,6},{6,8},{8,10},{10,12},{12,14},{14,16},{16... | collective-permute-start | bytes 2359304 | tf_op jit(solution)/shard_map/ppermute | solution.py:32
  52.4 24.8 %collective-permute-start.15 = (f32[3,4,128,128]{3,2,1,0:T(8,128)S(1)}, f32[3,4,128,128]{3,2,1,0:T(8,128)}, u32[]{:S(2)}, u32[]{:S(2)}) collective-permute-start(f32[3,4,128,128]{3,2,1,0:T(8,128)S(1)} %get-tuple-element.24), channel_id=1, source_target_pairs={{2,0},{4,2},{6,4},{8,6},{10,8},{12,10},{14,12},{16,14},{18,16},{20... | collective-permute-start | bytes 2359304 | tf_op jit(solution)/shard_map/ppermute | solution.py:32
  59.2 4.3 %collective-permute-start.6 = (f32[48,128]{1,0:T(8,128)S(1)}, f32[48,128]{1,0:T(8,128)S(1)}, u32[]{:S(2)}, u32[]{:S(2)}) collective-permute-start(f32[48,128]{1,0:T(8,128)S(1)} %fusion.14), channel_id=1, source_target_pairs={{0,32},{2,226},{4,228},{6,230},{8,232},{10,234},{12,236},{14,238},... | collective-permute-start | bytes 73736 | tf_op jit(solution)/shard_map/ppermute | solution.py:329
  63.5 5.2 %collective-permute-start.7 = (f32[48,128]{1,0:T(8,128)S(1)}, f32[48,128]{1,0:T(8,128)S(1)}, u32[]{:S(2)}, u32[]{:S(2)}) collective-permute-start(f32[48,128]{1,0:T(8,128)S(1)} %add.206), channel_id=1, source_target_pairs={{0,64},{2,194},{4,196},{6,198},{8,200},{10,202},{12,204},{14,206},... | collective-permute-start | bytes 73736 | tf_op jit(solution)/shard_map/ppermute | solution.py:329
  68.7 7.0 %collective-permute-start.8 = (f32[48,128]{1,0:T(8,128)S(1)}, f32[48,128]{1,0:T(8,128)S(1)}, u32[]{:S(2)}, u32[]{:S(2)}) collective-permute-start(f32[48,128]{1,0:T(8,128)S(1)} %add.207), channel_id=1, source_target_pairs={{0,128},{2,130},{4,132},{6,134},{8,136},{10,138},{12,140},{14,142}... | collective-permute-start | bytes 73736 | tf_op jit(solution)/shard_map/ppermute | solution.py:329
  75.7 3.0 %collective-permute-start.11 = (f32[48,128]{1,0:T(8,128)S(1)}, f32[48,128]{1,0:T(8,128)S(1)}, u32[]{:S(2)}, u32[]{:S(2)}) collective-permute-start(f32[48,128]{1,0:T(8,128)S(1)} %add.208), channel_id=1, source_target_pairs={{0,24},{8,0},{16,8},{24,16},{1,25},{9,1},{17,9},{25,17},{2,26},{10... | collective-permute-start | bytes 73736 | tf_op jit(solution)/shard_map/ppermute | solution.py:381
  75.7 4.6 %collective-permute-start.10 = (f32[48,128]{1,0:T(8,128)S(1)}, f32[48,128]{1,0:T(8,128)S(1)}, u32[]{:S(2)}, u32[]{:S(2)}) collective-permute-start(f32[48,128]{1,0:T(8,128)S(1)} %add.208), channel_id=1, source_target_pairs={{0,16},{8,24},{16,0},{24,8},{1,17},{9,25},{17,1},{25,9},{2,18},{10... | collective-permute-start | bytes 73736 | tf_op jit(solution)/shard_map/ppermute | solution.py:381
  75.8 5.0 %collective-permute-start.9 = (f32[48,128]{1,0:T(8,128)S(1)}, f32[48,128]{1,0:T(8,128)S(1)}, u32[]{:S(2)}, u32[]{:S(2)}) collective-permute-start(f32[48,128]{1,0:T(8,128)S(1)} %add.208), channel_id=1, source_target_pairs={{0,8},{8,16},{16,24},{24,0},{1,9},{9,17},{17,25},{25,1},{2,10},{10... | collective-permute-start | bytes 73736 | tf_op jit(solution)/shard_map/ppermute | solution.py:381
  80.8 10.1 %collective-permute-start.18 = (f32[48,128]{1,0:T(8,128)S(1)}, f32[48,128]{1,0:T(8,128)S(1)}, u32[]{:S(2)}, u32[]{:S(2)}) collective-permute-start(f32[48,128]{1,0:T(8,128)S(1)} %add_add_fusion.5), channel_id=1, source_target_pairs={{2,0},{4,2},{6,4},{0,6},{3,1},{5,3},{7,5},{1,7},{10,8},{12,10},{14... | collective-permute-start | bytes 73736 | tf_op jit(solution)/shard_map/ppermute | solution.py:358
  80.9 10.0 %collective-permute-start.17 = (f32[48,128]{1,0:T(8,128)S(1)}, f32[48,128]{1,0:T(8,128)S(1)}, u32[]{:S(2)}, u32[]{:S(2)}) collective-permute-start(f32[48,128]{1,0:T(8,128)S(1)} %add_add_fusion.5), channel_id=1, source_target_pairs={{4,0},{6,2},{0,4},{2,6},{5,1},{7,3},{1,5},{3,7},{12,8},{14,10},{8,... | collective-permute-start | bytes 73736 | tf_op jit(solution)/shard_map/ppermute | solution.py:358
  81.0 9.9 %collective-permute-start.16 = (f32[48,128]{1,0:T(8,128)S(1)}, f32[48,128]{1,0:T(8,128)S(1)}, u32[]{:S(2)}, u32[]{:S(2)}) collective-permute-start(f32[48,128]{1,0:T(8,128)S(1)} %add_add_fusion.5), channel_id=1, source_target_pairs={{6,0},{0,2},{2,4},{4,6},{7,1},{1,3},{3,5},{5,7},{14,8},{8,10},{10,... | collective-permute-start | bytes 73736 | tf_op jit(solution)/shard_map/ppermute | solution.py:358
  83.7 11.3 %copy-start.4 = (f32[2,128,128]{2,1,0:T(8,128)S(1)}, f32[2,128,128]{2,1,0:T(8,128)}, u32[]{:S(2)}) copy-start(f32[2,128,128]{2,1,0:T(8,128)} %refs_3_.1) | copy-start | bytes 393220
  83.8 11.9 %copy-start = (f32[2,4,256,128]{3,2,1,0:T(8,128)}, f32[2,4,256,128]{3,2,1,0:T(8,128)S(1)}, u32[]{:S(2)}) copy-start(f32[2,4,256,128]{3,2,1,0:T(8,128)S(1)} %pad_maximum_fusion.refs_6_) | copy-start | bytes 3145732
  83.8 11.9 %collective-permute-start.20 = (f32[2,4,256,128]{3,2,1,0:T(8,128)S(1)}, f32[2,4,256,128]{3,2,1,0:T(8,128)S(1)}, u32[]{:S(2)}, u32[]{:S(2)}) collective-permute-start(f32[2,4,256,128]{3,2,1,0:T(8,128)S(1)} %pad_maximum_fusion.refs_6_), channel_id=1, source_target_pairs={{0,1},{1,0},{2,3},{3,2},{4,5},{5,4},{6,7},{7,6},{8,9},{9,8},{10,11... | collective-permute-start | bytes 3145736 | tf_op jit(solution)/shard_map/ppermute | solution.py:27
  90.9 4.0 %collective-permute-start.19 = (f32[192,128]{1,0:T(8,128)S(1)}, f32[192,128]{1,0:T(8,128)S(1)}, u32[]{:S(2)}, u32[]{:S(2)}) collective-permute-start(f32[192,128]{1,0:T(8,128)S(1)} %pad_maximum_fusion.4), channel_id=1, source_target_pairs={{0,1},{1,0},{2,3},{3,2},{4,5},{5,4},{6,7},{7,6},{8,9},{9,8},{10,11... | collective-permute-start | bytes 294920 | tf_op jit(solution)/shard_map/ppermute | solution.py:27
  95.6 1.0 copy-start.5
  105.5 39.2 %copy-start.1 = (f32[3,4,128,128]{3,2,1,0:T(8,128)S(1)}, f32[3,4,128,128]{3,2,1,0:T(8,128)}, u32[]{:S(2)}) copy-start(f32[3,4,128,128]{3,2,1,0:T(8,128)} %get-tuple-element.28) | copy-start | bytes 2359300
  105.5 6.6 %collective-permute-start.22 = (f32[4,48,128]{2,1,0:T(8,128)}, f32[4,48,128]{2,1,0:T(8,128)S(1)}, u32[]{:S(2)}, u32[]{:S(2)}) collective-permute-start(f32[4,48,128]{2,1,0:T(8,128)} %get-tuple-element.31), channel_id=1, source_target_pairs={{0,1},{1,0},{2,3},{3,2},{4,5},{5,4},{6,7},{7,6},{8,9},{9,8},{10,11... | collective-permute-start | bytes 294920 | tf_op jit(solution)/shard_map/ppermute | solution.py:27
  110.9 9.0 %collective-permute-start.32 = (f32[3,4,128,128]{3,2,1,0:T(8,128)}, f32[3,4,128,128]{3,2,1,0:T(8,128)S(1)}, u32[]{:S(2)}, u32[]{:S(2)}) collective-permute-start(f32[3,4,128,128]{3,2,1,0:T(8,128)} %get-tuple-element.33), channel_id=1, source_target_pairs={{0,1},{1,0},{2,3},{3,2},{4,5},{5,4},{6,7},{7,6},{8,9},{9,8},{10,11... | collective-permute-start | bytes 2359304 | tf_op jit(solution)/shard_map/ppermute | solution.py:27
  113.0 4.7 %collective-permute-start.23 = (f32[48,128]{1,0:T(8,128)S(1)}, f32[48,128]{1,0:T(8,128)S(1)}, u32[]{:S(2)}, u32[]{:S(2)}) collective-permute-start(f32[48,128]{1,0:T(8,128)S(1)} %get-tuple-element.48), channel_id=1, source_target_pairs={{0,2},{2,4},{4,6},{6,0},{1,3},{3,5},{5,7},{7,1},{8,10},{10,12},{12... | collective-permute-start | bytes 73736 | tf_op jit(solution)/shard_map/ppermute | solution.py:346
  113.1 4.6 %collective-permute-start.25 = (f32[48,128]{1,0:T(8,128)S(1)}, f32[48,128]{1,0:T(8,128)S(1)}, u32[]{:S(2)}, u32[]{:S(2)}) collective-permute-start(f32[48,128]{1,0:T(8,128)S(1)} %get-tuple-element.49), channel_id=1, source_target_pairs={{0,6},{2,0},{4,2},{6,4},{1,7},{3,1},{5,3},{7,5},{8,14},{10,8},{12,... | collective-permute-start | bytes 73736 | tf_op jit(solution)/shard_map/ppermute | solution.py:346
  115.7 4.2 %collective-permute-start.24 = (f32[48,128]{1,0:T(8,128)S(1)}, f32[48,128]{1,0:T(8,128)S(1)}, u32[]{:S(2)}, u32[]{:S(2)}) collective-permute-start(f32[48,128]{1,0:T(8,128)S(1)} %get-tuple-element.50), channel_id=1, source_target_pairs={{0,4},{2,6},{4,0},{6,2},{1,5},{3,7},{5,1},{7,3},{8,12},{10,14},{12... | collective-permute-start | bytes 73736 | tf_op jit(solution)/shard_map/ppermute | solution.py:346
  116.7 25.6 %collective-permute-start.21 = (f32[3,4,128,128]{3,2,1,0:T(8,128)}, f32[3,4,128,128]{3,2,1,0:T(8,128)S(1)}, u32[]{:S(2)}, u32[]{:S(2)}) collective-permute-start(f32[3,4,128,128]{3,2,1,0:T(8,128)} %get-tuple-element.29), channel_id=1, source_target_pairs={{0,1},{1,0},{2,3},{3,2},{4,5},{5,4},{6,7},{7,6},{8,9},{9,8},{10,11... | collective-permute-start | bytes 2359304 | tf_op jit(solution)/shard_map/ppermute | solution.py:27
  121.2 23.5 %collective-permute-start.33 = (f32[3,4,128,128]{3,2,1,0:T(8,128)S(1)}, f32[3,4,128,128]{3,2,1,0:T(8,128)S(1)}, u32[]{:S(2)}, u32[]{:S(2)}) collective-permute-start(f32[3,4,128,128]{3,2,1,0:T(8,128)S(1)} %add_add_fusion), channel_id=1, source_target_pairs={{254,0},{0,2},{2,4},{4,6},{6,8},{8,10},{10,12},{12,14},{14,16},{16... | collective-permute-start | bytes 2359304 | tf_op jit(solution)/shard_map/ppermute | solution.py:32
  121.3 4.0 %collective-permute-start.26 = (f32[48,128]{1,0:T(8,128)S(1)}, f32[48,128]{1,0:T(8,128)S(1)}, u32[]{:S(2)}, u32[]{:S(2)}) collective-permute-start(f32[48,128]{1,0:T(8,128)S(1)} %fusion.11), channel_id=1, source_target_pairs={{0,32},{2,226},{4,228},{6,230},{8,232},{10,234},{12,236},{14,238},... | collective-permute-start | bytes 73736 | tf_op jit(solution)/shard_map/ppermute | solution.py:329
  125.2 4.8 %collective-permute-start.27 = (f32[48,128]{1,0:T(8,128)S(1)}, f32[48,128]{1,0:T(8,128)S(1)}, u32[]{:S(2)}, u32[]{:S(2)}) collective-permute-start(f32[48,128]{1,0:T(8,128)S(1)} %add.235), channel_id=1, source_target_pairs={{0,64},{2,194},{4,196},{6,198},{8,200},{10,202},{12,204},{14,206},... | collective-permute-start | bytes 73736 | tf_op jit(solution)/shard_map/ppermute | solution.py:329
  130.0 6.9 %collective-permute-start.28 = (f32[48,128]{1,0:T(8,128)S(1)}, f32[48,128]{1,0:T(8,128)S(1)}, u32[]{:S(2)}, u32[]{:S(2)}) collective-permute-start(f32[48,128]{1,0:T(8,128)S(1)} %add.236), channel_id=1, source_target_pairs={{0,128},{2,130},{4,132},{6,134},{8,136},{10,138},{12,140},{14,142}... | collective-permute-start | bytes 73736 | tf_op jit(solution)/shard_map/ppermute | solution.py:329
  136.9 3.0 %collective-permute-start.31 = (f32[48,128]{1,0:T(8,128)S(1)}, f32[48,128]{1,0:T(8,128)S(1)}, u32[]{:S(2)}, u32[]{:S(2)}) collective-permute-start(f32[48,128]{1,0:T(8,128)S(1)} %add.237), channel_id=1, source_target_pairs={{0,24},{8,0},{16,8},{24,16},{1,25},{9,1},{17,9},{25,17},{2,26},{10... | collective-permute-start | bytes 73736 | tf_op jit(solution)/shard_map/ppermute | solution.py:381
  136.9 4.6 %collective-permute-start.30 = (f32[48,128]{1,0:T(8,128)S(1)}, f32[48,128]{1,0:T(8,128)S(1)}, u32[]{:S(2)}, u32[]{:S(2)}) collective-permute-start(f32[48,128]{1,0:T(8,128)S(1)} %add.237), channel_id=1, source_target_pairs={{0,16},{8,24},{16,0},{24,8},{1,17},{9,25},{17,1},{25,9},{2,18},{10... | collective-permute-start | bytes 73736 | tf_op jit(solution)/shard_map/ppermute | solution.py:381
  137.0 5.3 %collective-permute-start.29 = (f32[48,128]{1,0:T(8,128)S(1)}, f32[48,128]{1,0:T(8,128)S(1)}, u32[]{:S(2)}, u32[]{:S(2)}) collective-permute-start(f32[48,128]{1,0:T(8,128)S(1)} %add.237), channel_id=1, source_target_pairs={{0,8},{8,16},{16,24},{24,0},{1,9},{9,17},{17,25},{25,1},{2,10},{10... | collective-permute-start | bytes 73736 | tf_op jit(solution)/shard_map/ppermute | solution.py:381
  145.2 10.7 %collective-permute-start.34 = (f32[2,128,512]{1,2,0:T(8,128)S(1)}, f32[2,128,512]{1,2,0:T(8,128)S(1)}, u32[]{:S(2)}, u32[]{:S(2)}) collective-permute-start(f32[2,128,512]{1,2,0:T(8,128)S(1)} %bitcast.56), channel_id=1, source_target_pairs={{0,1},{1,0},{2,3},{3,2},{4,5},{5,4},{6,7},{7,6},{8,9},{9,8},{10,11... | collective-permute-start | bytes 1572872 | tf_op jit(solution)/shard_map/ppermute | solution.py:27
  149.4 3.2 %collective-permute-start.37 = (f32[48,128]{1,0:T(8,128)S(1)}, f32[48,128]{1,0:T(8,128)S(1)}, u32[]{:S(2)}, u32[]{:S(2)}) collective-permute-start(f32[48,128]{1,0:T(8,128)S(1)} %add_add_fusion.4), channel_id=1, source_target_pairs={{2,0},{4,2},{6,4},{0,6},{3,1},{5,3},{7,5},{1,7},{10,8},{12,10},{14... | collective-permute-start | bytes 73736 | tf_op jit(solution)/shard_map/ppermute | solution.py:358
  151.7 4.2 %collective-permute-start.36 = (f32[48,128]{1,0:T(8,128)S(1)}, f32[48,128]{1,0:T(8,128)S(1)}, u32[]{:S(2)}, u32[]{:S(2)}) collective-permute-start(f32[48,128]{1,0:T(8,128)S(1)} %add_add_fusion.4), channel_id=1, source_target_pairs={{4,0},{6,2},{0,4},{2,6},{5,1},{7,3},{1,5},{3,7},{12,8},{14,10},{8,... | collective-permute-start | bytes 73736 | tf_op jit(solution)/shard_map/ppermute | solution.py:358
  151.7 4.2 %collective-permute-start.35 = (f32[48,128]{1,0:T(8,128)S(1)}, f32[48,128]{1,0:T(8,128)S(1)}, u32[]{:S(2)}, u32[]{:S(2)}) collective-permute-start(f32[48,128]{1,0:T(8,128)S(1)} %add_add_fusion.4), channel_id=1, source_target_pairs={{6,0},{0,2},{2,4},{4,6},{7,1},{1,3},{3,5},{5,7},{14,8},{8,10},{10,... | collective-permute-start | bytes 73736 | tf_op jit(solution)/shard_map/ppermute | solution.py:358
  156.1 3.0 %collective-permute-start.38 = (f32[192,128]{1,0:T(8,128)S(1)}, f32[192,128]{1,0:T(8,128)S(1)}, u32[]{:S(2)}, u32[]{:S(2)}) collective-permute-start(f32[192,128]{1,0:T(8,128)S(1)} %maximum_add_fusion), channel_id=1, source_target_pairs={{0,1},{1,0},{2,3},{3,2},{4,5},{5,4},{6,7},{7,6},{8,9},{9,8},{10,11... | collective-permute-start | bytes 294920 | tf_op jit(solution)/shard_map/ppermute | solution.py:27
  157.7 1.4 copy-start.2
